TPU v7x, 128 devices: a whole 4x4x4 slice. The times are simulated.
128 devices in a mesh: row: 16 (over x, y), col: 8 (over z, core).
Axes of the slice: x: 4, y: 4, z: 4, core: 2. Of those that a mesh axis runs over, the one named last changes fastest.
Arguments:
- feats: bfloat16 [65536, 512], P('row', 'col'), may hold values from -6 to 6
- weight: bfloat16 [512, 512], replicated, may hold values from -0.25 to 0.25
- tile_vals: bfloat16 [2048, 256, 256], P('row'), may hold values from 0 to 1
- tile_rows: int32 [2048], P('row'), may hold values from 0 to 255, as said below
- tile_cols: int32 [2048], P('row'), may hold values from 0 to 255, as said below
- tile_nnz: int32 [2048], P('row'), may hold values from 0 to 65536, as said below
- cotangent: bfloat16 [65536, 512], P('row', 'col'), may hold values from -6 to 6
Outputs:
- hidden: bfloat16 [65536, 512], P('row', 'col')
- grad_weight: float32 [512, 512], P('row', 'col')
- grad_feats: bfloat16 [65536, 512], P('row', 'col')
Inputs may be any that keep to these rules, and one draw needn't show every extreme that they name: `tile_rows`: the tile slots of one index of row name only that index's 16 row blocks, each by 8 slots. `tile_cols`: of the tile slots of one index of row, at most 8 name column blocks of any one index of row (blocks i * 16 to (i + 1) * 16 - 1 belong to index i). `tile_nnz`: 0 marks an empty slot; every row block has at least one slot that is not empty.
All inputs are finite; a program needn't handle non-finite values.
Results may differ from a plain program's by a relative error of at most 0.023.
Values may be sent and summed in bfloat16 or wider, within the bound.
No kernel may reach another device: no remote copies, remote signals or barrier semaphores. Data moves between devices by JAX's collectives and lax.ppermute only.
A program may use at most 128 MiB of HBM per device.

v0:
```python
import jax
import jax.numpy as jnp
from jax import lax
from jax.sharding import PartitionSpec as P

BLK = 256


highest = lax.Precision.HIGHEST


def body(feats, weight, tile_vals, tile_rows, tile_cols, tile_nnz, cotangent):
    node_rows, col_width = feats.shape
    block_count = node_rows // BLK
    row_count = lax.axis_size("row")
    row_index = lax.axis_index("row")
    col_index = lax.axis_index("col")
    total_blocks = block_count * row_count
    alive_mask = (tile_nnz > 0).astype(jnp.float32)
    local_rows = tile_rows - row_index * block_count
    row_select = (local_rows[None, :] == jnp.arange(block_count, dtype=jnp.int32)[:, None]).astype(
        jnp.float32
    ) * alive_mask[None, :]
    row_sums = jnp.sum(tile_vals, axis=2, dtype=jnp.float32)
    degree = 1.0 + jnp.dot(row_select, row_sums, precision=highest)
    row_scale = lax.rsqrt(degree).reshape(node_rows, 1)
    all_feats = lax.all_gather(feats, "row", axis=0, tiled=True)
    source_blocks = all_feats.reshape(total_blocks, BLK, col_width)[tile_cols]
    tile_terms = jnp.einsum(
        "tij,tjk->tik", tile_vals, source_blocks, preferred_element_type=jnp.float32
    )
    spread = jnp.einsum("bt,tik->bik", row_select, tile_terms, precision=highest).reshape(
        node_rows, col_width
    )
    mixed = (feats.astype(jnp.float32) + row_scale * spread).astype(jnp.bfloat16)
    mixed_full = lax.all_gather(mixed, "col", axis=1, tiled=True)
    weight_cols = lax.dynamic_slice_in_dim(weight, col_index * col_width, col_width, 1)
    pre = jnp.dot(mixed_full, weight_cols, preferred_element_type=jnp.float32)
    hidden = jax.nn.gelu(pre, approximate=True).astype(jnp.bfloat16)
    _, pullback = jax.vjp(lambda value: jax.nn.gelu(value, approximate=True), pre)
    grad_pre = pullback(cotangent.astype(jnp.float32))[0].astype(jnp.bfloat16)
    weight_part = jnp.dot(mixed_full.T, grad_pre, preferred_element_type=jnp.float32)
    grad_weight = lax.psum_scatter(
        weight_part.astype(jnp.bfloat16), "row", scatter_dimension=0, tiled=True
    ).astype(jnp.float32)
    grad_mixed = (
        lax.psum_scatter(
            lax.dot_general(
                weight_cols, grad_pre, (((1,), (1,)), ((), ())), preferred_element_type=jnp.float32
            ).astype(jnp.bfloat16),
            "col",
            scatter_dimension=0,
            tiled=True,
        )
        .astype(jnp.float32)
        .T
    )
    scaled_grad = (row_scale * grad_mixed).astype(jnp.bfloat16).reshape(block_count, BLK, col_width)
    picked_blocks = scaled_grad[local_rows]
    adjoint_terms = jnp.einsum(
        "tij,tik->tjk", tile_vals, picked_blocks, preferred_element_type=jnp.float32
    )
    col_select = (tile_cols[None, :] == jnp.arange(total_blocks, dtype=jnp.int32)[:, None]).astype(
        jnp.float32
    ) * alive_mask[None, :]
    summed = jnp.einsum("bt,tjk->bjk", col_select, adjoint_terms, precision=highest)
    back = lax.psum_scatter(
        summed.reshape(lax.axis_size("row") * node_rows, col_width).astype(jnp.bfloat16),
        "row",
        scatter_dimension=0,
        tiled=True,
    ).astype(jnp.float32)
    grad_feats = (grad_mixed + back).astype(jnp.bfloat16)
    return (hidden, grad_weight, grad_feats)


def solution(mesh):
    placed = (
        P("row", "col"),
        P(),
        P("row", None, None),
        P("row"),
        P("row"),
        P("row"),
        P("row", "col"),
    )
    return jax.shard_map(
        body,
        mesh=mesh,
        in_specs=placed,
        out_specs=(P("row", "col"), P("row", "col"), P("row", "col")),
        check_vma=False,
    )
```

profile of v0, /device:TPU:0, one launch (start us, length us, event | category | flops | bytes accessed | tf_op | source)
XLA Modules:
  0.0 372.2 jit_solution(3916679451612586570)
XLA Ops:
  7.2 0.0 copy-start
  7.2 0.0 all-gather.3.cloned.1.call-start
  7.2 0.7 all-gather.3.cloned.1.call-update
  7.9 0.0 all-gather.5.cloned.1.call-start
  8.0 0.7 compare_convert_fusion
  8.6 0.7 compare_select_fusion
  9.3 0.0 copy-start.5
  9.3 7.6 %convert_reduce_fusion = f32[128,256]{1,0:T(8,128)S(1)} fusion(bf16[128,256,256]{2,1,0:T(8,128)(2,1)} %param.9), kind=kLoop, calls=%fused_computation.2 | loop fusion | flops 16744448 | bytes 16908288 | tf_op jit(solution)/shard_map/reduce_sum | solution.py:24
  16.9 0.2 fusion.8
  17.1 0.0 copy-done.5
  17.1 66.2 %all-gather.3.cloned.1.call-done = bf16[65536,64]{0,1:T(8,128)(2,1)} async-done(((bf16[4096,64]{0,1:T(8,128)(2,1)}), bf16[65536,64]{0,1:T(8,128)(2,1)}) %all-gather.3.cloned.1.call-update) | async-done | bytes 8388624 | tf_op jit(solution)/shard_map/all_gather | solution.py:27
  83.3 7.8 %copy.28 = bf16[8,256,8,256]{3,2,0,1:T(8,128)(2,1)} copy(bf16[8,256,8,256]{3,2,1,0:T(8,128)(2,1)} %bitcast.47) | data formatting | bytes 16777216 | tf_op jit(solution)/shard_map/reshape | solution.py:28
  91.1 6.2 %gather_fusion = bf16[128,256,64]{1,2,0:T(8,128)(2,1)} fusion(bf16[256,256,64]{1,2,0:T(8,128)(2,1)} %bitcast.44, s32[1024]{0:T(1024)S(1)} %pad_clamp_fusion.1), kind=kCustom, calls=%fused_computation | custom fusion | bytes 8389120 | tf_op jit(solution)/shard_map/gather | solution.py:28
  97.3 12.7 %convolution_bitcast_fusion.1 = f32[128,256,64]{1,2,0:T(8,128)} fusion(bf16[128,256,64]{1,2,0:T(8,128)(2,1)} %gather_fusion, bf16[128,256,256]{2,1,0:T(8,128)(2,1)} %param.9), kind=kOutput, calls=%fused_computation.11 | convolution fusion | flops 1073741824 | bytes 29360128 | tf_op jit(solution)/shard_map/tij,tjk->tik/dot_general | solution.py:29
  110.0 0.0 copy-start.3
  110.0 12.3 %fusion.2 = f32[16,256,64]{1,0,2:T(8,128)S(1)} fusion(f32[128,256,64]{1,2,0:T(8,128)} %convolution_bitcast_fusion.1, f32[128]{0:T(128)S(1)} %compare_convert_fusion, s32[128]{0:T(128)S(1)} %get-tuple-element.4), kind=kOutput, calls=%fused_computation.6 | convolution fusion | flops 402657280 | bytes 9438208 | tf_op jit(solution)/shard_map/bt,tik->bik/dot_general | solution.py:32
  122.3 0.0 copy-start.4
  122.3 0.6 copy.18
  123.0 0.0 copy-done.3
  123.0 0.9 add_convert_fusion
  123.9 0.0 all-gather.5.cloned.1.call-update
  123.9 0.2 reduce-scatter.6.cloned.1.call-start
  124.2 32.0 %all-gather.5.cloned.1.call-done = bf16[4096,512]{0,1:T(8,128)(2,1)} async-done(((bf16[4096,64]{0,1:T(8,128)(2,1)}), bf16[4096,512]{0,1:T(8,128)(2,1)}) %all-gather.5.cloned.1.call-update) | async-done | bytes 4194320 | tf_op jit(solution)/shard_map/all_gather | solution.py:36
  156.1 0.0 copy-done
  156.1 4.1 %multiply_convert_fusion = (bf16[4096,64]{0,1:T(8,128)(2,1)}, f32[4096,64]{0,1:T(8,128)S(1)}) fusion(bf16[4096,512]{0,1:T(8,128)(2,1)} %all-gather.5.cloned.1.call-done, bf16[512,512]{1,0:T(8,128)(2,1)S(1)} %copy-done, s32[]{:T(128)S(6)} %select_n.10), kind=kOutput, calls=%fused_computation.34 | convolution fusion | flops 270794752 | bytes 5898244 | tf_op jit(solution)/shard_map/dot_general | solution.py:38
  160.2 0.0 copy-done.4
  160.2 3.3 convolution_convert_fusion
  163.5 0.0 reduce-scatter.6.cloned.1.call-update
  163.6 0.0 reduce-scatter.4.cloned.1.call-start
  163.6 4.2 %convolution_convert_fusion.1 = bf16[512,64]{1,0:T(8,128)(2,1)} fusion(bf16[4096,512]{0,1:T(8,128)(2,1)} %all-gather.5.cloned.1.call-done, bf16[4096,64]{0,1:T(8,128)(2,1)S(1)} %copy-done.4, f32[4096,64]{0,1:T(8,128)S(1)} %get-tuple-element.6), kind=kOutput, calls=%fused_computation.16 | convolution fusion | flops 273973248 | bytes 5832704 | tf_op jit(solution)/shard_map/dot_general | solution.py:42
  167.8 0.0 reduce-scatter.4.cloned.1.call-update
  167.9 0.0 reduce-scatter.8.cloned.1.call-start
  167.9 33.8 %reduce-scatter.6.cloned.1.call-done = bf16[64,4096]{1,0:T(8,128)(2,1)} async-done(((bf16[512,4096]{1,0:T(8,128)(2,1)}), bf16[64,4096]{1,0:T(8,128)(2,1)}) %reduce-scatter.6.cloned.1.call-update) | async-done | bytes 524304 | tf_op jit(solution)/shard_map/reduce_scatter | solution.py:47
  201.7 1.1 fusion.19
  202.9 2.8 gather_fusion.1
  205.7 10.1 %convolution_bitcast_fusion = f32[128,256,64]{1,2,0:T(8,128)S(1)} fusion(bf16[128,256,64]{1,2,0:T(8,128)(2,1)} %gather_fusion.1, bf16[128,256,256]{2,1,0:T(8,128)(2,1)} %param.9), kind=kOutput, calls=%fused_computation.10 | convolution fusion | flops 1073741824 | bytes 29360128 | tf_op jit(solution)/shard_map/tij,tik->tjk/dot_general | solution.py:60
  215.7 22.7 %fusion.4 = bf16[256,256,64]{1,0,2:T(8,128)(2,1)} fusion(f32[128,256,64]{1,2,0:T(8,128)S(1)} %convolution_bitcast_fusion, f32[128]{0:T(128)S(1)} %compare_convert_fusion, s32[128]{0:T(128)S(1)} %copy-done.5), kind=kOutput, calls=%fused_computation.8 | convolution fusion | flops 6446710784 | bytes 16778240 | tf_op jit(solution)/shard_map/bt,tjk->bjk/dot_general | solution.py:66
  238.4 0.0 copy-start.1
  238.4 11.8 %copy.19 = bf16[8,8,256,256]{3,1,2,0:T(8,128)(2,1)} copy(bf16[8,8,256,256]{3,2,1,0:T(8,128)(2,1)} %bitcast.46) | data formatting | bytes 16777216
  250.3 0.0 copy-start.2
  250.3 0.0 reduce-scatter.8.cloned.1.call-update
  250.3 25.5 %reduce-scatter.4.cloned.1.call-done = bf16[32,64]{1,0:T(8,128)(2,1)} async-done(((bf16[512,64]{1,0:T(8,128)(2,1)}), bf16[32,64]{1,0:T(8,128)(2,1)}) %reduce-scatter.4.cloned.1.call-update) | async-done | bytes 4112 | tf_op jit(solution)/shard_map/reduce_scatter | solution.py:43
  275.8 1.3 convert_element_type.56
  277.1 86.6 %reduce-scatter.8.cloned.1.call-done = bf16[4096,64]{0,1:T(8,128)(2,1)} async-done(((bf16[65536,64]{0,1:T(8,128)(2,1)}), bf16[4096,64]{0,1:T(8,128)(2,1)}) %reduce-scatter.8.cloned.1.call-update) | async-done | bytes 524304 | tf_op jit(solution)/shard_map/reduce_scatter | solution.py:67
  363.7 0.0 copy-done.2
  363.7 2.0 fusion.20
  365.7 0.0 copy-done.1
  (5 shorter events, 0.1 us)
Async XLA Ops:
  7.2 149.0 %copy-start = (bf16[512,512]{1,0:T(8,128)(2,1)S(1)}, bf16[512,512]{1,0:T(8,128)(2,1)}, u32[]{:S(2)}) copy-start(bf16[512,512]{1,0:T(8,128)(2,1)} %param.8) | copy-start | bytes 1572868
  7.2 76.1 %all-gather.3.cloned.1.call-start = ((), (), s32[]{:S(2)}) async-start(), calls=%async_computation.3 | async-start | bytes 8912896 | tf_op jit(solution)/shard_map/all_gather | solution.py:27
  7.9 148.2 %all-gather.5.cloned.1.call-start = ((), (), s32[]{:S(2)}) async-start(), calls=%async_computation.4 | async-start | bytes 4718592 | tf_op jit(solution)/shard_map/all_gather | solution.py:36
  9.3 7.8 %copy-start.5 = (s32[128]{0:T(128)S(1)}, s32[128]{0:T(128)}, u32[]{:S(2)}) copy-start(s32[128]{0:T(128)} %param.11) | copy-start | bytes 1540
  110.0 13.0 %copy-start.3 = (bf16[4096,64]{0,1:T(8,128)(2,1)S(1)}, bf16[4096,64]{0,1:T(8,128)(2,1)}, u32[]{:S(2)}) copy-start(bf16[4096,64]{0,1:T(8,128)(2,1)} %param.7) | copy-start | bytes 1572868
  122.3 37.9 %copy-start.4 = (bf16[4096,64]{0,1:T(8,128)(2,1)S(1)}, bf16[4096,64]{0,1:T(8,128)(2,1)}, u32[]{:S(2)}) copy-start(bf16[4096,64]{0,1:T(8,128)(2,1)} %param.13) | copy-start | bytes 1572868
  123.9 77.8 %reduce-scatter.6.cloned.1.call-start = ((), (), s32[]{:S(2)}) async-start(), calls=%async_computation.6 | async-start | bytes 4718592 | tf_op jit(solution)/shard_map/reduce_scatter | solution.py:47
  163.6 112.3 %reduce-scatter.4.cloned.1.call-start = ((), (), s32[]{:S(2)}) async-start(), calls=%async_computation.5 | async-start | bytes 139264 | tf_op jit(solution)/shard_map/reduce_scatter | solution.py:43
  167.9 195.8 %reduce-scatter.8.cloned.1.call-start = ((), (), s32[]{:S(2)}) async-start(), calls=%async_computation.7 | async-start | bytes 8912896 | tf_op jit(solution)/shard_map/reduce_scatter | solution.py:67
  238.4 127.2 %copy-start.1 = (bf16[512,512]{1,0:T(8,128)(2,1)S(1)}, bf16[512,512]{1,0:T(8,128)(2,1)}, u32[]{:S(2)}) copy-start(bf16[512,512]{1,0:T(8,128)(2,1)} %param.8) | copy-start | bytes 1572868
  250.3 113.4 %copy-start.2 = (bf16[64,4096]{1,0:T(8,128)(2,1)S(1)}, bf16[64,4096]{1,0:T(8,128)(2,1)}, u32[]{:S(2)}) copy-start(bf16[64,4096]{1,0:T(8,128)(2,1)} %reduce-scatter.6.cloned.1.call-done) | copy-start | bytes 1572868
Sparse Core Ops, SparseCore 0:
  10.2 73.0 all-gather.2
  124.1 32.0 all-gather.4
  163.7 37.9 reduce-scatter.5
  205.3 70.4 reduce-scatter.3
  279.5 84.1 reduce-scatter.7
where the time goes:
time: 373 us; the launch traced here: 372 us
  waiting for transfers between devices  245 us (66%)
  matrix products  69.6 us (19%)
  local copies, waits for them, and re-layouts  29.2 us (8%)
  other arithmetic  14.2 us (4%)
  between operations  13.9 us (4%)
    reduce_scatter x1, waiting for transfers between devices, body(): lax.psum_scatter(summed.reshape(lax.axis_size('row') * node_rows, col_wid...  86.6 us
    all_gather x1, waiting for transfers between devices, body(): all_feats = lax.all_gather(feats, 'row', axis=0, tiled=True)  66.2 us
    reduce_scatter x1, waiting for transfers between devices, body(): lax.psum_scatter(lax.dot_general(weight_cols, grad_pre, (((1,), (1,)), ((...  33.8 us
    all_gather x1, waiting for transfers between devices, body(): mixed_full = lax.all_gather(mixed, 'col', axis=1, tiled=True)  32 us
    reduce_scatter x1, waiting for transfers between devices, body(): lax.psum_scatter(weight_part.astype(jnp.bfloat16), 'row', scatter_dimensi...  25.5 us
    dot_general x1, matrix products, body(): jnp.einsum('bt,tjk->bjk', col_select, adjoint_terms, precision=highest)  22.7 us
    dot_general x1, matrix products, body(): jnp.einsum('tij,tjk->tik', tile_vals, source_blocks, preferred_element_ty...  12.7 us
    unnamed x15, local copies, waits for them, and re-layouts  12.5 us
  transfers between devices with their start and end apart: 5, of which 5 were waited for; matrix products, arithmetic and copies ran while one was open for 17% of the time, Pallas kernels for 0%

commit v1 on v0

v1 whole, which is shorter than its diff:
```python
import functools

import jax
import jax.numpy as jnp
from jax import lax
from jax.experimental import pallas as pl
from jax.experimental.pallas import tpu as pltpu
from jax.sharding import PartitionSpec as P

BLK = 256
SLOTS = 8
VMEM_LIMIT = 48 * 1024 * 1024
GELU_C = 0.7978845608028654
GELU_A = 0.044715


def params():
    return pltpu.CompilerParams(vmem_limit_bytes=VMEM_LIMIT)


def gather_kernel(req, feats_ref, out_ref):
    i = pl.program_id(0)
    width = feats_ref.shape[0]
    for s in range(SLOTS):
        start = pl.multiple_of(req[i * SLOTS + s] * BLK, BLK)
        out_ref[0, s * width : (s + 1) * width, :] = feats_ref[:, pl.ds(start, BLK)]


def gather_blocks(req, feats_t):
    width, nodes = feats_t.shape
    peers = req.shape[0] // SLOTS
    return pl.pallas_call(
        gather_kernel,
        out_shape=jax.ShapeDtypeStruct((peers, SLOTS * width, BLK), jnp.bfloat16),
        grid_spec=pltpu.PrefetchScalarGridSpec(
            num_scalar_prefetch=1,
            grid=(peers,),
            in_specs=[pl.BlockSpec((width, nodes), lambda i, req: (0, 0))],
            out_specs=pl.BlockSpec((1, SLOTS * width, BLK), lambda i, req: (i, 0, 0)),
        ),
        compiler_params=params(),
        name="gather_blocks",
    )(req, feats_t)


def spread_kernel(order, source, alive, recv_ref, feats_ref, *refs):
    tiles, (mixed_ref, scale_ref) = refs[:SLOTS], refs[SLOTS:]
    b = pl.program_id(0)
    width = feats_ref.shape[0]
    ones = jnp.ones((16, BLK), jnp.bfloat16)
    total = jnp.zeros((width + 16, BLK), jnp.float32)
    for s in range(SLOTS):
        q = b * SLOTS + s
        flag = alive[q].astype(jnp.float32).astype(jnp.bfloat16)
        left = jnp.concatenate([recv_ref[source[q]], ones], axis=0) * flag
        total += lax.dot_general(
            left, tiles[s][0], (((1,), (1,)), ((), ())), preferred_element_type=jnp.float32
        )
    scale = lax.rsqrt(1.0 + total[width : width + 1, :])
    scale_ref[...] = scale
    mixed = feats_ref[...].astype(jnp.float32) + scale * total[:width, :]
    mixed_ref[0] = mixed.astype(jnp.bfloat16)


def spread_mixed(order, source, alive, recv, feats_t, tile_vals):
    width, nodes = feats_t.shape
    blocks = nodes // BLK
    count = tile_vals.shape[0]

    def tile_spec(s):
        return pl.BlockSpec((1, BLK, BLK), lambda b, order, source, alive: (order[b * SLOTS + s], 0, 0))

    return pl.pallas_call(
        spread_kernel,
        out_shape=(
            jax.ShapeDtypeStruct((blocks // 2, width, 2 * BLK), jnp.bfloat16),
            jax.ShapeDtypeStruct((1, nodes), jnp.float32),
        ),
        grid_spec=pltpu.PrefetchScalarGridSpec(
            num_scalar_prefetch=3,
            grid=(blocks,),
            in_specs=[
                pl.BlockSpec((count, width, BLK), lambda b, *_: (0, 0, 0)),
                pl.BlockSpec((width, BLK), lambda b, *_: (0, b)),
            ]
            + [tile_spec(s) for s in range(SLOTS)],
            out_specs=(
                pl.BlockSpec((1, width, BLK), lambda b, *_: (b // 2, 0, b % 2)),
                pl.BlockSpec((1, BLK), lambda b, *_: (0, b)),
            ),
        ),
        compiler_params=params(),
        name="spread_mixed",
    )(order, source, alive, recv, feats_t, *([tile_vals] * SLOTS))


def dense_kernel(mixed_ref, cot_ref, weight_ref, weight_t_ref, hidden_ref, grad_ref, gw_ref, gp_ref):
    step = 128
    mixed = mixed_ref[...]
    for lo in range(0, weight_ref.shape[1], step):
        rows = slice(lo, lo + step)
        pre = jnp.dot(weight_t_ref[rows, :], mixed, preferred_element_type=jnp.float32)
        square = pre * pre
        tanh = jnp.tanh(GELU_C * (pre + GELU_A * (pre * square)))
        half = 0.5 * (1.0 + tanh)
        hidden_ref[rows, :] = (pre * half).astype(jnp.bfloat16)
        slope = half + 0.5 * pre * (1.0 - tanh * tanh) * (GELU_C * (1.0 + 3.0 * GELU_A * square))
        gp_ref[rows, :] = (cot_ref[rows, :].astype(jnp.float32) * slope).astype(jnp.bfloat16)
    grad_pre = gp_ref[...]
    grad_ref[...] = jnp.dot(weight_ref[...], grad_pre, preferred_element_type=jnp.float32).astype(
        jnp.bfloat16
    )
    gw_ref[...] = lax.dot_general(
        grad_pre, mixed, (((1,), (1,)), ((), ())), preferred_element_type=jnp.float32
    ).astype(jnp.bfloat16)


def dense(mixed, cot, weight, weight_t):
    full = jax.ShapeDtypeStruct(mixed.shape, jnp.bfloat16)
    return pl.pallas_call(
        dense_kernel,
        out_shape=(full, full, jax.ShapeDtypeStruct(weight.shape, jnp.bfloat16)),
        scratch_shapes=[pltpu.VMEM(mixed.shape, jnp.bfloat16)],
        compiler_params=params(),
        name="dense",
    )(mixed, cot, weight, weight_t)


def back_kernel(order, rows, alive, grad_ref, scale_ref, *refs):
    tiles, (out_ref,) = refs[:SLOTS], refs[SLOTS:]
    j = pl.program_id(0)
    width = grad_ref.shape[1]
    for s in range(SLOTS):
        q = j * SLOTS + s
        b = rows[q]
        flag = alive[q].astype(jnp.float32)
        start = pl.multiple_of(b * BLK, BLK)
        inner = pl.multiple_of((b % 2) * BLK, BLK)
        scale = scale_ref[:, pl.ds(start, BLK)] * flag
        grad = grad_ref[b // 2, :, pl.ds(inner, BLK)].astype(jnp.float32)
        out_ref[0, s * width : (s + 1) * width, :] = jnp.dot(
            (grad * scale).astype(jnp.bfloat16), tiles[s][0], preferred_element_type=jnp.float32
        ).astype(jnp.bfloat16)


def back_products(order, rows, alive, grad, scale, tile_vals):
    chunks, width, chunk = grad.shape
    count = tile_vals.shape[0]

    def tile_spec(s):
        return pl.BlockSpec((1, BLK, BLK), lambda j, order, rows, alive: (order[j * SLOTS + s], 0, 0))

    return pl.pallas_call(
        back_kernel,
        out_shape=jax.ShapeDtypeStruct((count // SLOTS, SLOTS * width, BLK), jnp.bfloat16),
        grid_spec=pltpu.PrefetchScalarGridSpec(
            num_scalar_prefetch=3,
            grid=(count // SLOTS,),
            in_specs=[
                pl.BlockSpec((chunks, width, chunk), lambda j, *_: (0, 0, 0)),
                pl.BlockSpec((1, chunks * chunk), lambda j, *_: (0, 0)),
            ]
            + [tile_spec(s) for s in range(SLOTS)],
            out_specs=pl.BlockSpec((1, SLOTS * width, BLK), lambda j, *_: (j, 0, 0)),
        ),
        compiler_params=params(),
        name="back_products",
    )(order, rows, alive, grad, scale, *([tile_vals] * SLOTS))


def final_kernel(asked, recv_ref, grad_ref, out_ref, total_ref):
    i = pl.program_id(0)
    chunks, width, chunk = grad_ref.shape

    @pl.when(i == 0)
    def _():
        for c in range(chunks):
            total_ref[:, c * chunk : (c + 1) * chunk] = grad_ref[c].astype(jnp.float32)

    for s in range(SLOTS):
        start = pl.multiple_of(asked[i * SLOTS + s] * BLK, BLK)
        total_ref[:, pl.ds(start, BLK)] += recv_ref[0, s * width : (s + 1) * width, :].astype(jnp.float32)

    @pl.when(i == pl.num_programs(0) - 1)
    def _():
        out_ref[...] = total_ref[...].astype(jnp.bfloat16)


def final_sum(asked, recv, grad):
    chunks, width, chunk = grad.shape
    peers = recv.shape[0]
    return pl.pallas_call(
        final_kernel,
        out_shape=jax.ShapeDtypeStruct((width, chunks * chunk), jnp.bfloat16),
        grid_spec=pltpu.PrefetchScalarGridSpec(
            num_scalar_prefetch=1,
            grid=(peers,),
            in_specs=[
                pl.BlockSpec((1, SLOTS * width, BLK), lambda i, asked: (i, 0, 0)),
                pl.BlockSpec((chunks, width, chunk), lambda i, asked: (0, 0, 0)),
            ],
            out_specs=pl.BlockSpec((width, chunks * chunk), lambda i, asked: (0, 0)),
            scratch_shapes=[pltpu.VMEM((width, chunks * chunk), jnp.float32)],
        ),
        compiler_params=params(),
        name="final_sum",
    )(asked, recv, grad)


def places(group):
    index = jnp.arange(group.shape[0], dtype=jnp.int32)
    earlier = (group[None, :] == group[:, None]) & (index[None, :] < index[:, None])
    return group * SLOTS + jnp.sum(earlier.astype(jnp.int32), axis=1)


def put(place, value):
    index = jnp.arange(place.shape[0], dtype=jnp.int32)
    return jnp.sum(jnp.where(place[None, :] == index[:, None], value[None, :], 0), axis=1)


def body(feats, weight, tile_vals, tile_rows, tile_cols, tile_nnz, cotangent):
    node_rows, width = feats.shape
    blocks = node_rows // BLK
    peers = lax.axis_size("row")
    chunks = lax.axis_size("col")
    chunk = node_rows // chunks
    count = tile_rows.shape[0]
    exchange = functools.partial(lax.all_to_all, split_axis=0, concat_axis=0, tiled=True)

    feats_t = feats.T
    weight_t = weight.T
    index = jnp.arange(count, dtype=jnp.int32)
    alive = (tile_nnz > 0).astype(jnp.int32)
    local_rows = tile_rows - lax.axis_index("row") * blocks
    by_col = places(tile_cols // blocks)
    by_row = places(local_rows)

    wanted = put(by_col, tile_cols % blocks)
    asked = exchange(wanted.reshape(peers, SLOTS), "row").reshape(count)
    sent = gather_blocks(asked, feats_t)
    recv = exchange(sent, "row").reshape(count, width, BLK)

    cot = exchange(jnp.swapaxes(cotangent.T.reshape(width, chunks, chunk), 0, 1), "col")

    mixed, scale = spread_mixed(
        put(by_row, index), put(by_row, by_col), put(by_row, alive), recv, feats_t, tile_vals
    )
    mixed_full = exchange(mixed, "col").reshape(chunks * width, chunk)
    hidden_t, grad_t, gw_t = dense(mixed_full, cot.reshape(chunks * width, chunk), weight, weight_t)
    grad = exchange(grad_t.reshape(chunks, width, chunk), "col")
    products = back_products(
        put(by_col, index), put(by_col, local_rows), put(by_col, alive), grad, scale, tile_vals
    )
    returned = exchange(products, "row")

    both = jnp.concatenate(
        [hidden_t.reshape(chunks, width, chunk), gw_t.reshape(chunks, width, weight.shape[0])], axis=2
    )
    both = exchange(both, "col")
    hidden = jnp.swapaxes(both[:, :, :chunk], 0, 1).reshape(width, node_rows).T
    gw_part = jnp.sum(both[:, :, chunk:].astype(jnp.float32), axis=0).astype(jnp.bfloat16)
    gw_part = jnp.swapaxes(gw_part.reshape(width, peers, -1), 0, 1)
    gw = jnp.sum(exchange(gw_part, "row").astype(jnp.float32), axis=0).T

    grad_feats = final_sum(asked, returned, grad).T
    return (hidden, gw, grad_feats)


def solution(mesh):
    placed = (
        P("row", "col"),
        P(),
        P("row", None, None),
        P("row"),
        P("row"),
        P("row"),
        P("row", "col"),
    )
    return jax.shard_map(
        body,
        mesh=mesh,
        in_specs=placed,
        out_specs=(P("row", "col"), P("row", "col"), P("row", "col")),
        check_vma=False,
    )
```

time: 373 us -> 249 us (0.67)
  waiting for transfers between devices: 245 us -> 126 us
  matrix products: 69.6 us -> 0 us
  Pallas kernels: 0 us -> 44.9 us
  blocking collectives: 0 us -> 33 us
  starting transfers between devices: 0.38 us -> 30.2 us
  local copies, waits for them, and re-layouts: 29.2 us -> 8.58 us
  between operations: 13.9 us -> 0.8 us
  other arithmetic: 14.2 us -> 3.41 us
    reduce_scatter x3 -> x0, waiting for transfers between devices: 146 us -> none  [the longest x1 86.6 us: body(): lax.psum_scatter(summed.reshape(lax.axis_size('row') * node_rows, col_wid...]
    all_to_all x0 -> x6, waiting for transfers between devices: none -> 126 us  [the longest x1 53.7 us: body(): recv = exchange(sent, 'row').reshape(count, width, BLK)]
    all_gather x2 -> x0, waiting for transfers between devices: 98.2 us -> none  [the longest x1 66.2 us: body(): all_feats = lax.all_gather(feats, 'row', axis=0, tiled=True)]
    dot_general x8 -> x0, matrix products: 69.6 us -> none  [the longest x1 22.7 us: body(): jnp.einsum('bt,tjk->bjk', col_select, adjoint_terms, precision=highest)]
    pallas_call x0 -> x5, Pallas kernels: none -> 44.9 us  [the longest x1 17.8 us: spread_mixed(): pl.pallas_call(spread_kernel, out_shape=(jax.ShapeDtypeStruct((blocks //...]
    all_to_all x0 -> x2, blocking collectives: none -> 33 us  [the longest x1 18.5 us: body(): both = exchange(both, 'col')]
    all_to_all x0 -> x6, starting transfers between devices: none -> 30.2 us  [the longest x1 7.24 us: body(): returned = exchange(products, 'row')]
    gather x2 -> x0, local copies, waits for them, and re-layouts: 8.93 us -> none  [the longest x1 6.16 us: body(): source_blocks = all_feats.reshape(total_blocks, BLK, col_width)[tile_cols]]
  transfers between devices with their start and end apart: 5 -> 6, of which waited for: 5 -> 4; matrix products, arithmetic and copies ran while one was open for 17% -> 2% of each run, Pallas kernels for 0% -> 13%
where the time goes in v1:
time: 249 us; the launch traced here: 247 us
  waiting for transfers between devices  126 us (51%)
  Pallas kernels  44.9 us (18%)
  blocking collectives  33 us (13%)
  starting transfers between devices  30.2 us (12%)
  local copies, waits for them, and re-layouts  8.58 us (3%)
  other arithmetic  3.41 us (1%)
    all_to_all x1, waiting for transfers between devices, body(): recv = exchange(sent, 'row').reshape(count, width, BLK)  53.7 us
    all_to_all x1, waiting for transfers between devices, body(): returned = exchange(products, 'row')  52.8 us
    all_to_all x1, blocking collectives, body(): both = exchange(both, 'col')  18.5 us
    pallas_call x1, Pallas kernels, spread_mixed(): pl.pallas_call(spread_kernel, out_shape=(jax.ShapeDtypeStruct((blocks //...  17.8 us
    all_to_all x1, blocking collectives, body(): asked = exchange(wanted.reshape(peers, SLOTS), 'row').reshape(count)  14.5 us
    pallas_call x1, Pallas kernels, back_products(): pl.pallas_call(back_kernel, out_shape=jax.ShapeDtypeStruct((count // SLOT...  13.8 us
    all_to_all x1, waiting for transfers between devices, body(): mixed_full = exchange(mixed, 'col').reshape(chunks * width, chunk)  10.1 us
    pallas_call x1, Pallas kernels, final_sum(): pl.pallas_call(final_kernel, out_shape=jax.ShapeDtypeStruct((width, chunk...  9.84 us
  transfers between devices with their start and end apart: 6, of which 4 were waited for; matrix products, arithmetic and copies ran while one was open for 2% of the time, Pallas kernels for 13%

profile of v1, /device:TPU:0, one launch (start us, length us, event | category | flops | bytes accessed | tf_op | source)
XLA Modules:
  0.0 246.9 jit_solution(5221943666262872556)
XLA Ops:
  0.6 0.7 compare_convert_fusion
  1.3 0.7 and_select_fusion
  2.0 0.2 convert_reduce_fusion.1
  2.2 0.2 select_reduce_fusion
  2.4 0.1 all_to_all.27
  2.5 14.5 %all_to_all.44 = s32[16,1,8]{2,1,0:T(1,128)S(1)} all-to-all(s32[16,1,8]{2,1,0:T(1,128)S(1)} %bitcast.42), channel_id=1, replica_groups=mesh['row'=16,'col'=8] {'row'}, dimensions={0} | all-to-all | bytes 1024 | tf_op jit(solution)/shard_map/all_to_all | solution.py:239
  16.9 0.5 broadcast.42
  17.5 0.7 reduce.4
  18.1 0.1 reshape.49.req.asked
  18.2 0.0 copy-start.2
  18.2 1.0 copy-done.2
  19.3 1.3 gather_blocks.1
  20.6 0.0 copy-start
  20.6 2.0 copy-done
  22.6 0.0 copy-start.5
  22.6 0.0 copy-start.3
  22.6 4.7 %all-to-all-start.1 = ((bf16[16,512,256]{2,1,0:T(8,128)(2,1)}), bf16[16,512,256]{2,1,0:T(8,128)(2,1)}, u32[]{:S(2)}, u32[]{:S(2)}) async-start(bf16[16,512,256]{2,1,0:T(8,128)(2,1)} %copy-done), calls=%async_computation.1 | async-start | bytes 8388608 | tf_op jit(solution)/shard_map/all_to_all | solution.py:241
  27.3 0.0 copy-done.5
  27.3 0.8 copy.29
  28.1 53.7 %all-to-all-done.1 = bf16[16,512,256]{2,1,0:T(8,128)(2,1)} async-done(((bf16[16,512,256]{2,1,0:T(8,128)(2,1)}), bf16[16,512,256]{2,1,0:T(8,128)(2,1)}, u32[]{:S(2)}, u32[]{:S(2)}) %all-to-all-start.1) | async-done | bytes 4194336 | tf_op jit(solution)/shard_map/all_to_all | solution.py:241
  81.9 5.3 %all-to-all-start.3 = ((bf16[8,64,512]{2,1,0:T(8,128)(2,1)}), bf16[8,64,512]{2,1,0:T(8,128)(2,1)S(1)}, u32[]{:S(2)}, u32[]{:S(2)}) async-start(bf16[8,64,512]{2,1,0:T(8,128)(2,1)} %bitcast.30), calls=%async_computation.3 | async-start | bytes 1048576 | tf_op jit(solution)/shard_map/all_to_all | solution.py:243
  87.2 0.1 select_reduce_fusion.4
  87.3 0.0 copy-done.3
  87.3 0.0 copy-start.4
  87.3 17.8 %spread_mixed.1 = (bf16[8,64,512]{2,1,0:T(8,128)(2,1)}, f32[1,4096]{1,0:T(1,128)S(1)}) custom-call(s32[128]{0:T(128)S(1)} %get-tuple-element.20.order, s32[128]{0:T(128)S(1)} %get-tuple-element.19.source, s32[128]{0:T(128)S(1)} %get-tuple-element.18.alive, bf16[128,64,256]{2,1,0:T(8,128)(2,1)} %bitcast.2.recv_ref, bf16[64,4096]{1,0:T(8,128)(2,1)S(1)} %bitcast.32, ...), custom_call_target="tpu_custom_call" | custom-call | tf_op jit(solution)/shard_map/spread_mixed/pallas_call | solution.py:73
  105.2 0.0 all-to-all-done.3
  105.2 4.8 %all-to-all-start.2 = ((bf16[8,64,512]{2,1,0:T(8,128)(2,1)}), bf16[8,64,512]{2,1,0:T(8,128)(2,1)S(1)}, u32[]{:S(2)}, u32[]{:S(2)}) async-start(bf16[8,64,512]{2,1,0:T(8,128)(2,1)} %get-tuple-element.8), calls=%async_computation.2 | async-start | bytes 1048576 | tf_op jit(solution)/shard_map/all_to_all | solution.py:248
  110.0 0.0 copy-done.4
  110.0 0.2 copy.23
  110.2 10.1 %all-to-all-done.2 = bf16[8,64,512]{2,1,0:T(8,128)(2,1)S(1)} async-done(((bf16[8,64,512]{2,1,0:T(8,128)(2,1)}), bf16[8,64,512]{2,1,0:T(8,128)(2,1)S(1)}, u32[]{:S(2)}, u32[]{:S(2)}) %all-to-all-start.2) | async-done | bytes 524320 | tf_op jit(solution)/shard_map/all_to_all | solution.py:248
  120.4 2.1 dense.1
  122.4 0.1 pad_maximum_fusion
  122.5 18.5 %all_to_all.45 = bf16[8,64,1024]{2,1,0:T(8,128)(2,1)S(1)} all-to-all(bf16[8,64,1024]{2,1,0:T(8,128)(2,1)S(1)} %pad_maximum_fusion), channel_id=1, replica_groups=mesh['row'=16,'col'=8] {'col'}, dimensions={0} | all-to-all | bytes 2097152 | tf_op jit(solution)/shard_map/all_to_all | solution.py:259
  141.1 3.5 %all-to-all-start.6 = ((bf16[8,64,512]{2,1,0:T(8,128)(2,1)}), bf16[8,64,512]{2,1,0:T(8,128)(2,1)S(1)}, u32[]{:S(2)}, u32[]{:S(2)}) async-start(bf16[8,64,512]{2,1,0:T(8,128)(2,1)} %bitcast.15), calls=%async_computation.6 | async-start | bytes 1048576 | tf_op jit(solution)/shard_map/all_to_all | solution.py:250
  144.6 0.1 slice_reduce_fusion
  144.7 0.1 copy.25
  144.8 0.8 reshape.68
  145.6 9.3 %all-to-all-done.6.grad_ref = bf16[8,64,512]{2,1,0:T(8,128)(2,1)S(1)} async-done(((bf16[8,64,512]{2,1,0:T(8,128)(2,1)}), bf16[8,64,512]{2,1,0:T(8,128)(2,1)S(1)}, u32[]{:S(2)}, u32[]{:S(2)}) %all-to-all-start.6) | async-done | bytes 524320 | tf_op jit(solution)/shard_map/all_to_all | solution.py:250
  154.8 4.7 %all-to-all-start.5 = ((bf16[16,2,1024]{2,1,0:T(2,128)(2,1)}), bf16[16,2,1024]{2,1,0:T(2,128)(2,1)S(1)}, u32[]{:S(2)}, u32[]{:S(2)}) async-start(bf16[16,2,1024]{2,1,0:T(2,128)(2,1)} %reshape.68), calls=%async_computation.5 | async-start | bytes 131072 | tf_op jit(solution)/shard_map/all_to_all | solution.py:263
  159.5 13.8 %back_products.1 = bf16[16,512,256]{2,1,0:T(8,128)(2,1)S(1)} custom-call(s32[128]{0:T(128)S(1)} %get-tuple-element.17.order, s32[128]{0:T(128)S(1)} %get-tuple-element.15.rows, s32[128]{0:T(128)S(1)} %get-tuple-element.13.alive, bf16[8,64,512]{2,1,0:T(8,128)(2,1)S(1)} %all-to-all-done.6.grad_ref, f32[1,4096]{1,0:T(1,128)S(1)} %get-tuple-element.12.scale_ref, ...), custom_call_target="tpu_custom_call" | custom-call | tf_op jit(solution)/shard_map/back_products/pallas_call | solution.py:153
  173.3 0.0 copy-start.1
  173.4 2.0 copy-done.1
  175.3 0.0 all-to-all-done.5
  175.3 7.2 %all-to-all-start.7 = ((bf16[16,512,256]{2,1,0:T(8,128)(2,1)}), bf16[16,512,256]{2,1,0:T(8,128)(2,1)}, u32[]{:S(2)}, u32[]{:S(2)}) async-start(bf16[16,512,256]{2,1,0:T(8,128)(2,1)} %copy-done.1), calls=%async_computation.7 | async-start | bytes 8388608 | tf_op jit(solution)/shard_map/all_to_all | solution.py:254
  182.6 0.8 copy.27
  183.4 0.1 reshape.69
  183.6 0.6 convert_reduce_fusion
  184.2 52.8 %all-to-all-done.7.recv_ref = bf16[16,512,256]{2,1,0:T(8,128)(2,1)} async-done(((bf16[16,512,256]{2,1,0:T(8,128)(2,1)}), bf16[16,512,256]{2,1,0:T(8,128)(2,1)}, u32[]{:S(2)}, u32[]{:S(2)}) %all-to-all-start.7) | async-done | bytes 4194336 | tf_op jit(solution)/shard_map/all_to_all | solution.py:254
  237.0 9.8 %final_sum.1 = bf16[64,4096]{1,0:T(8,128)(2,1)} custom-call(s32[128]{0:T(128)S(1)} %reshape.49.req.asked, bf16[16,512,256]{2,1,0:T(8,128)(2,1)} %all-to-all-done.7.recv_ref, bf16[8,64,512]{2,1,0:T(8,128)(2,1)S(1)} %all-to-all-done.6.grad_ref), custom_call_target="tpu_custom_call" | custom-call | tf_op jit(solution)/shard_map/final_sum/pallas_call | solution.py:192
  (2 shorter events, 0.0 us)
Async XLA Ops:
  18.2 1.0 copy-start.2
  20.6 2.0 copy-start
  22.6 4.7 %copy-start.5 = (bf16[4096,64]{0,1:T(8,128)(2,1)S(1)}, bf16[4096,64]{0,1:T(8,128)(2,1)}, u32[]{:S(2)}) copy-start(bf16[4096,64]{0,1:T(8,128)(2,1)} %param.13) | copy-start | bytes 1572868
  22.6 64.7 %copy-start.3 = (bf16[4096,64]{0,1:T(8,128)(2,1)S(1)}, bf16[4096,64]{0,1:T(8,128)(2,1)}, u32[]{:S(2)}) copy-start(bf16[4096,64]{0,1:T(8,128)(2,1)} %param.7) | copy-start | bytes 1572868
  22.6 59.3 %all-to-all-start.1 = ((bf16[16,512,256]{2,1,0:T(8,128)(2,1)}), bf16[16,512,256]{2,1,0:T(8,128)(2,1)}, u32[]{:S(2)}, u32[]{:S(2)}) async-start(bf16[16,512,256]{2,1,0:T(8,128)(2,1)} %copy-done), calls=%async_computation.1 | async-start | bytes 8388608 | tf_op jit(solution)/shard_map/all_to_all | solution.py:241
  81.9 23.3 %all-to-all-start.3 = ((bf16[8,64,512]{2,1,0:T(8,128)(2,1)}), bf16[8,64,512]{2,1,0:T(8,128)(2,1)S(1)}, u32[]{:S(2)}, u32[]{:S(2)}) async-start(bf16[8,64,512]{2,1,0:T(8,128)(2,1)} %bitcast.30), calls=%async_computation.3 | async-start | bytes 1048576 | tf_op jit(solution)/shard_map/all_to_all | solution.py:243
  87.3 22.7 %copy-start.4 = (bf16[512,512]{1,0:T(8,128)(2,1)S(1)}, bf16[512,512]{1,0:T(8,128)(2,1)}, u32[]{:S(2)}) copy-start(bf16[512,512]{1,0:T(8,128)(2,1)} %weight_ref.1) | copy-start | bytes 1572868
  105.2 15.2 %all-to-all-start.2 = ((bf16[8,64,512]{2,1,0:T(8,128)(2,1)}), bf16[8,64,512]{2,1,0:T(8,128)(2,1)S(1)}, u32[]{:S(2)}, u32[]{:S(2)}) async-start(bf16[8,64,512]{2,1,0:T(8,128)(2,1)} %get-tuple-element.8), calls=%async_computation.2 | async-start | bytes 1048576 | tf_op jit(solution)/shard_map/all_to_all | solution.py:248
  141.1 13.8 %all-to-all-start.6 = ((bf16[8,64,512]{2,1,0:T(8,128)(2,1)}), bf16[8,64,512]{2,1,0:T(8,128)(2,1)S(1)}, u32[]{:S(2)}, u32[]{:S(2)}) async-start(bf16[8,64,512]{2,1,0:T(8,128)(2,1)} %bitcast.15), calls=%async_computation.6 | async-start | bytes 1048576 | tf_op jit(solution)/shard_map/all_to_all | solution.py:250
  154.8 20.5 %all-to-all-start.5 = ((bf16[16,2,1024]{2,1,0:T(2,128)(2,1)}), bf16[16,2,1024]{2,1,0:T(2,128)(2,1)S(1)}, u32[]{:S(2)}, u32[]{:S(2)}) async-start(bf16[16,2,1024]{2,1,0:T(2,128)(2,1)} %reshape.68), calls=%async_computation.5 | async-start | bytes 131072 | tf_op jit(solution)/shard_map/all_to_all | solution.py:263
  173.3 2.0 copy-start.1
  175.3 61.7 %all-to-all-start.7 = ((bf16[16,512,256]{2,1,0:T(8,128)(2,1)}), bf16[16,512,256]{2,1,0:T(8,128)(2,1)}, u32[]{:S(2)}, u32[]{:S(2)}) async-start(bf16[16,512,256]{2,1,0:T(8,128)(2,1)} %copy-done.1), calls=%async_computation.7 | async-start | bytes 8388608 | tf_op jit(solution)/shard_map/all_to_all | solution.py:254

commit v2 on v0

v2 whole, which is shorter than its diff:
```python
import functools

import jax
import jax.numpy as jnp
from jax import lax
from jax.experimental import pallas as pl
from jax.experimental.pallas import tpu as pltpu
from jax.sharding import PartitionSpec as P

BLK = 256
SLOTS = 8
SIDE = 4
PART = SIDE * SLOTS
VMEM_LIMIT = 32 * 1024 * 1024
GELU_C = 0.7978845608028654
GELU_A = 0.044715


def params():
    return pltpu.CompilerParams(vmem_limit_bytes=VMEM_LIMIT)


def scalars(n):
    return [pl.BlockSpec(memory_space=pltpu.SMEM)] * n


def arrays(n):
    return [pl.BlockSpec(memory_space=pltpu.VMEM)] * n


def encode(index, col_block, row_block, alive):
    return index + 128 * col_block + 2048 * row_block + 32768 * alive


def col_block_of(code):
    return (code >> 7) & 15


def row_block_of(code):
    return (code >> 11) & 15


def gather_kernel(*refs):
    count = (len(refs) - SIDE) // 2
    codes, slabs, outs = refs[:count], refs[count : count + SIDE], refs[count + SIDE :]
    for code_ref, out_ref in zip(codes, outs):
        for q in range(PART):
            start = pl.multiple_of(col_block_of(code_ref[q]) * BLK, BLK)
            out_ref[q] = slabs[q // SLOTS][:, pl.ds(start, BLK)]


def gather_blocks(codes, slabs):
    width = slabs[0].shape[0]
    return pl.pallas_call(
        gather_kernel,
        out_shape=[jax.ShapeDtypeStruct((PART, width, BLK), jnp.bfloat16)] * len(codes),
        in_specs=scalars(len(codes)) + arrays(SIDE),
        out_specs=arrays(len(codes)),
        compiler_params=params(),
        name="gather_blocks",
    )(*codes, *slabs)


def load_tiles(code_refs, tiles_ref, buf_ref, sems):
    for part, code_ref in enumerate(code_refs):

        def start(q, carry):
            pltpu.make_async_copy(
                tiles_ref.at[code_ref[q] & 127],
                buf_ref.at[part * SIDE + q // SLOTS, q % SLOTS],
                sems.at[part * SIDE + q // SLOTS],
            ).start()
            return carry

        lax.fori_loop(0, PART, start, 0)


def wait_tiles(tiles_ref, buf_ref, sems, group):
    pltpu.make_async_copy(tiles_ref.at[pl.ds(0, SLOTS)], buf_ref.at[group], sems.at[group]).wait()


def spread_kernel(parts, first, last, *refs):
    codes, recvs = refs[:parts], refs[parts : 2 * parts]
    tiles_ref = refs[2 * parts]
    rest = list(refs[2 * parts + 1 :])
    before_ref = None if first else rest.pop(0)
    feats_ref = rest.pop(0) if last else None
    buf_ref, sems = rest[-2:]
    total_ref = rest[-3] if last else rest[0]
    load_tiles(codes, tiles_ref, buf_ref, sems)
    total_ref[...] = jnp.zeros_like(total_ref) if first else before_ref[...]
    ones = jnp.ones((16, BLK), jnp.bfloat16)
    for part in range(parts):

        def step(d, carry):
            group = part * SIDE + d
            wait_tiles(tiles_ref, buf_ref, sems, group)
            for s in range(SLOTS):
                q = d * SLOTS + s
                code = codes[part][q]
                flag = (code >> 15).astype(jnp.float32).astype(jnp.bfloat16)
                left = jnp.concatenate([recvs[part][q], ones], axis=0) * flag
                start = pl.multiple_of(row_block_of(code) * BLK, BLK)
                total_ref[:, pl.ds(start, BLK)] += lax.dot_general(
                    left, buf_ref[group, s], (((1,), (1,)), ((), ())), preferred_element_type=jnp.float32
                )
            return carry

        lax.fori_loop(0, SIDE, step, 0)
    if last:
        mixed_ref, scale_ref = rest[:2]
        chunks, width, chunk = mixed_ref.shape
        scale = lax.rsqrt(1.0 + total_ref[width : width + 1, :])
        scale_ref[...] = scale
        for c in range(chunks):
            part = slice(c * chunk, (c + 1) * chunk)
            mixed = feats_ref[:, part].astype(jnp.float32) + scale[:, part] * total_ref[:width, part]
            mixed_ref[c] = mixed.astype(jnp.bfloat16)


def spread(codes, recvs, tile_vals, before, feats_t, chunks):
    parts, width = len(codes), recvs[0].shape[1]
    first, last = before is None, feats_t is not None
    nodes = tile_vals.shape[0] // SLOTS * BLK
    total = jax.ShapeDtypeStruct((width + 16, nodes), jnp.float32)
    scratch = [
        pltpu.VMEM((parts * SIDE, SLOTS, BLK, BLK), jnp.bfloat16),
        pltpu.SemaphoreType.DMA((parts * SIDE,)),
    ]
    if last:
        out_shape = (
            jax.ShapeDtypeStruct((chunks, width, nodes // chunks), jnp.bfloat16),
            jax.ShapeDtypeStruct((1, nodes), jnp.float32),
        )
        scratch = [pltpu.VMEM(total.shape, total.dtype)] + scratch
    else:
        out_shape = (total,)
    extra = ([] if first else [before]) + ([feats_t] if last else [])
    return pl.pallas_call(
        functools.partial(spread_kernel, parts, first, last),
        out_shape=out_shape,
        in_specs=scalars(parts) + arrays(parts) + [pl.BlockSpec(memory_space=pl.ANY)] + arrays(len(extra)),
        out_specs=tuple(arrays(len(out_shape))),
        scratch_shapes=scratch,
        compiler_params=params(),
        name="spread",
    )(*codes, *recvs, tile_vals, *extra)


def dense_kernel(mixed_ref, cot_ref, weight_ref, weight_t_ref, hidden_ref, grad_ref, gw_ref, gp_ref):
    step = 128
    mixed = mixed_ref[...]
    for lo in range(0, weight_ref.shape[1], step):
        rows = slice(lo, lo + step)
        pre = jnp.dot(weight_t_ref[rows, :], mixed, preferred_element_type=jnp.float32)
        square = pre * pre
        tanh = jnp.tanh(GELU_C * (pre + GELU_A * (pre * square)))
        half = 0.5 * (1.0 + tanh)
        hidden_ref[rows, :] = (pre * half).astype(jnp.bfloat16)
        slope = half + 0.5 * pre * (1.0 - tanh * tanh) * (GELU_C * (1.0 + 3.0 * GELU_A * square))
        gp_ref[rows, :] = (cot_ref[rows, :].astype(jnp.float32) * slope).astype(jnp.bfloat16)
    grad_pre = gp_ref[...]
    grad_ref[...] = jnp.dot(weight_ref[...], grad_pre, preferred_element_type=jnp.float32).astype(
        jnp.bfloat16
    )
    gw_ref[...] = lax.dot_general(
        grad_pre, mixed, (((1,), (1,)), ((), ())), preferred_element_type=jnp.float32
    ).astype(jnp.bfloat16)


def dense(mixed, cot, weight, weight_t):
    full = jax.ShapeDtypeStruct(mixed.shape, jnp.bfloat16)
    return pl.pallas_call(
        dense_kernel,
        out_shape=(full, full, jax.ShapeDtypeStruct(weight.shape, jnp.bfloat16)),
        scratch_shapes=[pltpu.VMEM(mixed.shape, jnp.bfloat16)],
        compiler_params=params(),
        name="dense",
    )(mixed, cot, weight, weight_t)


def back_kernel(code_ref, grad_ref, scale_ref, tiles_ref, out_ref, buf_ref, sems):
    load_tiles([code_ref], tiles_ref, buf_ref, sems)

    def step(d, carry):
        wait_tiles(tiles_ref, buf_ref, sems, d)
        for s in range(SLOTS):
            q = d * SLOTS + s
            code = code_ref[q]
            b = row_block_of(code)
            start = pl.multiple_of(b * BLK, BLK)
            inner = pl.multiple_of((b % 2) * BLK, BLK)
            scale = scale_ref[:, pl.ds(start, BLK)] * (code >> 15).astype(jnp.float32)
            grad = grad_ref[b // 2, :, pl.ds(inner, BLK)].astype(jnp.float32)
            out_ref[q] = jnp.dot(
                (grad * scale).astype(jnp.bfloat16), buf_ref[d, s], preferred_element_type=jnp.float32
            ).astype(jnp.bfloat16)
        return carry

    lax.fori_loop(0, SIDE, step, 0)


def back_products(code, grad, scale, tile_vals):
    return pl.pallas_call(
        back_kernel,
        out_shape=jax.ShapeDtypeStruct((PART, grad.shape[1], BLK), jnp.bfloat16),
        in_specs=scalars(1) + arrays(2) + [pl.BlockSpec(memory_space=pl.ANY)],
        out_specs=arrays(1)[0],
        scratch_shapes=[
            pltpu.VMEM((SIDE, SLOTS, BLK, BLK), jnp.bfloat16),
            pltpu.SemaphoreType.DMA((SIDE,)),
        ],
        compiler_params=params(),
        name="back_products",
    )(code, grad, scale, tile_vals)


def collect_kernel(parts, first, last, *refs):
    codes, pieces = refs[:parts], refs[parts : 2 * parts]
    rest = list(refs[2 * parts :])
    before_ref = None if first else rest.pop(0)
    total_ref = rest[-1]
    total_ref[...] = jnp.zeros_like(total_ref) if first else before_ref[...]
    for code_ref, piece_ref in zip(codes, pieces):
        for q in range(PART):
            start = pl.multiple_of(col_block_of(code_ref[q]) * BLK, BLK)
            total_ref[q // SLOTS, :, pl.ds(start, BLK)] += piece_ref[q].astype(jnp.float32)
    if last:
        for d in range(SIDE):
            rest[d][...] = total_ref[d].astype(jnp.bfloat16)


def collect(codes, pieces, before, nodes, last):
    parts, width = len(codes), pieces[0].shape[1]
    first = before is None
    total = jax.ShapeDtypeStruct((SIDE, width, nodes), jnp.float32)
    slab = jax.ShapeDtypeStruct((width, nodes), jnp.bfloat16)
    out_shape = (slab,) * SIDE if last else (total,)
    extra = [] if first else [before]
    return pl.pallas_call(
        functools.partial(collect_kernel, parts, first, last),
        out_shape=out_shape,
        in_specs=scalars(parts) + arrays(parts + len(extra)),
        out_specs=tuple(arrays(len(out_shape))),
        scratch_shapes=[pltpu.VMEM(total.shape, total.dtype)] if last else [],
        compiler_params=params(),
        name="collect",
    )(*codes, *pieces, *extra)


def final_kernel(grad_ref, *refs):
    slabs, out_ref = refs[:-1], refs[-1]
    chunks, width, chunk = grad_ref.shape
    for c in range(chunks):
        part = slice(c * chunk, (c + 1) * chunk)
        total = grad_ref[c].astype(jnp.float32)
        for slab_ref in slabs:
            total += slab_ref[:, part].astype(jnp.float32)
        out_ref[:, part] = total.astype(jnp.bfloat16)


def final_sum(grad, slabs):
    chunks, width, chunk = grad.shape
    return pl.pallas_call(
        final_kernel,
        out_shape=jax.ShapeDtypeStruct((width, chunks * chunk), jnp.bfloat16),
        in_specs=arrays(1 + len(slabs)),
        out_specs=arrays(1)[0],
        compiler_params=params(),
        name="final_sum",
    )(grad, *slabs)


def shift(value, first, by):
    peers, chunks = lax.axis_size("row"), lax.axis_size("col")
    pairs = []
    for r in range(peers):
        for c in range(chunks):
            x, y = divmod(r, SIDE)
            if (c % 2 == 0) == first:
                x = (x + by) % SIDE
            else:
                y = (y + by) % SIDE
            pairs.append((r * chunks + c, (x * SIDE + y) * chunks + c))
    return lax.ppermute(value, ("row", "col"), pairs)


def sorted_codes(tile_rows, tile_cols, tile_nnz, blocks):
    count = tile_rows.shape[0]
    row, core = lax.axis_index("row"), lax.axis_index("col") % 2
    owner = tile_cols // blocks
    back_x = (row // SIDE - owner // SIDE) % SIDE
    back_y = (row % SIDE - owner % SIDE) % SIDE
    group = jnp.where(core == 0, back_y * SIDE + back_x, back_x * SIDE + back_y)
    index = jnp.arange(count, dtype=jnp.int32)
    code = encode(index, tile_cols % blocks, tile_rows - row * blocks, (tile_nnz > 0).astype(jnp.int32))
    earlier = (group[None, :] == group[:, None]) & (index[None, :] < index[:, None])
    place = group * SLOTS + jnp.sum(earlier.astype(jnp.int32), axis=1)
    return jnp.sum(jnp.where(place[None, :] == index[:, None], code[None, :], 0), axis=1)


def body(feats, weight, tile_vals, tile_rows, tile_cols, tile_nnz, cotangent):
    node_rows, width = feats.shape
    peers = lax.axis_size("row")
    chunks = lax.axis_size("col")
    chunk = node_rows // chunks
    exchange = functools.partial(lax.all_to_all, split_axis=0, concat_axis=0, tiled=True)
    tie = lax.optimization_barrier

    feats_t = feats.T
    weight_t = weight.T
    slabs = [feats_t] + [shift(feats_t, True, d) for d in range(1, SIDE)]
    codes = sorted_codes(tile_rows, tile_cols, tile_nnz, node_rows // BLK).reshape(SIDE, PART)
    asked = [codes[0]] + [shift(codes[e], False, -e) for e in range(1, SIDE)]
    codes = [codes[e] for e in range(SIDE)]

    sent = gather_blocks(asked[1:], slabs)
    recv = [None] + [shift(sent[e - 1], False, e) for e in range(1, SIDE)]
    (recv[0],) = gather_blocks(asked[:1], slabs)
    cot = exchange(jnp.swapaxes(cotangent.T.reshape(width, chunks, chunk), 0, 1), "col")

    (total,) = spread(codes[:1], recv[:1], tile_vals, None, None, chunks)
    (total,) = spread([codes[1], codes[3]], [recv[1], recv[3]], tile_vals, total, None, chunks)
    mixed, scale = spread(codes[2:3], recv[2:3], tile_vals, total, feats_t, chunks)
    mixed_full = exchange(mixed, "col").reshape(chunks * width, chunk)
    hidden_t, grad_t, gw_t = dense(mixed_full, cot.reshape(chunks * width, chunk), weight, weight_t)
    grad = exchange(grad_t.reshape(chunks, width, chunk), "col")

    pieces = [None] * SIDE
    for e in (2, 1, 3):
        pieces[e] = shift(back_products(codes[e], grad, scale, tile_vals), False, -e)
    pieces[0] = back_products(codes[0], grad, scale, tile_vals)
    both = jnp.concatenate(
        [hidden_t.reshape(chunks, width, chunk), gw_t.reshape(chunks, width, weight.shape[0])], axis=2
    )
    both, pieces[0] = tie((both, pieces[0]))
    both = exchange(both, "col")
    hidden = jnp.swapaxes(both[:, :, :chunk], 0, 1).reshape(width, node_rows).T
    gw_part = jnp.sum(both[:, :, chunk:].astype(jnp.float32), axis=0).astype(jnp.bfloat16)
    gw_part = jnp.swapaxes(gw_part.reshape(width, peers, -1), 0, 1)

    (total,) = collect([asked[0], asked[2]], [pieces[0], pieces[2]], None, node_rows, False)
    returned = collect([asked[1], asked[3]], [pieces[1], pieces[3]], total, node_rows, True)
    gw = jnp.sum(exchange(gw_part, "row").astype(jnp.float32), axis=0).T
    slabs = [returned[0]] + [shift(returned[d], True, -d) for d in range(1, SIDE)]
    grad_feats = final_sum(grad, slabs).T
    return (hidden, gw, grad_feats)


def solution(mesh):
    placed = (
        P("row", "col"),
        P(),
        P("row", None, None),
        P("row"),
        P("row"),
        P("row"),
        P("row", "col"),
    )
    return jax.shard_map(
        body,
        mesh=mesh,
        in_specs=placed,
        out_specs=(P("row", "col"), P("row", "col"), P("row", "col")),
        check_vma=False,
    )
```

time: 373 us -> 208 us (0.56)
  waiting for transfers between devices: 245 us -> 33.2 us
  Pallas kernels: 0 us -> 79.3 us
  matrix products: 69.6 us -> 0 us
  starting transfers between devices: 0.38 us -> 41.9 us
  between operations: 13.9 us -> 0.88 us
  blocking collectives: 0 us -> 12.8 us
  other arithmetic: 14.2 us -> 4.86 us
  local copies, waits for them, and re-layouts: 29.2 us -> 33.9 us
    reduce_scatter x3 -> x0, waiting for transfers between devices: 146 us -> none  [the longest x1 86.6 us: body(): lax.psum_scatter(summed.reshape(lax.axis_size('row') * node_rows, col_wid...]
    all_gather x2 -> x0, waiting for transfers between devices: 98.2 us -> none  [the longest x1 66.2 us: body(): all_feats = lax.all_gather(feats, 'row', axis=0, tiled=True)]
    pallas_call x0 -> x13, Pallas kernels: none -> 79.3 us  [the longest x3 35.4 us: spread(): pl.pallas_call(functools.partial(spread_kernel, parts, first, last), out_...]
    dot_general x8 -> x0, matrix products: 69.6 us -> none  [the longest x1 22.7 us: body(): jnp.einsum('bt,tjk->bjk', col_select, adjoint_terms, precision=highest)]
    all_to_all x0 -> x4, waiting for transfers between devices: none -> 23.3 us  [the longest x1 10.1 us: body(): mixed_full = exchange(mixed, 'col').reshape(chunks * width, chunk)]
    ppermute x0 -> x15, starting transfers between devices: none -> 22.7 us  [shift(): return lax.ppermute(value, ('row', 'col'), pairs)]
    all_to_all x0 -> x4, starting transfers between devices: none -> 19.2 us  [the longest x1 5.31 us: body(): exchange(jnp.swapaxes(cotangent.T.reshape(width, chunks, chunk), 0, 1), '...]
    unnamed x15 -> x21, local copies, waits for them, and re-layouts: 12.5 us -> 31 us
  transfers between devices with their start and end apart: 5 -> 19, of which waited for: 5 -> 6; matrix products, arithmetic and copies ran while one was open for 17% -> 4% of each run, Pallas kernels for 0% -> 32%
where the time goes in v2:
time: 208 us; the launch traced here: 207 us
  Pallas kernels  79.3 us (38%)
  starting transfers between devices  41.9 us (20%)
  local copies, waits for them, and re-layouts  33.9 us (16%)
  waiting for transfers between devices  33.2 us (16%)
  blocking collectives  12.8 us (6%)
  other arithmetic  4.86 us (2%)
    pallas_call x3, Pallas kernels, spread(): pl.pallas_call(functools.partial(spread_kernel, parts, first, last), out_...  35.4 us
    pallas_call x4, Pallas kernels, back_products(): pl.pallas_call(back_kernel, out_shape=jax.ShapeDtypeStruct((PART, grad.sh...  32.4 us
    unnamed x21, local copies, waits for them, and re-layouts  31 us
    ppermute x15, starting transfers between devices, shift(): return lax.ppermute(value, ('row', 'col'), pairs)  22.7 us
    all_to_all x1, blocking collectives, body(): grad = exchange(grad_t.reshape(chunks, width, chunk), 'col')  12.8 us
    all_to_all x1, waiting for transfers between devices, body(): mixed_full = exchange(mixed, 'col').reshape(chunks * width, chunk)  10.1 us
    ppermute x15, waiting for transfers between devices, shift(): return lax.ppermute(value, ('row', 'col'), pairs)  9.89 us
    all_to_all x1, waiting for transfers between devices, body(): both = exchange(both, 'col')  7.36 us
  transfers between devices with their start and end apart: 19, of which 6 were waited for; matrix products, arithmetic and copies ran while one was open for 4% of the time, Pallas kernels for 32%

profile of v2, /device:TPU:0, one launch (start us, length us, event | category | flops | bytes accessed | tf_op | source)
XLA Modules:
  0.0 206.8 jit_solution(17187376793128381058)
XLA Ops:
  0.6 2.9 %collective-permute-start.5 = (bf16[64,4096]{1,0:T(8,128)(2,1)}, bf16[64,4096]{1,0:T(8,128)(2,1)S(1)}, u32[]{:S(2)}, u32[]{:S(2)}) collective-permute-start(bf16[64,4096]{1,0:T(8,128)(2,1)} %bitcast.29), channel_id=1, source_target_pairs={{0,96},{1,25},{2,98},{3,27},{4,100},{5,29},{6,102},{7,31},{8,104},... | collective-permute-start | bytes 1572872 | tf_op jit(solution)/shard_map/ppermute | solution.py:285
  3.5 0.8 collective-permute-start.4
  4.3 0.9 collective-permute-start.3
  5.2 0.7 broadcast_select_fusion
  5.9 0.2 convert_reduce_fusion.1
  6.1 0.1 select_reduce_fusion
  6.2 0.1 fusion.8
  6.3 1.6 collective-permute-start.2
  7.9 1.7 collective-permute-start
  9.6 3.8 %collective-permute-done.2.refs_2_.refs_1_ = s32[32]{0:T(128)S(1)} collective-permute-done((s32[32]{0:T(128)S(1)}, s32[32]{0:T(128)S(1)}, u32[]{:S(2)}, u32[]{:S(2)}) %collective-permute-start.2) | collective-permute-done | bytes 160 | tf_op jit(solution)/shard_map/ppermute | solution.py:285
  13.3 0.6 collective-permute-start.1
  14.0 4.5 %collective-permute-done.1.refs_1_ = s32[32]{0:T(128)S(1)} collective-permute-done((s32[32]{0:T(128)S(1)}, s32[32]{0:T(128)S(1)}, u32[]{:S(2)}, u32[]{:S(2)}) %collective-permute-start.1) | collective-permute-done | bytes 160 | tf_op jit(solution)/shard_map/ppermute | solution.py:285
  18.5 1.6 collective-permute-done.3.refs_4_.refs_2_
  20.1 1.0 copy-done.5
  21.1 2.6 %gather_blocks.2 = (bf16[32,64,256]{2,1,0:T(8,128)(2,1)}, bf16[32,64,256]{2,1,0:T(8,128)(2,1)}, bf16[32,64,256]{2,1,0:T(8,128)(2,1)}) custom-call(s32[32]{0:T(128)S(1)} %collective-permute-done.refs_0_, s32[32]{0:T(128)S(1)} %collective-permute-done.1.refs_1_, s32[32]{0:T(128)S(1)} %collective-permute-done.2.refs_2_.refs_1_, bf16[64,4096]{1,0:T(8,128)(2,1)S(1)} %bitcast.32, ...), custom_call_target="tpu_custom_call" | custom-call | tf_op jit(solution)/shard_map/gather_blocks/pallas_call | solution.py:54
  23.7 1.6 collective-permute-start.7
  25.3 1.7 collective-permute-start.8
  26.9 2.0 collective-permute-start.6
  28.9 0.8 copy.27
  29.8 5.3 %all-to-all-start.1 = ((bf16[8,64,512]{2,1,0:T(8,128)(2,1)}), bf16[8,64,512]{2,1,0:T(8,128)(2,1)S(1)}, u32[]{:S(2)}, u32[]{:S(2)}) async-start(bf16[8,64,512]{2,1,0:T(8,128)(2,1)} %bitcast.28), calls=%async_computation.1 | async-start | bytes 1048576 | tf_op jit(solution)/shard_map/all_to_all | solution.py:320
  35.1 0.7 gather_blocks.3.refs_1_
  35.8 0.0 copy-start
  35.8 5.8 %copy-done = bf16[128,256,256]{2,1,0:T(8,128)(2,1)S(1)} copy-done((bf16[128,256,256]{2,1,0:T(8,128)(2,1)S(1)}, bf16[128,256,256]{2,1,0:T(8,128)(2,1)}, u32[]{:S(2)}) %copy-start) | copy-done | bytes 16777240
  41.6 8.3 %spread.3.refs_5_ = f32[80,4096]{1,0:T(8,128)S(1)} custom-call(s32[32]{0:T(128)S(1)} %get-tuple-element.33.refs_0_.code_ref, bf16[32,64,256]{2,1,0:T(8,128)(2,1)S(1)} %gather_blocks.3.refs_1_, bf16[128,256,256]{2,1,0:T(8,128)(2,1)S(1)} %copy-done), custom_call_target="tpu_custom_call" | custom-call | tf_op jit(solution)/shard_map/spread/pallas_call | solution.py:139
  49.9 0.0 collective-permute-done.8.refs_3_
  49.9 0.0 copy-start.1
  49.9 5.8 %copy-done.1 = bf16[128,256,256]{2,1,0:T(8,128)(2,1)S(1)} copy-done((bf16[128,256,256]{2,1,0:T(8,128)(2,1)S(1)}, bf16[128,256,256]{2,1,0:T(8,128)(2,1)}, u32[]{:S(2)}) %copy-start.1) | copy-done | bytes 16777240
  55.7 17.1 %spread.4.refs_3_ = f32[80,4096]{1,0:T(8,128)S(1)} custom-call(s32[32]{0:T(128)S(1)} %get-tuple-element.35.refs_0_.code_ref, s32[32]{0:T(128)S(1)} %get-tuple-element.34.refs_1_.code_ref, bf16[32,64,256]{2,1,0:T(8,128)(2,1)} %collective-permute-done.7.refs_2_, bf16[32,64,256]{2,1,0:T(8,128)(2,1)} %collective-permute-done.8.refs_3_, ...), custom_call_target="tpu_custom_call" | custom-call | tf_op jit(solution)/shard_map/spread/pallas_call | solution.py:139
  72.8 0.0 copy-start.2
  72.8 5.8 %copy-done.2 = bf16[128,256,256]{2,1,0:T(8,128)(2,1)S(1)} copy-done((bf16[128,256,256]{2,1,0:T(8,128)(2,1)S(1)}, bf16[128,256,256]{2,1,0:T(8,128)(2,1)}, u32[]{:S(2)}) %copy-start.2) | copy-done | bytes 16777240
  78.6 10.0 %spread.5 = (bf16[8,64,512]{2,1,0:T(8,128)(2,1)}, f32[1,4096]{1,0:T(1,128)S(1)}) custom-call(s32[32]{0:T(128)S(1)} %get-tuple-element.36.refs_0_.code_ref, bf16[32,64,256]{2,1,0:T(8,128)(2,1)} %collective-permute-done.6.refs_1_, bf16[128,256,256]{2,1,0:T(8,128)(2,1)S(1)} %copy-done.2, f32[80,4096]{1,0:T(8,128)S(1)} %spread.4.refs_3_, ...), custom_call_target="tpu_custom_call" | custom-call | tf_op jit(solution)/shard_map/spread/pallas_call | solution.py:139
  88.6 0.0 all-to-all-done.1
  88.6 4.8 %all-to-all-start = ((bf16[8,64,512]{2,1,0:T(8,128)(2,1)}), bf16[8,64,512]{2,1,0:T(8,128)(2,1)S(1)}, u32[]{:S(2)}, u32[]{:S(2)}) async-start(bf16[8,64,512]{2,1,0:T(8,128)(2,1)} %get-tuple-element.20), calls=%async_computation | async-start | bytes 1048576 | tf_op jit(solution)/shard_map/all_to_all | solution.py:325
  93.4 0.2 copy.21
  93.7 10.1 %all-to-all-done = bf16[8,64,512]{2,1,0:T(8,128)(2,1)S(1)} async-done(((bf16[8,64,512]{2,1,0:T(8,128)(2,1)}), bf16[8,64,512]{2,1,0:T(8,128)(2,1)S(1)}, u32[]{:S(2)}, u32[]{:S(2)}) %all-to-all-start) | async-done | bytes 524320 | tf_op jit(solution)/shard_map/all_to_all | solution.py:325
  103.8 1.5 dense.1
  105.3 12.8 %all_to_all.25.grad_ref = bf16[8,64,512]{2,1,0:T(8,128)(2,1)S(1)} all-to-all(bf16[8,64,512]{2,1,0:T(8,128)(2,1)S(1)} %bitcast.38), channel_id=1, replica_groups=mesh['row'=16,'col'=8] {'col'}, dimensions={0} | all-to-all | bytes 1048576 | tf_op jit(solution)/shard_map/all_to_all | solution.py:327
  118.1 5.8 %copy-done.3 = bf16[128,256,256]{2,1,0:T(8,128)(2,1)S(1)} copy-done((bf16[128,256,256]{2,1,0:T(8,128)(2,1)S(1)}, bf16[128,256,256]{2,1,0:T(8,128)(2,1)}, u32[]{:S(2)}) %copy-start.3) | copy-done | bytes 16777240
  123.9 8.6 %back_products.7 = bf16[32,64,256]{2,1,0:T(8,128)(2,1)} custom-call(s32[32]{0:T(128)S(1)} %get-tuple-element.36.refs_0_.code_ref, bf16[8,64,512]{2,1,0:T(8,128)(2,1)S(1)} %all_to_all.25.grad_ref, f32[1,4096]{1,0:T(1,128)S(1)} %get-tuple-element.24.scale_ref, bf16[128,256,256]{2,1,0:T(8,128)(2,1)S(1)} %copy-done.3), custom_call_target="tpu_custom_call" | custom-call | tf_op jit(solution)/shard_map/back_products/pallas_call | solution.py:204
  132.5 3.9 %collective-permute-start.11 = (bf16[32,64,256]{2,1,0:T(8,128)(2,1)}, bf16[32,64,256]{2,1,0:T(8,128)(2,1)}, u32[]{:S(2)}, u32[]{:S(2)}) collective-permute-start(bf16[32,64,256]{2,1,0:T(8,128)(2,1)} %back_products.7), channel_id=1, source_target_pairs={{0,16},{1,65},{2,18},{3,67},{4,20},{5,69},{6,22},{7,71},{8,24},{9,... | collective-permute-start | bytes 3145736 | tf_op jit(solution)/shard_map/ppermute | solution.py:285
  136.4 7.6 %back_products.5 = bf16[32,64,256]{2,1,0:T(8,128)(2,1)S(1)} custom-call(s32[32]{0:T(128)S(1)} %get-tuple-element.35.refs_0_.code_ref, bf16[8,64,512]{2,1,0:T(8,128)(2,1)S(1)} %all_to_all.25.grad_ref, f32[1,4096]{1,0:T(1,128)S(1)} %get-tuple-element.24.scale_ref, bf16[128,256,256]{2,1,0:T(8,128)(2,1)S(1)} %copy-done.3), custom_call_target="tpu_custom_call" | custom-call | tf_op jit(solution)/shard_map/back_products/pallas_call | solution.py:204
  144.1 1.3 collective-permute-start.9
  145.4 8.6 %back_products.6 = bf16[32,64,256]{2,1,0:T(8,128)(2,1)} custom-call(s32[32]{0:T(128)S(1)} %get-tuple-element.34.refs_1_.code_ref, bf16[8,64,512]{2,1,0:T(8,128)(2,1)S(1)} %all_to_all.25.grad_ref, f32[1,4096]{1,0:T(1,128)S(1)} %get-tuple-element.24.scale_ref, bf16[128,256,256]{2,1,0:T(8,128)(2,1)S(1)} %copy-done.3), custom_call_target="tpu_custom_call" | custom-call | tf_op jit(solution)/shard_map/back_products/pallas_call | solution.py:204
  154.0 0.9 collective-permute-start.10
  154.9 1.1 pad_maximum_fusion
  156.0 5.8 %copy-done.4 = bf16[128,256,256]{2,1,0:T(8,128)(2,1)S(1)} copy-done((bf16[128,256,256]{2,1,0:T(8,128)(2,1)S(1)}, bf16[128,256,256]{2,1,0:T(8,128)(2,1)}, u32[]{:S(2)}) %copy-start.4) | copy-done | bytes 16777240
  161.8 7.6 %back_products.4.refs_2_ = bf16[32,64,256]{2,1,0:T(8,128)(2,1)S(1)} custom-call(s32[32]{0:T(128)S(1)} %get-tuple-element.33.refs_0_.code_ref, bf16[8,64,512]{2,1,0:T(8,128)(2,1)S(1)} %all_to_all.25.grad_ref, f32[1,4096]{1,0:T(1,128)S(1)} %get-tuple-element.24.scale_ref, bf16[128,256,256]{2,1,0:T(8,128)(2,1)S(1)} %copy-done.4), custom_call_target="tpu_custom_call" | custom-call | tf_op jit(solution)/shard_map/back_products/pallas_call | solution.py:204
  169.4 4.4 %all-to-all-start.3 = ((bf16[8,64,1024]{2,1,0:T(8,128)(2,1)}), bf16[8,64,1024]{2,1,0:T(8,128)(2,1)}, u32[]{:S(2)}, u32[]{:S(2)}) async-start(bf16[8,64,1024]{2,1,0:T(8,128)(2,1)} %pad_maximum_fusion), calls=%async_computation.3 | async-start | bytes 2097152 | tf_op jit(solution)/shard_map/all_to_all | solution.py:337
  173.8 0.0 collective-permute-done.11.refs_3_
  173.9 2.0 collect.2.refs_4_
  175.9 3.5 %collect.3 = (bf16[64,4096]{1,0:T(8,128)(2,1)S(1)}, bf16[64,4096]{1,0:T(8,128)(2,1)}, bf16[64,4096]{1,0:T(8,128)(2,1)}, bf16[64,4096]{1,0:T(8,128)(2,1)S(1)}) custom-call(s32[32]{0:T(128)S(1)} %collective-permute-done.refs_0_, s32[32]{0:T(128)S(1)} %collective-permute-done.2.refs_2_.refs_1_, bf16[32,64,256]{2,1,0:T(8,128)(2,1)} %collective-permute-done.9.refs_2_, ...), custom_call_target="tpu_custom_call" | custom-call | tf_op jit(solution)/shard_map/collect/pallas_call | solution.py:240
  179.4 1.2 collective-permute-start.12
  180.6 0.8 collective-permute-start.13
  181.4 0.9 collective-permute-start.14
  182.3 7.4 %all-to-all-done.3 = bf16[8,64,1024]{2,1,0:T(8,128)(2,1)} async-done(((bf16[8,64,1024]{2,1,0:T(8,128)(2,1)}), bf16[8,64,1024]{2,1,0:T(8,128)(2,1)}, u32[]{:S(2)}, u32[]{:S(2)}) %all-to-all-start.3) | async-done | bytes 1048608 | tf_op jit(solution)/shard_map/all_to_all | solution.py:337
  189.6 2.1 %slice_reduce_fusion = (bf16[64,512]{1,0:T(8,128)(2,1)S(1)}, bf16[8,8,8,512]{3,2,1,0:T(8,128)(2,1)}) fusion(bf16[8,64,1024]{2,1,0:T(8,128)(2,1)} %all-to-all-done.3), kind=kLoop, calls=%fused_computation.2 | loop fusion | flops 229376 | bytes 1638400 | tf_op jit(solution)/shard_map/reduce_sum | solution.py:339
  191.7 0.1 copy.23
  191.8 0.8 reshape.51
  192.6 4.6 %all-to-all-start.4 = ((bf16[16,2,1024]{2,1,0:T(2,128)(2,1)}), bf16[16,2,1024]{2,1,0:T(2,128)(2,1)S(1)}, u32[]{:S(2)}, u32[]{:S(2)}) async-start(bf16[16,2,1024]{2,1,0:T(2,128)(2,1)} %reshape.51), calls=%async_computation.4 | async-start | bytes 131072 | tf_op jit(solution)/shard_map/all_to_all | solution.py:344
  197.2 1.9 copy.25
  199.1 5.8 %all-to-all-done.4 = bf16[16,2,1024]{2,1,0:T(2,128)(2,1)S(1)} async-done(((bf16[16,2,1024]{2,1,0:T(2,128)(2,1)}), bf16[16,2,1024]{2,1,0:T(2,128)(2,1)S(1)}, u32[]{:S(2)}, u32[]{:S(2)}) %all-to-all-start.4) | async-done | bytes 65568 | tf_op jit(solution)/shard_map/all_to_all | solution.py:344
  204.9 0.1 reshape.52
  205.1 0.6 convert_reduce_fusion
  205.7 1.1 final_sum.1
  (20 shorter events, 0.0 us)
Async XLA Ops:
  0.6 17.8 %collective-permute-start.5 = (bf16[64,4096]{1,0:T(8,128)(2,1)}, bf16[64,4096]{1,0:T(8,128)(2,1)S(1)}, u32[]{:S(2)}, u32[]{:S(2)}) collective-permute-start(bf16[64,4096]{1,0:T(8,128)(2,1)} %bitcast.29), channel_id=1, source_target_pairs={{0,96},{1,25},{2,98},{3,27},{4,100},{5,29},{6,102},{7,31},{8,104},... | collective-permute-start | bytes 1572872 | tf_op jit(solution)/shard_map/ppermute | solution.py:285
  3.5 14.9 %collective-permute-start.4 = (bf16[64,4096]{1,0:T(8,128)(2,1)}, bf16[64,4096]{1,0:T(8,128)(2,1)S(1)}, u32[]{:S(2)}, u32[]{:S(2)}) collective-permute-start(bf16[64,4096]{1,0:T(8,128)(2,1)} %bitcast.30), channel_id=1, source_target_pairs={{0,64},{1,17},{2,66},{3,19},{4,68},{5,21},{6,70},{7,23},{8,72},{9,... | collective-permute-start | bytes 1572872 | tf_op jit(solution)/shard_map/ppermute | solution.py:285
  4.3 15.7 %collective-permute-start.3 = (bf16[64,4096]{1,0:T(8,128)(2,1)}, bf16[64,4096]{1,0:T(8,128)(2,1)S(1)}, u32[]{:S(2)}, u32[]{:S(2)}) collective-permute-start(bf16[64,4096]{1,0:T(8,128)(2,1)} %bitcast.31), channel_id=1, source_target_pairs={{0,32},{1,9},{2,34},{3,11},{4,36},{5,13},{6,38},{7,15},{8,40},{9,1... | collective-permute-start | bytes 1572872 | tf_op jit(solution)/shard_map/ppermute | solution.py:285
  6.3 7.0 %collective-permute-start.2 = (s32[32]{0:T(128)S(1)}, s32[32]{0:T(128)S(1)}, u32[]{:S(2)}, u32[]{:S(2)}) collective-permute-start(s32[32]{0:T(128)S(1)} %get-tuple-element.34.refs_1_.code_ref), channel_id=1, source_target_pairs={{0,8},{1,33},{2,10},{3,35},{4,12},{5,37},{6,14},{7,39},{8,16},{9,4... | collective-permute-start | bytes 392 | tf_op jit(solution)/shard_map/ppermute | solution.py:285
  7.9 6.1 %collective-permute-start = (s32[32]{0:T(128)S(1)}, s32[32]{0:T(128)S(1)}, u32[]{:S(2)}, u32[]{:S(2)}) collective-permute-start(s32[32]{0:T(128)S(1)} %get-tuple-element.35.refs_0_.code_ref), channel_id=1, source_target_pairs={{0,24},{1,97},{2,26},{3,99},{4,28},{5,101},{6,30},{7,103},{8,0},{9... | collective-permute-start | bytes 392 | tf_op jit(solution)/shard_map/ppermute | solution.py:285
  13.3 5.1 %collective-permute-start.1 = (s32[32]{0:T(128)S(1)}, s32[32]{0:T(128)S(1)}, u32[]{:S(2)}, u32[]{:S(2)}) collective-permute-start(s32[32]{0:T(128)S(1)} %get-tuple-element.36.refs_0_.code_ref), channel_id=1, source_target_pairs={{0,16},{1,65},{2,18},{3,67},{4,20},{5,69},{6,22},{7,71},{8,24},{9,... | collective-permute-start | bytes 392 | tf_op jit(solution)/shard_map/ppermute | solution.py:285
  20.1 1.0 copy-start.5
  21.1 7.8 %copy-start.8 = (bf16[4096,64]{0,1:T(8,128)(2,1)S(1)}, bf16[4096,64]{0,1:T(8,128)(2,1)}, u32[]{:S(2)}) copy-start(bf16[4096,64]{0,1:T(8,128)(2,1)} %param.13) | copy-start | bytes 1572868
  21.1 14.0 %copy-start.6 = (bf16[4096,64]{0,1:T(8,128)(2,1)S(1)}, bf16[4096,64]{0,1:T(8,128)(2,1)}, u32[]{:S(2)}) copy-start(bf16[4096,64]{0,1:T(8,128)(2,1)} %param.7) | copy-start | bytes 1572868
  23.7 26.2 %collective-permute-start.7 = (bf16[32,64,256]{2,1,0:T(8,128)(2,1)}, bf16[32,64,256]{2,1,0:T(8,128)(2,1)}, u32[]{:S(2)}, u32[]{:S(2)}) collective-permute-start(bf16[32,64,256]{2,1,0:T(8,128)(2,1)} %get-tuple-element.18), channel_id=1, source_target_pairs={{0,8},{1,33},{2,10},{3,35},{4,12},{5,37},{6,14},{7,39},{8,16},{9,4... | collective-permute-start | bytes 3145736 | tf_op jit(solution)/shard_map/ppermute | solution.py:285
  25.3 24.6 %collective-permute-start.8 = (bf16[32,64,256]{2,1,0:T(8,128)(2,1)}, bf16[32,64,256]{2,1,0:T(8,128)(2,1)}, u32[]{:S(2)}, u32[]{:S(2)}) collective-permute-start(bf16[32,64,256]{2,1,0:T(8,128)(2,1)} %get-tuple-element.19), channel_id=1, source_target_pairs={{0,24},{1,97},{2,26},{3,99},{4,28},{5,101},{6,30},{7,103},{8,0},{9... | collective-permute-start | bytes 3145736 | tf_op jit(solution)/shard_map/ppermute | solution.py:285
  26.9 45.9 %collective-permute-start.6 = (bf16[32,64,256]{2,1,0:T(8,128)(2,1)}, bf16[32,64,256]{2,1,0:T(8,128)(2,1)}, u32[]{:S(2)}, u32[]{:S(2)}) collective-permute-start(bf16[32,64,256]{2,1,0:T(8,128)(2,1)} %get-tuple-element.17), channel_id=1, source_target_pairs={{0,16},{1,65},{2,18},{3,67},{4,20},{5,69},{6,22},{7,71},{8,24},{9,... | collective-permute-start | bytes 3145736 | tf_op jit(solution)/shard_map/ppermute | solution.py:285
  29.8 58.8 %all-to-all-start.1 = ((bf16[8,64,512]{2,1,0:T(8,128)(2,1)}), bf16[8,64,512]{2,1,0:T(8,128)(2,1)S(1)}, u32[]{:S(2)}, u32[]{:S(2)}) async-start(bf16[8,64,512]{2,1,0:T(8,128)(2,1)} %bitcast.28), calls=%async_computation.1 | async-start | bytes 1048576 | tf_op jit(solution)/shard_map/all_to_all | solution.py:320
  35.8 5.8 %copy-start = (bf16[128,256,256]{2,1,0:T(8,128)(2,1)S(1)}, bf16[128,256,256]{2,1,0:T(8,128)(2,1)}, u32[]{:S(2)}) copy-start(bf16[128,256,256]{2,1,0:T(8,128)(2,1)} %tiles_ref.7) | copy-start | bytes 50331652
  49.9 5.8 %copy-start.1 = (bf16[128,256,256]{2,1,0:T(8,128)(2,1)S(1)}, bf16[128,256,256]{2,1,0:T(8,128)(2,1)}, u32[]{:S(2)}) copy-start(bf16[128,256,256]{2,1,0:T(8,128)(2,1)} %tiles_ref.7) | copy-start | bytes 50331652
  72.8 5.8 %copy-start.2 = (bf16[128,256,256]{2,1,0:T(8,128)(2,1)S(1)}, bf16[128,256,256]{2,1,0:T(8,128)(2,1)}, u32[]{:S(2)}) copy-start(bf16[128,256,256]{2,1,0:T(8,128)(2,1)} %tiles_ref.7) | copy-start | bytes 50331652
  78.6 14.9 %copy-start.7 = (bf16[512,512]{1,0:T(8,128)(2,1)S(1)}, bf16[512,512]{1,0:T(8,128)(2,1)}, u32[]{:S(2)}) copy-start(bf16[512,512]{1,0:T(8,128)(2,1)} %weight_ref.1) | copy-start | bytes 1572868
  88.6 15.2 %all-to-all-start = ((bf16[8,64,512]{2,1,0:T(8,128)(2,1)}), bf16[8,64,512]{2,1,0:T(8,128)(2,1)S(1)}, u32[]{:S(2)}, u32[]{:S(2)}) async-start(bf16[8,64,512]{2,1,0:T(8,128)(2,1)} %get-tuple-element.20), calls=%async_computation | async-start | bytes 1048576 | tf_op jit(solution)/shard_map/all_to_all | solution.py:325
  118.1 5.8 %copy-start.3 = (bf16[128,256,256]{2,1,0:T(8,128)(2,1)S(1)}, bf16[128,256,256]{2,1,0:T(8,128)(2,1)}, u32[]{:S(2)}) copy-start(bf16[128,256,256]{2,1,0:T(8,128)(2,1)} %tiles_ref.7) | copy-start | bytes 50331652
  132.5 41.3 %collective-permute-start.11 = (bf16[32,64,256]{2,1,0:T(8,128)(2,1)}, bf16[32,64,256]{2,1,0:T(8,128)(2,1)}, u32[]{:S(2)}, u32[]{:S(2)}) collective-permute-start(bf16[32,64,256]{2,1,0:T(8,128)(2,1)} %back_products.7), channel_id=1, source_target_pairs={{0,16},{1,65},{2,18},{3,67},{4,20},{5,69},{6,22},{7,71},{8,24},{9,... | collective-permute-start | bytes 3145736 | tf_op jit(solution)/shard_map/ppermute | solution.py:285
  144.1 31.9 %collective-permute-start.9 = (bf16[32,64,256]{2,1,0:T(8,128)(2,1)S(1)}, bf16[32,64,256]{2,1,0:T(8,128)(2,1)}, u32[]{:S(2)}, u32[]{:S(2)}) collective-permute-start(bf16[32,64,256]{2,1,0:T(8,128)(2,1)S(1)} %back_products.5), channel_id=1, source_target_pairs={{0,24},{1,97},{2,26},{3,99},{4,28},{5,101},{6,30},{7,103},{8,0},{9... | collective-permute-start | bytes 3145736 | tf_op jit(solution)/shard_map/ppermute | solution.py:285
  154.0 21.9 %collective-permute-start.10 = (bf16[32,64,256]{2,1,0:T(8,128)(2,1)}, bf16[32,64,256]{2,1,0:T(8,128)(2,1)}, u32[]{:S(2)}, u32[]{:S(2)}) collective-permute-start(bf16[32,64,256]{2,1,0:T(8,128)(2,1)} %back_products.6), channel_id=1, source_target_pairs={{0,8},{1,33},{2,10},{3,35},{4,12},{5,37},{6,14},{7,39},{8,16},{9,4... | collective-permute-start | bytes 3145736 | tf_op jit(solution)/shard_map/ppermute | solution.py:285
  156.0 5.8 %copy-start.4 = (bf16[128,256,256]{2,1,0:T(8,128)(2,1)S(1)}, bf16[128,256,256]{2,1,0:T(8,128)(2,1)}, u32[]{:S(2)}) copy-start(bf16[128,256,256]{2,1,0:T(8,128)(2,1)} %tiles_ref.7) | copy-start | bytes 50331652
  169.4 20.2 %all-to-all-start.3 = ((bf16[8,64,1024]{2,1,0:T(8,128)(2,1)}), bf16[8,64,1024]{2,1,0:T(8,128)(2,1)}, u32[]{:S(2)}, u32[]{:S(2)}) async-start(bf16[8,64,1024]{2,1,0:T(8,128)(2,1)} %pad_maximum_fusion), calls=%async_computation.3 | async-start | bytes 2097152 | tf_op jit(solution)/shard_map/all_to_all | solution.py:337
  179.4 26.3 %collective-permute-start.12 = (bf16[64,4096]{1,0:T(8,128)(2,1)}, bf16[64,4096]{1,0:T(8,128)(2,1)S(1)}, u32[]{:S(2)}, u32[]{:S(2)}) collective-permute-start(bf16[64,4096]{1,0:T(8,128)(2,1)} %get-tuple-element.28), channel_id=1, source_target_pairs={{0,96},{1,25},{2,98},{3,27},{4,100},{5,29},{6,102},{7,31},{8,104},... | collective-permute-start | bytes 1572872 | tf_op jit(solution)/shard_map/ppermute | solution.py:285
  180.6 25.1 %collective-permute-start.13 = (bf16[64,4096]{1,0:T(8,128)(2,1)}, bf16[64,4096]{1,0:T(8,128)(2,1)S(1)}, u32[]{:S(2)}, u32[]{:S(2)}) collective-permute-start(bf16[64,4096]{1,0:T(8,128)(2,1)} %get-tuple-element.29), channel_id=1, source_target_pairs={{0,64},{1,17},{2,66},{3,19},{4,68},{5,21},{6,70},{7,23},{8,72},{9,... | collective-permute-start | bytes 1572872 | tf_op jit(solution)/shard_map/ppermute | solution.py:285
  181.4 24.3 %collective-permute-start.14 = (bf16[64,4096]{1,0:T(8,128)(2,1)S(1)}, bf16[64,4096]{1,0:T(8,128)(2,1)S(1)}, u32[]{:S(2)}, u32[]{:S(2)}) collective-permute-start(bf16[64,4096]{1,0:T(8,128)(2,1)S(1)} %get-tuple-element.30), channel_id=1, source_target_pairs={{0,32},{1,9},{2,34},{3,11},{4,36},{5,13},{6,38},{7,15},{8,40},{9,1... | collective-permute-start | bytes 1572872 | tf_op jit(solution)/shard_map/ppermute | solution.py:285
  192.6 12.3 %all-to-all-start.4 = ((bf16[16,2,1024]{2,1,0:T(2,128)(2,1)}), bf16[16,2,1024]{2,1,0:T(2,128)(2,1)S(1)}, u32[]{:S(2)}, u32[]{:S(2)}) async-start(bf16[16,2,1024]{2,1,0:T(2,128)(2,1)} %reshape.51), calls=%async_computation.4 | async-start | bytes 131072 | tf_op jit(solution)/shard_map/all_to_all | solution.py:344

commit v3 on v2

--- a/solution.py
+++ b/solution.py
@@ -12,12 +12,13 @@
 SIDE = 4
 PART = SIDE * SLOTS
 VMEM_LIMIT = 32 * 1024 * 1024
+TILES_VMEM_LIMIT = 50 * 1024 * 1024
 GELU_C = 0.7978845608028654
 GELU_A = 0.044715
 
 
-def params():
-    return pltpu.CompilerParams(vmem_limit_bytes=VMEM_LIMIT)
+def params(limit=VMEM_LIMIT):
+    return pltpu.CompilerParams(vmem_limit_bytes=limit)
 
 
 def scalars(n):
@@ -142,7 +143,7 @@
         in_specs=scalars(parts) + arrays(parts) + [pl.BlockSpec(memory_space=pl.ANY)] + arrays(len(extra)),
         out_specs=tuple(arrays(len(out_shape))),
         scratch_shapes=scratch,
-        compiler_params=params(),
+        compiler_params=params(TILES_VMEM_LIMIT),
         name="spread",
     )(*codes, *recvs, tile_vals, *extra)
 
@@ -210,7 +211,7 @@
             pltpu.VMEM((SIDE, SLOTS, BLK, BLK), jnp.bfloat16),
             pltpu.SemaphoreType.DMA((SIDE,)),
         ],
-        compiler_params=params(),
+        compiler_params=params(TILES_VMEM_LIMIT),
         name="back_products",
     )(code, grad, scale, tile_vals)
 
@@ -326,14 +327,16 @@
     hidden_t, grad_t, gw_t = dense(mixed_full, cot.reshape(chunks * width, chunk), weight, weight_t)
     grad = exchange(grad_t.reshape(chunks, width, chunk), "col")
 
-    pieces = [None] * SIDE
-    for e in (2, 1, 3):
-        pieces[e] = shift(back_products(codes[e], grad, scale, tile_vals), False, -e)
-    pieces[0] = back_products(codes[0], grad, scale, tile_vals)
     both = jnp.concatenate(
         [hidden_t.reshape(chunks, width, chunk), gw_t.reshape(chunks, width, weight.shape[0])], axis=2
     )
-    both, pieces[0] = tie((both, pieces[0]))
+    pieces = [None] * SIDE
+    for e in (2, 1, 3, 0):
+        pieces[e] = back_products(codes[e], grad, scale, tile_vals)
+        if e == 2:
+            pieces[e], both = tie((pieces[e], both))
+        if e > 0:
+            pieces[e] = shift(pieces[e], False, -e)
     both = exchange(both, "col")
     hidden = jnp.swapaxes(both[:, :, :chunk], 0, 1).reshape(width, node_rows).T
     gw_part = jnp.sum(both[:, :, chunk:].astype(jnp.float32), axis=0).astype(jnp.bfloat16)

time: 208 us -> 155 us (0.75)
  Pallas kernels: 79.3 us -> 41.9 us
  local copies, waits for them, and re-layouts: 33.9 us -> 6.15 us
  waiting for transfers between devices: 33.2 us -> 48.2 us
  blocking collectives: 12.8 us -> 0 us
  starting transfers between devices: 41.9 us -> 51.9 us
    unnamed x21 -> x13, local copies, waits for them, and re-layouts: 31 us -> 3.23 us
    pallas_call x3, Pallas kernels: 35.4 us -> 16.1 us  [spread(): pl.pallas_call(functools.partial(spread_kernel, parts, first, last), out_...]
    pallas_call x4, Pallas kernels: 32.4 us -> 13.7 us  [back_products(): pl.pallas_call(back_kernel, out_shape=jax.ShapeDtypeStruct((PART, grad.sh...]
    ppermute x15, waiting for transfers between devices: 9.89 us -> 23 us  [shift(): return lax.ppermute(value, ('row', 'col'), pairs)]
    all_to_all x1 -> x0, blocking collectives: 12.8 us -> none  [body(): grad = exchange(grad_t.reshape(chunks, width, chunk), 'col')]
    all_to_all x0 -> x1, waiting for transfers between devices: none -> 9.12 us  [body(): grad = exchange(grad_t.reshape(chunks, width, chunk), 'col')]
    all_to_all x1, waiting for transfers between devices: 7.36 us -> 0.01 us  [body(): both = exchange(both, 'col')]
    all_to_all x0 -> x1, starting transfers between devices: none -> 3.49 us  [body(): grad = exchange(grad_t.reshape(chunks, width, chunk), 'col')]
  transfers between devices with their start and end apart: 19 -> 20, of which waited for: 6 -> 8; matrix products, arithmetic and copies ran while one was open for 4% -> 6% of each run, Pallas kernels for 32% -> 21%
where the time goes in v3:
time: 155 us; the launch traced here: 154 us
  starting transfers between devices  51.9 us (33%)
  waiting for transfers between devices  48.2 us (31%)
  Pallas kernels  41.9 us (27%)
  local copies, waits for them, and re-layouts  6.15 us (4%)
  other arithmetic  4.88 us (3%)
    ppermute x15, starting transfers between devices, shift(): return lax.ppermute(value, ('row', 'col'), pairs)  23.9 us
    ppermute x15, waiting for transfers between devices, shift(): return lax.ppermute(value, ('row', 'col'), pairs)  23 us
    pallas_call x3, Pallas kernels, spread(): pl.pallas_call(functools.partial(spread_kernel, parts, first, last), out_...  16.1 us
    pallas_call x4, Pallas kernels, back_products(): pl.pallas_call(back_kernel, out_shape=jax.ShapeDtypeStruct((PART, grad.sh...  13.7 us
    all_to_all x1, waiting for transfers between devices, body(): mixed_full = exchange(mixed, 'col').reshape(chunks * width, chunk)  10.1 us
    all_to_all x1, waiting for transfers between devices, body(): grad = exchange(grad_t.reshape(chunks, width, chunk), 'col')  9.12 us
    all_to_all x1, starting transfers between devices, body(): mixed_full = exchange(mixed, 'col').reshape(chunks * width, chunk)  8.22 us
    all_to_all x1, starting transfers between devices, body(): gw = jnp.sum(exchange(gw_part, 'row').astype(jnp.float32), axis=0).T  6.75 us
  transfers between devices with their start and end apart: 20, of which 8 were waited for; matrix products, arithmetic and copies ran while one was open for 6% of the time, Pallas kernels for 21%

profile of v3, /device:TPU:0, one launch (start us, length us, event | category | flops | bytes accessed | tf_op | source)
XLA Modules:
  0.0 153.9 jit_solution(12406391744762458097)
XLA Ops:
  0.6 2.9 %collective-permute-start.5 = (bf16[64,4096]{1,0:T(8,128)(2,1)}, bf16[64,4096]{1,0:T(8,128)(2,1)S(1)}, u32[]{:S(2)}, u32[]{:S(2)}) collective-permute-start(bf16[64,4096]{1,0:T(8,128)(2,1)} %bitcast.29), channel_id=1, source_target_pairs={{0,96},{1,25},{2,98},{3,27},{4,100},{5,29},{6,102},{7,31},{8,104},... | collective-permute-start | bytes 1572872 | tf_op jit(solution)/shard_map/ppermute | solution.py:286
  3.5 0.8 collective-permute-start.4
  4.3 0.9 collective-permute-start.3
  5.2 0.7 broadcast_select_fusion
  5.9 0.2 convert_reduce_fusion.1
  6.1 0.1 select_reduce_fusion
  6.2 0.1 fusion.8
  6.3 1.6 %collective-permute-start.2 = (s32[32]{0:T(128)S(1)}, s32[32]{0:T(128)S(1)}, u32[]{:S(2)}, u32[]{:S(2)}) collective-permute-start(s32[32]{0:T(128)S(1)} %get-tuple-element.34.refs_1_.code_ref), channel_id=1, source_target_pairs={{0,8},{1,33},{2,10},{3,35},{4,12},{5,37},{6,14},{7,39},{8,16},{9,4... | collective-permute-start | bytes 392 | tf_op jit(solution)/shard_map/ppermute | solution.py:286
  7.9 1.7 %collective-permute-start = (s32[32]{0:T(128)S(1)}, s32[32]{0:T(128)S(1)}, u32[]{:S(2)}, u32[]{:S(2)}) collective-permute-start(s32[32]{0:T(128)S(1)} %get-tuple-element.35.refs_0_.code_ref), channel_id=1, source_target_pairs={{0,24},{1,97},{2,26},{3,99},{4,28},{5,101},{6,30},{7,103},{8,0},{9... | collective-permute-start | bytes 392 | tf_op jit(solution)/shard_map/ppermute | solution.py:286
  9.6 3.8 %collective-permute-done.2.refs_2_.refs_1_ = s32[32]{0:T(128)S(1)} collective-permute-done((s32[32]{0:T(128)S(1)}, s32[32]{0:T(128)S(1)}, u32[]{:S(2)}, u32[]{:S(2)}) %collective-permute-start.2) | collective-permute-done | bytes 160 | tf_op jit(solution)/shard_map/ppermute | solution.py:286
  13.3 0.6 collective-permute-start.1
  14.0 0.0 collective-permute-done.refs_0_
  14.0 4.5 %collective-permute-done.1.refs_1_ = s32[32]{0:T(128)S(1)} collective-permute-done((s32[32]{0:T(128)S(1)}, s32[32]{0:T(128)S(1)}, u32[]{:S(2)}, u32[]{:S(2)}) %collective-permute-start.1) | collective-permute-done | bytes 160 | tf_op jit(solution)/shard_map/ppermute | solution.py:286
  18.5 0.0 collective-permute-done.5.refs_6_.refs_4_
  18.5 1.6 %collective-permute-done.3.refs_4_.refs_2_ = bf16[64,4096]{1,0:T(8,128)(2,1)S(1)} collective-permute-done((bf16[64,4096]{1,0:T(8,128)(2,1)}, bf16[64,4096]{1,0:T(8,128)(2,1)S(1)}, u32[]{:S(2)}, u32[]{:S(2)}) %collective-permute-start.3) | collective-permute-done | bytes 524320 | tf_op jit(solution)/shard_map/ppermute | solution.py:286
  20.1 1.0 copy-done.1
  21.1 2.6 %gather_blocks.2 = (bf16[32,64,256]{2,1,0:T(8,128)(2,1)}, bf16[32,64,256]{2,1,0:T(8,128)(2,1)}, bf16[32,64,256]{2,1,0:T(8,128)(2,1)}) custom-call(s32[32]{0:T(128)S(1)} %collective-permute-done.refs_0_, s32[32]{0:T(128)S(1)} %collective-permute-done.1.refs_1_, s32[32]{0:T(128)S(1)} %collective-permute-done.2.refs_2_.refs_1_, bf16[64,4096]{1,0:T(8,128)(2,1)S(1)} %bitcast.32, ...), custom_call_target="tpu_custom_call" | custom-call | tf_op jit(solution)/shard_map/gather_blocks/pallas_call | solution.py:55
  23.7 1.6 %collective-permute-start.7 = (bf16[32,64,256]{2,1,0:T(8,128)(2,1)}, bf16[32,64,256]{2,1,0:T(8,128)(2,1)}, u32[]{:S(2)}, u32[]{:S(2)}) collective-permute-start(bf16[32,64,256]{2,1,0:T(8,128)(2,1)} %get-tuple-element.18), channel_id=1, source_target_pairs={{0,8},{1,33},{2,10},{3,35},{4,12},{5,37},{6,14},{7,39},{8,16},{9,4... | collective-permute-start | bytes 3145736 | tf_op jit(solution)/shard_map/ppermute | solution.py:286
  25.3 1.7 %collective-permute-start.8 = (bf16[32,64,256]{2,1,0:T(8,128)(2,1)}, bf16[32,64,256]{2,1,0:T(8,128)(2,1)}, u32[]{:S(2)}, u32[]{:S(2)}) collective-permute-start(bf16[32,64,256]{2,1,0:T(8,128)(2,1)} %get-tuple-element.19), channel_id=1, source_target_pairs={{0,24},{1,97},{2,26},{3,99},{4,28},{5,101},{6,30},{7,103},{8,0},{9... | collective-permute-start | bytes 3145736 | tf_op jit(solution)/shard_map/ppermute | solution.py:286
  27.0 2.0 %collective-permute-start.6 = (bf16[32,64,256]{2,1,0:T(8,128)(2,1)}, bf16[32,64,256]{2,1,0:T(8,128)(2,1)}, u32[]{:S(2)}, u32[]{:S(2)}) collective-permute-start(bf16[32,64,256]{2,1,0:T(8,128)(2,1)} %get-tuple-element.17), channel_id=1, source_target_pairs={{0,16},{1,65},{2,18},{3,67},{4,20},{5,69},{6,22},{7,71},{8,24},{9,... | collective-permute-start | bytes 3145736 | tf_op jit(solution)/shard_map/ppermute | solution.py:286
  29.0 0.8 copy.27
  29.8 5.3 %all-to-all-start.1 = ((bf16[8,64,512]{2,1,0:T(8,128)(2,1)}), bf16[8,64,512]{2,1,0:T(8,128)(2,1)S(1)}, u32[]{:S(2)}, u32[]{:S(2)}) async-start(bf16[8,64,512]{2,1,0:T(8,128)(2,1)} %bitcast.28), calls=%async_computation.1 | async-start | bytes 1048576 | tf_op jit(solution)/shard_map/all_to_all | solution.py:321
  35.1 0.7 gather_blocks.3.refs_1_
  35.8 3.7 %spread.3.refs_5_ = f32[80,4096]{1,0:T(8,128)S(1)} custom-call(s32[32]{0:T(128)S(1)} %get-tuple-element.33.refs_0_.code_ref, bf16[32,64,256]{2,1,0:T(8,128)(2,1)S(1)} %gather_blocks.3.refs_1_, bf16[128,256,256]{2,1,0:T(8,128)(2,1)} %tiles_ref.7), custom_call_target="tpu_custom_call" | custom-call | tf_op jit(solution)/shard_map/spread/pallas_call | solution.py:140
  39.6 1.1 copy-done
  40.6 0.0 collective-permute-done.7.refs_2_
  40.6 0.0 collective-permute-done.8.refs_3_
  40.6 7.0 %spread.4.refs_3_ = f32[80,4096]{1,0:T(8,128)S(1)} custom-call(s32[32]{0:T(128)S(1)} %get-tuple-element.35.refs_0_.code_ref, s32[32]{0:T(128)S(1)} %get-tuple-element.34.refs_1_.code_ref, bf16[32,64,256]{2,1,0:T(8,128)(2,1)} %collective-permute-done.7.refs_2_, bf16[32,64,256]{2,1,0:T(8,128)(2,1)} %collective-permute-done.8.refs_3_, ...), custom_call_target="tpu_custom_call" | custom-call | tf_op jit(solution)/shard_map/spread/pallas_call | solution.py:140
  47.7 0.0 copy-start.3
  47.7 4.8 %collective-permute-done.6.refs_1_ = bf16[32,64,256]{2,1,0:T(8,128)(2,1)} collective-permute-done((bf16[32,64,256]{2,1,0:T(8,128)(2,1)}, bf16[32,64,256]{2,1,0:T(8,128)(2,1)}, u32[]{:S(2)}, u32[]{:S(2)}) %collective-permute-start.6) | collective-permute-done | bytes 1048608 | tf_op jit(solution)/shard_map/ppermute | solution.py:286
  52.5 5.4 %spread.5 = (bf16[8,64,512]{2,1,0:T(8,128)(2,1)}, f32[1,4096]{1,0:T(1,128)S(1)}) custom-call(s32[32]{0:T(128)S(1)} %get-tuple-element.36.refs_0_.code_ref, bf16[32,64,256]{2,1,0:T(8,128)(2,1)} %collective-permute-done.6.refs_1_, bf16[128,256,256]{2,1,0:T(8,128)(2,1)} %tiles_ref.7, f32[80,4096]{1,0:T(8,128)S(1)} %spread.4.refs_3_, bf16[64,4096]{1,0:T(8,128)(2,1)S(1)} %bitcast.34), custom_call_target="tpu_custom_call" | custom-call | tf_op jit(solution)/shard_map/spread/pallas_call | solution.py:140
  57.9 0.0 all-to-all-done.1
  57.9 8.2 %all-to-all-start = ((bf16[8,64,512]{2,1,0:T(8,128)(2,1)}), bf16[8,64,512]{2,1,0:T(8,128)(2,1)S(1)}, u32[]{:S(2)}, u32[]{:S(2)}) async-start(bf16[8,64,512]{2,1,0:T(8,128)(2,1)} %get-tuple-element.20), calls=%async_computation | async-start | bytes 1048576 | tf_op jit(solution)/shard_map/all_to_all | solution.py:326
  66.1 0.2 copy.21
  66.3 10.1 %all-to-all-done = bf16[8,64,512]{2,1,0:T(8,128)(2,1)S(1)} async-done(((bf16[8,64,512]{2,1,0:T(8,128)(2,1)}), bf16[8,64,512]{2,1,0:T(8,128)(2,1)S(1)}, u32[]{:S(2)}, u32[]{:S(2)}) %all-to-all-start) | async-done | bytes 524320 | tf_op jit(solution)/shard_map/all_to_all | solution.py:326
  76.5 2.1 %dense.1 = (bf16[512,512]{1,0:T(8,128)(2,1)S(1)}, bf16[512,512]{1,0:T(8,128)(2,1)}, bf16[512,512]{1,0:T(8,128)(2,1)S(1)}) custom-call(bf16[512,512]{1,0:T(8,128)(2,1)S(1)} %bitcast.36, bf16[512,512]{1,0:T(8,128)(2,1)S(1)} %bitcast.35, bf16[512,512]{1,0:T(8,128)(2,1)S(1)} %copy-done.3, bf16[512,512]{1,0:T(8,128)(2,1)S(1)} %bitcast.37), custom_call_target="tpu_custom_call" | custom-call | tf_op jit(solution)/shard_map/dense/pallas_call | solution.py:174
  78.5 3.5 %all-to-all-start.2 = ((bf16[8,64,512]{2,1,0:T(8,128)(2,1)}), bf16[8,64,512]{2,1,0:T(8,128)(2,1)S(1)}, u32[]{:S(2)}, u32[]{:S(2)}) async-start(bf16[8,64,512]{2,1,0:T(8,128)(2,1)} %bitcast.6), calls=%async_computation.2 | async-start | bytes 1048576 | tf_op jit(solution)/shard_map/all_to_all | solution.py:328
  82.0 1.1 pad_maximum_fusion
  83.2 9.1 %all-to-all-done.2.grad_ref = bf16[8,64,512]{2,1,0:T(8,128)(2,1)S(1)} async-done(((bf16[8,64,512]{2,1,0:T(8,128)(2,1)}), bf16[8,64,512]{2,1,0:T(8,128)(2,1)S(1)}, u32[]{:S(2)}, u32[]{:S(2)}) %all-to-all-start.2) | async-done | bytes 524320 | tf_op jit(solution)/shard_map/all_to_all | solution.py:328
  92.3 4.2 %back_products.4 = bf16[32,64,256]{2,1,0:T(8,128)(2,1)} custom-call(s32[32]{0:T(128)S(1)} %get-tuple-element.36.refs_0_.code_ref, bf16[8,64,512]{2,1,0:T(8,128)(2,1)S(1)} %all-to-all-done.2.grad_ref, f32[1,4096]{1,0:T(1,128)S(1)} %get-tuple-element.22.scale_ref, bf16[128,256,256]{2,1,0:T(8,128)(2,1)} %tiles_ref.7), custom_call_target="tpu_custom_call" | custom-call | tf_op jit(solution)/shard_map/back_products/pallas_call | solution.py:205
  96.5 5.1 %collective-permute-start.11 = (bf16[32,64,256]{2,1,0:T(8,128)(2,1)}, bf16[32,64,256]{2,1,0:T(8,128)(2,1)}, u32[]{:S(2)}, u32[]{:S(2)}) collective-permute-start(bf16[32,64,256]{2,1,0:T(8,128)(2,1)} %back_products.4), channel_id=1, source_target_pairs={{0,16},{1,65},{2,18},{3,67},{4,20},{5,69},{6,22},{7,71},{8,24},{9,... | collective-permute-start | bytes 3145736 | tf_op jit(solution)/shard_map/ppermute | solution.py:286
  101.6 3.2 %back_products.5 = bf16[32,64,256]{2,1,0:T(8,128)(2,1)S(1)} custom-call(s32[32]{0:T(128)S(1)} %get-tuple-element.35.refs_0_.code_ref, bf16[8,64,512]{2,1,0:T(8,128)(2,1)S(1)} %all-to-all-done.2.grad_ref, f32[1,4096]{1,0:T(1,128)S(1)} %get-tuple-element.22.scale_ref, bf16[128,256,256]{2,1,0:T(8,128)(2,1)} %tiles_ref.7), custom_call_target="tpu_custom_call" | custom-call | tf_op jit(solution)/shard_map/back_products/pallas_call | solution.py:205
  104.7 1.3 collective-permute-start.9
  106.1 3.2 %back_products.6 = bf16[32,64,256]{2,1,0:T(8,128)(2,1)S(1)} custom-call(s32[32]{0:T(128)S(1)} %get-tuple-element.34.refs_1_.code_ref, bf16[8,64,512]{2,1,0:T(8,128)(2,1)S(1)} %all-to-all-done.2.grad_ref, f32[1,4096]{1,0:T(1,128)S(1)} %get-tuple-element.22.scale_ref, bf16[128,256,256]{2,1,0:T(8,128)(2,1)} %tiles_ref.7), custom_call_target="tpu_custom_call" | custom-call | tf_op jit(solution)/shard_map/back_products/pallas_call | solution.py:205
  109.3 0.9 collective-permute-start.10
  110.2 4.2 %all-to-all-start.3 = ((bf16[8,64,1024]{2,1,0:T(8,128)(2,1)}), bf16[8,64,1024]{2,1,0:T(8,128)(2,1)}, u32[]{:S(2)}, u32[]{:S(2)}) async-start(bf16[8,64,1024]{2,1,0:T(8,128)(2,1)} %pad_maximum_fusion), calls=%async_computation.3 | async-start | bytes 2097152 | tf_op jit(solution)/shard_map/all_to_all | solution.py:340
  114.4 3.2 %back_products.7.refs_2_ = bf16[32,64,256]{2,1,0:T(8,128)(2,1)S(1)} custom-call(s32[32]{0:T(128)S(1)} %get-tuple-element.33.refs_0_.code_ref, bf16[8,64,512]{2,1,0:T(8,128)(2,1)S(1)} %all-to-all-done.2.grad_ref, f32[1,4096]{1,0:T(1,128)S(1)} %get-tuple-element.22.scale_ref, bf16[128,256,256]{2,1,0:T(8,128)(2,1)} %tiles_ref.7), custom_call_target="tpu_custom_call" | custom-call | tf_op jit(solution)/shard_map/back_products/pallas_call | solution.py:205
  117.6 2.0 %collect.2.refs_4_ = f32[4,64,4096]{2,1,0:T(8,128)S(1)} custom-call(s32[32]{0:T(128)S(1)} %get-tuple-element.33.refs_0_.code_ref, s32[32]{0:T(128)S(1)} %collective-permute-done.1.refs_1_, bf16[32,64,256]{2,1,0:T(8,128)(2,1)S(1)} %back_products.7.refs_2_, bf16[32,64,256]{2,1,0:T(8,128)(2,1)} %collective-permute-done.11.refs_3_), custom_call_target="tpu_custom_call" | custom-call | tf_op jit(solution)/shard_map/collect/pallas_call | solution.py:241
  119.7 8.3 %collective-permute-done.9.refs_2_ = bf16[32,64,256]{2,1,0:T(8,128)(2,1)} collective-permute-done((bf16[32,64,256]{2,1,0:T(8,128)(2,1)S(1)}, bf16[32,64,256]{2,1,0:T(8,128)(2,1)}, u32[]{:S(2)}, u32[]{:S(2)}) %collective-permute-start.9) | collective-permute-done | bytes 1048608 | tf_op jit(solution)/shard_map/ppermute | solution.py:286
  128.0 0.0 collective-permute-done.10.refs_3_
  128.0 3.5 %collect.3 = (bf16[64,4096]{1,0:T(8,128)(2,1)S(1)}, bf16[64,4096]{1,0:T(8,128)(2,1)}, bf16[64,4096]{1,0:T(8,128)(2,1)}, bf16[64,4096]{1,0:T(8,128)(2,1)S(1)}) custom-call(s32[32]{0:T(128)S(1)} %collective-permute-done.refs_0_, s32[32]{0:T(128)S(1)} %collective-permute-done.2.refs_2_.refs_1_, bf16[32,64,256]{2,1,0:T(8,128)(2,1)} %collective-permute-done.9.refs_2_, ...), custom_call_target="tpu_custom_call" | custom-call | tf_op jit(solution)/shard_map/collect/pallas_call | solution.py:241
  131.5 1.2 collective-permute-start.12
  132.7 0.8 collective-permute-start.13
  133.5 0.9 collective-permute-start.14
  134.4 0.0 all-to-all-done.3
  134.4 2.1 %slice_reduce_fusion = (bf16[64,512]{1,0:T(8,128)(2,1)S(1)}, bf16[8,8,8,512]{3,2,1,0:T(8,128)(2,1)}) fusion(bf16[8,64,1024]{2,1,0:T(8,128)(2,1)} %all-to-all-done.3), kind=kLoop, calls=%fused_computation.2 | loop fusion | flops 229376 | bytes 1638400 | tf_op jit(solution)/shard_map/reduce_sum | solution.py:342
  136.5 0.1 copy.23
  136.6 0.8 reshape.51
  137.4 6.8 %all-to-all-start.4 = ((bf16[16,2,1024]{2,1,0:T(2,128)(2,1)}), bf16[16,2,1024]{2,1,0:T(2,128)(2,1)S(1)}, u32[]{:S(2)}, u32[]{:S(2)}) async-start(bf16[16,2,1024]{2,1,0:T(2,128)(2,1)} %reshape.51), calls=%async_computation.4 | async-start | bytes 131072 | tf_op jit(solution)/shard_map/all_to_all | solution.py:347
  144.1 1.9 %copy.25 = bf16[8,8,8,512]{3,2,0,1:T(8,128)(2,1)} copy(bf16[8,8,8,512]{3,2,1,0:T(8,128)(2,1)} %get-tuple-element.32) | data formatting | bytes 1048576 | tf_op jit(solution)/shard_map/reshape | solution.py:341
  146.0 5.9 %all-to-all-done.4 = bf16[16,2,1024]{2,1,0:T(2,128)(2,1)S(1)} async-done(((bf16[16,2,1024]{2,1,0:T(2,128)(2,1)}), bf16[16,2,1024]{2,1,0:T(2,128)(2,1)S(1)}, u32[]{:S(2)}, u32[]{:S(2)}) %all-to-all-start.4) | async-done | bytes 65568 | tf_op jit(solution)/shard_map/all_to_all | solution.py:347
  151.9 0.1 reshape.52
  152.1 0.6 convert_reduce_fusion
  152.7 1.1 final_sum.1
  (13 shorter events, 0.0 us)
Async XLA Ops:
  0.6 17.8 %collective-permute-start.5 = (bf16[64,4096]{1,0:T(8,128)(2,1)}, bf16[64,4096]{1,0:T(8,128)(2,1)S(1)}, u32[]{:S(2)}, u32[]{:S(2)}) collective-permute-start(bf16[64,4096]{1,0:T(8,128)(2,1)} %bitcast.29), channel_id=1, source_target_pairs={{0,96},{1,25},{2,98},{3,27},{4,100},{5,29},{6,102},{7,31},{8,104},... | collective-permute-start | bytes 1572872 | tf_op jit(solution)/shard_map/ppermute | solution.py:286
  3.5 14.9 %collective-permute-start.4 = (bf16[64,4096]{1,0:T(8,128)(2,1)}, bf16[64,4096]{1,0:T(8,128)(2,1)S(1)}, u32[]{:S(2)}, u32[]{:S(2)}) collective-permute-start(bf16[64,4096]{1,0:T(8,128)(2,1)} %bitcast.30), channel_id=1, source_target_pairs={{0,64},{1,17},{2,66},{3,19},{4,68},{5,21},{6,70},{7,23},{8,72},{9,... | collective-permute-start | bytes 1572872 | tf_op jit(solution)/shard_map/ppermute | solution.py:286
  4.3 15.7 %collective-permute-start.3 = (bf16[64,4096]{1,0:T(8,128)(2,1)}, bf16[64,4096]{1,0:T(8,128)(2,1)S(1)}, u32[]{:S(2)}, u32[]{:S(2)}) collective-permute-start(bf16[64,4096]{1,0:T(8,128)(2,1)} %bitcast.31), channel_id=1, source_target_pairs={{0,32},{1,9},{2,34},{3,11},{4,36},{5,13},{6,38},{7,15},{8,40},{9,1... | collective-permute-start | bytes 1572872 | tf_op jit(solution)/shard_map/ppermute | solution.py:286
  6.3 7.0 %collective-permute-start.2 = (s32[32]{0:T(128)S(1)}, s32[32]{0:T(128)S(1)}, u32[]{:S(2)}, u32[]{:S(2)}) collective-permute-start(s32[32]{0:T(128)S(1)} %get-tuple-element.34.refs_1_.code_ref), channel_id=1, source_target_pairs={{0,8},{1,33},{2,10},{3,35},{4,12},{5,37},{6,14},{7,39},{8,16},{9,4... | collective-permute-start | bytes 392 | tf_op jit(solution)/shard_map/ppermute | solution.py:286
  7.9 6.1 %collective-permute-start = (s32[32]{0:T(128)S(1)}, s32[32]{0:T(128)S(1)}, u32[]{:S(2)}, u32[]{:S(2)}) collective-permute-start(s32[32]{0:T(128)S(1)} %get-tuple-element.35.refs_0_.code_ref), channel_id=1, source_target_pairs={{0,24},{1,97},{2,26},{3,99},{4,28},{5,101},{6,30},{7,103},{8,0},{9... | collective-permute-start | bytes 392 | tf_op jit(solution)/shard_map/ppermute | solution.py:286
  13.3 5.1 %collective-permute-start.1 = (s32[32]{0:T(128)S(1)}, s32[32]{0:T(128)S(1)}, u32[]{:S(2)}, u32[]{:S(2)}) collective-permute-start(s32[32]{0:T(128)S(1)} %get-tuple-element.36.refs_0_.code_ref), channel_id=1, source_target_pairs={{0,16},{1,65},{2,18},{3,67},{4,20},{5,69},{6,22},{7,71},{8,24},{9,... | collective-permute-start | bytes 392 | tf_op jit(solution)/shard_map/ppermute | solution.py:286
  20.1 1.0 copy-start.1
  21.1 7.8 %copy-start.4 = (bf16[4096,64]{0,1:T(8,128)(2,1)S(1)}, bf16[4096,64]{0,1:T(8,128)(2,1)}, u32[]{:S(2)}) copy-start(bf16[4096,64]{0,1:T(8,128)(2,1)} %param.13) | copy-start | bytes 1572868
  21.1 14.0 %copy-start.2 = (bf16[4096,64]{0,1:T(8,128)(2,1)S(1)}, bf16[4096,64]{0,1:T(8,128)(2,1)}, u32[]{:S(2)}) copy-start(bf16[4096,64]{0,1:T(8,128)(2,1)} %param.7) | copy-start | bytes 1572868
  23.7 16.9 %collective-permute-start.7 = (bf16[32,64,256]{2,1,0:T(8,128)(2,1)}, bf16[32,64,256]{2,1,0:T(8,128)(2,1)}, u32[]{:S(2)}, u32[]{:S(2)}) collective-permute-start(bf16[32,64,256]{2,1,0:T(8,128)(2,1)} %get-tuple-element.18), channel_id=1, source_target_pairs={{0,8},{1,33},{2,10},{3,35},{4,12},{5,37},{6,14},{7,39},{8,16},{9,4... | collective-permute-start | bytes 3145736 | tf_op jit(solution)/shard_map/ppermute | solution.py:286
  25.3 15.3 %collective-permute-start.8 = (bf16[32,64,256]{2,1,0:T(8,128)(2,1)}, bf16[32,64,256]{2,1,0:T(8,128)(2,1)}, u32[]{:S(2)}, u32[]{:S(2)}) collective-permute-start(bf16[32,64,256]{2,1,0:T(8,128)(2,1)} %get-tuple-element.19), channel_id=1, source_target_pairs={{0,24},{1,97},{2,26},{3,99},{4,28},{5,101},{6,30},{7,103},{8,0},{9... | collective-permute-start | bytes 3145736 | tf_op jit(solution)/shard_map/ppermute | solution.py:286
  27.0 25.6 %collective-permute-start.6 = (bf16[32,64,256]{2,1,0:T(8,128)(2,1)}, bf16[32,64,256]{2,1,0:T(8,128)(2,1)}, u32[]{:S(2)}, u32[]{:S(2)}) collective-permute-start(bf16[32,64,256]{2,1,0:T(8,128)(2,1)} %get-tuple-element.17), channel_id=1, source_target_pairs={{0,16},{1,65},{2,18},{3,67},{4,20},{5,69},{6,22},{7,71},{8,24},{9,... | collective-permute-start | bytes 3145736 | tf_op jit(solution)/shard_map/ppermute | solution.py:286
  29.8 28.1 %all-to-all-start.1 = ((bf16[8,64,512]{2,1,0:T(8,128)(2,1)}), bf16[8,64,512]{2,1,0:T(8,128)(2,1)S(1)}, u32[]{:S(2)}, u32[]{:S(2)}) async-start(bf16[8,64,512]{2,1,0:T(8,128)(2,1)} %bitcast.28), calls=%async_computation.1 | async-start | bytes 1048576 | tf_op jit(solution)/shard_map/all_to_all | solution.py:321
  39.6 1.1 copy-start
  47.7 18.4 %copy-start.3 = (bf16[512,512]{1,0:T(8,128)(2,1)S(1)}, bf16[512,512]{1,0:T(8,128)(2,1)}, u32[]{:S(2)}) copy-start(bf16[512,512]{1,0:T(8,128)(2,1)} %weight_ref.1) | copy-start | bytes 1572868
  57.9 18.6 %all-to-all-start = ((bf16[8,64,512]{2,1,0:T(8,128)(2,1)}), bf16[8,64,512]{2,1,0:T(8,128)(2,1)S(1)}, u32[]{:S(2)}, u32[]{:S(2)}) async-start(bf16[8,64,512]{2,1,0:T(8,128)(2,1)} %get-tuple-element.20), calls=%async_computation | async-start | bytes 1048576 | tf_op jit(solution)/shard_map/all_to_all | solution.py:326
  78.5 13.8 %all-to-all-start.2 = ((bf16[8,64,512]{2,1,0:T(8,128)(2,1)}), bf16[8,64,512]{2,1,0:T(8,128)(2,1)S(1)}, u32[]{:S(2)}, u32[]{:S(2)}) async-start(bf16[8,64,512]{2,1,0:T(8,128)(2,1)} %bitcast.6), calls=%async_computation.2 | async-start | bytes 1048576 | tf_op jit(solution)/shard_map/all_to_all | solution.py:328
  96.5 21.1 %collective-permute-start.11 = (bf16[32,64,256]{2,1,0:T(8,128)(2,1)}, bf16[32,64,256]{2,1,0:T(8,128)(2,1)}, u32[]{:S(2)}, u32[]{:S(2)}) collective-permute-start(bf16[32,64,256]{2,1,0:T(8,128)(2,1)} %back_products.4), channel_id=1, source_target_pairs={{0,16},{1,65},{2,18},{3,67},{4,20},{5,69},{6,22},{7,71},{8,24},{9,... | collective-permute-start | bytes 3145736 | tf_op jit(solution)/shard_map/ppermute | solution.py:286
  104.7 23.3 %collective-permute-start.9 = (bf16[32,64,256]{2,1,0:T(8,128)(2,1)S(1)}, bf16[32,64,256]{2,1,0:T(8,128)(2,1)}, u32[]{:S(2)}, u32[]{:S(2)}) collective-permute-start(bf16[32,64,256]{2,1,0:T(8,128)(2,1)S(1)} %back_products.5), channel_id=1, source_target_pairs={{0,24},{1,97},{2,26},{3,99},{4,28},{5,101},{6,30},{7,103},{8,0},{9... | collective-permute-start | bytes 3145736 | tf_op jit(solution)/shard_map/ppermute | solution.py:286
  109.3 18.8 %collective-permute-start.10 = (bf16[32,64,256]{2,1,0:T(8,128)(2,1)S(1)}, bf16[32,64,256]{2,1,0:T(8,128)(2,1)}, u32[]{:S(2)}, u32[]{:S(2)}) collective-permute-start(bf16[32,64,256]{2,1,0:T(8,128)(2,1)S(1)} %back_products.6), channel_id=1, source_target_pairs={{0,8},{1,33},{2,10},{3,35},{4,12},{5,37},{6,14},{7,39},{8,16},{9,4... | collective-permute-start | bytes 3145736 | tf_op jit(solution)/shard_map/ppermute | solution.py:286
  110.2 24.2 %all-to-all-start.3 = ((bf16[8,64,1024]{2,1,0:T(8,128)(2,1)}), bf16[8,64,1024]{2,1,0:T(8,128)(2,1)}, u32[]{:S(2)}, u32[]{:S(2)}) async-start(bf16[8,64,1024]{2,1,0:T(8,128)(2,1)} %pad_maximum_fusion), calls=%async_computation.3 | async-start | bytes 2097152 | tf_op jit(solution)/shard_map/all_to_all | solution.py:340
  131.5 21.2 %collective-permute-start.12 = (bf16[64,4096]{1,0:T(8,128)(2,1)}, bf16[64,4096]{1,0:T(8,128)(2,1)S(1)}, u32[]{:S(2)}, u32[]{:S(2)}) collective-permute-start(bf16[64,4096]{1,0:T(8,128)(2,1)} %get-tuple-element.28), channel_id=1, source_target_pairs={{0,96},{1,25},{2,98},{3,27},{4,100},{5,29},{6,102},{7,31},{8,104},... | collective-permute-start | bytes 1572872 | tf_op jit(solution)/shard_map/ppermute | solution.py:286
  132.7 20.0 %collective-permute-start.13 = (bf16[64,4096]{1,0:T(8,128)(2,1)}, bf16[64,4096]{1,0:T(8,128)(2,1)S(1)}, u32[]{:S(2)}, u32[]{:S(2)}) collective-permute-start(bf16[64,4096]{1,0:T(8,128)(2,1)} %get-tuple-element.29), channel_id=1, source_target_pairs={{0,64},{1,17},{2,66},{3,19},{4,68},{5,21},{6,70},{7,23},{8,72},{9,... | collective-permute-start | bytes 1572872 | tf_op jit(solution)/shard_map/ppermute | solution.py:286
  133.5 19.2 %collective-permute-start.14 = (bf16[64,4096]{1,0:T(8,128)(2,1)S(1)}, bf16[64,4096]{1,0:T(8,128)(2,1)S(1)}, u32[]{:S(2)}, u32[]{:S(2)}) collective-permute-start(bf16[64,4096]{1,0:T(8,128)(2,1)S(1)} %get-tuple-element.30), channel_id=1, source_target_pairs={{0,32},{1,9},{2,34},{3,11},{4,36},{5,13},{6,38},{7,15},{8,40},{9,1... | collective-permute-start | bytes 1572872 | tf_op jit(solution)/shard_map/ppermute | solution.py:286
  137.4 14.6 %all-to-all-start.4 = ((bf16[16,2,1024]{2,1,0:T(2,128)(2,1)}), bf16[16,2,1024]{2,1,0:T(2,128)(2,1)S(1)}, u32[]{:S(2)}, u32[]{:S(2)}) async-start(bf16[16,2,1024]{2,1,0:T(2,128)(2,1)} %reshape.51), calls=%async_computation.4 | async-start | bytes 131072 | tf_op jit(solution)/shard_map/all_to_all | solution.py:347

commit v4 on v3

v4 whole, which is shorter than its diff:
```python
import functools

import jax
import jax.numpy as jnp
from jax import lax
from jax.experimental import pallas as pl
from jax.experimental.pallas import tpu as pltpu
from jax.sharding import PartitionSpec as P

BLK = 256
SLOTS = 8
SIDE = 4
PART = SIDE * SLOTS
VMEM_LIMIT = 16 * 1024 * 1024
TILES_VMEM_LIMIT = 38 * 1024 * 1024
GELU_C = 0.7978845608028654
GELU_A = 0.044715


def params(limit=VMEM_LIMIT):
    return pltpu.CompilerParams(vmem_limit_bytes=limit)


def scalars(n):
    return [pl.BlockSpec(memory_space=pltpu.SMEM)] * n


def arrays(n):
    return [pl.BlockSpec(memory_space=pltpu.VMEM)] * n


def anywhere(n):
    return [pl.BlockSpec(memory_space=pl.ANY)] * n


def chunk_ahead(place_ref, dz, other):
    core = place_ref[0]
    return 2 * ((place_ref[1] + dz) % SIDE) + (1 - core if other else core)


def chunk_behind(place_ref, dz, other):
    return chunk_ahead(place_ref, SIDE - dz, other)


def encode(index, col_block, row_block, alive):
    return index + 128 * col_block + 2048 * row_block + 32768 * alive


def col_block_of(code):
    return (code >> 7) & 15


def row_block_of(code):
    return (code >> 11) & 15


def keep_kernel(value_ref, after_ref, out_ref):
    out_ref[...] = value_ref[...]


def keep(value, after):
    return pl.pallas_call(
        keep_kernel,
        out_shape=jax.ShapeDtypeStruct(value.shape, value.dtype),
        in_specs=arrays(1) + anywhere(1),
        out_specs=arrays(1)[0],
        compiler_params=params(),
        name="keep",
    )(value, after)


def halves_kernel(back1_ref, back3_ref, after1_ref, after2_ref, low_ref, high_ref):
    half = low_ref.shape[0]
    low_ref[...] = back1_ref[:half, :]
    high_ref[...] = back3_ref[half:, :]


def halves(back1, back3, after):
    width, nodes = back1.shape
    half = jax.ShapeDtypeStruct((width // 2, nodes), back1.dtype)
    return pl.pallas_call(
        halves_kernel,
        out_shape=(half, half),
        in_specs=arrays(2) + anywhere(2),
        out_specs=tuple(arrays(2)),
        compiler_params=params(),
        name="halves",
    )(back1, back3, *after)


def later_kernel(value_ref, after_ref, out_ref):
    for i in range(value_ref.shape[0]):
        out_ref[i] = value_ref[i]


def later(value, after):
    return pl.pallas_call(
        later_kernel,
        out_shape=jax.ShapeDtypeStruct(value.shape, value.dtype),
        in_specs=scalars(1) + anywhere(1),
        out_specs=scalars(1)[0],
        compiler_params=params(),
        name="later",
    )(value, after)


def gather_kernel(code_ref, own_ref, back1_ref, low_ref, high_ref, back3_ref, *refs):
    out_ref = refs[-1]
    half = low_ref.shape[0]
    for q in range(PART):
        columns = pl.ds(pl.multiple_of(col_block_of(code_ref[q]) * BLK, BLK), BLK)
        d = q // SLOTS
        if d == 2:
            out_ref[q, :half, :] = low_ref[:, columns]
            out_ref[q, half:, :] = high_ref[:, columns]
        else:
            out_ref[q] = (own_ref, back1_ref, None, back3_ref)[d][:, columns]


def gather_blocks(code, slabs, after):
    width = slabs[0].shape[0]
    return pl.pallas_call(
        gather_kernel,
        out_shape=jax.ShapeDtypeStruct((PART, width, BLK), jnp.bfloat16),
        in_specs=scalars(1) + arrays(len(slabs)) + anywhere(len(after)),
        out_specs=arrays(1)[0],
        compiler_params=params(),
        name="gather_blocks",
    )(code, *slabs, *after)


def load_tiles(code_refs, tiles_ref, buf_ref, sems):
    for part, code_ref in enumerate(code_refs):

        def start(q, carry):
            pltpu.make_async_copy(
                tiles_ref.at[code_ref[q] & 127],
                buf_ref.at[part * SIDE + q // SLOTS, q % SLOTS],
                sems.at[part * SIDE + q // SLOTS],
            ).start()
            return carry

        lax.fori_loop(0, PART, start, 0)


def wait_tiles(tiles_ref, buf_ref, sems, group):
    pltpu.make_async_copy(tiles_ref.at[pl.ds(0, SLOTS)], buf_ref.at[group], sems.at[group]).wait()


def add_products(codes, recvs, buf_ref, total_ref, wait):
    ones = jnp.ones((16, BLK), jnp.bfloat16)
    for part, (code_ref, recv_ref) in enumerate(zip(codes, recvs)):

        def step(d, carry):
            group = part * SIDE + d
            wait(group)
            for s in range(SLOTS):
                q = d * SLOTS + s
                code = code_ref[q]
                flag = (code >> 15).astype(jnp.float32).astype(jnp.bfloat16)
                left = jnp.concatenate([recv_ref[q], ones], axis=0) * flag
                start = pl.multiple_of(row_block_of(code) * BLK, BLK)
                total_ref[:, pl.ds(start, BLK)] += lax.dot_general(
                    left, buf_ref[group, s], (((1,), (1,)), ((), ())), preferred_element_type=jnp.float32
                )
            return carry

        lax.fori_loop(0, SIDE, step, 0)


def spread_kernel(parts, first, *refs):
    codes, recvs, tiles_ref = refs[:parts], refs[parts : 2 * parts], refs[2 * parts]
    if first:
        total_ref, buf_ref, sems = refs[2 * parts + 1 :]
    else:
        before_ref, next_code_ref, total_ref, next_ref, buf_ref, sems, next_sems = refs[2 * parts + 1 :]
    load_tiles(codes, tiles_ref, buf_ref, sems)
    if first:
        total_ref[...] = jnp.zeros_like(total_ref)
    else:
        load_tiles([next_code_ref], tiles_ref, next_ref, next_sems)
        total_ref[...] = before_ref[...]
    add_products(codes, recvs, buf_ref, total_ref, lambda group: wait_tiles(tiles_ref, buf_ref, sems, group))
    if not first:
        for d in range(SIDE):
            wait_tiles(tiles_ref, next_ref, next_sems, d)


def tile_scratch(parts):
    return [
        pltpu.VMEM((parts * SIDE, SLOTS, BLK, BLK), jnp.bfloat16),
        pltpu.SemaphoreType.DMA((parts * SIDE,)),
    ]


def first_spread(code, recv, tile_vals):
    total = jax.ShapeDtypeStruct((recv.shape[1] + 16, SIDE * SIDE * BLK), jnp.float32)
    return pl.pallas_call(
        functools.partial(spread_kernel, 1, True),
        out_shape=total,
        in_specs=scalars(1) + arrays(1) + anywhere(1),
        out_specs=arrays(1)[0],
        scratch_shapes=tile_scratch(1),
        compiler_params=params(TILES_VMEM_LIMIT),
        name="spread",
    )(code, recv, tile_vals)


def spread(codes, recvs, tile_vals, before, next_code):
    parts = len(codes)
    tiles = jax.ShapeDtypeStruct((SIDE, SLOTS, BLK, BLK), jnp.bfloat16)
    return pl.pallas_call(
        functools.partial(spread_kernel, parts, False),
        out_shape=(jax.ShapeDtypeStruct(before.shape, before.dtype), tiles),
        in_specs=scalars(parts) + arrays(parts) + anywhere(1) + arrays(1) + scalars(1),
        out_specs=tuple(arrays(2)),
        scratch_shapes=tile_scratch(parts) + [pltpu.SemaphoreType.DMA((SIDE,))],
        compiler_params=params(TILES_VMEM_LIMIT),
        name="spread",
    )(*codes, *recvs, tile_vals, before, next_code)


def mixed_kernel(place_ref, code_ref, recv_ref, tiles_ref, before_ref, feats_ref, after_ref, *refs):
    own_ref, other_ref, scale_ref, total_ref = refs
    total_ref[...] = before_ref[...]
    add_products([code_ref], [recv_ref], tiles_ref, total_ref, lambda group: None)
    _, width, chunk = own_ref.shape
    scale_ref[...] = lax.rsqrt(1.0 + total_ref[width : width + 1, :])
    for dz in range(SIDE):
        for other, out_ref in enumerate((own_ref, other_ref)):
            start = chunk_ahead(place_ref, dz, other) * chunk
            part = pl.ds(pl.multiple_of(start, chunk), chunk)
            mixed = feats_ref[:, part].astype(jnp.float32) + scale_ref[:, part] * total_ref[:width, part]
            out_ref[dz] = mixed.astype(jnp.bfloat16)


def spread_mixed(place, code, recv, tiles, before, feats_t, after):
    width, nodes = feats_t.shape
    half = jax.ShapeDtypeStruct((SIDE, width, nodes // SIDE // 2), jnp.bfloat16)
    return pl.pallas_call(
        mixed_kernel,
        out_shape=(half, half, jax.ShapeDtypeStruct((1, nodes), jnp.float32)),
        in_specs=scalars(2) + arrays(4) + anywhere(1),
        out_specs=tuple(arrays(3)),
        scratch_shapes=[pltpu.VMEM(before.shape, before.dtype)],
        compiler_params=params(),
        name="spread_mixed",
    )(place, code, recv, tiles, before, feats_t, after)


def assemble(place_ref, pieces, out_ref):
    rows = pieces[0].shape[1]
    for dz, piece_ref in enumerate(pieces):
        for other in range(2):
            start = chunk_behind(place_ref, dz, other) * rows
            out_ref[pl.ds(pl.multiple_of(start, rows), rows), :] = piece_ref[other]


def join_kernel(place_ref, *refs):
    assemble(place_ref, refs[:SIDE], refs[SIDE + 1])


def join(place, pieces, after):
    _, width, chunk = pieces[0].shape
    return pl.pallas_call(
        join_kernel,
        out_shape=jax.ShapeDtypeStruct((2 * SIDE * width, chunk), pieces[0].dtype),
        in_specs=scalars(1) + arrays(SIDE) + anywhere(1),
        out_specs=arrays(1)[0],
        compiler_params=params(),
        name="join",
    )(place, *pieces, after)


def dense_kernel(place_ref, *refs):
    pieces, cot_ref, weight_ref, weight_t_ref = refs[:SIDE], *refs[SIDE : SIDE + 3]
    hidden_own_ref, hidden_other_ref, own_ref, other_ref, gw_own_ref = refs[SIDE + 3 : SIDE + 8]
    hidden_ref, mixed_ref, gp_ref, grad_ref, gw_ref = refs[SIDE + 8 :]
    assemble(place_ref, pieces, mixed_ref)
    step = 128
    mixed = mixed_ref[...]
    for lo in range(0, weight_ref.shape[1], step):
        rows = slice(lo, lo + step)
        pre = jnp.dot(weight_t_ref[rows, :], mixed, preferred_element_type=jnp.float32)
        square = pre * pre
        tanh = jnp.tanh(GELU_C * (pre + GELU_A * (pre * square)))
        half = 0.5 * (1.0 + tanh)
        hidden_ref[rows, :] = (pre * half).astype(jnp.bfloat16)
        slope = half + 0.5 * pre * (1.0 - tanh * tanh) * (GELU_C * (1.0 + 3.0 * GELU_A * square))
        gp_ref[rows, :] = (cot_ref[rows, :].astype(jnp.float32) * slope).astype(jnp.bfloat16)
    grad_pre = gp_ref[...]
    grad_ref[...] = jnp.dot(weight_ref[...], grad_pre, preferred_element_type=jnp.float32).astype(
        jnp.bfloat16
    )
    rows = own_ref.shape[1]
    split_rows(place_ref, grad_ref, own_ref, other_ref)
    split_rows(place_ref, hidden_ref, hidden_own_ref, hidden_other_ref)
    gw_ref[...] = lax.dot_general(
        grad_pre, mixed, (((1,), (1,)), ((), ())), preferred_element_type=jnp.float32
    ).astype(jnp.bfloat16)
    for j in range(SIDE):
        start = 2 * (place_ref[1] ^ j) * rows
        mine = pl.multiple_of(start + place_ref[0] * rows, rows)
        others = pl.multiple_of(start + (1 - place_ref[0]) * rows, rows)
        gw_own_ref[j] = gw_ref[pl.ds(mine, rows), :]
        other_ref[j, rows:, :] = gw_ref[pl.ds(others, rows), :]


def split_rows(place_ref, src_ref, own_ref, other_ref):
    rows = own_ref.shape[1]
    for dz in range(SIDE):
        for other, out_ref in enumerate((own_ref, other_ref)):
            start = chunk_ahead(place_ref, dz, other) * rows
            out_ref[dz, :rows, :] = src_ref[pl.ds(pl.multiple_of(start, rows), rows), :]


def dense(place, mixed, cot, weight, weight_t):
    _, width, chunk = mixed[0].shape
    full = jax.ShapeDtypeStruct((weight.shape[1], chunk), jnp.bfloat16)
    half = jax.ShapeDtypeStruct((SIDE, width, chunk), jnp.bfloat16)
    both = jax.ShapeDtypeStruct((SIDE, 2 * width, chunk), jnp.bfloat16)
    return pl.pallas_call(
        dense_kernel,
        out_shape=(half, half, half, both, half),
        in_specs=scalars(1) + arrays(SIDE + 3),
        out_specs=tuple(arrays(5)),
        scratch_shapes=[pltpu.VMEM(full.shape, full.dtype)] * 5,
        compiler_params=params(),
        name="dense",
    )(place, *mixed, cot, weight, weight_t)


def split_kernel(place_ref, src_ref, after_ref, own_ref, other_ref):
    chunk = own_ref.shape[2]
    for dz in range(SIDE):
        for other, out_ref in enumerate((own_ref, other_ref)):
            start = chunk_ahead(place_ref, dz, other) * chunk
            out_ref[dz] = src_ref[:, pl.ds(pl.multiple_of(start, chunk), chunk)]


def split(place, value, after):
    width, nodes = value.shape
    half = jax.ShapeDtypeStruct((SIDE, width, nodes // SIDE // 2), value.dtype)
    return pl.pallas_call(
        split_kernel,
        out_shape=(half, half),
        in_specs=scalars(1) + arrays(1) + anywhere(1),
        out_specs=tuple(arrays(2)),
        compiler_params=params(),
        name="split",
    )(place, value, after)


def unpack_kernel(place_ref, *refs):
    pieces, hidden_ref = refs[:SIDE], refs[SIDE]
    chunk = pieces[0].shape[2]
    for dz, piece_ref in enumerate(pieces):
        for other in range(2):
            start = chunk_behind(place_ref, dz, other) * chunk
            hidden_ref[:, pl.ds(pl.multiple_of(start, chunk), chunk)] = piece_ref[other]


def unpack(place, pieces):
    _, width, chunk = pieces[0].shape
    return pl.pallas_call(
        unpack_kernel,
        out_shape=jax.ShapeDtypeStruct((width, 2 * SIDE * chunk), jnp.bfloat16),
        in_specs=scalars(1) + arrays(SIDE),
        out_specs=arrays(1)[0],
        compiler_params=params(),
        name="unpack",
    )(place, *pieces)


def gw_add_kernel(own_ref, got_ref, after_ref, keep_ref, send_ref):
    rows = own_ref.shape[1]
    for j in range(keep_ref.shape[0]):
        for k, out_ref in enumerate((keep_ref, send_ref)):
            got = got_ref[2 * j + k, got_ref.shape[1] - rows :, :].astype(jnp.float32)
            out_ref[j] = (own_ref[2 * j + k].astype(jnp.float32) + got).astype(jnp.bfloat16)


def gw_add(own, got, after):
    half = jax.ShapeDtypeStruct((own.shape[0] // 2,) + own.shape[1:], jnp.bfloat16)
    return pl.pallas_call(
        gw_add_kernel,
        out_shape=(half, half),
        in_specs=arrays(2) + anywhere(1),
        out_specs=tuple(arrays(2)),
        compiler_params=params(),
        name="gw_add",
    )(own, got, after)


def swap_z(value, bit):
    chunks = lax.axis_size("col")
    return lax.ppermute(value, "col", [(c, c ^ (2 * bit)) for c in range(chunks)])


def gw_order_kernel(place_ref, own_ref, got_ref, after_ref, *outs):
    width, depth = own_ref.shape[1:]
    share = depth // SIDE // SIDE
    source = lax.broadcasted_iota(jnp.int32, (depth, depth), 0)
    column = lax.broadcasted_iota(jnp.int32, (depth, depth), 1)
    second, first = column // (SIDE * share), column // share % SIDE
    core, row = place_ref[0], place_ref[2]
    back_x = jnp.where(core == 0, first, second)
    back_y = jnp.where(core == 0, second, first)
    owner = (row // SIDE - back_x + SIDE) % SIDE * SIDE + (row % SIDE - back_y + SIDE) % SIDE
    pick = (source == owner * share + column % share).astype(jnp.float32).astype(jnp.bfloat16)
    total = (own_ref[0].astype(jnp.float32) + got_ref[0].astype(jnp.float32)).astype(jnp.bfloat16)
    ordered = jnp.dot(total, pick, preferred_element_type=jnp.float32)
    for e, out_ref in enumerate(outs):
        out_ref[...] = ordered[:, e * SIDE * share : (e + 1) * SIDE * share].astype(jnp.bfloat16)


def gw_order(place, own, got, after):
    _, width, depth = own.shape
    part = jax.ShapeDtypeStruct((width, depth // SIDE), jnp.bfloat16)
    return pl.pallas_call(
        gw_order_kernel,
        out_shape=(part,) * SIDE,
        in_specs=scalars(1) + arrays(2) + anywhere(1),
        out_specs=tuple(arrays(SIDE)),
        compiler_params=params(),
        name="gw_order",
    )(place, own, got, after)


def back_step(code_ref, grad_ref, tiles_ref, out_ref, wait):
    def step(d, carry):
        wait(d)
        for s in range(SLOTS):
            q = d * SLOTS + s
            code = code_ref[q]
            columns = pl.ds(pl.multiple_of(row_block_of(code) * BLK, BLK), BLK)
            flag = (code >> 15).astype(jnp.float32).astype(jnp.bfloat16)
            out_ref[q] = jnp.dot(
                grad_ref[:, columns] * flag, tiles_ref[d, s], preferred_element_type=jnp.float32
            ).astype(jnp.bfloat16)
        return carry

    lax.fori_loop(0, SIDE, step, 0)


def first_back_kernel(place_ref, code_ref, *refs):
    pieces, (scale_ref, tiles_ref, out_ref, scaled_ref, grad_ref) = refs[:SIDE], refs[SIDE:]
    chunk = pieces[0].shape[2]
    for dz, piece_ref in enumerate(pieces):
        for other in range(2):
            start = chunk_behind(place_ref, dz, other) * chunk
            columns = pl.ds(pl.multiple_of(start, chunk), chunk)
            grad = piece_ref[other]
            grad_ref[:, columns] = grad
            scaled = grad.astype(jnp.float32) * scale_ref[:, columns]
            scaled_ref[:, columns] = scaled.astype(jnp.bfloat16)
    back_step(code_ref, scaled_ref, tiles_ref, out_ref, lambda d: None)


def back_kernel(code_ref, scaled_ref, tiles_ref, after_ref, out_ref, buf_ref, sems):
    load_tiles([code_ref], tiles_ref, buf_ref, sems)
    back_step(code_ref, scaled_ref, buf_ref, out_ref, lambda d: wait_tiles(tiles_ref, buf_ref, sems, d))


def first_back_products(place, code, pieces, scale, tiles):
    width, nodes = pieces[0].shape[1], scale.shape[1]
    grad = jax.ShapeDtypeStruct((width, nodes), jnp.bfloat16)
    return pl.pallas_call(
        first_back_kernel,
        out_shape=(jax.ShapeDtypeStruct((PART, width, BLK), jnp.bfloat16), grad, grad),
        in_specs=scalars(2) + arrays(SIDE + 2),
        out_specs=tuple(arrays(3)),
        compiler_params=params(),
        name="back_products",
    )(place, code, *pieces, scale, tiles)


def back_products(code, scaled, tile_vals, after):
    return pl.pallas_call(
        back_kernel,
        out_shape=jax.ShapeDtypeStruct((PART, scaled.shape[0], BLK), jnp.bfloat16),
        in_specs=scalars(1) + arrays(1) + anywhere(2),
        out_specs=arrays(1)[0],
        scratch_shapes=tile_scratch(1),
        compiler_params=params(TILES_VMEM_LIMIT),
        name="back_products",
    )(code, scaled, tile_vals, after)


def add_blocks(code_ref, piece_ref, q, total_ref):
    columns = pl.ds(pl.multiple_of(col_block_of(code_ref[q]) * BLK, BLK), BLK)
    total_ref[:, columns] += piece_ref[q].astype(jnp.float32)


def collect_kernel(parts, first, *refs):
    codes, pieces = refs[:parts], refs[parts : 2 * parts]
    total_ref = refs[-1]
    total_ref[...] = jnp.zeros_like(total_ref) if first else refs[-2][...]
    for code_ref, piece_ref in zip(codes, pieces):
        for q in range(PART):
            add_blocks(code_ref, piece_ref, q, total_ref.at[q // SLOTS])


def collect(codes, pieces, before, nodes, after):
    parts, width = len(codes), pieces[0].shape[1]
    total = jax.ShapeDtypeStruct((SIDE, width, nodes), jnp.float32)
    extra = [] if before is None else [before]
    return pl.pallas_call(
        functools.partial(collect_kernel, parts, before is None),
        out_shape=total,
        in_specs=scalars(parts) + arrays(parts) + anywhere(1) + arrays(len(extra)),
        out_specs=arrays(1)[0],
        compiler_params=params(),
        cost_estimate=pl.CostEstimate(flops=0, bytes_accessed=60 * 2**20, transcendentals=0),
        name="collect",
    )(*codes, *pieces, after, *extra)


def slab_kernel(d, code_ref, piece_ref, before_ref, *refs):
    gw_refs, out_ref, total_ref = refs[:-2], refs[-2], refs[-1]
    nodes = total_ref.shape[1]
    total_ref[...] = before_ref[d]
    for q in range(d * SLOTS, (d + 1) * SLOTS):
        add_blocks(code_ref, piece_ref, q, total_ref)
    out_ref[:, :nodes] = total_ref[...].astype(jnp.bfloat16)
    gw = gw_refs[0][...].astype(jnp.float32)
    for gw_ref in gw_refs[1:]:
        gw += gw_ref[...].astype(jnp.float32)
    out_ref[:, nodes:] = gw.astype(jnp.bfloat16)


def slab(d, code, piece, before, gw_parts):
    width, nodes = before.shape[1:]
    beside = gw_parts[0].shape[1]
    return pl.pallas_call(
        functools.partial(slab_kernel, d),
        out_shape=jax.ShapeDtypeStruct((width, nodes + beside), jnp.bfloat16),
        in_specs=scalars(1) + arrays(2 + len(gw_parts)),
        out_specs=arrays(1)[0],
        scratch_shapes=[pltpu.VMEM((width, nodes), jnp.float32)],
        compiler_params=params(),
        name="slab",
    )(code, piece, before, *gw_parts)


def final_kernel(grad_ref, *refs):
    slabs, out_ref, gw_ref = refs[:SIDE], refs[SIDE], refs[SIDE + 1]
    step, nodes, share = 512, out_ref.shape[1], gw_ref.shape[0]
    gw = jnp.zeros((out_ref.shape[0], share), jnp.float32)
    for d, slab_ref in enumerate(slabs):
        beside = slab_ref[:, nodes:].astype(jnp.float32)
        gw += beside[:, d * share : (d + 1) * share]
    width = gw.shape[0]
    eye = lax.broadcasted_iota(jnp.int32, (width, width), 0) == lax.broadcasted_iota(jnp.int32, (width, width), 1)
    gw_ref[...] = lax.dot_general(
        gw,
        eye.astype(jnp.float32),
        (((0,), (0,)), ((), ())),
        precision=lax.Precision.HIGHEST,
        preferred_element_type=jnp.float32,
    )
    for lo in range(0, nodes, step):
        part = slice(lo, lo + step)
        total = grad_ref[:, part].astype(jnp.float32)
        for slab_ref in slabs:
            total += slab_ref[:, part].astype(jnp.float32)
        out_ref[:, part] = total.astype(jnp.bfloat16)


def final_sum(grad, slabs):
    width, nodes = grad.shape
    share = (slabs[0].shape[1] - nodes) // SIDE
    return pl.pallas_call(
        final_kernel,
        out_shape=(
            jax.ShapeDtypeStruct(grad.shape, jnp.bfloat16),
            jax.ShapeDtypeStruct((share, width), jnp.float32),
        ),
        in_specs=arrays(1 + SIDE),
        out_specs=tuple(arrays(2)),
        compiler_params=params(),
        name="final_sum",
    )(grad, *slabs)


def shift(value, first, by):
    peers, chunks = lax.axis_size("row"), lax.axis_size("col")
    pairs = []
    for r in range(peers):
        for c in range(chunks):
            x, y = divmod(r, SIDE)
            if (c % 2 == 0) == first:
                x = (x + by) % SIDE
            else:
                y = (y + by) % SIDE
            pairs.append((r * chunks + c, (x * SIDE + y) * chunks + c))
    return lax.ppermute(value, ("row", "col"), pairs)


def pair_kernel(own_ref, got_ref, after_ref, out_ref):
    out_ref[0] = own_ref[...]
    out_ref[1] = got_ref[...]


def pair(own, got, after):
    return pl.pallas_call(
        pair_kernel,
        out_shape=jax.ShapeDtypeStruct((2,) + own.shape, own.dtype),
        in_specs=arrays(2) + anywhere(1),
        out_specs=arrays(1)[0],
        compiler_params=params(),
        name="pair",
    )(own, got, after)


def regroup(own, other):
    return spread_z(own, swap_core(other))


def swap_core(value):
    chunks = lax.axis_size("col")
    return lax.ppermute(value, "col", [(c, c ^ 1) for c in range(chunks)])


def spread_z(own, got, after=None):
    chunks, rows = lax.axis_size("col"), own.shape[1]
    pieces = []
    for dz in (0, 1, 3, 2):
        if dz < 2 or after is None:
            piece = jnp.stack([own[dz], got[dz, :rows]])
        else:
            piece = pair(own[dz], got[dz], after)
        if dz > 0:
            piece = lax.ppermute(piece, "col", [(c, (c + 2 * dz) % chunks) for c in range(chunks)])
        pieces.append(piece)
    return [pieces[0], pieces[1], pieces[3], pieces[2]]


def sorted_codes(tile_rows, tile_cols, tile_nnz, blocks):
    count = tile_rows.shape[0]
    row, core = lax.axis_index("row"), lax.axis_index("col") % 2
    owner = tile_cols // blocks
    back_x = (row // SIDE - owner // SIDE) % SIDE
    back_y = (row % SIDE - owner % SIDE) % SIDE
    group = jnp.where(core == 0, back_y * SIDE + back_x, back_x * SIDE + back_y)
    index = jnp.arange(count, dtype=jnp.int32)
    code = encode(index, tile_cols % blocks, tile_rows - row * blocks, (tile_nnz > 0).astype(jnp.int32))
    earlier = (group[None, :] == group[:, None]) & (index[None, :] < index[:, None])
    place = group * SLOTS + jnp.sum(earlier.astype(jnp.int32), axis=1)
    return jnp.sum(jnp.where(place[None, :] == index[:, None], code[None, :], 0), axis=1)


def body(feats, weight, tile_vals, tile_rows, tile_cols, tile_nnz, cotangent):
    node_rows, width = feats.shape
    col = lax.axis_index("col")
    place = jnp.stack([col % 2, col // 2, lax.axis_index("row")]).astype(jnp.int32)

    feats_t = feats.T
    weight_t = weight.T
    back1, back3 = shift(feats_t, True, 1), shift(feats_t, True, -1)
    codes = sorted_codes(tile_rows, tile_cols, tile_nnz, node_rows // BLK).reshape(SIDE, PART)
    codes = [codes[e] for e in range(SIDE)]
    asked = [codes[0]] + [shift(codes[e], False, -e) for e in range(1, SIDE)]
    own = keep(feats_t, asked[1])
    low, high = halves(back1, back3, [asked[2], asked[3]])
    slabs = [own, back1, shift(low, True, 1), shift(high, True, -1), back3]

    recv = [None] * SIDE
    sent = own
    for e in (1, 3):
        sent = gather_blocks(asked[e], slabs, [sent])
        recv[e] = shift(sent, False, e)
    recv[0] = gather_blocks(asked[0], slabs, [sent])
    total = first_spread(codes[0], recv[0], tile_vals)
    cot_own, cot_other = split(place, cotangent.T, total)
    cot_got = swap_core(cot_other)
    sent = gather_blocks(asked[2], slabs, [total, recv[1]])
    recv[2] = shift(sent, False, 2)
    total, far_tiles = spread([codes[1], codes[3]], [recv[1], recv[3]], tile_vals, total, codes[2])
    cot = join(place, spread_z(cot_own, cot_got, sent), total)
    own, other, scale = spread_mixed(place, codes[2], recv[2], far_tiles, total, feats_t, cot)
    hidden_own, hidden_other, own, other, gw_own = dense(place, regroup(own, other), cot, weight, weight_t)

    got = swap_core(other)
    gw_own, gw_other = gw_add(gw_own, got, got)
    gw_got = swap_z(gw_other, 1)
    sent, scaled, grad = first_back_products(place, codes[2], spread_z(own, got), scale, far_tiles)
    gw_own, gw_other = gw_add(gw_own, gw_got, sent)
    gw_got = swap_z(gw_other, 2)
    pieces = [None] * SIDE
    pieces[2] = shift(sent, False, -2)
    pieces[1] = shift(back_products(codes[1], scaled, tile_vals, scale), False, -1)
    sent = back_products(codes[3], scaled, tile_vals, scale)
    pieces[3] = shift(sent, False, -3)
    pieces[0] = back_products(codes[0], scaled, tile_vals, sent)
    gw = gw_order(place, gw_own, gw_got, pieces[0])
    gw = [gw[0]] + [shift(gw[e], False, -e) for e in range(1, SIDE)]
    total = collect([asked[0], asked[2]], [pieces[0], pieces[2]], None, node_rows, pieces[0])
    total = collect([asked[1]], [pieces[1]], total, node_rows, gw[0])
    slabs = [slab(d, asked[3], pieces[3], total, gw) for d in range(SIDE)]
    hidden = unpack(place, regroup(hidden_own, keep(hidden_other, slabs[1])))
    slabs = [slabs[0]] + [shift(slabs[d], True, -d) for d in (1, 2, 3)]
    grad_feats, gw = final_sum(grad, slabs)
    return (hidden.T, gw, grad_feats.T)


def solution(mesh):
    placed = (
        P("row", "col"),
        P(),
        P("row", None, None),
        P("row"),
        P("row"),
        P("row"),
        P("row", "col"),
    )
    return jax.shard_map(
        body,
        mesh=mesh,
        in_specs=placed,
        out_specs=(P("row", "col"), P("row", "col"), P("row", "col")),
        check_vma=False,
    )
```

time: 155 us -> 145 us (0.935)
  waiting for transfers between devices: 48.2 us -> 43.2 us
  other arithmetic: 4.88 us -> 1.29 us
  local copies, waits for them, and re-layouts: 6.15 us -> 2.9 us
  starting transfers between devices: 51.9 us -> 54.7 us
    all_to_all x5 -> x0, starting transfers between devices: 28 us -> none  [the longest x1 8.22 us: body(): mixed_full = exchange(mixed, 'col').reshape(chunks * width, chunk)]
    ppermute x0 -> x18, waiting for transfers between devices: none -> 27.3 us  [the longest x12 17.9 us: spread_z(): lax.ppermute(piece, 'col', [(c, (c + 2 * dz) % chunks) for c in range(chu...]
    all_to_all x5 -> x0, waiting for transfers between devices: 25.2 us -> none  [the longest x1 10.1 us: body(): mixed_full = exchange(mixed, 'col').reshape(chunks * width, chunk)]
    ppermute x0 -> x18, starting transfers between devices: none -> 24.5 us  [the longest x12 21 us: spread_z(): lax.ppermute(piece, 'col', [(c, (c + 2 * dz) % chunks) for c in range(chu...]
    ppermute x15 -> x19, waiting for transfers between devices: 23 us -> 15.9 us  [shift(): return lax.ppermute(value, ('row', 'col'), pairs)]
    ppermute x15 -> x19, starting transfers between devices: 23.9 us -> 30.2 us  [shift(): return lax.ppermute(value, ('row', 'col'), pairs)]
    reduce_sum x2 -> x0, other arithmetic: 2.74 us -> none  [the longest x1 2.1 us: body(): jnp.sum(both[:, :, chunk:].astype(jnp.float32), axis=0).astype(jnp.bfloat16)]
    reshape x2 -> x0, local copies, waits for them, and re-layouts: 2.73 us -> none  [the longest x1 1.88 us: body(): hidden = jnp.swapaxes(both[:, :, :chunk], 0, 1).reshape(width, node_rows).T]
  transfers between devices with their start and end apart: 20 -> 37, of which waited for: 8 -> 19; matrix products, arithmetic and copies ran while one was open for 6% -> 1% of each run, Pallas kernels for 21% -> 21%
where the time goes in v4:
time: 145 us
  starting transfers between devices  54.7 us (38%)
  waiting for transfers between devices  43.2 us (30%)
  Pallas kernels  41.9 us (29%)
  local copies, waits for them, and re-layouts  2.9 us (2%)
    ppermute x19, starting transfers between devices, shift(): return lax.ppermute(value, ('row', 'col'), pairs)  30.2 us
    ppermute x12, starting transfers between devices, spread_z(): lax.ppermute(piece, 'col', [(c, (c + 2 * dz) % chunks) for c in range(chu...  21 us
    ppermute x12, waiting for transfers between devices, spread_z(): lax.ppermute(piece, 'col', [(c, (c + 2 * dz) % chunks) for c in range(chu...  17.9 us
    ppermute x19, waiting for transfers between devices, shift(): return lax.ppermute(value, ('row', 'col'), pairs)  15.9 us
    pallas_call x3, Pallas kernels, back_products(): pl.pallas_call(back_kernel, out_shape=jax.ShapeDtypeStruct((PART, scaled....  9.55 us
    pallas_call x1, Pallas kernels, spread(): pl.pallas_call(functools.partial(spread_kernel, parts, False), out_shape=...  6.41 us
    ppermute x4, waiting for transfers between devices, swap_core(): return lax.ppermute(value, 'col', [(c, c ^ 1) for c in range(chunks)])  4.86 us
    ppermute x2, waiting for transfers between devices, swap_z(): return lax.ppermute(value, 'col', [(c, c ^ 2 * bit) for c in range(chunks)])  4.53 us
  transfers between devices with their start and end apart: 37, of which 19 were waited for; matrix products, arithmetic and copies ran while one was open for 1% of the time, Pallas kernels for 21%

profile of v4, /device:TPU:0, one launch (start us, length us, event | category | flops | bytes accessed | tf_op | source)
XLA Modules:
  0.0 145.1 jit_solution(5539479018044367575)
XLA Ops:
  0.6 2.9 %collective-permute-start.3 = (bf16[64,4096]{1,0:T(8,128)(2,1)}, bf16[64,4096]{1,0:T(8,128)(2,1)S(1)}, u32[]{:S(2)}, u32[]{:S(2)}) collective-permute-start(bf16[64,4096]{1,0:T(8,128)(2,1)} %bitcast.17), channel_id=1, source_target_pairs={{0,96},{1,25},{2,98},{3,27},{4,100},{5,29},{6,102},{7,31},{8,104},... | collective-permute-start | bytes 1572872 | tf_op jit(solution)/shard_map/ppermute | solution.py:597
  3.5 0.7 broadcast_select_fusion
  4.6 1.6 %collective-permute-start.4 = (s32[32]{0:T(128)S(1)}, s32[32]{0:T(128)S(1)}, u32[]{:S(2)}, u32[]{:S(2)}) collective-permute-start(s32[32]{0:T(128)S(1)} %get-tuple-element.90.refs_1_.code_ref), channel_id=1, source_target_pairs={{0,8},{1,33},{2,10},{3,35},{4,12},{5,37},{6,14},{7,39},{8,16},{9,4... | collective-permute-start | bytes 392 | tf_op jit(solution)/shard_map/ppermute | solution.py:597
  6.2 2.9 %collective-permute-start = (s32[32]{0:T(128)S(1)}, s32[32]{0:T(128)S(1)}, u32[]{:S(2)}, u32[]{:S(2)}) collective-permute-start(s32[32]{0:T(128)S(1)} %get-tuple-element.92.refs_6_.code_ref), channel_id=1, source_target_pairs={{0,16},{1,65},{2,18},{3,67},{4,20},{5,69},{6,22},{7,71},{8,24},{9,... | collective-permute-start | bytes 392 | tf_op jit(solution)/shard_map/ppermute | solution.py:597
  9.5 1.9 %collective-permute-done.after1_ref.code_ref.refs_1_ = s32[32]{0:T(128)S(1)} collective-permute-done((s32[32]{0:T(128)S(1)}, s32[32]{0:T(128)S(1)}, u32[]{:S(2)}, u32[]{:S(2)}) %collective-permute-start) | collective-permute-done | bytes 160 | tf_op jit(solution)/shard_map/ppermute | solution.py:597
  11.4 2.8 %collective-permute-done.2.back1_ref = bf16[64,4096]{1,0:T(8,128)(2,1)S(1)} collective-permute-done((bf16[64,4096]{1,0:T(8,128)(2,1)}, bf16[64,4096]{1,0:T(8,128)(2,1)S(1)}, u32[]{:S(2)}, u32[]{:S(2)}) %collective-permute-start.2) | collective-permute-done | bytes 524320 | tf_op jit(solution)/shard_map/ppermute | solution.py:597
  14.3 3.2 %collective-permute-start.6 = (bf16[32,4096]{1,0:T(8,128)(2,1)S(1)}, bf16[32,4096]{1,0:T(8,128)(2,1)S(1)}, u32[]{:S(2)}, u32[]{:S(2)}) collective-permute-start(bf16[32,4096]{1,0:T(8,128)(2,1)S(1)} %get-tuple-element.31), channel_id=1, source_target_pairs={{0,96},{1,25},{2,98},{3,27},{4,100},{5,29},{6,102},{7,31},{8,104},... | collective-permute-start | bytes 786440 | tf_op jit(solution)/shard_map/ppermute | solution.py:597
  17.5 3.0 %collective-permute-start.1 = (s32[32]{0:T(128)S(1)}, s32[32]{0:T(128)S(1)}, u32[]{:S(2)}, u32[]{:S(2)}) collective-permute-start(s32[32]{0:T(128)S(1)} %get-tuple-element.91.refs_0_.code_ref), channel_id=1, source_target_pairs={{0,24},{1,97},{2,26},{3,99},{4,28},{5,101},{6,30},{7,103},{8,0},{9... | collective-permute-start | bytes 392 | tf_op jit(solution)/shard_map/ppermute | solution.py:597
  20.5 1.3 collective-permute-done.1.after_ref.code_ref.refs_0_
  21.8 1.0 copy-done.5
  23.6 0.9 collective-permute-start.7
  24.5 1.7 %gather_blocks.5.refs_0_ = bf16[32,64,256]{2,1,0:T(8,128)(2,1)} custom-call(s32[32]{0:T(128)S(1)} %collective-permute-done.4.after2_ref.code_ref, bf16[64,4096]{1,0:T(8,128)(2,1)S(1)} %keep.2.own_ref.refs_0_, bf16[64,4096]{1,0:T(8,128)(2,1)S(1)} %collective-permute-done.2.back1_ref, bf16[32,4096]{1,0:T(8,128)(2,1)S(1)} %collective-permute-done.5.low_ref, ...), custom_call_target="tpu_custom_call" | custom-call | tf_op jit(solution)/shard_map/gather_blocks/pallas_call | solution.py:122
  26.1 2.7 %collective-permute-start.9 = (bf16[32,64,256]{2,1,0:T(8,128)(2,1)}, bf16[32,64,256]{2,1,0:T(8,128)(2,1)}, u32[]{:S(2)}, u32[]{:S(2)}) collective-permute-start(bf16[32,64,256]{2,1,0:T(8,128)(2,1)} %gather_blocks.5.refs_0_), channel_id=1, source_target_pairs={{0,24},{1,97},{2,26},{3,99},{4,28},{5,101},{6,30},{7,103},{8,0},{9... | collective-permute-start | bytes 3145736 | tf_op jit(solution)/shard_map/ppermute | solution.py:597
  29.5 3.7 %spread.2.refs_0_.refs_5_.after_ref = f32[80,4096]{1,0:T(8,128)S(1)} custom-call(s32[32]{0:T(128)S(1)} %get-tuple-element.89.code_ref.refs_0_, bf16[32,64,256]{2,1,0:T(8,128)(2,1)S(1)} %gather_blocks.6.refs_1_, bf16[128,256,256]{2,1,0:T(8,128)(2,1)} %tiles_ref.5), custom_call_target="tpu_custom_call" | custom-call | tf_op jit(solution)/shard_map/spread/pallas_call | solution.py:198
  33.3 6.7 %collective-permute-done.7.refs_1_.refs_2_ = bf16[32,64,256]{2,1,0:T(8,128)(2,1)S(1)} collective-permute-done((bf16[32,64,256]{2,1,0:T(8,128)(2,1)S(1)}, bf16[32,64,256]{2,1,0:T(8,128)(2,1)S(1)}, u32[]{:S(2)}, u32[]{:S(2)}) %collective-permute-start.7) | collective-permute-done | bytes 1048608 | tf_op jit(solution)/shard_map/ppermute | solution.py:597
  40.9 1.0 collective-permute-start.8
  42.0 1.1 copy-done.7
  43.8 1.5 %collective-permute-done.10 = bf16[4,64,512]{2,1,0:T(8,128)(2,1)S(1)} collective-permute-done((bf16[4,64,512]{2,1,0:T(8,128)(2,1)S(1)}, bf16[4,64,512]{2,1,0:T(8,128)(2,1)S(1)}, u32[]{:S(2)}, u32[]{:S(2)}) %collective-permute-start.10) | collective-permute-done | bytes 262176 | tf_op jit(solution)/shard_map/ppermute | solution.py:622
  45.3 2.0 %collective-permute-start.11 = (bf16[2,64,512]{2,1,0:T(8,128)(2,1)S(1)}, bf16[2,64,512]{2,1,0:T(8,128)(2,1)S(1)}, u32[]{:S(2)}, u32[]{:S(2)}) collective-permute-start(bf16[2,64,512]{2,1,0:T(8,128)(2,1)S(1)} %pad_maximum_fusion.1), channel_id=1, source_target_pairs={{0,2},{1,3},{2,4},{3,5},{4,6},{5,7},{6,0},{7,1},{8,10},{9,11},{10,... | collective-permute-start | bytes 393224 | tf_op jit(solution)/shard_map/ppermute | solution.py:634
  47.3 3.7 %collective-permute-start.12 = (bf16[2,64,512]{2,1,0:T(8,128)(2,1)S(1)}, bf16[2,64,512]{2,1,0:T(8,128)(2,1)S(1)}, u32[]{:S(2)}, u32[]{:S(2)}) collective-permute-start(bf16[2,64,512]{2,1,0:T(8,128)(2,1)S(1)} %pair.2), channel_id=1, source_target_pairs={{0,4},{1,5},{2,6},{3,7},{4,0},{5,1},{6,2},{7,3},{8,12},{9,13},{10,... | collective-permute-start | bytes 393224 | tf_op jit(solution)/shard_map/ppermute | solution.py:634
  51.0 1.1 collective-permute-start.13
  52.1 6.4 %spread.3 = (f32[80,4096]{1,0:T(8,128)S(1)}, bf16[4,8,256,256]{3,2,1,0:T(8,128)(2,1)S(1)}) custom-call(s32[32]{0:T(128)S(1)} %get-tuple-element.91.refs_0_.code_ref, s32[32]{0:T(128)S(1)} %get-tuple-element.90.refs_1_.code_ref, bf16[32,64,256]{2,1,0:T(8,128)(2,1)S(1)} %copy-done.3, bf16[32,64,256]{2,1,0:T(8,128)(2,1)} %collective-permute-done.9.refs_3_, ...), custom_call_target="tpu_custom_call" | custom-call | tf_op jit(solution)/shard_map/spread/pallas_call | solution.py:212
  59.2 4.2 %spread_mixed.1 = (bf16[4,64,512]{2,1,0:T(8,128)(2,1)S(1)}, bf16[4,64,512]{2,1,0:T(8,128)(2,1)S(1)}, f32[1,4096]{1,0:T(1,128)S(1)}) custom-call(s32[3]{0:T(128)S(1)} %pad_add_fusion.place_ref, s32[32]{0:T(128)S(1)} %get-tuple-element.92.refs_6_.code_ref, bf16[32,64,256]{2,1,0:T(8,128)(2,1)} %collective-permute-done.8.recv_ref, ...), custom_call_target="tpu_custom_call" | custom-call | tf_op jit(solution)/shard_map/spread_mixed/pallas_call | solution.py:240
  63.5 1.5 %collective-permute-done.14 = bf16[4,64,512]{2,1,0:T(8,128)(2,1)S(1)} collective-permute-done((bf16[4,64,512]{2,1,0:T(8,128)(2,1)S(1)}, bf16[4,64,512]{2,1,0:T(8,128)(2,1)S(1)}, u32[]{:S(2)}, u32[]{:S(2)}) %collective-permute-start.14) | collective-permute-done | bytes 262176 | tf_op jit(solution)/shard_map/ppermute | solution.py:622
  65.1 1.1 collective-permute-start.15
  66.2 1.9 %collective-permute-start.16 = (bf16[2,64,512]{2,1,0:T(8,128)(2,1)S(1)}, bf16[2,64,512]{2,1,0:T(8,128)(2,1)S(1)}, u32[]{:S(2)}, u32[]{:S(2)}) collective-permute-start(bf16[2,64,512]{2,1,0:T(8,128)(2,1)S(1)} %pad_maximum_fusion.4), channel_id=1, source_target_pairs={{0,4},{1,5},{2,6},{3,7},{4,0},{5,1},{6,2},{7,3},{8,12},{9,13},{10,... | collective-permute-start | bytes 393224 | tf_op jit(solution)/shard_map/ppermute | solution.py:634
  68.1 1.1 collective-permute-start.17
  69.4 5.3 %collective-permute-done.15.refs_1_ = bf16[2,64,512]{2,1,0:T(8,128)(2,1)S(1)} collective-permute-done((bf16[2,64,512]{2,1,0:T(8,128)(2,1)S(1)}, bf16[2,64,512]{2,1,0:T(8,128)(2,1)S(1)}, u32[]{:S(2)}, u32[]{:S(2)}) %collective-permute-start.15) | collective-permute-done | bytes 131104 | tf_op jit(solution)/shard_map/ppermute | solution.py:634
  75.4 2.2 %dense.1 = (bf16[4,64,512]{2,1,0:T(8,128)(2,1)S(1)}, bf16[4,64,512]{2,1,0:T(8,128)(2,1)S(1)}, bf16[4,64,512]{2,1,0:T(8,128)(2,1)S(1)}, bf16[4,128,512]{2,1,0:T(8,128)(2,1)S(1)}, bf16[4,64,512]{2,1,0:T(8,128)(2,1)S(1)}) custom-call(s32[3]{0:T(128)S(1)} %pad_add_fusion.place_ref, bf16[2,64,512]{2,1,0:T(8,128)(2,1)S(1)} %pad_maximum_fusion.2.refs_0_, ...), custom_call_target="tpu_custom_call" | custom-call | tf_op jit(solution)/shard_map/dense/pallas_call | solution.py:322
  77.7 1.9 %collective-permute-done.18.got_ref.after_ref = bf16[4,128,512]{2,1,0:T(8,128)(2,1)S(1)} collective-permute-done((bf16[4,128,512]{2,1,0:T(8,128)(2,1)S(1)}, bf16[4,128,512]{2,1,0:T(8,128)(2,1)S(1)}, u32[]{:S(2)}, u32[]{:S(2)}) %collective-permute-start.18) | collective-permute-done | bytes 524320 | tf_op jit(solution)/shard_map/ppermute | solution.py:622
  79.6 0.8 collective-permute-start.19
  80.5 3.6 %collective-permute-start.20 = (bf16[2,64,512]{2,1,0:T(8,128)(2,1)S(1)}, bf16[2,64,512]{2,1,0:T(8,128)(2,1)S(1)}, u32[]{:S(2)}, u32[]{:S(2)}) collective-permute-start(bf16[2,64,512]{2,1,0:T(8,128)(2,1)S(1)} %pad_maximum_fusion.8), channel_id=1, source_target_pairs={{0,4},{1,5},{2,6},{3,7},{4,0},{5,1},{6,2},{7,3},{8,12},{9,13},{10,... | collective-permute-start | bytes 393224 | tf_op jit(solution)/shard_map/ppermute | solution.py:634
  84.2 2.2 %collective-permute-done.19.refs_1_ = bf16[2,64,512]{2,1,0:T(8,128)(2,1)S(1)} collective-permute-done((bf16[2,64,512]{2,1,0:T(8,128)(2,1)S(1)}, bf16[2,64,512]{2,1,0:T(8,128)(2,1)S(1)}, u32[]{:S(2)}, u32[]{:S(2)}) %collective-permute-start.19) | collective-permute-done | bytes 131104 | tf_op jit(solution)/shard_map/ppermute | solution.py:634
  86.4 3.7 %collective-permute-done.20.refs_2_ = bf16[2,64,512]{2,1,0:T(8,128)(2,1)S(1)} collective-permute-done((bf16[2,64,512]{2,1,0:T(8,128)(2,1)S(1)}, bf16[2,64,512]{2,1,0:T(8,128)(2,1)S(1)}, u32[]{:S(2)}, u32[]{:S(2)}) %collective-permute-start.20) | collective-permute-done | bytes 131104 | tf_op jit(solution)/shard_map/ppermute | solution.py:634
  90.2 1.9 %back_products.4 = (bf16[32,64,256]{2,1,0:T(8,128)(2,1)S(1)}, bf16[64,4096]{1,0:T(8,128)(2,1)S(1)}, bf16[64,4096]{1,0:T(8,128)(2,1)S(1)}) custom-call(s32[3]{0:T(128)S(1)} %pad_add_fusion.place_ref, s32[32]{0:T(128)S(1)} %get-tuple-element.92.refs_6_.code_ref, bf16[2,64,512]{2,1,0:T(8,128)(2,1)S(1)} %pad_maximum_fusion.6.refs_0_, ...), custom_call_target="tpu_custom_call" | custom-call | tf_op jit(solution)/shard_map/back_products/pallas_call | solution.py:468
  92.0 2.6 %collective-permute-start.26 = (bf16[32,64,256]{2,1,0:T(8,128)(2,1)S(1)}, bf16[32,64,256]{2,1,0:T(8,128)(2,1)S(1)}, u32[]{:S(2)}, u32[]{:S(2)}) collective-permute-start(bf16[32,64,256]{2,1,0:T(8,128)(2,1)S(1)} %get-tuple-element.47.after_ref), channel_id=1, source_target_pairs={{0,16},{1,65},{2,18},{3,67},{4,20},{5,69},{6,22},{7,71},{8,24},{9,... | collective-permute-start | bytes 3145736 | tf_op jit(solution)/shard_map/ppermute | solution.py:597
  94.6 3.2 %back_products.6 = bf16[32,64,256]{2,1,0:T(8,128)(2,1)S(1)} custom-call(s32[32]{0:T(128)S(1)} %get-tuple-element.91.refs_0_.code_ref, bf16[64,4096]{1,0:T(8,128)(2,1)S(1)} %get-tuple-element.43.scaled_ref, bf16[128,256,256]{2,1,0:T(8,128)(2,1)} %tiles_ref.5, f32[1,4096]{1,0:T(1,128)S(1)} %get-tuple-element.42.refs_4_.after_ref), custom_call_target="tpu_custom_call" | custom-call | tf_op jit(solution)/shard_map/back_products/pallas_call | solution.py:479
  97.8 2.1 %collective-permute-start.23 = (bf16[32,64,256]{2,1,0:T(8,128)(2,1)S(1)}, bf16[32,64,256]{2,1,0:T(8,128)(2,1)S(1)}, u32[]{:S(2)}, u32[]{:S(2)}) collective-permute-start(bf16[32,64,256]{2,1,0:T(8,128)(2,1)S(1)} %back_products.6), channel_id=1, source_target_pairs={{0,24},{1,97},{2,26},{3,99},{4,28},{5,101},{6,30},{7,103},{8,0},{9... | collective-permute-start | bytes 3145736 | tf_op jit(solution)/shard_map/ppermute | solution.py:597
  99.9 3.2 %back_products.5.after_ref = bf16[32,64,256]{2,1,0:T(8,128)(2,1)S(1)} custom-call(s32[32]{0:T(128)S(1)} %get-tuple-element.90.refs_1_.code_ref, bf16[64,4096]{1,0:T(8,128)(2,1)S(1)} %get-tuple-element.43.scaled_ref, bf16[128,256,256]{2,1,0:T(8,128)(2,1)} %tiles_ref.5, f32[1,4096]{1,0:T(1,128)S(1)} %get-tuple-element.42.refs_4_.after_ref), custom_call_target="tpu_custom_call" | custom-call | tf_op jit(solution)/shard_map/back_products/pallas_call | solution.py:479
  103.3 0.8 collective-permute-start.24
  104.0 4.3 %collective-permute-done.24.got_ref = bf16[2,64,512]{2,1,0:T(8,128)(2,1)S(1)} collective-permute-done((bf16[2,64,512]{2,1,0:T(8,128)(2,1)S(1)}, bf16[2,64,512]{2,1,0:T(8,128)(2,1)S(1)}, u32[]{:S(2)}, u32[]{:S(2)}) %collective-permute-start.24) | collective-permute-done | bytes 131104 | tf_op jit(solution)/shard_map/ppermute | solution.py:397
  108.3 2.4 %collective-permute-start.25 = (bf16[1,64,512]{2,1,0:T(8,128)(2,1)S(1)}, bf16[1,64,512]{2,1,0:T(8,128)(2,1)S(1)}, u32[]{:S(2)}, u32[]{:S(2)}) collective-permute-start(bf16[1,64,512]{2,1,0:T(8,128)(2,1)S(1)} %get-tuple-element.49), channel_id=1, source_target_pairs={{0,4},{1,5},{2,6},{3,7},{4,0},{5,1},{6,2},{7,3},{8,12},{9,13},{10,... | collective-permute-start | bytes 196616 | tf_op jit(solution)/shard_map/ppermute | solution.py:397
  110.7 3.2 %back_products.7.after_ref.refs_2_.refs_4_ = bf16[32,64,256]{2,1,0:T(8,128)(2,1)S(1)} custom-call(s32[32]{0:T(128)S(1)} %get-tuple-element.89.code_ref.refs_0_, bf16[64,4096]{1,0:T(8,128)(2,1)S(1)} %get-tuple-element.43.scaled_ref, bf16[128,256,256]{2,1,0:T(8,128)(2,1)} %tiles_ref.5, bf16[32,64,256]{2,1,0:T(8,128)(2,1)S(1)} %back_products.5.after_ref), custom_call_target="tpu_custom_call" | custom-call | tf_op jit(solution)/shard_map/back_products/pallas_call | solution.py:479
  114.2 0.8 gw_order.1
  115.0 3.5 %collective-permute-start.27 = (bf16[64,128]{1,0:T(8,128)(2,1)S(1)}, bf16[64,128]{1,0:T(8,128)(2,1)S(1)}, u32[]{:S(2)}, u32[]{:S(2)}) collective-permute-start(bf16[64,128]{1,0:T(8,128)(2,1)S(1)} %get-tuple-element.51), channel_id=1, source_target_pairs={{0,24},{1,97},{2,26},{3,99},{4,28},{5,101},{6,30},{7,103},{8,0},{9... | collective-permute-start | bytes 49160 | tf_op jit(solution)/shard_map/ppermute | solution.py:597
  118.5 0.9 collective-permute-start.29
  119.4 1.3 collect.2.refs_3_
  120.8 1.1 collect.3.before_ref
  121.9 1.8 %collective-permute-done.28.refs_2_ = bf16[64,128]{1,0:T(8,128)(2,1)S(1)} collective-permute-done((bf16[64,128]{1,0:T(8,128)(2,1)S(1)}, bf16[64,128]{1,0:T(8,128)(2,1)S(1)}, u32[]{:S(2)}, u32[]{:S(2)}) %collective-permute-start.28) | collective-permute-done | bytes 16416 | tf_op jit(solution)/shard_map/ppermute | solution.py:597
  123.7 0.7 slab.4.after_ref
  124.6 1.7 %collective-permute-start.34 = (bf16[64,4224]{1,0:T(8,128)(2,1)S(1)}, bf16[64,4224]{1,0:T(8,128)(2,1)S(1)}, u32[]{:S(2)}, u32[]{:S(2)}) collective-permute-start(bf16[64,4224]{1,0:T(8,128)(2,1)S(1)} %slab.4.after_ref), channel_id=1, source_target_pairs={{0,96},{1,25},{2,98},{3,27},{4,100},{5,29},{6,102},{7,31},{8,104},... | collective-permute-start | bytes 1622024 | tf_op jit(solution)/shard_map/ppermute | solution.py:597
  126.3 0.7 slab.6
  127.1 0.7 slab.7
  127.9 0.9 collective-permute-start.36
  128.8 0.9 collective-permute-start.31
  129.7 3.3 %collective-permute-start.32 = (bf16[2,64,512]{2,1,0:T(8,128)(2,1)S(1)}, bf16[2,64,512]{2,1,0:T(8,128)(2,1)S(1)}, u32[]{:S(2)}, u32[]{:S(2)}) collective-permute-start(bf16[2,64,512]{2,1,0:T(8,128)(2,1)S(1)} %pad_maximum_fusion.12), channel_id=1, source_target_pairs={{0,4},{1,5},{2,6},{3,7},{4,0},{5,1},{6,2},{7,3},{8,12},{9,13},{10,... | collective-permute-start | bytes 393224 | tf_op jit(solution)/shard_map/ppermute | solution.py:634
  133.0 3.1 %collective-permute-done.31.refs_1_ = bf16[2,64,512]{2,1,0:T(8,128)(2,1)S(1)} collective-permute-done((bf16[2,64,512]{2,1,0:T(8,128)(2,1)S(1)}, bf16[2,64,512]{2,1,0:T(8,128)(2,1)S(1)}, u32[]{:S(2)}, u32[]{:S(2)}) %collective-permute-start.31) | collective-permute-done | bytes 131104 | tf_op jit(solution)/shard_map/ppermute | solution.py:634
  136.1 1.6 %collective-permute-start.33 = (bf16[2,64,512]{2,1,0:T(8,128)(2,1)S(1)}, bf16[2,64,512]{2,1,0:T(8,128)(2,1)S(1)}, u32[]{:S(2)}, u32[]{:S(2)}) collective-permute-start(bf16[2,64,512]{2,1,0:T(8,128)(2,1)S(1)} %pad_maximum_fusion.13), channel_id=1, source_target_pairs={{0,6},{1,7},{2,0},{3,1},{4,2},{5,3},{6,4},{7,5},{8,14},{9,15},{10,... | collective-permute-start | bytes 393224 | tf_op jit(solution)/shard_map/ppermute | solution.py:634
  137.7 0.7 slab.5.refs_0_
  138.5 1.1 collective-permute-done.32.refs_2_
  139.6 1.8 %collective-permute-done.33.refs_3_ = bf16[2,64,512]{2,1,0:T(8,128)(2,1)S(1)} collective-permute-done((bf16[2,64,512]{2,1,0:T(8,128)(2,1)S(1)}, bf16[2,64,512]{2,1,0:T(8,128)(2,1)S(1)}, u32[]{:S(2)}, u32[]{:S(2)}) %collective-permute-start.33) | collective-permute-done | bytes 131104 | tf_op jit(solution)/shard_map/ppermute | solution.py:634
  141.3 1.4 unpack.1
  142.7 1.0 collective-permute-done.36.refs_3_
  143.8 1.4 final_sum.1
  (85 shorter events, 6.7 us)
Async XLA Ops:
  0.6 10.7 %collective-permute-start.3 = (bf16[64,4096]{1,0:T(8,128)(2,1)}, bf16[64,4096]{1,0:T(8,128)(2,1)S(1)}, u32[]{:S(2)}, u32[]{:S(2)}) collective-permute-start(bf16[64,4096]{1,0:T(8,128)(2,1)} %bitcast.17), channel_id=1, source_target_pairs={{0,96},{1,25},{2,98},{3,27},{4,100},{5,29},{6,102},{7,31},{8,104},... | collective-permute-start | bytes 1572872 | tf_op jit(solution)/shard_map/ppermute | solution.py:597
  3.5 10.6 %collective-permute-start.2 = (bf16[64,4096]{1,0:T(8,128)(2,1)}, bf16[64,4096]{1,0:T(8,128)(2,1)S(1)}, u32[]{:S(2)}, u32[]{:S(2)}) collective-permute-start(bf16[64,4096]{1,0:T(8,128)(2,1)} %bitcast.18), channel_id=1, source_target_pairs={{0,32},{1,9},{2,34},{3,11},{4,36},{5,13},{6,38},{7,15},{8,40},{9,1... | collective-permute-start | bytes 1572872 | tf_op jit(solution)/shard_map/ppermute | solution.py:597
  4.6 4.8 %collective-permute-start.4 = (s32[32]{0:T(128)S(1)}, s32[32]{0:T(128)S(1)}, u32[]{:S(2)}, u32[]{:S(2)}) collective-permute-start(s32[32]{0:T(128)S(1)} %get-tuple-element.90.refs_1_.code_ref), channel_id=1, source_target_pairs={{0,8},{1,33},{2,10},{3,35},{4,12},{5,37},{6,14},{7,39},{8,16},{9,4... | collective-permute-start | bytes 392 | tf_op jit(solution)/shard_map/ppermute | solution.py:597
  6.2 5.1 %collective-permute-start = (s32[32]{0:T(128)S(1)}, s32[32]{0:T(128)S(1)}, u32[]{:S(2)}, u32[]{:S(2)}) collective-permute-start(s32[32]{0:T(128)S(1)} %get-tuple-element.92.refs_6_.code_ref), channel_id=1, source_target_pairs={{0,16},{1,65},{2,18},{3,67},{4,20},{5,69},{6,22},{7,71},{8,24},{9,... | collective-permute-start | bytes 392 | tf_op jit(solution)/shard_map/ppermute | solution.py:597
  14.2 8.7 %collective-permute-start.5 = (bf16[32,4096]{1,0:T(8,128)(2,1)S(1)}, bf16[32,4096]{1,0:T(8,128)(2,1)S(1)}, u32[]{:S(2)}, u32[]{:S(2)}) collective-permute-start(bf16[32,4096]{1,0:T(8,128)(2,1)S(1)} %get-tuple-element.30), channel_id=1, source_target_pairs={{0,32},{1,9},{2,34},{3,11},{4,36},{5,13},{6,38},{7,15},{8,40},{9,1... | collective-permute-start | bytes 786440 | tf_op jit(solution)/shard_map/ppermute | solution.py:597
  14.3 8.6 %collective-permute-start.6 = (bf16[32,4096]{1,0:T(8,128)(2,1)S(1)}, bf16[32,4096]{1,0:T(8,128)(2,1)S(1)}, u32[]{:S(2)}, u32[]{:S(2)}) collective-permute-start(bf16[32,4096]{1,0:T(8,128)(2,1)S(1)} %get-tuple-element.31), channel_id=1, source_target_pairs={{0,96},{1,25},{2,98},{3,27},{4,100},{5,29},{6,102},{7,31},{8,104},... | collective-permute-start | bytes 786440 | tf_op jit(solution)/shard_map/ppermute | solution.py:597
  17.5 4.3 %collective-permute-start.1 = (s32[32]{0:T(128)S(1)}, s32[32]{0:T(128)S(1)}, u32[]{:S(2)}, u32[]{:S(2)}) collective-permute-start(s32[32]{0:T(128)S(1)} %get-tuple-element.91.refs_0_.code_ref), channel_id=1, source_target_pairs={{0,24},{1,97},{2,26},{3,99},{4,28},{5,101},{6,30},{7,103},{8,0},{9... | collective-permute-start | bytes 392 | tf_op jit(solution)/shard_map/ppermute | solution.py:597
  21.8 1.0 copy-start.5
  23.6 16.3 %collective-permute-start.7 = (bf16[32,64,256]{2,1,0:T(8,128)(2,1)S(1)}, bf16[32,64,256]{2,1,0:T(8,128)(2,1)S(1)}, u32[]{:S(2)}, u32[]{:S(2)}) collective-permute-start(bf16[32,64,256]{2,1,0:T(8,128)(2,1)S(1)} %gather_blocks.4.refs_0_), channel_id=1, source_target_pairs={{0,8},{1,33},{2,10},{3,35},{4,12},{5,37},{6,14},{7,39},{8,16},{9,4... | collective-permute-start | bytes 3145736 | tf_op jit(solution)/shard_map/ppermute | solution.py:597
  26.1 26.0 %collective-permute-start.9 = (bf16[32,64,256]{2,1,0:T(8,128)(2,1)}, bf16[32,64,256]{2,1,0:T(8,128)(2,1)}, u32[]{:S(2)}, u32[]{:S(2)}) collective-permute-start(bf16[32,64,256]{2,1,0:T(8,128)(2,1)} %gather_blocks.5.refs_0_), channel_id=1, source_target_pairs={{0,24},{1,97},{2,26},{3,99},{4,28},{5,101},{6,30},{7,103},{8,0},{9... | collective-permute-start | bytes 3145736 | tf_op jit(solution)/shard_map/ppermute | solution.py:597
  39.9 1.0 copy-start.2
  40.9 18.3 %collective-permute-start.8 = (bf16[32,64,256]{2,1,0:T(8,128)(2,1)S(1)}, bf16[32,64,256]{2,1,0:T(8,128)(2,1)}, u32[]{:S(2)}, u32[]{:S(2)}) collective-permute-start(bf16[32,64,256]{2,1,0:T(8,128)(2,1)S(1)} %gather_blocks.7.after_ref), channel_id=1, source_target_pairs={{0,16},{1,65},{2,18},{3,67},{4,20},{5,69},{6,22},{7,71},{8,24},{9,... | collective-permute-start | bytes 3145736 | tf_op jit(solution)/shard_map/ppermute | solution.py:597
  41.9 10.2 %copy-start.3 = (bf16[32,64,256]{2,1,0:T(8,128)(2,1)S(1)}, bf16[32,64,256]{2,1,0:T(8,128)(2,1)}, u32[]{:S(2)}) copy-start(bf16[32,64,256]{2,1,0:T(8,128)(2,1)} %copy-done.2) | copy-start | bytes 3145732
  42.0 1.1 copy-start.7
  43.7 1.6 %collective-permute-start.10 = (bf16[4,64,512]{2,1,0:T(8,128)(2,1)S(1)}, bf16[4,64,512]{2,1,0:T(8,128)(2,1)S(1)}, u32[]{:S(2)}, u32[]{:S(2)}) collective-permute-start(bf16[4,64,512]{2,1,0:T(8,128)(2,1)S(1)} %get-tuple-element.35), channel_id=1, source_target_pairs={{0,1},{1,0},{2,3},{3,2},{4,5},{5,4},{6,7},{7,6},{8,9},{9,8},{10,11... | collective-permute-start | bytes 786440 | tf_op jit(solution)/shard_map/ppermute | solution.py:622
  45.3 13.2 %collective-permute-start.11 = (bf16[2,64,512]{2,1,0:T(8,128)(2,1)S(1)}, bf16[2,64,512]{2,1,0:T(8,128)(2,1)S(1)}, u32[]{:S(2)}, u32[]{:S(2)}) collective-permute-start(bf16[2,64,512]{2,1,0:T(8,128)(2,1)S(1)} %pad_maximum_fusion.1), channel_id=1, source_target_pairs={{0,2},{1,3},{2,4},{3,5},{4,6},{5,7},{6,0},{7,1},{8,10},{9,11},{10,... | collective-permute-start | bytes 393224 | tf_op jit(solution)/shard_map/ppermute | solution.py:634
  47.3 11.2 %collective-permute-start.12 = (bf16[2,64,512]{2,1,0:T(8,128)(2,1)S(1)}, bf16[2,64,512]{2,1,0:T(8,128)(2,1)S(1)}, u32[]{:S(2)}, u32[]{:S(2)}) collective-permute-start(bf16[2,64,512]{2,1,0:T(8,128)(2,1)S(1)} %pair.2), channel_id=1, source_target_pairs={{0,4},{1,5},{2,6},{3,7},{4,0},{5,1},{6,2},{7,3},{8,12},{9,13},{10,... | collective-permute-start | bytes 393224 | tf_op jit(solution)/shard_map/ppermute | solution.py:634
  51.0 7.6 %collective-permute-start.13 = (bf16[2,64,512]{2,1,0:T(8,128)(2,1)S(1)}, bf16[2,64,512]{2,1,0:T(8,128)(2,1)S(1)}, u32[]{:S(2)}, u32[]{:S(2)}) collective-permute-start(bf16[2,64,512]{2,1,0:T(8,128)(2,1)S(1)} %pair.3), channel_id=1, source_target_pairs={{0,6},{1,7},{2,0},{3,1},{4,2},{5,3},{6,4},{7,5},{8,14},{9,15},{10,... | collective-permute-start | bytes 393224 | tf_op jit(solution)/shard_map/ppermute | solution.py:634
  52.1 7.1 %copy-start.6 = (bf16[4096,64]{0,1:T(8,128)(2,1)S(1)}, bf16[4096,64]{0,1:T(8,128)(2,1)}, u32[]{:S(2)}) copy-start(bf16[4096,64]{0,1:T(8,128)(2,1)} %param.7) | copy-start | bytes 1572868
  58.5 4.9 %copy-start = (bf16[4,8,256,256]{3,2,1,0:T(8,128)(2,1)}, bf16[4,8,256,256]{3,2,1,0:T(8,128)(2,1)S(1)}, u32[]{:S(2)}) copy-start(bf16[4,8,256,256]{3,2,1,0:T(8,128)(2,1)S(1)} %get-tuple-element.32.tiles_ref.refs_5_) | copy-start | bytes 12582916
  59.2 9.9 %copy-start.4 = (bf16[512,512]{1,0:T(8,128)(2,1)S(1)}, bf16[512,512]{1,0:T(8,128)(2,1)}, u32[]{:S(2)}) copy-start(bf16[512,512]{1,0:T(8,128)(2,1)} %refs_5_.1) | copy-start | bytes 1572868
  63.4 1.6 %collective-permute-start.14 = (bf16[4,64,512]{2,1,0:T(8,128)(2,1)S(1)}, bf16[4,64,512]{2,1,0:T(8,128)(2,1)S(1)}, u32[]{:S(2)}, u32[]{:S(2)}) collective-permute-start(bf16[4,64,512]{2,1,0:T(8,128)(2,1)S(1)} %get-tuple-element.37), channel_id=1, source_target_pairs={{0,1},{1,0},{2,3},{3,2},{4,5},{5,4},{6,7},{7,6},{8,9},{9,8},{10,11... | collective-permute-start | bytes 786440 | tf_op jit(solution)/shard_map/ppermute | solution.py:622
  65.1 9.6 %collective-permute-start.15 = (bf16[2,64,512]{2,1,0:T(8,128)(2,1)S(1)}, bf16[2,64,512]{2,1,0:T(8,128)(2,1)S(1)}, u32[]{:S(2)}, u32[]{:S(2)}) collective-permute-start(bf16[2,64,512]{2,1,0:T(8,128)(2,1)S(1)} %pad_maximum_fusion.3), channel_id=1, source_target_pairs={{0,2},{1,3},{2,4},{3,5},{4,6},{5,7},{6,0},{7,1},{8,10},{9,11},{10,... | collective-permute-start | bytes 393224 | tf_op jit(solution)/shard_map/ppermute | solution.py:634
  66.2 8.5 %collective-permute-start.16 = (bf16[2,64,512]{2,1,0:T(8,128)(2,1)S(1)}, bf16[2,64,512]{2,1,0:T(8,128)(2,1)S(1)}, u32[]{:S(2)}, u32[]{:S(2)}) collective-permute-start(bf16[2,64,512]{2,1,0:T(8,128)(2,1)S(1)} %pad_maximum_fusion.4), channel_id=1, source_target_pairs={{0,4},{1,5},{2,6},{3,7},{4,0},{5,1},{6,2},{7,3},{8,12},{9,13},{10,... | collective-permute-start | bytes 393224 | tf_op jit(solution)/shard_map/ppermute | solution.py:634
  68.1 7.3 %collective-permute-start.17 = (bf16[2,64,512]{2,1,0:T(8,128)(2,1)S(1)}, bf16[2,64,512]{2,1,0:T(8,128)(2,1)S(1)}, u32[]{:S(2)}, u32[]{:S(2)}) collective-permute-start(bf16[2,64,512]{2,1,0:T(8,128)(2,1)S(1)} %pad_maximum_fusion.5), channel_id=1, source_target_pairs={{0,6},{1,7},{2,0},{3,1},{4,2},{5,3},{6,4},{7,5},{8,14},{9,15},{10,... | collective-permute-start | bytes 393224 | tf_op jit(solution)/shard_map/ppermute | solution.py:634
  69.4 20.8 %copy-start.1 = (bf16[4,8,256,256]{3,2,1,0:T(8,128)(2,1)S(1)}, bf16[4,8,256,256]{3,2,1,0:T(8,128)(2,1)}, u32[]{:S(2)}) copy-start(bf16[4,8,256,256]{3,2,1,0:T(8,128)(2,1)} %copy-done) | copy-start | bytes 12582916
  77.6 2.0 %collective-permute-start.18 = (bf16[4,128,512]{2,1,0:T(8,128)(2,1)S(1)}, bf16[4,128,512]{2,1,0:T(8,128)(2,1)S(1)}, u32[]{:S(2)}, u32[]{:S(2)}) collective-permute-start(bf16[4,128,512]{2,1,0:T(8,128)(2,1)S(1)} %get-tuple-element.41), channel_id=1, source_target_pairs={{0,1},{1,0},{2,3},{3,2},{4,5},{5,4},{6,7},{7,6},{8,9},{9,8},{10,11... | collective-permute-start | bytes 1572872 | tf_op jit(solution)/shard_map/ppermute | solution.py:622
  79.6 6.8 %collective-permute-start.19 = (bf16[2,64,512]{2,1,0:T(8,128)(2,1)S(1)}, bf16[2,64,512]{2,1,0:T(8,128)(2,1)S(1)}, u32[]{:S(2)}, u32[]{:S(2)}) collective-permute-start(bf16[2,64,512]{2,1,0:T(8,128)(2,1)S(1)} %pad_maximum_fusion.7), channel_id=1, source_target_pairs={{0,2},{1,3},{2,4},{3,5},{4,6},{5,7},{6,0},{7,1},{8,10},{9,11},{10,... | collective-permute-start | bytes 393224 | tf_op jit(solution)/shard_map/ppermute | solution.py:634
  80.5 9.7 %collective-permute-start.20 = (bf16[2,64,512]{2,1,0:T(8,128)(2,1)S(1)}, bf16[2,64,512]{2,1,0:T(8,128)(2,1)S(1)}, u32[]{:S(2)}, u32[]{:S(2)}) collective-permute-start(bf16[2,64,512]{2,1,0:T(8,128)(2,1)S(1)} %pad_maximum_fusion.8), channel_id=1, source_target_pairs={{0,4},{1,5},{2,6},{3,7},{4,0},{5,1},{6,2},{7,3},{8,12},{9,13},{10,... | collective-permute-start | bytes 393224 | tf_op jit(solution)/shard_map/ppermute | solution.py:634
  84.1 6.0 %collective-permute-start.21 = (bf16[2,64,512]{2,1,0:T(8,128)(2,1)S(1)}, bf16[2,64,512]{2,1,0:T(8,128)(2,1)S(1)}, u32[]{:S(2)}, u32[]{:S(2)}) collective-permute-start(bf16[2,64,512]{2,1,0:T(8,128)(2,1)S(1)} %pad_maximum_fusion.9), channel_id=1, source_target_pairs={{0,6},{1,7},{2,0},{3,1},{4,2},{5,3},{6,4},{7,5},{8,14},{9,15},{10,... | collective-permute-start | bytes 393224 | tf_op jit(solution)/shard_map/ppermute | solution.py:634
  92.0 26.5 %collective-permute-start.26 = (bf16[32,64,256]{2,1,0:T(8,128)(2,1)S(1)}, bf16[32,64,256]{2,1,0:T(8,128)(2,1)S(1)}, u32[]{:S(2)}, u32[]{:S(2)}) collective-permute-start(bf16[32,64,256]{2,1,0:T(8,128)(2,1)S(1)} %get-tuple-element.47.after_ref), channel_id=1, source_target_pairs={{0,16},{1,65},{2,18},{3,67},{4,20},{5,69},{6,22},{7,71},{8,24},{9,... | collective-permute-start | bytes 3145736 | tf_op jit(solution)/shard_map/ppermute | solution.py:597
  97.8 22.9 %collective-permute-start.23 = (bf16[32,64,256]{2,1,0:T(8,128)(2,1)S(1)}, bf16[32,64,256]{2,1,0:T(8,128)(2,1)S(1)}, u32[]{:S(2)}, u32[]{:S(2)}) collective-permute-start(bf16[32,64,256]{2,1,0:T(8,128)(2,1)S(1)} %back_products.6), channel_id=1, source_target_pairs={{0,24},{1,97},{2,26},{3,99},{4,28},{5,101},{6,30},{7,103},{8,0},{9... | collective-permute-start | bytes 3145736 | tf_op jit(solution)/shard_map/ppermute | solution.py:597
  103.1 20.6 %collective-permute-start.22 = (bf16[32,64,256]{2,1,0:T(8,128)(2,1)S(1)}, bf16[32,64,256]{2,1,0:T(8,128)(2,1)S(1)}, u32[]{:S(2)}, u32[]{:S(2)}) collective-permute-start(bf16[32,64,256]{2,1,0:T(8,128)(2,1)S(1)} %back_products.5.after_ref), channel_id=1, source_target_pairs={{0,8},{1,33},{2,10},{3,35},{4,12},{5,37},{6,14},{7,39},{8,16},{9,4... | collective-permute-start | bytes 3145736 | tf_op jit(solution)/shard_map/ppermute | solution.py:597
  103.3 5.0 %collective-permute-start.24 = (bf16[2,64,512]{2,1,0:T(8,128)(2,1)S(1)}, bf16[2,64,512]{2,1,0:T(8,128)(2,1)S(1)}, u32[]{:S(2)}, u32[]{:S(2)}) collective-permute-start(bf16[2,64,512]{2,1,0:T(8,128)(2,1)S(1)} %get-tuple-element.46), channel_id=1, source_target_pairs={{0,2},{1,3},{2,0},{3,1},{4,6},{5,7},{6,4},{7,5},{8,10},{9,11},{10,... | collective-permute-start | bytes 393224 | tf_op jit(solution)/shard_map/ppermute | solution.py:397
  108.3 5.8 %collective-permute-start.25 = (bf16[1,64,512]{2,1,0:T(8,128)(2,1)S(1)}, bf16[1,64,512]{2,1,0:T(8,128)(2,1)S(1)}, u32[]{:S(2)}, u32[]{:S(2)}) collective-permute-start(bf16[1,64,512]{2,1,0:T(8,128)(2,1)S(1)} %get-tuple-element.49), channel_id=1, source_target_pairs={{0,4},{1,5},{2,6},{3,7},{4,0},{5,1},{6,2},{7,3},{8,12},{9,13},{10,... | collective-permute-start | bytes 196616 | tf_op jit(solution)/shard_map/ppermute | solution.py:397
  115.0 6.9 %collective-permute-start.27 = (bf16[64,128]{1,0:T(8,128)(2,1)S(1)}, bf16[64,128]{1,0:T(8,128)(2,1)S(1)}, u32[]{:S(2)}, u32[]{:S(2)}) collective-permute-start(bf16[64,128]{1,0:T(8,128)(2,1)S(1)} %get-tuple-element.51), channel_id=1, source_target_pairs={{0,24},{1,97},{2,26},{3,99},{4,28},{5,101},{6,30},{7,103},{8,0},{9... | collective-permute-start | bytes 49160 | tf_op jit(solution)/shard_map/ppermute | solution.py:597
  118.5 5.2 %collective-permute-start.28 = (bf16[64,128]{1,0:T(8,128)(2,1)S(1)}, bf16[64,128]{1,0:T(8,128)(2,1)S(1)}, u32[]{:S(2)}, u32[]{:S(2)}) collective-permute-start(bf16[64,128]{1,0:T(8,128)(2,1)S(1)} %get-tuple-element.52), channel_id=1, source_target_pairs={{0,16},{1,65},{2,18},{3,67},{4,20},{5,69},{6,22},{7,71},{8,24},{9,... | collective-permute-start | bytes 49160 | tf_op jit(solution)/shard_map/ppermute | solution.py:597
  118.5 5.2 %collective-permute-start.29 = (bf16[64,128]{1,0:T(8,128)(2,1)S(1)}, bf16[64,128]{1,0:T(8,128)(2,1)S(1)}, u32[]{:S(2)}, u32[]{:S(2)}) collective-permute-start(bf16[64,128]{1,0:T(8,128)(2,1)S(1)} %get-tuple-element.53), channel_id=1, source_target_pairs={{0,8},{1,33},{2,10},{3,35},{4,12},{5,37},{6,14},{7,39},{8,16},{9,4... | collective-permute-start | bytes 49160 | tf_op jit(solution)/shard_map/ppermute | solution.py:597
  124.5 4.3 %collective-permute-start.30 = (bf16[4,64,512]{2,1,0:T(8,128)(2,1)S(1)}, bf16[4,64,512]{2,1,0:T(8,128)(2,1)S(1)}, u32[]{:S(2)}, u32[]{:S(2)}) collective-permute-start(bf16[4,64,512]{2,1,0:T(8,128)(2,1)S(1)} %keep.3), channel_id=1, source_target_pairs={{0,1},{1,0},{2,3},{3,2},{4,5},{5,4},{6,7},{7,6},{8,9},{9,8},{10,11... | collective-permute-start | bytes 786440 | tf_op jit(solution)/shard_map/ppermute | solution.py:622
  124.6 19.2 %collective-permute-start.34 = (bf16[64,4224]{1,0:T(8,128)(2,1)S(1)}, bf16[64,4224]{1,0:T(8,128)(2,1)S(1)}, u32[]{:S(2)}, u32[]{:S(2)}) collective-permute-start(bf16[64,4224]{1,0:T(8,128)(2,1)S(1)} %slab.4.after_ref), channel_id=1, source_target_pairs={{0,96},{1,25},{2,98},{3,27},{4,100},{5,29},{6,102},{7,31},{8,104},... | collective-permute-start | bytes 1622024 | tf_op jit(solution)/shard_map/ppermute | solution.py:597
  127.0 15.7 %collective-permute-start.35 = (bf16[64,4224]{1,0:T(8,128)(2,1)S(1)}, bf16[64,4224]{1,0:T(8,128)(2,1)S(1)}, u32[]{:S(2)}, u32[]{:S(2)}) collective-permute-start(bf16[64,4224]{1,0:T(8,128)(2,1)S(1)} %slab.6), channel_id=1, source_target_pairs={{0,64},{1,17},{2,66},{3,19},{4,68},{5,21},{6,70},{7,23},{8,72},{9,... | collective-permute-start | bytes 1622024 | tf_op jit(solution)/shard_map/ppermute | solution.py:597
  127.9 15.9 %collective-permute-start.36 = (bf16[64,4224]{1,0:T(8,128)(2,1)S(1)}, bf16[64,4224]{1,0:T(8,128)(2,1)S(1)}, u32[]{:S(2)}, u32[]{:S(2)}) collective-permute-start(bf16[64,4224]{1,0:T(8,128)(2,1)S(1)} %slab.7), channel_id=1, source_target_pairs={{0,32},{1,9},{2,34},{3,11},{4,36},{5,13},{6,38},{7,15},{8,40},{9,1... | collective-permute-start | bytes 1622024 | tf_op jit(solution)/shard_map/ppermute | solution.py:597
  128.8 7.3 %collective-permute-start.31 = (bf16[2,64,512]{2,1,0:T(8,128)(2,1)S(1)}, bf16[2,64,512]{2,1,0:T(8,128)(2,1)S(1)}, u32[]{:S(2)}, u32[]{:S(2)}) collective-permute-start(bf16[2,64,512]{2,1,0:T(8,128)(2,1)S(1)} %pad_maximum_fusion.11), channel_id=1, source_target_pairs={{0,2},{1,3},{2,4},{3,5},{4,6},{5,7},{6,0},{7,1},{8,10},{9,11},{10,... | collective-permute-start | bytes 393224 | tf_op jit(solution)/shard_map/ppermute | solution.py:634
  129.7 9.8 %collective-permute-start.32 = (bf16[2,64,512]{2,1,0:T(8,128)(2,1)S(1)}, bf16[2,64,512]{2,1,0:T(8,128)(2,1)S(1)}, u32[]{:S(2)}, u32[]{:S(2)}) collective-permute-start(bf16[2,64,512]{2,1,0:T(8,128)(2,1)S(1)} %pad_maximum_fusion.12), channel_id=1, source_target_pairs={{0,4},{1,5},{2,6},{3,7},{4,0},{5,1},{6,2},{7,3},{8,12},{9,13},{10,... | collective-permute-start | bytes 393224 | tf_op jit(solution)/shard_map/ppermute | solution.py:634
  136.1 5.2 %collective-permute-start.33 = (bf16[2,64,512]{2,1,0:T(8,128)(2,1)S(1)}, bf16[2,64,512]{2,1,0:T(8,128)(2,1)S(1)}, u32[]{:S(2)}, u32[]{:S(2)}) collective-permute-start(bf16[2,64,512]{2,1,0:T(8,128)(2,1)S(1)} %pad_maximum_fusion.13), channel_id=1, source_target_pairs={{0,6},{1,7},{2,0},{3,1},{4,2},{5,3},{6,4},{7,5},{8,14},{9,15},{10,... | collective-permute-start | bytes 393224 | tf_op jit(solution)/shard_map/ppermute | solution.py:634

commit v5 on v4

--- a/solution.py
+++ b/solution.py
@@ -69,7 +69,8 @@
     )(value, after)
 
 
-def halves_kernel(back1_ref, back3_ref, after1_ref, after2_ref, low_ref, high_ref):
+def halves_kernel(back1_ref, back3_ref, *refs):
+    low_ref, high_ref = refs[-2:]
     half = low_ref.shape[0]
     low_ref[...] = back1_ref[:half, :]
     high_ref[...] = back3_ref[half:, :]
@@ -81,7 +82,7 @@
     return pl.pallas_call(
         halves_kernel,
         out_shape=(half, half),
-        in_specs=arrays(2) + anywhere(2),
+        in_specs=arrays(2) + anywhere(len(after)),
         out_specs=tuple(arrays(2)),
         compiler_params=params(),
         name="halves",
@@ -173,7 +174,7 @@
     if first:
         total_ref, buf_ref, sems = refs[2 * parts + 1 :]
     else:
-        before_ref, next_code_ref, total_ref, next_ref, buf_ref, sems, next_sems = refs[2 * parts + 1 :]
+        before_ref, next_code_ref, _, total_ref, next_ref, buf_ref, sems, next_sems = refs[2 * parts + 1 :]
     load_tiles(codes, tiles_ref, buf_ref, sems)
     if first:
         total_ref[...] = jnp.zeros_like(total_ref)
@@ -206,18 +207,18 @@
     )(code, recv, tile_vals)
 
 
-def spread(codes, recvs, tile_vals, before, next_code):
+def spread(codes, recvs, tile_vals, before, next_code, after):
     parts = len(codes)
     tiles = jax.ShapeDtypeStruct((SIDE, SLOTS, BLK, BLK), jnp.bfloat16)
     return pl.pallas_call(
         functools.partial(spread_kernel, parts, False),
         out_shape=(jax.ShapeDtypeStruct(before.shape, before.dtype), tiles),
-        in_specs=scalars(parts) + arrays(parts) + anywhere(1) + arrays(1) + scalars(1),
+        in_specs=scalars(parts) + arrays(parts) + anywhere(1) + arrays(1) + scalars(1) + anywhere(1),
         out_specs=tuple(arrays(2)),
         scratch_shapes=tile_scratch(parts) + [pltpu.SemaphoreType.DMA((SIDE,))],
         compiler_params=params(TILES_VMEM_LIMIT),
         name="spread",
-    )(*codes, *recvs, tile_vals, before, next_code)
+    )(*codes, *recvs, tile_vals, before, next_code, after)
 
 
 def mixed_kernel(place_ref, code_ref, recv_ref, tiles_ref, before_ref, feats_ref, after_ref, *refs):
@@ -274,8 +275,8 @@
 
 def dense_kernel(place_ref, *refs):
     pieces, cot_ref, weight_ref, weight_t_ref = refs[:SIDE], *refs[SIDE : SIDE + 3]
-    hidden_own_ref, hidden_other_ref, own_ref, other_ref, gw_own_ref = refs[SIDE + 3 : SIDE + 8]
-    hidden_ref, mixed_ref, gp_ref, grad_ref, gw_ref = refs[SIDE + 8 :]
+    hidden_own_ref, own_ref, other_ref, gw_own_ref = refs[SIDE + 3 : SIDE + 7]
+    hidden_ref, mixed_ref, gp_ref, grad_ref, gw_ref = refs[SIDE + 7 :]
     assemble(place_ref, pieces, mixed_ref)
     step = 128
     mixed = mixed_ref[...]
@@ -293,8 +294,8 @@
         jnp.bfloat16
     )
     rows = own_ref.shape[1]
-    split_rows(place_ref, grad_ref, own_ref, other_ref)
-    split_rows(place_ref, hidden_ref, hidden_own_ref, hidden_other_ref)
+    split_rows(place_ref, grad_ref, own_ref, other_ref, 0)
+    split_rows(place_ref, hidden_ref, hidden_own_ref, other_ref, 2 * rows)
     gw_ref[...] = lax.dot_general(
         grad_pre, mixed, (((1,), (1,)), ((), ())), preferred_element_type=jnp.float32
     ).astype(jnp.bfloat16)
@@ -303,27 +304,28 @@
         mine = pl.multiple_of(start + place_ref[0] * rows, rows)
         others = pl.multiple_of(start + (1 - place_ref[0]) * rows, rows)
         gw_own_ref[j] = gw_ref[pl.ds(mine, rows), :]
-        other_ref[j, rows:, :] = gw_ref[pl.ds(others, rows), :]
-
-
-def split_rows(place_ref, src_ref, own_ref, other_ref):
+        other_ref[j, rows : 2 * rows, :] = gw_ref[pl.ds(others, rows), :]
+
+
+def split_rows(place_ref, src_ref, own_ref, other_ref, first):
     rows = own_ref.shape[1]
     for dz in range(SIDE):
-        for other, out_ref in enumerate((own_ref, other_ref)):
-            start = chunk_ahead(place_ref, dz, other) * rows
-            out_ref[dz, :rows, :] = src_ref[pl.ds(pl.multiple_of(start, rows), rows), :]
+        mine = pl.multiple_of(chunk_ahead(place_ref, dz, False) * rows, rows)
+        others = pl.multiple_of(chunk_ahead(place_ref, dz, True) * rows, rows)
+        own_ref[dz] = src_ref[pl.ds(mine, rows), :]
+        other_ref[dz, first : first + rows, :] = src_ref[pl.ds(others, rows), :]
 
 
 def dense(place, mixed, cot, weight, weight_t):
     _, width, chunk = mixed[0].shape
     full = jax.ShapeDtypeStruct((weight.shape[1], chunk), jnp.bfloat16)
     half = jax.ShapeDtypeStruct((SIDE, width, chunk), jnp.bfloat16)
-    both = jax.ShapeDtypeStruct((SIDE, 2 * width, chunk), jnp.bfloat16)
+    rest = jax.ShapeDtypeStruct((SIDE, 3 * width, chunk), jnp.bfloat16)
     return pl.pallas_call(
         dense_kernel,
-        out_shape=(half, half, half, both, half),
+        out_shape=(half, half, rest, half),
         in_specs=scalars(1) + arrays(SIDE + 3),
-        out_specs=tuple(arrays(5)),
+        out_specs=tuple(arrays(4)),
         scratch_shapes=[pltpu.VMEM(full.shape, full.dtype)] * 5,
         compiler_params=params(),
         name="dense",
@@ -351,32 +353,12 @@
     )(place, value, after)
 
 
-def unpack_kernel(place_ref, *refs):
-    pieces, hidden_ref = refs[:SIDE], refs[SIDE]
-    chunk = pieces[0].shape[2]
-    for dz, piece_ref in enumerate(pieces):
-        for other in range(2):
-            start = chunk_behind(place_ref, dz, other) * chunk
-            hidden_ref[:, pl.ds(pl.multiple_of(start, chunk), chunk)] = piece_ref[other]
-
-
-def unpack(place, pieces):
-    _, width, chunk = pieces[0].shape
-    return pl.pallas_call(
-        unpack_kernel,
-        out_shape=jax.ShapeDtypeStruct((width, 2 * SIDE * chunk), jnp.bfloat16),
-        in_specs=scalars(1) + arrays(SIDE),
-        out_specs=arrays(1)[0],
-        compiler_params=params(),
-        name="unpack",
-    )(place, *pieces)
-
-
 def gw_add_kernel(own_ref, got_ref, after_ref, keep_ref, send_ref):
     rows = own_ref.shape[1]
+    first = rows if got_ref.shape[1] > rows else 0
     for j in range(keep_ref.shape[0]):
         for k, out_ref in enumerate((keep_ref, send_ref)):
-            got = got_ref[2 * j + k, got_ref.shape[1] - rows :, :].astype(jnp.float32)
+            got = got_ref[2 * j + k, first : first + rows, :].astype(jnp.float32)
             out_ref[j] = (own_ref[2 * j + k].astype(jnp.float32) + got).astype(jnp.bfloat16)
 
 
@@ -516,35 +498,38 @@
     )(*codes, *pieces, after, *extra)
 
 
-def slab_kernel(d, code_ref, piece_ref, before_ref, *refs):
-    gw_refs, out_ref, total_ref = refs[:-2], refs[-2], refs[-1]
-    nodes = total_ref.shape[1]
-    total_ref[...] = before_ref[d]
-    for q in range(d * SLOTS, (d + 1) * SLOTS):
-        add_blocks(code_ref, piece_ref, q, total_ref)
-    out_ref[:, :nodes] = total_ref[...].astype(jnp.bfloat16)
+def slabs_kernel(code_ref, piece_ref, before_ref, *refs):
+    gw_refs, outs, total_ref = refs[:SIDE], refs[SIDE : 2 * SIDE], refs[-1]
+    nodes = total_ref.shape[2]
     gw = gw_refs[0][...].astype(jnp.float32)
     for gw_ref in gw_refs[1:]:
         gw += gw_ref[...].astype(jnp.float32)
-    out_ref[:, nodes:] = gw.astype(jnp.bfloat16)
-
-
-def slab(d, code, piece, before, gw_parts):
-    width, nodes = before.shape[1:]
-    beside = gw_parts[0].shape[1]
-    return pl.pallas_call(
-        functools.partial(slab_kernel, d),
-        out_shape=jax.ShapeDtypeStruct((width, nodes + beside), jnp.bfloat16),
-        in_specs=scalars(1) + arrays(2 + len(gw_parts)),
-        out_specs=arrays(1)[0],
-        scratch_shapes=[pltpu.VMEM((width, nodes), jnp.float32)],
-        compiler_params=params(),
-        name="slab",
+    gw = gw.astype(jnp.bfloat16)
+    total_ref[...] = before_ref[...]
+    for q in range(PART):
+        d, s = q % SIDE, q // SIDE
+        add_blocks(code_ref, piece_ref, d * SLOTS + s, total_ref.at[d])
+    for d, out_ref in enumerate(outs):
+        out_ref[:, :nodes] = total_ref[d].astype(jnp.bfloat16)
+        out_ref[:, nodes:] = gw
+
+
+def finish_slabs(code, piece, before, gw_parts):
+    _, width, nodes = before.shape
+    out = jax.ShapeDtypeStruct((width, nodes + gw_parts[0].shape[1]), jnp.bfloat16)
+    return pl.pallas_call(
+        slabs_kernel,
+        out_shape=(out,) * SIDE,
+        in_specs=scalars(1) + arrays(2 + SIDE),
+        out_specs=tuple(arrays(SIDE)),
+        scratch_shapes=[pltpu.VMEM(before.shape, jnp.float32)],
+        compiler_params=params(),
+        name="finish_slabs",
     )(code, piece, before, *gw_parts)
 
 
-def final_kernel(grad_ref, *refs):
-    slabs, out_ref, gw_ref = refs[:SIDE], refs[SIDE], refs[SIDE + 1]
+def final_kernel(place_ref, grad_ref, *refs):
+    slabs, pieces, (out_ref, gw_ref, hidden_ref) = refs[:SIDE], refs[SIDE : 2 * SIDE], refs[2 * SIDE :]
     step, nodes, share = 512, out_ref.shape[1], gw_ref.shape[0]
     gw = jnp.zeros((out_ref.shape[0], share), jnp.float32)
     for d, slab_ref in enumerate(slabs):
@@ -565,22 +550,25 @@
         for slab_ref in slabs:
             total += slab_ref[:, part].astype(jnp.float32)
         out_ref[:, part] = total.astype(jnp.bfloat16)
-
-
-def final_sum(grad, slabs):
+    chunk = pieces[0].shape[2]
+    for dz, piece_ref in enumerate(pieces):
+        for other in range(2):
+            start = chunk_behind(place_ref, dz, other) * chunk
+            hidden_ref[:, pl.ds(pl.multiple_of(start, chunk), chunk)] = piece_ref[other]
+
+
+def finish(place, grad, slabs, hidden):
     width, nodes = grad.shape
     share = (slabs[0].shape[1] - nodes) // SIDE
+    out = jax.ShapeDtypeStruct(grad.shape, jnp.bfloat16)
     return pl.pallas_call(
         final_kernel,
-        out_shape=(
-            jax.ShapeDtypeStruct(grad.shape, jnp.bfloat16),
-            jax.ShapeDtypeStruct((share, width), jnp.float32),
-        ),
-        in_specs=arrays(1 + SIDE),
-        out_specs=tuple(arrays(2)),
-        compiler_params=params(),
-        name="final_sum",
-    )(grad, *slabs)
+        out_shape=(out, jax.ShapeDtypeStruct((share, width), jnp.float32), out),
+        in_specs=scalars(1) + arrays(1 + 2 * SIDE),
+        out_specs=tuple(arrays(3)),
+        compiler_params=params(),
+        name="finish",
+    )(place, grad, *slabs, *hidden)
 
 
 def shift(value, first, by):
@@ -597,19 +585,22 @@
     return lax.ppermute(value, ("row", "col"), pairs)
 
 
-def pair_kernel(own_ref, got_ref, after_ref, out_ref):
-    out_ref[0] = own_ref[...]
-    out_ref[1] = got_ref[...]
-
-
-def pair(own, got, after):
-    return pl.pallas_call(
-        pair_kernel,
-        out_shape=jax.ShapeDtypeStruct((2,) + own.shape, own.dtype),
+def pairs_kernel(own_ref, got_ref, after_ref, *outs):
+    rows = own_ref.shape[1]
+    for dz, out_ref in enumerate(outs):
+        out_ref[0] = own_ref[dz]
+        out_ref[1] = got_ref[dz, got_ref.shape[1] - rows :, :]
+
+
+def pairs(own, got, after):
+    pair = jax.ShapeDtypeStruct((2,) + own.shape[1:], own.dtype)
+    return pl.pallas_call(
+        pairs_kernel,
+        out_shape=(pair,) * SIDE,
         in_specs=arrays(2) + anywhere(1),
-        out_specs=arrays(1)[0],
-        compiler_params=params(),
-        name="pair",
+        out_specs=tuple(arrays(SIDE)),
+        compiler_params=params(),
+        name="pairs",
     )(own, got, after)
 
 
@@ -622,18 +613,19 @@
     return lax.ppermute(value, "col", [(c, c ^ 1) for c in range(chunks)])
 
 
-def spread_z(own, got, after=None):
-    chunks, rows = lax.axis_size("col"), own.shape[1]
-    pieces = []
-    for dz in (0, 1, 3, 2):
-        if dz < 2 or after is None:
-            piece = jnp.stack([own[dz], got[dz, :rows]])
-        else:
-            piece = pair(own[dz], got[dz], after)
-        if dz > 0:
-            piece = lax.ppermute(piece, "col", [(c, (c + 2 * dz) % chunks) for c in range(chunks)])
-        pieces.append(piece)
-    return [pieces[0], pieces[1], pieces[3], pieces[2]]
+def shift_z(value, dz):
+    chunks = lax.axis_size("col")
+    return lax.ppermute(value, "col", [(c, (c + 2 * dz) % chunks) for c in range(chunks)])
+
+
+def spread_z(own, got):
+    rows = own.shape[1]
+    return send_z([jnp.stack([own[dz], got[dz, :rows]]) for dz in range(SIDE)])
+
+
+def send_z(pieces):
+    sent = {dz: shift_z(pieces[dz], dz) for dz in (1, 2, 3)}
+    return [pieces[0]] + [sent[dz] for dz in range(1, SIDE)]
 
 
 def sorted_codes(tile_rows, tile_cols, tile_nnz, blocks):
@@ -662,24 +654,20 @@
     codes = [codes[e] for e in range(SIDE)]
     asked = [codes[0]] + [shift(codes[e], False, -e) for e in range(1, SIDE)]
     own = keep(feats_t, asked[1])
-    low, high = halves(back1, back3, [asked[2], asked[3]])
+    low, high = halves(back1, back3, [own] + asked[1:])
     slabs = [own, back1, shift(low, True, 1), shift(high, True, -1), back3]
 
     recv = [None] * SIDE
     sent = own
-    for e in (1, 3):
+    for e in (1, 3, 2):
         sent = gather_blocks(asked[e], slabs, [sent])
         recv[e] = shift(sent, False, e)
     recv[0] = gather_blocks(asked[0], slabs, [sent])
     total = first_spread(codes[0], recv[0], tile_vals)
-    cot_own, cot_other = split(place, cotangent.T, total)
-    cot_got = swap_core(cot_other)
-    sent = gather_blocks(asked[2], slabs, [total, recv[1]])
-    recv[2] = shift(sent, False, 2)
-    total, far_tiles = spread([codes[1], codes[3]], [recv[1], recv[3]], tile_vals, total, codes[2])
-    cot = join(place, spread_z(cot_own, cot_got, sent), total)
+    cot = join(place, regroup(*split(place, cotangent.T, total)), total)
+    total, far_tiles = spread([codes[1], codes[3]], [recv[1], recv[3]], tile_vals, total, codes[2], cot)
     own, other, scale = spread_mixed(place, codes[2], recv[2], far_tiles, total, feats_t, cot)
-    hidden_own, hidden_other, own, other, gw_own = dense(place, regroup(own, other), cot, weight, weight_t)
+    hidden_own, own, other, gw_own = dense(place, regroup(own, other), cot, weight, weight_t)
 
     got = swap_core(other)
     gw_own, gw_other = gw_add(gw_own, got, got)
@@ -690,17 +678,17 @@
     pieces = [None] * SIDE
     pieces[2] = shift(sent, False, -2)
     pieces[1] = shift(back_products(codes[1], scaled, tile_vals, scale), False, -1)
-    sent = back_products(codes[3], scaled, tile_vals, scale)
+    sent = back_products(codes[3], scaled, tile_vals, gw_own)
     pieces[3] = shift(sent, False, -3)
     pieces[0] = back_products(codes[0], scaled, tile_vals, sent)
     gw = gw_order(place, gw_own, gw_got, pieces[0])
     gw = [gw[0]] + [shift(gw[e], False, -e) for e in range(1, SIDE)]
     total = collect([asked[0], asked[2]], [pieces[0], pieces[2]], None, node_rows, pieces[0])
     total = collect([asked[1]], [pieces[1]], total, node_rows, gw[0])
-    slabs = [slab(d, asked[3], pieces[3], total, gw) for d in range(SIDE)]
-    hidden = unpack(place, regroup(hidden_own, keep(hidden_other, slabs[1])))
+    slabs = finish_slabs(asked[3], pieces[3], total, gw)
+    hidden = send_z(pairs(hidden_own, got, slabs[1]))
     slabs = [slabs[0]] + [shift(slabs[d], True, -d) for d in (1, 2, 3)]
-    grad_feats, gw = final_sum(grad, slabs)
+    grad_feats, gw, hidden = finish(place, grad, slabs, hidden)
     return (hidden.T, gw, grad_feats.T)
 
 

time: 145 us -> 142 us (0.979)
  Pallas kernels: 41.9 us -> 36.3 us
  starting transfers between devices: 54.7 us -> 57.5 us
    ppermute x12, waiting for transfers between devices: 17.9 us -> 25.5 us  [shift_z(): lax.ppermute(value, 'col', [(c, (c + 2 * dz) % chunks) for c in range(chu...]
    ppermute x2, waiting for transfers between devices: 4.53 us -> 0.24 us  [swap_z(): return lax.ppermute(value, 'col', [(c, c ^ 2 * bit) for c in range(chunks)])]
    ppermute x19, waiting for transfers between devices: 15.9 us -> 13 us  [shift(): return lax.ppermute(value, ('row', 'col'), pairs)]
    pallas_call x9 -> x4, Pallas kernels: 7.87 us -> 5.58 us  [the longest x1 2.21 us: dense(): pl.pallas_call(dense_kernel, out_shape=(half, half, rest, half), in_specs...]
    ppermute x19, starting transfers between devices: 30.2 us -> 32.2 us  [shift(): return lax.ppermute(value, ('row', 'col'), pairs)]
    pallas_call x1, Pallas kernels: 4.17 us -> 2.64 us  [spread_mixed(): pl.pallas_call(mixed_kernel, out_shape=(half, half, jax.ShapeDtypeStruct(...]
    ppermute x4 -> x3, waiting for transfers between devices: 4.86 us -> 5.23 us  [swap_core(): return lax.ppermute(value, 'col', [(c, c ^ 1) for c in range(chunks)])]
  transfers between devices with their start and end apart: 37 -> 36, of which waited for: 19 -> 18; matrix products, arithmetic and copies ran while one was open for 1% -> 1% of each run, Pallas kernels for 21% -> 19%
where the time goes in v5:
time: 142 us
  starting transfers between devices  57.5 us (40%)
  waiting for transfers between devices  43.9 us (31%)
  Pallas kernels  36.3 us (26%)
  local copies, waits for them, and re-layouts  1.47 us (1%)
    ppermute x19, starting transfers between devices, shift(): return lax.ppermute(value, ('row', 'col'), pairs)  32.2 us
    ppermute x12, waiting for transfers between devices, shift_z(): lax.ppermute(value, 'col', [(c, (c + 2 * dz) % chunks) for c in range(chu...  25.5 us
    ppermute x12, starting transfers between devices, shift_z(): lax.ppermute(value, 'col', [(c, (c + 2 * dz) % chunks) for c in range(chu...  20.7 us
    ppermute x19, waiting for transfers between devices, shift(): return lax.ppermute(value, ('row', 'col'), pairs)  13 us
    pallas_call x3, Pallas kernels, back_products(): pl.pallas_call(back_kernel, out_shape=jax.ShapeDtypeStruct((PART, scaled....  9.56 us
    pallas_call x1, Pallas kernels, spread(): pl.pallas_call(functools.partial(spread_kernel, parts, False), out_shape=...  5.7 us
    ppermute x3, waiting for transfers between devices, swap_core(): return lax.ppermute(value, 'col', [(c, c ^ 1) for c in range(chunks)])  5.23 us
    ppermute x2, starting transfers between devices, swap_z(): return lax.ppermute(value, 'col', [(c, c ^ 2 * bit) for c in range(chunks)])  4.43 us
  transfers between devices with their start and end apart: 36, of which 18 were waited for; matrix products, arithmetic and copies ran while one was open for 1% of the time, Pallas kernels for 19%

profile of v5, /device:TPU:0, one launch (start us, length us, event | category | flops | bytes accessed | tf_op | source)
XLA Modules:
  0.0 141.6 jit_solution(18300128983199277368)
XLA Ops:
  0.6 2.9 %collective-permute-start.3 = (bf16[64,4096]{1,0:T(8,128)(2,1)}, bf16[64,4096]{1,0:T(8,128)(2,1)S(1)}, u32[]{:S(2)}, u32[]{:S(2)}) collective-permute-start(bf16[64,4096]{1,0:T(8,128)(2,1)} %bitcast.9), channel_id=1, source_target_pairs={{0,96},{1,25},{2,98},{3,27},{4,100},{5,29},{6,102},{7,31},{8,104},... | collective-permute-start | bytes 1572872 | tf_op jit(solution)/shard_map/ppermute | solution.py:585
  3.5 0.7 broadcast_select_fusion
  4.6 1.6 %collective-permute-start.4 = (s32[32]{0:T(128)S(1)}, s32[32]{0:T(128)S(1)}, u32[]{:S(2)}, u32[]{:S(2)}) collective-permute-start(s32[32]{0:T(128)S(1)} %get-tuple-element.98.refs_1_.code_ref), channel_id=1, source_target_pairs={{0,8},{1,33},{2,10},{3,35},{4,12},{5,37},{6,14},{7,39},{8,16},{9,4... | collective-permute-start | bytes 392 | tf_op jit(solution)/shard_map/ppermute | solution.py:585
  6.2 1.7 %collective-permute-start.1 = (s32[32]{0:T(128)S(1)}, s32[32]{0:T(128)S(1)}, u32[]{:S(2)}, u32[]{:S(2)}) collective-permute-start(s32[32]{0:T(128)S(1)} %get-tuple-element.99.refs_0_.code_ref), channel_id=1, source_target_pairs={{0,24},{1,97},{2,26},{3,99},{4,28},{5,101},{6,30},{7,103},{8,0},{9... | collective-permute-start | bytes 392 | tf_op jit(solution)/shard_map/ppermute | solution.py:585
  7.9 2.0 %collective-permute-start = (s32[32]{0:T(128)S(1)}, s32[32]{0:T(128)S(1)}, u32[]{:S(2)}, u32[]{:S(2)}) collective-permute-start(s32[32]{0:T(128)S(1)} %get-tuple-element.100.refs_6_.code_ref), channel_id=1, source_target_pairs={{0,16},{1,65},{2,18},{3,67},{4,20},{5,69},{6,22},{7,71},{8,24},{9,... | collective-permute-start | bytes 392 | tf_op jit(solution)/shard_map/ppermute | solution.py:585
  9.9 1.0 copy-done.3
  11.0 2.0 %collective-permute-done.refs_2_.code_ref.refs_1_ = s32[32]{0:T(128)S(1)} collective-permute-done((s32[32]{0:T(128)S(1)}, s32[32]{0:T(128)S(1)}, u32[]{:S(2)}, u32[]{:S(2)}) %collective-permute-start) | collective-permute-done | bytes 160 | tf_op jit(solution)/shard_map/ppermute | solution.py:585
  12.9 1.2 collective-permute-done.2.back1_ref
  14.3 3.2 %collective-permute-start.6 = (bf16[32,4096]{1,0:T(8,128)(2,1)S(1)}, bf16[32,4096]{1,0:T(8,128)(2,1)S(1)}, u32[]{:S(2)}, u32[]{:S(2)}) collective-permute-start(bf16[32,4096]{1,0:T(8,128)(2,1)S(1)} %get-tuple-element.39), channel_id=1, source_target_pairs={{0,96},{1,25},{2,98},{3,27},{4,100},{5,29},{6,102},{7,31},{8,104},... | collective-permute-start | bytes 786440 | tf_op jit(solution)/shard_map/ppermute | solution.py:585
  17.5 4.3 %collective-permute-done.5.low_ref = bf16[32,4096]{1,0:T(8,128)(2,1)S(1)} collective-permute-done((bf16[32,4096]{1,0:T(8,128)(2,1)S(1)}, bf16[32,4096]{1,0:T(8,128)(2,1)S(1)}, u32[]{:S(2)}, u32[]{:S(2)}) %collective-permute-start.5) | collective-permute-done | bytes 262176 | tf_op jit(solution)/shard_map/ppermute | solution.py:585
  21.8 0.7 gather_blocks.4.refs_0_
  22.5 1.6 %collective-permute-start.8 = (bf16[32,64,256]{2,1,0:T(8,128)(2,1)S(1)}, bf16[32,64,256]{2,1,0:T(8,128)(2,1)S(1)}, u32[]{:S(2)}, u32[]{:S(2)}) collective-permute-start(bf16[32,64,256]{2,1,0:T(8,128)(2,1)S(1)} %gather_blocks.4.refs_0_), channel_id=1, source_target_pairs={{0,8},{1,33},{2,10},{3,35},{4,12},{5,37},{6,14},{7,39},{8,16},{9,4... | collective-permute-start | bytes 3145736 | tf_op jit(solution)/shard_map/ppermute | solution.py:585
  24.2 0.7 gather_blocks.5.refs_0_
  24.9 1.7 %collective-permute-start.9 = (bf16[32,64,256]{2,1,0:T(8,128)(2,1)S(1)}, bf16[32,64,256]{2,1,0:T(8,128)(2,1)S(1)}, u32[]{:S(2)}, u32[]{:S(2)}) collective-permute-start(bf16[32,64,256]{2,1,0:T(8,128)(2,1)S(1)} %gather_blocks.5.refs_0_), channel_id=1, source_target_pairs={{0,24},{1,97},{2,26},{3,99},{4,28},{5,101},{6,30},{7,103},{8,0},{9... | collective-permute-start | bytes 3145736 | tf_op jit(solution)/shard_map/ppermute | solution.py:585
  26.6 0.7 gather_blocks.6.refs_0_
  27.3 2.1 %collective-permute-start.7 = (bf16[32,64,256]{2,1,0:T(8,128)(2,1)S(1)}, bf16[32,64,256]{2,1,0:T(8,128)(2,1)S(1)}, u32[]{:S(2)}, u32[]{:S(2)}) collective-permute-start(bf16[32,64,256]{2,1,0:T(8,128)(2,1)S(1)} %gather_blocks.6.refs_0_), channel_id=1, source_target_pairs={{0,16},{1,65},{2,18},{3,67},{4,20},{5,69},{6,22},{7,71},{8,24},{9,... | collective-permute-start | bytes 3145736 | tf_op jit(solution)/shard_map/ppermute | solution.py:585
  29.4 0.7 gather_blocks.7.refs_1_
  30.1 3.7 %spread.2.after_ref.refs_4_.refs_5_ = f32[80,4096]{1,0:T(8,128)S(1)} custom-call(s32[32]{0:T(128)S(1)} %get-tuple-element.97.code_ref.refs_0_, bf16[32,64,256]{2,1,0:T(8,128)(2,1)S(1)} %gather_blocks.7.refs_1_, bf16[128,256,256]{2,1,0:T(8,128)(2,1)} %tiles_ref.5), custom_call_target="tpu_custom_call" | custom-call | tf_op jit(solution)/shard_map/spread/pallas_call | solution.py:199
  33.9 0.6 split.1
  34.6 1.5 %collective-permute-done.10 = bf16[4,64,512]{2,1,0:T(8,128)(2,1)S(1)} collective-permute-done((bf16[4,64,512]{2,1,0:T(8,128)(2,1)S(1)}, bf16[4,64,512]{2,1,0:T(8,128)(2,1)S(1)}, u32[]{:S(2)}, u32[]{:S(2)}) %collective-permute-start.10) | collective-permute-done | bytes 262176 | tf_op jit(solution)/shard_map/ppermute | solution.py:613
  36.1 2.0 %collective-permute-start.11 = (bf16[2,64,512]{2,1,0:T(8,128)(2,1)S(1)}, bf16[2,64,512]{2,1,0:T(8,128)(2,1)S(1)}, u32[]{:S(2)}, u32[]{:S(2)}) collective-permute-start(bf16[2,64,512]{2,1,0:T(8,128)(2,1)S(1)} %pad_maximum_fusion.1), channel_id=1, source_target_pairs={{0,2},{1,3},{2,4},{3,5},{4,6},{5,7},{6,0},{7,1},{8,10},{9,11},{10,... | collective-permute-start | bytes 393224 | tf_op jit(solution)/shard_map/ppermute | solution.py:618
  38.1 3.7 %collective-permute-start.12 = (bf16[2,64,512]{2,1,0:T(8,128)(2,1)S(1)}, bf16[2,64,512]{2,1,0:T(8,128)(2,1)S(1)}, u32[]{:S(2)}, u32[]{:S(2)}) collective-permute-start(bf16[2,64,512]{2,1,0:T(8,128)(2,1)S(1)} %pad_maximum_fusion.2), channel_id=1, source_target_pairs={{0,4},{1,5},{2,6},{3,7},{4,0},{5,1},{6,2},{7,3},{8,12},{9,13},{10,... | collective-permute-start | bytes 393224 | tf_op jit(solution)/shard_map/ppermute | solution.py:618
  41.8 2.2 %collective-permute-done.11.refs_1_ = bf16[2,64,512]{2,1,0:T(8,128)(2,1)S(1)} collective-permute-done((bf16[2,64,512]{2,1,0:T(8,128)(2,1)S(1)}, bf16[2,64,512]{2,1,0:T(8,128)(2,1)S(1)}, u32[]{:S(2)}, u32[]{:S(2)}) %collective-permute-start.11) | collective-permute-done | bytes 131104 | tf_op jit(solution)/shard_map/ppermute | solution.py:618
  44.1 2.5 %collective-permute-start.13 = (bf16[2,64,512]{2,1,0:T(8,128)(2,1)S(1)}, bf16[2,64,512]{2,1,0:T(8,128)(2,1)S(1)}, u32[]{:S(2)}, u32[]{:S(2)}) collective-permute-start(bf16[2,64,512]{2,1,0:T(8,128)(2,1)S(1)} %pad_maximum_fusion.3), channel_id=1, source_target_pairs={{0,6},{1,7},{2,0},{3,1},{4,2},{5,3},{6,4},{7,5},{8,14},{9,15},{10,... | collective-permute-start | bytes 393224 | tf_op jit(solution)/shard_map/ppermute | solution.py:618
  46.6 1.4 %collective-permute-done.12.refs_2_ = bf16[2,64,512]{2,1,0:T(8,128)(2,1)S(1)} collective-permute-done((bf16[2,64,512]{2,1,0:T(8,128)(2,1)S(1)}, bf16[2,64,512]{2,1,0:T(8,128)(2,1)S(1)}, u32[]{:S(2)}, u32[]{:S(2)}) %collective-permute-start.12) | collective-permute-done | bytes 131104 | tf_op jit(solution)/shard_map/ppermute | solution.py:618
  48.0 1.1 collective-permute-done.13.refs_3_
  49.1 0.6 join.1.refs_7_.after_ref.refs_4_
  49.7 5.7 %spread.3 = (f32[80,4096]{1,0:T(8,128)S(1)}, bf16[4,8,256,256]{3,2,1,0:T(8,128)(2,1)S(1)}) custom-call(s32[32]{0:T(128)S(1)} %get-tuple-element.99.refs_0_.code_ref, s32[32]{0:T(128)S(1)} %get-tuple-element.98.refs_1_.code_ref, bf16[32,64,256]{2,1,0:T(8,128)(2,1)S(1)} %collective-permute-done.8.refs_2_, ...), custom_call_target="tpu_custom_call" | custom-call | tf_op jit(solution)/shard_map/spread/pallas_call | solution.py:213
  55.5 2.6 %spread_mixed.1 = (bf16[4,64,512]{2,1,0:T(8,128)(2,1)S(1)}, bf16[4,64,512]{2,1,0:T(8,128)(2,1)S(1)}, f32[1,4096]{1,0:T(1,128)S(1)}) custom-call(s32[3]{0:T(128)S(1)} %pad_add_fusion.place_ref, s32[32]{0:T(128)S(1)} %get-tuple-element.100.refs_6_.code_ref, bf16[32,64,256]{2,1,0:T(8,128)(2,1)S(1)} %collective-permute-done.7.recv_ref, ...), custom_call_target="tpu_custom_call" | custom-call | tf_op jit(solution)/shard_map/spread_mixed/pallas_call | solution.py:241
  58.3 1.5 %collective-permute-done.14 = bf16[4,64,512]{2,1,0:T(8,128)(2,1)S(1)} collective-permute-done((bf16[4,64,512]{2,1,0:T(8,128)(2,1)S(1)}, bf16[4,64,512]{2,1,0:T(8,128)(2,1)S(1)}, u32[]{:S(2)}, u32[]{:S(2)}) %collective-permute-start.14) | collective-permute-done | bytes 262176 | tf_op jit(solution)/shard_map/ppermute | solution.py:613
  59.8 0.7 collective-permute-start.15
  60.5 4.6 %collective-permute-start.16 = (bf16[2,64,512]{2,1,0:T(8,128)(2,1)S(1)}, bf16[2,64,512]{2,1,0:T(8,128)(2,1)S(1)}, u32[]{:S(2)}, u32[]{:S(2)}) collective-permute-start(bf16[2,64,512]{2,1,0:T(8,128)(2,1)S(1)} %pad_maximum_fusion.6), channel_id=1, source_target_pairs={{0,4},{1,5},{2,6},{3,7},{4,0},{5,1},{6,2},{7,3},{8,12},{9,13},{10,... | collective-permute-start | bytes 393224 | tf_op jit(solution)/shard_map/ppermute | solution.py:618
  65.5 1.9 %collective-permute-done.15.refs_1_ = bf16[2,64,512]{2,1,0:T(8,128)(2,1)S(1)} collective-permute-done((bf16[2,64,512]{2,1,0:T(8,128)(2,1)S(1)}, bf16[2,64,512]{2,1,0:T(8,128)(2,1)S(1)}, u32[]{:S(2)}, u32[]{:S(2)}) %collective-permute-start.15) | collective-permute-done | bytes 131104 | tf_op jit(solution)/shard_map/ppermute | solution.py:618
  67.3 4.0 %collective-permute-done.16.refs_2_ = bf16[2,64,512]{2,1,0:T(8,128)(2,1)S(1)} collective-permute-done((bf16[2,64,512]{2,1,0:T(8,128)(2,1)S(1)}, bf16[2,64,512]{2,1,0:T(8,128)(2,1)S(1)}, u32[]{:S(2)}, u32[]{:S(2)}) %collective-permute-start.16) | collective-permute-done | bytes 131104 | tf_op jit(solution)/shard_map/ppermute | solution.py:618
  71.3 2.2 %dense.1 = (bf16[4,64,512]{2,1,0:T(8,128)(2,1)S(1)}, bf16[4,64,512]{2,1,0:T(8,128)(2,1)S(1)}, bf16[4,192,512]{2,1,0:T(8,128)(2,1)S(1)}, bf16[4,64,512]{2,1,0:T(8,128)(2,1)S(1)}) custom-call(s32[3]{0:T(128)S(1)} %pad_add_fusion.place_ref, bf16[2,64,512]{2,1,0:T(8,128)(2,1)S(1)} %pad_maximum_fusion.4.refs_0_, ...), custom_call_target="tpu_custom_call" | custom-call | tf_op jit(solution)/shard_map/dense/pallas_call | solution.py:324
  73.7 2.2 %collective-permute-done.18.got_ref.after_ref = bf16[4,192,512]{2,1,0:T(8,128)(2,1)S(1)} collective-permute-done((bf16[4,192,512]{2,1,0:T(8,128)(2,1)S(1)}, bf16[4,192,512]{2,1,0:T(8,128)(2,1)S(1)}, u32[]{:S(2)}, u32[]{:S(2)}) %collective-permute-start.18) | collective-permute-done | bytes 786464 | tf_op jit(solution)/shard_map/ppermute | solution.py:613
  76.1 3.8 %collective-permute-start.20 = (bf16[2,64,512]{2,1,0:T(8,128)(2,1)S(1)}, bf16[2,64,512]{2,1,0:T(8,128)(2,1)S(1)}, u32[]{:S(2)}, u32[]{:S(2)}) collective-permute-start(bf16[2,64,512]{2,1,0:T(8,128)(2,1)S(1)} %pad_maximum_fusion.10), channel_id=1, source_target_pairs={{0,4},{1,5},{2,6},{3,7},{4,0},{5,1},{6,2},{7,3},{8,12},{9,13},{10,... | collective-permute-start | bytes 393224 | tf_op jit(solution)/shard_map/ppermute | solution.py:618
  80.1 2.1 %collective-permute-start.22 = (bf16[2,64,512]{2,1,0:T(8,128)(2,1)S(1)}, bf16[2,64,512]{2,1,0:T(8,128)(2,1)S(1)}, u32[]{:S(2)}, u32[]{:S(2)}) collective-permute-start(bf16[2,64,512]{2,1,0:T(8,128)(2,1)S(1)} %get-tuple-element.53), channel_id=1, source_target_pairs={{0,2},{1,3},{2,0},{3,1},{4,6},{5,7},{6,4},{7,5},{8,10},{9,11},{10,... | collective-permute-start | bytes 393224 | tf_op jit(solution)/shard_map/ppermute | solution.py:379
  82.2 1.0 collective-permute-done.19.refs_1_
  83.2 3.6 %collective-permute-done.20.refs_2_ = bf16[2,64,512]{2,1,0:T(8,128)(2,1)S(1)} collective-permute-done((bf16[2,64,512]{2,1,0:T(8,128)(2,1)S(1)}, bf16[2,64,512]{2,1,0:T(8,128)(2,1)S(1)}, u32[]{:S(2)}, u32[]{:S(2)}) %collective-permute-start.20) | collective-permute-done | bytes 131104 | tf_op jit(solution)/shard_map/ppermute | solution.py:618
  86.8 0.8 collective-permute-done.21.refs_3_
  87.6 1.9 %back_products.4 = (bf16[32,64,256]{2,1,0:T(8,128)(2,1)S(1)}, bf16[64,4096]{1,0:T(8,128)(2,1)S(1)}, bf16[64,4096]{1,0:T(8,128)(2,1)S(1)}) custom-call(s32[3]{0:T(128)S(1)} %pad_add_fusion.place_ref, s32[32]{0:T(128)S(1)} %get-tuple-element.100.refs_6_.code_ref, bf16[2,64,512]{2,1,0:T(8,128)(2,1)S(1)} %pad_maximum_fusion.8.refs_0_, ...), custom_call_target="tpu_custom_call" | custom-call | tf_op jit(solution)/shard_map/back_products/pallas_call | solution.py:450
  89.4 2.5 %collective-permute-start.26 = (bf16[32,64,256]{2,1,0:T(8,128)(2,1)S(1)}, bf16[32,64,256]{2,1,0:T(8,128)(2,1)S(1)}, u32[]{:S(2)}, u32[]{:S(2)}) collective-permute-start(bf16[32,64,256]{2,1,0:T(8,128)(2,1)S(1)} %get-tuple-element.54.after_ref), channel_id=1, source_target_pairs={{0,16},{1,65},{2,18},{3,67},{4,20},{5,69},{6,22},{7,71},{8,24},{9,... | collective-permute-start | bytes 3145736 | tf_op jit(solution)/shard_map/ppermute | solution.py:585
  92.0 3.2 %back_products.6 = bf16[32,64,256]{2,1,0:T(8,128)(2,1)S(1)} custom-call(s32[32]{0:T(128)S(1)} %get-tuple-element.99.refs_0_.code_ref, bf16[64,4096]{1,0:T(8,128)(2,1)S(1)} %get-tuple-element.50.scaled_ref, bf16[128,256,256]{2,1,0:T(8,128)(2,1)} %tiles_ref.5, f32[1,4096]{1,0:T(1,128)S(1)} %get-tuple-element.48.refs_4_.after_ref), custom_call_target="tpu_custom_call" | custom-call | tf_op jit(solution)/shard_map/back_products/pallas_call | solution.py:461
  95.2 2.1 %collective-permute-start.24 = (bf16[32,64,256]{2,1,0:T(8,128)(2,1)S(1)}, bf16[32,64,256]{2,1,0:T(8,128)(2,1)S(1)}, u32[]{:S(2)}, u32[]{:S(2)}) collective-permute-start(bf16[32,64,256]{2,1,0:T(8,128)(2,1)S(1)} %back_products.6), channel_id=1, source_target_pairs={{0,24},{1,97},{2,26},{3,99},{4,28},{5,101},{6,30},{7,103},{8,0},{9... | collective-permute-start | bytes 3145736 | tf_op jit(solution)/shard_map/ppermute | solution.py:585
  97.3 3.2 %back_products.5.after_ref = bf16[32,64,256]{2,1,0:T(8,128)(2,1)S(1)} custom-call(s32[32]{0:T(128)S(1)} %get-tuple-element.98.refs_1_.code_ref, bf16[64,4096]{1,0:T(8,128)(2,1)S(1)} %get-tuple-element.50.scaled_ref, bf16[128,256,256]{2,1,0:T(8,128)(2,1)} %tiles_ref.5, bf16[1,64,512]{2,1,0:T(8,128)(2,1)S(1)} %get-tuple-element.55.after_ref.own_ref), custom_call_target="tpu_custom_call" | custom-call | tf_op jit(solution)/shard_map/back_products/pallas_call | solution.py:461
  100.5 0.9 collective-permute-start.23
  101.4 2.3 %collective-permute-start.25 = (bf16[1,64,512]{2,1,0:T(8,128)(2,1)S(1)}, bf16[1,64,512]{2,1,0:T(8,128)(2,1)S(1)}, u32[]{:S(2)}, u32[]{:S(2)}) collective-permute-start(bf16[1,64,512]{2,1,0:T(8,128)(2,1)S(1)} %get-tuple-element.56), channel_id=1, source_target_pairs={{0,4},{1,5},{2,6},{3,7},{4,0},{5,1},{6,2},{7,3},{8,12},{9,13},{10,... | collective-permute-start | bytes 196616 | tf_op jit(solution)/shard_map/ppermute | solution.py:379
  103.8 3.2 %back_products.7.after_ref.refs_2_.refs_4_ = bf16[32,64,256]{2,1,0:T(8,128)(2,1)S(1)} custom-call(s32[32]{0:T(128)S(1)} %get-tuple-element.97.code_ref.refs_0_, bf16[64,4096]{1,0:T(8,128)(2,1)S(1)} %get-tuple-element.50.scaled_ref, bf16[128,256,256]{2,1,0:T(8,128)(2,1)} %tiles_ref.5, bf16[32,64,256]{2,1,0:T(8,128)(2,1)S(1)} %back_products.5.after_ref), custom_call_target="tpu_custom_call" | custom-call | tf_op jit(solution)/shard_map/back_products/pallas_call | solution.py:461
  107.2 0.8 gw_order.1
  108.0 2.4 %collective-permute-start.27 = (bf16[64,128]{1,0:T(8,128)(2,1)S(1)}, bf16[64,128]{1,0:T(8,128)(2,1)S(1)}, u32[]{:S(2)}, u32[]{:S(2)}) collective-permute-start(bf16[64,128]{1,0:T(8,128)(2,1)S(1)} %get-tuple-element.58), channel_id=1, source_target_pairs={{0,24},{1,97},{2,26},{3,99},{4,28},{5,101},{6,30},{7,103},{8,0},{9... | collective-permute-start | bytes 49160 | tf_op jit(solution)/shard_map/ppermute | solution.py:585
  110.4 1.7 %collective-permute-start.28 = (bf16[64,128]{1,0:T(8,128)(2,1)S(1)}, bf16[64,128]{1,0:T(8,128)(2,1)S(1)}, u32[]{:S(2)}, u32[]{:S(2)}) collective-permute-start(bf16[64,128]{1,0:T(8,128)(2,1)S(1)} %get-tuple-element.59), channel_id=1, source_target_pairs={{0,16},{1,65},{2,18},{3,67},{4,20},{5,69},{6,22},{7,71},{8,24},{9,... | collective-permute-start | bytes 49160 | tf_op jit(solution)/shard_map/ppermute | solution.py:585
  112.1 1.3 collect.2.refs_3_
  113.5 5.4 %collective-permute-done.24.refs_1_ = bf16[32,64,256]{2,1,0:T(8,128)(2,1)S(1)} collective-permute-done((bf16[32,64,256]{2,1,0:T(8,128)(2,1)S(1)}, bf16[32,64,256]{2,1,0:T(8,128)(2,1)S(1)}, u32[]{:S(2)}, u32[]{:S(2)}) %collective-permute-start.24) | collective-permute-done | bytes 1048608 | tf_op jit(solution)/shard_map/ppermute | solution.py:585
  118.9 1.1 collect.3.before_ref
  120.0 1.3 finish_slabs.1
  121.3 2.4 %collective-permute-start.31 = (bf16[64,4224]{1,0:T(8,128)(2,1)S(1)}, bf16[64,4224]{1,0:T(8,128)(2,1)S(1)}, u32[]{:S(2)}, u32[]{:S(2)}) collective-permute-start(bf16[64,4224]{1,0:T(8,128)(2,1)S(1)} %get-tuple-element.63), channel_id=1, source_target_pairs={{0,64},{1,17},{2,66},{3,19},{4,68},{5,21},{6,70},{7,23},{8,72},{9,... | collective-permute-start | bytes 1622024 | tf_op jit(solution)/shard_map/ppermute | solution.py:585
  123.7 1.8 %collective-permute-start.32 = (bf16[64,4224]{1,0:T(8,128)(2,1)S(1)}, bf16[64,4224]{1,0:T(8,128)(2,1)S(1)}, u32[]{:S(2)}, u32[]{:S(2)}) collective-permute-start(bf16[64,4224]{1,0:T(8,128)(2,1)S(1)} %get-tuple-element.64), channel_id=1, source_target_pairs={{0,32},{1,9},{2,34},{3,11},{4,36},{5,13},{6,38},{7,15},{8,40},{9,1... | collective-permute-start | bytes 1622024 | tf_op jit(solution)/shard_map/ppermute | solution.py:585
  125.5 1.4 collective-permute-start.30
  127.0 0.7 collective-permute-start.33
  127.6 2.4 %collective-permute-start.34 = (bf16[2,64,512]{2,1,0:T(8,128)(2,1)S(1)}, bf16[2,64,512]{2,1,0:T(8,128)(2,1)S(1)}, u32[]{:S(2)}, u32[]{:S(2)}) collective-permute-start(bf16[2,64,512]{2,1,0:T(8,128)(2,1)S(1)} %get-tuple-element.68), channel_id=1, source_target_pairs={{0,4},{1,5},{2,6},{3,7},{4,0},{5,1},{6,2},{7,3},{8,12},{9,13},{10,... | collective-permute-start | bytes 393224 | tf_op jit(solution)/shard_map/ppermute | solution.py:618
  130.0 4.6 %collective-permute-done.33.refs_5_ = bf16[2,64,512]{2,1,0:T(8,128)(2,1)S(1)} collective-permute-done((bf16[2,64,512]{2,1,0:T(8,128)(2,1)S(1)}, bf16[2,64,512]{2,1,0:T(8,128)(2,1)S(1)}, u32[]{:S(2)}, u32[]{:S(2)}) %collective-permute-start.33) | collective-permute-done | bytes 131104 | tf_op jit(solution)/shard_map/ppermute | solution.py:618
  134.6 5.0 %collective-permute-done.35.refs_7_ = bf16[2,64,512]{2,1,0:T(8,128)(2,1)S(1)} collective-permute-done((bf16[2,64,512]{2,1,0:T(8,128)(2,1)S(1)}, bf16[2,64,512]{2,1,0:T(8,128)(2,1)S(1)}, u32[]{:S(2)}, u32[]{:S(2)}) %collective-permute-start.35) | collective-permute-done | bytes 131104 | tf_op jit(solution)/shard_map/ppermute | solution.py:618
  139.6 2.0 %finish.1 = (bf16[64,4096]{1,0:T(8,128)(2,1)}, f32[32,64]{1,0:T(8,128)}, bf16[64,4096]{1,0:T(8,128)(2,1)}) custom-call(s32[3]{0:T(128)S(1)} %pad_add_fusion.place_ref, bf16[64,4096]{1,0:T(8,128)(2,1)S(1)} %get-tuple-element.49.grad_ref, bf16[64,4224]{1,0:T(8,128)(2,1)S(1)} %get-tuple-element.61.refs_0_, ...), custom_call_target="tpu_custom_call" | custom-call | tf_op jit(solution)/shard_map/finish/pallas_call | solution.py:564
  (69 shorter events, 2.1 us)
Async XLA Ops:
  0.6 12.3 %collective-permute-start.3 = (bf16[64,4096]{1,0:T(8,128)(2,1)}, bf16[64,4096]{1,0:T(8,128)(2,1)S(1)}, u32[]{:S(2)}, u32[]{:S(2)}) collective-permute-start(bf16[64,4096]{1,0:T(8,128)(2,1)} %bitcast.9), channel_id=1, source_target_pairs={{0,96},{1,25},{2,98},{3,27},{4,100},{5,29},{6,102},{7,31},{8,104},... | collective-permute-start | bytes 1572872 | tf_op jit(solution)/shard_map/ppermute | solution.py:585
  3.5 10.6 %collective-permute-start.2 = (bf16[64,4096]{1,0:T(8,128)(2,1)}, bf16[64,4096]{1,0:T(8,128)(2,1)S(1)}, u32[]{:S(2)}, u32[]{:S(2)}) collective-permute-start(bf16[64,4096]{1,0:T(8,128)(2,1)} %bitcast.10), channel_id=1, source_target_pairs={{0,32},{1,9},{2,34},{3,11},{4,36},{5,13},{6,38},{7,15},{8,40},{9,1... | collective-permute-start | bytes 1572872 | tf_op jit(solution)/shard_map/ppermute | solution.py:585
  4.6 6.3 %collective-permute-start.4 = (s32[32]{0:T(128)S(1)}, s32[32]{0:T(128)S(1)}, u32[]{:S(2)}, u32[]{:S(2)}) collective-permute-start(s32[32]{0:T(128)S(1)} %get-tuple-element.98.refs_1_.code_ref), channel_id=1, source_target_pairs={{0,8},{1,33},{2,10},{3,35},{4,12},{5,37},{6,14},{7,39},{8,16},{9,4... | collective-permute-start | bytes 392 | tf_op jit(solution)/shard_map/ppermute | solution.py:585
  6.2 3.6 %collective-permute-start.1 = (s32[32]{0:T(128)S(1)}, s32[32]{0:T(128)S(1)}, u32[]{:S(2)}, u32[]{:S(2)}) collective-permute-start(s32[32]{0:T(128)S(1)} %get-tuple-element.99.refs_0_.code_ref), channel_id=1, source_target_pairs={{0,24},{1,97},{2,26},{3,99},{4,28},{5,101},{6,30},{7,103},{8,0},{9... | collective-permute-start | bytes 392 | tf_op jit(solution)/shard_map/ppermute | solution.py:585
  7.9 5.0 %collective-permute-start = (s32[32]{0:T(128)S(1)}, s32[32]{0:T(128)S(1)}, u32[]{:S(2)}, u32[]{:S(2)}) collective-permute-start(s32[32]{0:T(128)S(1)} %get-tuple-element.100.refs_6_.code_ref), channel_id=1, source_target_pairs={{0,16},{1,65},{2,18},{3,67},{4,20},{5,69},{6,22},{7,71},{8,24},{9,... | collective-permute-start | bytes 392 | tf_op jit(solution)/shard_map/ppermute | solution.py:585
  9.9 1.0 copy-start.3
  14.2 7.7 %collective-permute-start.5 = (bf16[32,4096]{1,0:T(8,128)(2,1)S(1)}, bf16[32,4096]{1,0:T(8,128)(2,1)S(1)}, u32[]{:S(2)}, u32[]{:S(2)}) collective-permute-start(bf16[32,4096]{1,0:T(8,128)(2,1)S(1)} %get-tuple-element.38), channel_id=1, source_target_pairs={{0,32},{1,9},{2,34},{3,11},{4,36},{5,13},{6,38},{7,15},{8,40},{9,1... | collective-permute-start | bytes 786440 | tf_op jit(solution)/shard_map/ppermute | solution.py:585
  14.3 7.6 %collective-permute-start.6 = (bf16[32,4096]{1,0:T(8,128)(2,1)S(1)}, bf16[32,4096]{1,0:T(8,128)(2,1)S(1)}, u32[]{:S(2)}, u32[]{:S(2)}) collective-permute-start(bf16[32,4096]{1,0:T(8,128)(2,1)S(1)} %get-tuple-element.39), channel_id=1, source_target_pairs={{0,96},{1,25},{2,98},{3,27},{4,100},{5,29},{6,102},{7,31},{8,104},... | collective-permute-start | bytes 786440 | tf_op jit(solution)/shard_map/ppermute | solution.py:585
  22.5 27.2 %collective-permute-start.8 = (bf16[32,64,256]{2,1,0:T(8,128)(2,1)S(1)}, bf16[32,64,256]{2,1,0:T(8,128)(2,1)S(1)}, u32[]{:S(2)}, u32[]{:S(2)}) collective-permute-start(bf16[32,64,256]{2,1,0:T(8,128)(2,1)S(1)} %gather_blocks.4.refs_0_), channel_id=1, source_target_pairs={{0,8},{1,33},{2,10},{3,35},{4,12},{5,37},{6,14},{7,39},{8,16},{9,4... | collective-permute-start | bytes 3145736 | tf_op jit(solution)/shard_map/ppermute | solution.py:585
  24.9 24.9 %collective-permute-start.9 = (bf16[32,64,256]{2,1,0:T(8,128)(2,1)S(1)}, bf16[32,64,256]{2,1,0:T(8,128)(2,1)S(1)}, u32[]{:S(2)}, u32[]{:S(2)}) collective-permute-start(bf16[32,64,256]{2,1,0:T(8,128)(2,1)S(1)} %gather_blocks.5.refs_0_), channel_id=1, source_target_pairs={{0,24},{1,97},{2,26},{3,99},{4,28},{5,101},{6,30},{7,103},{8,0},{9... | collective-permute-start | bytes 3145736 | tf_op jit(solution)/shard_map/ppermute | solution.py:585
  27.3 28.2 %collective-permute-start.7 = (bf16[32,64,256]{2,1,0:T(8,128)(2,1)S(1)}, bf16[32,64,256]{2,1,0:T(8,128)(2,1)S(1)}, u32[]{:S(2)}, u32[]{:S(2)}) collective-permute-start(bf16[32,64,256]{2,1,0:T(8,128)(2,1)S(1)} %gather_blocks.6.refs_0_), channel_id=1, source_target_pairs={{0,16},{1,65},{2,18},{3,67},{4,20},{5,69},{6,22},{7,71},{8,24},{9,... | collective-permute-start | bytes 3145736 | tf_op jit(solution)/shard_map/ppermute | solution.py:585
  30.1 3.8 %copy-start.5 = (bf16[4096,64]{0,1:T(8,128)(2,1)S(1)}, bf16[4096,64]{0,1:T(8,128)(2,1)}, u32[]{:S(2)}) copy-start(bf16[4096,64]{0,1:T(8,128)(2,1)} %param.13) | copy-start | bytes 1572868
  34.5 1.6 %collective-permute-start.10 = (bf16[4,64,512]{2,1,0:T(8,128)(2,1)S(1)}, bf16[4,64,512]{2,1,0:T(8,128)(2,1)S(1)}, u32[]{:S(2)}, u32[]{:S(2)}) collective-permute-start(bf16[4,64,512]{2,1,0:T(8,128)(2,1)S(1)} %get-tuple-element.41), channel_id=1, source_target_pairs={{0,1},{1,0},{2,3},{3,2},{4,5},{5,4},{6,7},{7,6},{8,9},{9,8},{10,11... | collective-permute-start | bytes 786440 | tf_op jit(solution)/shard_map/ppermute | solution.py:613
  36.1 7.9 %collective-permute-start.11 = (bf16[2,64,512]{2,1,0:T(8,128)(2,1)S(1)}, bf16[2,64,512]{2,1,0:T(8,128)(2,1)S(1)}, u32[]{:S(2)}, u32[]{:S(2)}) collective-permute-start(bf16[2,64,512]{2,1,0:T(8,128)(2,1)S(1)} %pad_maximum_fusion.1), channel_id=1, source_target_pairs={{0,2},{1,3},{2,4},{3,5},{4,6},{5,7},{6,0},{7,1},{8,10},{9,11},{10,... | collective-permute-start | bytes 393224 | tf_op jit(solution)/shard_map/ppermute | solution.py:618
  38.1 9.9 %collective-permute-start.12 = (bf16[2,64,512]{2,1,0:T(8,128)(2,1)S(1)}, bf16[2,64,512]{2,1,0:T(8,128)(2,1)S(1)}, u32[]{:S(2)}, u32[]{:S(2)}) collective-permute-start(bf16[2,64,512]{2,1,0:T(8,128)(2,1)S(1)} %pad_maximum_fusion.2), channel_id=1, source_target_pairs={{0,4},{1,5},{2,6},{3,7},{4,0},{5,1},{6,2},{7,3},{8,12},{9,13},{10,... | collective-permute-start | bytes 393224 | tf_op jit(solution)/shard_map/ppermute | solution.py:618
  44.1 5.1 %collective-permute-start.13 = (bf16[2,64,512]{2,1,0:T(8,128)(2,1)S(1)}, bf16[2,64,512]{2,1,0:T(8,128)(2,1)S(1)}, u32[]{:S(2)}, u32[]{:S(2)}) collective-permute-start(bf16[2,64,512]{2,1,0:T(8,128)(2,1)S(1)} %pad_maximum_fusion.3), channel_id=1, source_target_pairs={{0,6},{1,7},{2,0},{3,1},{4,2},{5,3},{6,4},{7,5},{8,14},{9,15},{10,... | collective-permute-start | bytes 393224 | tf_op jit(solution)/shard_map/ppermute | solution.py:618
  49.7 5.8 %copy-start.4 = (bf16[4096,64]{0,1:T(8,128)(2,1)S(1)}, bf16[4096,64]{0,1:T(8,128)(2,1)}, u32[]{:S(2)}) copy-start(bf16[4096,64]{0,1:T(8,128)(2,1)} %param.7) | copy-start | bytes 1572868
  55.5 4.3 %copy-start = (bf16[4,8,256,256]{3,2,1,0:T(8,128)(2,1)}, bf16[4,8,256,256]{3,2,1,0:T(8,128)(2,1)S(1)}, u32[]{:S(2)}) copy-start(bf16[4,8,256,256]{3,2,1,0:T(8,128)(2,1)S(1)} %get-tuple-element.42.tiles_ref.refs_5_) | copy-start | bytes 12582916
  55.5 9.7 %copy-start.2 = (bf16[512,512]{1,0:T(8,128)(2,1)S(1)}, bf16[512,512]{1,0:T(8,128)(2,1)}, u32[]{:S(2)}) copy-start(bf16[512,512]{1,0:T(8,128)(2,1)} %refs_5_.1) | copy-start | bytes 1572868
  58.1 1.6 %collective-permute-start.14 = (bf16[4,64,512]{2,1,0:T(8,128)(2,1)S(1)}, bf16[4,64,512]{2,1,0:T(8,128)(2,1)S(1)}, u32[]{:S(2)}, u32[]{:S(2)}) collective-permute-start(bf16[4,64,512]{2,1,0:T(8,128)(2,1)S(1)} %get-tuple-element.45), channel_id=1, source_target_pairs={{0,1},{1,0},{2,3},{3,2},{4,5},{5,4},{6,7},{7,6},{8,9},{9,8},{10,11... | collective-permute-start | bytes 786440 | tf_op jit(solution)/shard_map/ppermute | solution.py:613
  59.8 7.5 %collective-permute-start.15 = (bf16[2,64,512]{2,1,0:T(8,128)(2,1)S(1)}, bf16[2,64,512]{2,1,0:T(8,128)(2,1)S(1)}, u32[]{:S(2)}, u32[]{:S(2)}) collective-permute-start(bf16[2,64,512]{2,1,0:T(8,128)(2,1)S(1)} %pad_maximum_fusion.5), channel_id=1, source_target_pairs={{0,2},{1,3},{2,4},{3,5},{4,6},{5,7},{6,0},{7,1},{8,10},{9,11},{10,... | collective-permute-start | bytes 393224 | tf_op jit(solution)/shard_map/ppermute | solution.py:618
  60.5 10.8 %collective-permute-start.16 = (bf16[2,64,512]{2,1,0:T(8,128)(2,1)S(1)}, bf16[2,64,512]{2,1,0:T(8,128)(2,1)S(1)}, u32[]{:S(2)}, u32[]{:S(2)}) collective-permute-start(bf16[2,64,512]{2,1,0:T(8,128)(2,1)S(1)} %pad_maximum_fusion.6), channel_id=1, source_target_pairs={{0,4},{1,5},{2,6},{3,7},{4,0},{5,1},{6,2},{7,3},{8,12},{9,13},{10,... | collective-permute-start | bytes 393224 | tf_op jit(solution)/shard_map/ppermute | solution.py:618
  65.1 6.2 %collective-permute-start.17 = (bf16[2,64,512]{2,1,0:T(8,128)(2,1)S(1)}, bf16[2,64,512]{2,1,0:T(8,128)(2,1)S(1)}, u32[]{:S(2)}, u32[]{:S(2)}) collective-permute-start(bf16[2,64,512]{2,1,0:T(8,128)(2,1)S(1)} %pad_maximum_fusion.7), channel_id=1, source_target_pairs={{0,6},{1,7},{2,0},{3,1},{4,2},{5,3},{6,4},{7,5},{8,14},{9,15},{10,... | collective-permute-start | bytes 393224 | tf_op jit(solution)/shard_map/ppermute | solution.py:618
  65.4 22.1 %copy-start.1 = (bf16[4,8,256,256]{3,2,1,0:T(8,128)(2,1)S(1)}, bf16[4,8,256,256]{3,2,1,0:T(8,128)(2,1)}, u32[]{:S(2)}) copy-start(bf16[4,8,256,256]{3,2,1,0:T(8,128)(2,1)} %copy-done) | copy-start | bytes 12582916
  73.6 2.4 %collective-permute-start.18 = (bf16[4,192,512]{2,1,0:T(8,128)(2,1)S(1)}, bf16[4,192,512]{2,1,0:T(8,128)(2,1)S(1)}, u32[]{:S(2)}, u32[]{:S(2)}) collective-permute-start(bf16[4,192,512]{2,1,0:T(8,128)(2,1)S(1)} %get-tuple-element.47), channel_id=1, source_target_pairs={{0,1},{1,0},{2,3},{3,2},{4,5},{5,4},{6,7},{7,6},{8,9},{9,8},{10,11... | collective-permute-start | bytes 2359304 | tf_op jit(solution)/shard_map/ppermute | solution.py:613
  76.0 7.2 %collective-permute-start.19 = (bf16[2,64,512]{2,1,0:T(8,128)(2,1)S(1)}, bf16[2,64,512]{2,1,0:T(8,128)(2,1)S(1)}, u32[]{:S(2)}, u32[]{:S(2)}) collective-permute-start(bf16[2,64,512]{2,1,0:T(8,128)(2,1)S(1)} %pad_maximum_fusion.9), channel_id=1, source_target_pairs={{0,2},{1,3},{2,4},{3,5},{4,6},{5,7},{6,0},{7,1},{8,10},{9,11},{10,... | collective-permute-start | bytes 393224 | tf_op jit(solution)/shard_map/ppermute | solution.py:618
  76.1 10.7 %collective-permute-start.20 = (bf16[2,64,512]{2,1,0:T(8,128)(2,1)S(1)}, bf16[2,64,512]{2,1,0:T(8,128)(2,1)S(1)}, u32[]{:S(2)}, u32[]{:S(2)}) collective-permute-start(bf16[2,64,512]{2,1,0:T(8,128)(2,1)S(1)} %pad_maximum_fusion.10), channel_id=1, source_target_pairs={{0,4},{1,5},{2,6},{3,7},{4,0},{5,1},{6,2},{7,3},{8,12},{9,13},{10,... | collective-permute-start | bytes 393224 | tf_op jit(solution)/shard_map/ppermute | solution.py:618
  80.0 7.6 %collective-permute-start.21 = (bf16[2,64,512]{2,1,0:T(8,128)(2,1)S(1)}, bf16[2,64,512]{2,1,0:T(8,128)(2,1)S(1)}, u32[]{:S(2)}, u32[]{:S(2)}) collective-permute-start(bf16[2,64,512]{2,1,0:T(8,128)(2,1)S(1)} %pad_maximum_fusion.11), channel_id=1, source_target_pairs={{0,6},{1,7},{2,0},{3,1},{4,2},{5,3},{6,4},{7,5},{8,14},{9,15},{10,... | collective-permute-start | bytes 393224 | tf_op jit(solution)/shard_map/ppermute | solution.py:618
  80.1 17.2 %collective-permute-start.22 = (bf16[2,64,512]{2,1,0:T(8,128)(2,1)S(1)}, bf16[2,64,512]{2,1,0:T(8,128)(2,1)S(1)}, u32[]{:S(2)}, u32[]{:S(2)}) collective-permute-start(bf16[2,64,512]{2,1,0:T(8,128)(2,1)S(1)} %get-tuple-element.53), channel_id=1, source_target_pairs={{0,2},{1,3},{2,0},{3,1},{4,6},{5,7},{6,4},{7,5},{8,10},{9,11},{10,... | collective-permute-start | bytes 393224 | tf_op jit(solution)/shard_map/ppermute | solution.py:379
  89.4 22.7 %collective-permute-start.26 = (bf16[32,64,256]{2,1,0:T(8,128)(2,1)S(1)}, bf16[32,64,256]{2,1,0:T(8,128)(2,1)S(1)}, u32[]{:S(2)}, u32[]{:S(2)}) collective-permute-start(bf16[32,64,256]{2,1,0:T(8,128)(2,1)S(1)} %get-tuple-element.54.after_ref), channel_id=1, source_target_pairs={{0,16},{1,65},{2,18},{3,67},{4,20},{5,69},{6,22},{7,71},{8,24},{9,... | collective-permute-start | bytes 3145736 | tf_op jit(solution)/shard_map/ppermute | solution.py:585
  95.2 23.7 %collective-permute-start.24 = (bf16[32,64,256]{2,1,0:T(8,128)(2,1)S(1)}, bf16[32,64,256]{2,1,0:T(8,128)(2,1)S(1)}, u32[]{:S(2)}, u32[]{:S(2)}) collective-permute-start(bf16[32,64,256]{2,1,0:T(8,128)(2,1)S(1)} %back_products.6), channel_id=1, source_target_pairs={{0,24},{1,97},{2,26},{3,99},{4,28},{5,101},{6,30},{7,103},{8,0},{9... | collective-permute-start | bytes 3145736 | tf_op jit(solution)/shard_map/ppermute | solution.py:585
  100.5 19.5 %collective-permute-start.23 = (bf16[32,64,256]{2,1,0:T(8,128)(2,1)S(1)}, bf16[32,64,256]{2,1,0:T(8,128)(2,1)S(1)}, u32[]{:S(2)}, u32[]{:S(2)}) collective-permute-start(bf16[32,64,256]{2,1,0:T(8,128)(2,1)S(1)} %back_products.5.after_ref), channel_id=1, source_target_pairs={{0,8},{1,33},{2,10},{3,35},{4,12},{5,37},{6,14},{7,39},{8,16},{9,4... | collective-permute-start | bytes 3145736 | tf_op jit(solution)/shard_map/ppermute | solution.py:585
  101.4 5.8 %collective-permute-start.25 = (bf16[1,64,512]{2,1,0:T(8,128)(2,1)S(1)}, bf16[1,64,512]{2,1,0:T(8,128)(2,1)S(1)}, u32[]{:S(2)}, u32[]{:S(2)}) collective-permute-start(bf16[1,64,512]{2,1,0:T(8,128)(2,1)S(1)} %get-tuple-element.56), channel_id=1, source_target_pairs={{0,4},{1,5},{2,6},{3,7},{4,0},{5,1},{6,2},{7,3},{8,12},{9,13},{10,... | collective-permute-start | bytes 196616 | tf_op jit(solution)/shard_map/ppermute | solution.py:379
  108.0 12.0 %collective-permute-start.27 = (bf16[64,128]{1,0:T(8,128)(2,1)S(1)}, bf16[64,128]{1,0:T(8,128)(2,1)S(1)}, u32[]{:S(2)}, u32[]{:S(2)}) collective-permute-start(bf16[64,128]{1,0:T(8,128)(2,1)S(1)} %get-tuple-element.58), channel_id=1, source_target_pairs={{0,24},{1,97},{2,26},{3,99},{4,28},{5,101},{6,30},{7,103},{8,0},{9... | collective-permute-start | bytes 49160 | tf_op jit(solution)/shard_map/ppermute | solution.py:585
  110.4 9.6 %collective-permute-start.28 = (bf16[64,128]{1,0:T(8,128)(2,1)S(1)}, bf16[64,128]{1,0:T(8,128)(2,1)S(1)}, u32[]{:S(2)}, u32[]{:S(2)}) collective-permute-start(bf16[64,128]{1,0:T(8,128)(2,1)S(1)} %get-tuple-element.59), channel_id=1, source_target_pairs={{0,16},{1,65},{2,18},{3,67},{4,20},{5,69},{6,22},{7,71},{8,24},{9,... | collective-permute-start | bytes 49160 | tf_op jit(solution)/shard_map/ppermute | solution.py:585
  112.1 7.9 %collective-permute-start.29 = (bf16[64,128]{1,0:T(8,128)(2,1)S(1)}, bf16[64,128]{1,0:T(8,128)(2,1)S(1)}, u32[]{:S(2)}, u32[]{:S(2)}) collective-permute-start(bf16[64,128]{1,0:T(8,128)(2,1)S(1)} %get-tuple-element.60), channel_id=1, source_target_pairs={{0,8},{1,33},{2,10},{3,35},{4,12},{5,37},{6,14},{7,39},{8,16},{9,4... | collective-permute-start | bytes 49160 | tf_op jit(solution)/shard_map/ppermute | solution.py:585
  121.3 18.3 %collective-permute-start.31 = (bf16[64,4224]{1,0:T(8,128)(2,1)S(1)}, bf16[64,4224]{1,0:T(8,128)(2,1)S(1)}, u32[]{:S(2)}, u32[]{:S(2)}) collective-permute-start(bf16[64,4224]{1,0:T(8,128)(2,1)S(1)} %get-tuple-element.63), channel_id=1, source_target_pairs={{0,64},{1,17},{2,66},{3,19},{4,68},{5,21},{6,70},{7,23},{8,72},{9,... | collective-permute-start | bytes 1622024 | tf_op jit(solution)/shard_map/ppermute | solution.py:585
  123.7 15.9 %collective-permute-start.32 = (bf16[64,4224]{1,0:T(8,128)(2,1)S(1)}, bf16[64,4224]{1,0:T(8,128)(2,1)S(1)}, u32[]{:S(2)}, u32[]{:S(2)}) collective-permute-start(bf16[64,4224]{1,0:T(8,128)(2,1)S(1)} %get-tuple-element.64), channel_id=1, source_target_pairs={{0,32},{1,9},{2,34},{3,11},{4,36},{5,13},{6,38},{7,15},{8,40},{9,1... | collective-permute-start | bytes 1622024 | tf_op jit(solution)/shard_map/ppermute | solution.py:585
  125.5 14.1 %collective-permute-start.30 = (bf16[64,4224]{1,0:T(8,128)(2,1)S(1)}, bf16[64,4224]{1,0:T(8,128)(2,1)S(1)}, u32[]{:S(2)}, u32[]{:S(2)}) collective-permute-start(bf16[64,4224]{1,0:T(8,128)(2,1)S(1)} %get-tuple-element.62.after_ref), channel_id=1, source_target_pairs={{0,96},{1,25},{2,98},{3,27},{4,100},{5,29},{6,102},{7,31},{8,104},... | collective-permute-start | bytes 1622024 | tf_op jit(solution)/shard_map/ppermute | solution.py:585
  127.0 7.7 %collective-permute-start.33 = (bf16[2,64,512]{2,1,0:T(8,128)(2,1)S(1)}, bf16[2,64,512]{2,1,0:T(8,128)(2,1)S(1)}, u32[]{:S(2)}, u32[]{:S(2)}) collective-permute-start(bf16[2,64,512]{2,1,0:T(8,128)(2,1)S(1)} %get-tuple-element.67), channel_id=1, source_target_pairs={{0,2},{1,3},{2,4},{3,5},{4,6},{5,7},{6,0},{7,1},{8,10},{9,11},{10,... | collective-permute-start | bytes 393224 | tf_op jit(solution)/shard_map/ppermute | solution.py:618
  127.6 7.0 %collective-permute-start.34 = (bf16[2,64,512]{2,1,0:T(8,128)(2,1)S(1)}, bf16[2,64,512]{2,1,0:T(8,128)(2,1)S(1)}, u32[]{:S(2)}, u32[]{:S(2)}) collective-permute-start(bf16[2,64,512]{2,1,0:T(8,128)(2,1)S(1)} %get-tuple-element.68), channel_id=1, source_target_pairs={{0,4},{1,5},{2,6},{3,7},{4,0},{5,1},{6,2},{7,3},{8,12},{9,13},{10,... | collective-permute-start | bytes 393224 | tf_op jit(solution)/shard_map/ppermute | solution.py:618
  134.6 5.0 %collective-permute-start.35 = (bf16[2,64,512]{2,1,0:T(8,128)(2,1)S(1)}, bf16[2,64,512]{2,1,0:T(8,128)(2,1)S(1)}, u32[]{:S(2)}, u32[]{:S(2)}) collective-permute-start(bf16[2,64,512]{2,1,0:T(8,128)(2,1)S(1)} %get-tuple-element.69), channel_id=1, source_target_pairs={{0,6},{1,7},{2,0},{3,1},{4,2},{5,3},{6,4},{7,5},{8,14},{9,15},{10,... | collective-permute-start | bytes 393224 | tf_op jit(solution)/shard_map/ppermute | solution.py:618

commit v6 on v5

--- a/solution.py
+++ b/solution.py
@@ -69,53 +69,11 @@
     )(value, after)
 
 
-def halves_kernel(back1_ref, back3_ref, *refs):
-    low_ref, high_ref = refs[-2:]
-    half = low_ref.shape[0]
-    low_ref[...] = back1_ref[:half, :]
-    high_ref[...] = back3_ref[half:, :]
-
-
-def halves(back1, back3, after):
-    width, nodes = back1.shape
-    half = jax.ShapeDtypeStruct((width // 2, nodes), back1.dtype)
-    return pl.pallas_call(
-        halves_kernel,
-        out_shape=(half, half),
-        in_specs=arrays(2) + anywhere(len(after)),
-        out_specs=tuple(arrays(2)),
-        compiler_params=params(),
-        name="halves",
-    )(back1, back3, *after)
-
-
-def later_kernel(value_ref, after_ref, out_ref):
-    for i in range(value_ref.shape[0]):
-        out_ref[i] = value_ref[i]
-
-
-def later(value, after):
-    return pl.pallas_call(
-        later_kernel,
-        out_shape=jax.ShapeDtypeStruct(value.shape, value.dtype),
-        in_specs=scalars(1) + anywhere(1),
-        out_specs=scalars(1)[0],
-        compiler_params=params(),
-        name="later",
-    )(value, after)
-
-
-def gather_kernel(code_ref, own_ref, back1_ref, low_ref, high_ref, back3_ref, *refs):
-    out_ref = refs[-1]
-    half = low_ref.shape[0]
+def gather_kernel(code_ref, *refs):
+    slabs, out_ref = refs[:SIDE], refs[-1]
     for q in range(PART):
         columns = pl.ds(pl.multiple_of(col_block_of(code_ref[q]) * BLK, BLK), BLK)
-        d = q // SLOTS
-        if d == 2:
-            out_ref[q, :half, :] = low_ref[:, columns]
-            out_ref[q, half:, :] = high_ref[:, columns]
-        else:
-            out_ref[q] = (own_ref, back1_ref, None, back3_ref)[d][:, columns]
+        out_ref[q] = slabs[q // SLOTS][:, columns]
 
 
 def gather_blocks(code, slabs, after):
@@ -649,13 +607,12 @@
 
     feats_t = feats.T
     weight_t = weight.T
-    back1, back3 = shift(feats_t, True, 1), shift(feats_t, True, -1)
+    slabs = {d: shift(feats_t, True, d) for d in (2, 1, 3)}
     codes = sorted_codes(tile_rows, tile_cols, tile_nnz, node_rows // BLK).reshape(SIDE, PART)
     codes = [codes[e] for e in range(SIDE)]
     asked = [codes[0]] + [shift(codes[e], False, -e) for e in range(1, SIDE)]
     own = keep(feats_t, asked[1])
-    low, high = halves(back1, back3, [own] + asked[1:])
-    slabs = [own, back1, shift(low, True, 1), shift(high, True, -1), back3]
+    slabs = [own, slabs[1], slabs[2], slabs[3]]
 
     recv = [None] * SIDE
     sent = own

time: 142 us -> 138 us (0.972)
  starting transfers between devices: 57.5 us -> 55.4 us
    ppermute x19 -> x18, starting transfers between devices: 32.2 us -> 30 us  [shift(): return lax.ppermute(value, ('row', 'col'), pairs)]
    ppermute x19 -> x18, waiting for transfers between devices: 13 us -> 12 us  [shift(): return lax.ppermute(value, ('row', 'col'), pairs)]
  transfers between devices with their start and end apart: 36 -> 35, of which waited for: 18 -> 18; matrix products, arithmetic and copies ran while one was open for 1% -> 1% of each run, Pallas kernels for 19% -> 20%
where the time goes in v6:
time: 138 us
  starting transfers between devices  55.4 us (40%)
  waiting for transfers between devices  42.7 us (31%)
  Pallas kernels  36.3 us (26%)
  local copies, waits for them, and re-layouts  1.47 us (1%)
    ppermute x18, starting transfers between devices, shift(): return lax.ppermute(value, ('row', 'col'), pairs)  30 us
    ppermute x12, waiting for transfers between devices, shift_z(): lax.ppermute(value, 'col', [(c, (c + 2 * dz) % chunks) for c in range(chu...  25.3 us
    ppermute x12, starting transfers between devices, shift_z(): lax.ppermute(value, 'col', [(c, (c + 2 * dz) % chunks) for c in range(chu...  20.5 us
    ppermute x18, waiting for transfers between devices, shift(): return lax.ppermute(value, ('row', 'col'), pairs)  12 us
    pallas_call x3, Pallas kernels, back_products(): pl.pallas_call(back_kernel, out_shape=jax.ShapeDtypeStruct((PART, scaled....  9.56 us
    pallas_call x1, Pallas kernels, spread(): pl.pallas_call(functools.partial(spread_kernel, parts, False), out_shape=...  5.7 us
    ppermute x3, waiting for transfers between devices, swap_core(): return lax.ppermute(value, 'col', [(c, c ^ 1) for c in range(chunks)])  5.23 us
    ppermute x2, starting transfers between devices, swap_z(): return lax.ppermute(value, 'col', [(c, c ^ 2 * bit) for c in range(chunks)])  4.61 us
  transfers between devices with their start and end apart: 35, of which 18 were waited for; matrix products, arithmetic and copies ran while one was open for 1% of the time, Pallas kernels for 20%

profile of v6, /device:TPU:0, one launch (start us, length us, event | category | flops | bytes accessed | tf_op | source)
XLA Modules:
  0.0 138.2 jit_solution(9277024311890321873)
XLA Ops:
  0.6 2.9 %collective-permute-start.4 = (bf16[64,4096]{1,0:T(8,128)(2,1)}, bf16[64,4096]{1,0:T(8,128)(2,1)S(1)}, u32[]{:S(2)}, u32[]{:S(2)}) collective-permute-start(bf16[64,4096]{1,0:T(8,128)(2,1)} %bitcast.9), channel_id=1, source_target_pairs={{0,96},{1,25},{2,98},{3,27},{4,100},{5,29},{6,102},{7,31},{8,104},... | collective-permute-start | bytes 1572872 | tf_op jit(solution)/shard_map/ppermute | solution.py:543
  3.5 0.8 collective-permute-start.3
  4.3 0.9 collective-permute-start.2
  5.2 0.7 broadcast_select_fusion
  6.3 1.6 %collective-permute-start.5 = (s32[32]{0:T(128)S(1)}, s32[32]{0:T(128)S(1)}, u32[]{:S(2)}, u32[]{:S(2)}) collective-permute-start(s32[32]{0:T(128)S(1)} %get-tuple-element.94.refs_1_.code_ref), channel_id=1, source_target_pairs={{0,8},{1,33},{2,10},{3,35},{4,12},{5,37},{6,14},{7,39},{8,16},{9,4... | collective-permute-start | bytes 392 | tf_op jit(solution)/shard_map/ppermute | solution.py:543
  7.9 1.7 %collective-permute-start.1 = (s32[32]{0:T(128)S(1)}, s32[32]{0:T(128)S(1)}, u32[]{:S(2)}, u32[]{:S(2)}) collective-permute-start(s32[32]{0:T(128)S(1)} %get-tuple-element.95.refs_0_.code_ref), channel_id=1, source_target_pairs={{0,24},{1,97},{2,26},{3,99},{4,28},{5,101},{6,30},{7,103},{8,0},{9... | collective-permute-start | bytes 392 | tf_op jit(solution)/shard_map/ppermute | solution.py:543
  9.6 2.0 %collective-permute-done.1.after_ref.code_ref.refs_0_ = s32[32]{0:T(128)S(1)} collective-permute-done((s32[32]{0:T(128)S(1)}, s32[32]{0:T(128)S(1)}, u32[]{:S(2)}, u32[]{:S(2)}) %collective-permute-start.1) | collective-permute-done | bytes 160 | tf_op jit(solution)/shard_map/ppermute | solution.py:543
  11.5 2.9 %collective-permute-start = (s32[32]{0:T(128)S(1)}, s32[32]{0:T(128)S(1)}, u32[]{:S(2)}, u32[]{:S(2)}) collective-permute-start(s32[32]{0:T(128)S(1)} %get-tuple-element.96.refs_6_.code_ref), channel_id=1, source_target_pairs={{0,16},{1,65},{2,18},{3,67},{4,20},{5,69},{6,22},{7,71},{8,24},{9,... | collective-permute-start | bytes 392 | tf_op jit(solution)/shard_map/ppermute | solution.py:543
  14.4 1.0 copy-done.3
  15.5 0.7 collective-permute-done.4.refs_3_
  16.2 3.9 %collective-permute-done.2.refs_1_ = bf16[64,4096]{1,0:T(8,128)(2,1)S(1)} collective-permute-done((bf16[64,4096]{1,0:T(8,128)(2,1)}, bf16[64,4096]{1,0:T(8,128)(2,1)S(1)}, u32[]{:S(2)}, u32[]{:S(2)}) %collective-permute-start.2) | collective-permute-done | bytes 524320 | tf_op jit(solution)/shard_map/ppermute | solution.py:543
  20.1 0.7 gather_blocks.4.refs_4_
  20.8 1.6 %collective-permute-start.7 = (bf16[32,64,256]{2,1,0:T(8,128)(2,1)S(1)}, bf16[32,64,256]{2,1,0:T(8,128)(2,1)S(1)}, u32[]{:S(2)}, u32[]{:S(2)}) collective-permute-start(bf16[32,64,256]{2,1,0:T(8,128)(2,1)S(1)} %gather_blocks.4.refs_4_), channel_id=1, source_target_pairs={{0,8},{1,33},{2,10},{3,35},{4,12},{5,37},{6,14},{7,39},{8,16},{9,4... | collective-permute-start | bytes 3145736 | tf_op jit(solution)/shard_map/ppermute | solution.py:543
  22.4 0.7 gather_blocks.5.refs_4_
  23.1 1.7 %collective-permute-start.8 = (bf16[32,64,256]{2,1,0:T(8,128)(2,1)S(1)}, bf16[32,64,256]{2,1,0:T(8,128)(2,1)S(1)}, u32[]{:S(2)}, u32[]{:S(2)}) collective-permute-start(bf16[32,64,256]{2,1,0:T(8,128)(2,1)S(1)} %gather_blocks.5.refs_4_), channel_id=1, source_target_pairs={{0,24},{1,97},{2,26},{3,99},{4,28},{5,101},{6,30},{7,103},{8,0},{9... | collective-permute-start | bytes 3145736 | tf_op jit(solution)/shard_map/ppermute | solution.py:543
  24.8 0.7 gather_blocks.6.refs_4_
  25.5 2.1 %collective-permute-start.6 = (bf16[32,64,256]{2,1,0:T(8,128)(2,1)S(1)}, bf16[32,64,256]{2,1,0:T(8,128)(2,1)S(1)}, u32[]{:S(2)}, u32[]{:S(2)}) collective-permute-start(bf16[32,64,256]{2,1,0:T(8,128)(2,1)S(1)} %gather_blocks.6.refs_4_), channel_id=1, source_target_pairs={{0,16},{1,65},{2,18},{3,67},{4,20},{5,69},{6,22},{7,71},{8,24},{9,... | collective-permute-start | bytes 3145736 | tf_op jit(solution)/shard_map/ppermute | solution.py:543
  27.7 0.7 gather_blocks.7.refs_1_
  28.4 3.7 %spread.2.after_ref.refs_4_.refs_5_ = f32[80,4096]{1,0:T(8,128)S(1)} custom-call(s32[32]{0:T(128)S(1)} %get-tuple-element.93.code_ref.refs_0_, bf16[32,64,256]{2,1,0:T(8,128)(2,1)S(1)} %gather_blocks.7.refs_1_, bf16[128,256,256]{2,1,0:T(8,128)(2,1)} %tiles_ref.5), custom_call_target="tpu_custom_call" | custom-call | tf_op jit(solution)/shard_map/spread/pallas_call | solution.py:157
  32.1 0.6 split.1
  32.8 1.5 %collective-permute-done.9 = bf16[4,64,512]{2,1,0:T(8,128)(2,1)S(1)} collective-permute-done((bf16[4,64,512]{2,1,0:T(8,128)(2,1)S(1)}, bf16[4,64,512]{2,1,0:T(8,128)(2,1)S(1)}, u32[]{:S(2)}, u32[]{:S(2)}) %collective-permute-start.9) | collective-permute-done | bytes 262176 | tf_op jit(solution)/shard_map/ppermute | solution.py:571
  34.4 2.0 %collective-permute-start.10 = (bf16[2,64,512]{2,1,0:T(8,128)(2,1)S(1)}, bf16[2,64,512]{2,1,0:T(8,128)(2,1)S(1)}, u32[]{:S(2)}, u32[]{:S(2)}) collective-permute-start(bf16[2,64,512]{2,1,0:T(8,128)(2,1)S(1)} %pad_maximum_fusion.1), channel_id=1, source_target_pairs={{0,2},{1,3},{2,4},{3,5},{4,6},{5,7},{6,0},{7,1},{8,10},{9,11},{10,... | collective-permute-start | bytes 393224 | tf_op jit(solution)/shard_map/ppermute | solution.py:576
  36.4 3.7 %collective-permute-start.11 = (bf16[2,64,512]{2,1,0:T(8,128)(2,1)S(1)}, bf16[2,64,512]{2,1,0:T(8,128)(2,1)S(1)}, u32[]{:S(2)}, u32[]{:S(2)}) collective-permute-start(bf16[2,64,512]{2,1,0:T(8,128)(2,1)S(1)} %pad_maximum_fusion.2), channel_id=1, source_target_pairs={{0,4},{1,5},{2,6},{3,7},{4,0},{5,1},{6,2},{7,3},{8,12},{9,13},{10,... | collective-permute-start | bytes 393224 | tf_op jit(solution)/shard_map/ppermute | solution.py:576
  40.1 2.2 %collective-permute-done.10.refs_1_ = bf16[2,64,512]{2,1,0:T(8,128)(2,1)S(1)} collective-permute-done((bf16[2,64,512]{2,1,0:T(8,128)(2,1)S(1)}, bf16[2,64,512]{2,1,0:T(8,128)(2,1)S(1)}, u32[]{:S(2)}, u32[]{:S(2)}) %collective-permute-start.10) | collective-permute-done | bytes 131104 | tf_op jit(solution)/shard_map/ppermute | solution.py:576
  42.3 2.5 %collective-permute-start.12 = (bf16[2,64,512]{2,1,0:T(8,128)(2,1)S(1)}, bf16[2,64,512]{2,1,0:T(8,128)(2,1)S(1)}, u32[]{:S(2)}, u32[]{:S(2)}) collective-permute-start(bf16[2,64,512]{2,1,0:T(8,128)(2,1)S(1)} %pad_maximum_fusion.3), channel_id=1, source_target_pairs={{0,6},{1,7},{2,0},{3,1},{4,2},{5,3},{6,4},{7,5},{8,14},{9,15},{10,... | collective-permute-start | bytes 393224 | tf_op jit(solution)/shard_map/ppermute | solution.py:576
  44.8 1.4 %collective-permute-done.11.refs_2_ = bf16[2,64,512]{2,1,0:T(8,128)(2,1)S(1)} collective-permute-done((bf16[2,64,512]{2,1,0:T(8,128)(2,1)S(1)}, bf16[2,64,512]{2,1,0:T(8,128)(2,1)S(1)}, u32[]{:S(2)}, u32[]{:S(2)}) %collective-permute-start.11) | collective-permute-done | bytes 131104 | tf_op jit(solution)/shard_map/ppermute | solution.py:576
  46.3 1.1 collective-permute-done.12.refs_3_
  48.0 5.7 %spread.3 = (f32[80,4096]{1,0:T(8,128)S(1)}, bf16[4,8,256,256]{3,2,1,0:T(8,128)(2,1)S(1)}) custom-call(s32[32]{0:T(128)S(1)} %get-tuple-element.95.refs_0_.code_ref, s32[32]{0:T(128)S(1)} %get-tuple-element.94.refs_1_.code_ref, bf16[32,64,256]{2,1,0:T(8,128)(2,1)S(1)} %collective-permute-done.7.refs_2_, ...), custom_call_target="tpu_custom_call" | custom-call | tf_op jit(solution)/shard_map/spread/pallas_call | solution.py:171
  53.7 2.6 %spread_mixed.1 = (bf16[4,64,512]{2,1,0:T(8,128)(2,1)S(1)}, bf16[4,64,512]{2,1,0:T(8,128)(2,1)S(1)}, f32[1,4096]{1,0:T(1,128)S(1)}) custom-call(s32[3]{0:T(128)S(1)} %pad_add_fusion.place_ref, s32[32]{0:T(128)S(1)} %get-tuple-element.96.refs_6_.code_ref, bf16[32,64,256]{2,1,0:T(8,128)(2,1)S(1)} %collective-permute-done.6.recv_ref, ...), custom_call_target="tpu_custom_call" | custom-call | tf_op jit(solution)/shard_map/spread_mixed/pallas_call | solution.py:199
  56.5 1.5 %collective-permute-done.13 = bf16[4,64,512]{2,1,0:T(8,128)(2,1)S(1)} collective-permute-done((bf16[4,64,512]{2,1,0:T(8,128)(2,1)S(1)}, bf16[4,64,512]{2,1,0:T(8,128)(2,1)S(1)}, u32[]{:S(2)}, u32[]{:S(2)}) %collective-permute-start.13) | collective-permute-done | bytes 262176 | tf_op jit(solution)/shard_map/ppermute | solution.py:571
  58.0 0.7 collective-permute-start.14
  58.7 4.6 %collective-permute-start.15 = (bf16[2,64,512]{2,1,0:T(8,128)(2,1)S(1)}, bf16[2,64,512]{2,1,0:T(8,128)(2,1)S(1)}, u32[]{:S(2)}, u32[]{:S(2)}) collective-permute-start(bf16[2,64,512]{2,1,0:T(8,128)(2,1)S(1)} %pad_maximum_fusion.6), channel_id=1, source_target_pairs={{0,4},{1,5},{2,6},{3,7},{4,0},{5,1},{6,2},{7,3},{8,12},{9,13},{10,... | collective-permute-start | bytes 393224 | tf_op jit(solution)/shard_map/ppermute | solution.py:576
  63.7 1.9 %collective-permute-done.14.refs_1_ = bf16[2,64,512]{2,1,0:T(8,128)(2,1)S(1)} collective-permute-done((bf16[2,64,512]{2,1,0:T(8,128)(2,1)S(1)}, bf16[2,64,512]{2,1,0:T(8,128)(2,1)S(1)}, u32[]{:S(2)}, u32[]{:S(2)}) %collective-permute-start.14) | collective-permute-done | bytes 131104 | tf_op jit(solution)/shard_map/ppermute | solution.py:576
  65.6 4.0 %collective-permute-done.15.refs_2_ = bf16[2,64,512]{2,1,0:T(8,128)(2,1)S(1)} collective-permute-done((bf16[2,64,512]{2,1,0:T(8,128)(2,1)S(1)}, bf16[2,64,512]{2,1,0:T(8,128)(2,1)S(1)}, u32[]{:S(2)}, u32[]{:S(2)}) %collective-permute-start.15) | collective-permute-done | bytes 131104 | tf_op jit(solution)/shard_map/ppermute | solution.py:576
  69.6 2.2 %dense.1 = (bf16[4,64,512]{2,1,0:T(8,128)(2,1)S(1)}, bf16[4,64,512]{2,1,0:T(8,128)(2,1)S(1)}, bf16[4,192,512]{2,1,0:T(8,128)(2,1)S(1)}, bf16[4,64,512]{2,1,0:T(8,128)(2,1)S(1)}) custom-call(s32[3]{0:T(128)S(1)} %pad_add_fusion.place_ref, bf16[2,64,512]{2,1,0:T(8,128)(2,1)S(1)} %pad_maximum_fusion.4.refs_0_, ...), custom_call_target="tpu_custom_call" | custom-call | tf_op jit(solution)/shard_map/dense/pallas_call | solution.py:282
  71.9 2.2 %collective-permute-done.17.got_ref.after_ref = bf16[4,192,512]{2,1,0:T(8,128)(2,1)S(1)} collective-permute-done((bf16[4,192,512]{2,1,0:T(8,128)(2,1)S(1)}, bf16[4,192,512]{2,1,0:T(8,128)(2,1)S(1)}, u32[]{:S(2)}, u32[]{:S(2)}) %collective-permute-start.17) | collective-permute-done | bytes 786464 | tf_op jit(solution)/shard_map/ppermute | solution.py:571
  74.4 3.6 %collective-permute-start.19 = (bf16[2,64,512]{2,1,0:T(8,128)(2,1)S(1)}, bf16[2,64,512]{2,1,0:T(8,128)(2,1)S(1)}, u32[]{:S(2)}, u32[]{:S(2)}) collective-permute-start(bf16[2,64,512]{2,1,0:T(8,128)(2,1)S(1)} %pad_maximum_fusion.10), channel_id=1, source_target_pairs={{0,4},{1,5},{2,6},{3,7},{4,0},{5,1},{6,2},{7,3},{8,12},{9,13},{10,... | collective-permute-start | bytes 393224 | tf_op jit(solution)/shard_map/ppermute | solution.py:576
  78.2 2.3 %collective-permute-start.21 = (bf16[2,64,512]{2,1,0:T(8,128)(2,1)S(1)}, bf16[2,64,512]{2,1,0:T(8,128)(2,1)S(1)}, u32[]{:S(2)}, u32[]{:S(2)}) collective-permute-start(bf16[2,64,512]{2,1,0:T(8,128)(2,1)S(1)} %get-tuple-element.49), channel_id=1, source_target_pairs={{0,2},{1,3},{2,0},{3,1},{4,6},{5,7},{6,4},{7,5},{8,10},{9,11},{10,... | collective-permute-start | bytes 393224 | tf_op jit(solution)/shard_map/ppermute | solution.py:337
  80.5 0.9 collective-permute-done.18.refs_1_
  81.4 3.6 %collective-permute-done.19.refs_2_ = bf16[2,64,512]{2,1,0:T(8,128)(2,1)S(1)} collective-permute-done((bf16[2,64,512]{2,1,0:T(8,128)(2,1)S(1)}, bf16[2,64,512]{2,1,0:T(8,128)(2,1)S(1)}, u32[]{:S(2)}, u32[]{:S(2)}) %collective-permute-start.19) | collective-permute-done | bytes 131104 | tf_op jit(solution)/shard_map/ppermute | solution.py:576
  85.0 0.6 collective-permute-done.20.refs_3_
  85.6 1.9 %back_products.4 = (bf16[32,64,256]{2,1,0:T(8,128)(2,1)S(1)}, bf16[64,4096]{1,0:T(8,128)(2,1)S(1)}, bf16[64,4096]{1,0:T(8,128)(2,1)S(1)}) custom-call(s32[3]{0:T(128)S(1)} %pad_add_fusion.place_ref, s32[32]{0:T(128)S(1)} %get-tuple-element.96.refs_6_.code_ref, bf16[2,64,512]{2,1,0:T(8,128)(2,1)S(1)} %pad_maximum_fusion.8.refs_0_, ...), custom_call_target="tpu_custom_call" | custom-call | tf_op jit(solution)/shard_map/back_products/pallas_call | solution.py:408
  87.5 2.5 %collective-permute-start.25 = (bf16[32,64,256]{2,1,0:T(8,128)(2,1)S(1)}, bf16[32,64,256]{2,1,0:T(8,128)(2,1)S(1)}, u32[]{:S(2)}, u32[]{:S(2)}) collective-permute-start(bf16[32,64,256]{2,1,0:T(8,128)(2,1)S(1)} %get-tuple-element.50.after_ref), channel_id=1, source_target_pairs={{0,16},{1,65},{2,18},{3,67},{4,20},{5,69},{6,22},{7,71},{8,24},{9,... | collective-permute-start | bytes 3145736 | tf_op jit(solution)/shard_map/ppermute | solution.py:543
  90.0 3.2 %back_products.6 = bf16[32,64,256]{2,1,0:T(8,128)(2,1)S(1)} custom-call(s32[32]{0:T(128)S(1)} %get-tuple-element.95.refs_0_.code_ref, bf16[64,4096]{1,0:T(8,128)(2,1)S(1)} %get-tuple-element.46.scaled_ref, bf16[128,256,256]{2,1,0:T(8,128)(2,1)} %tiles_ref.5, f32[1,4096]{1,0:T(1,128)S(1)} %get-tuple-element.44.refs_4_.after_ref), custom_call_target="tpu_custom_call" | custom-call | tf_op jit(solution)/shard_map/back_products/pallas_call | solution.py:419
  93.2 2.1 %collective-permute-start.23 = (bf16[32,64,256]{2,1,0:T(8,128)(2,1)S(1)}, bf16[32,64,256]{2,1,0:T(8,128)(2,1)S(1)}, u32[]{:S(2)}, u32[]{:S(2)}) collective-permute-start(bf16[32,64,256]{2,1,0:T(8,128)(2,1)S(1)} %back_products.6), channel_id=1, source_target_pairs={{0,24},{1,97},{2,26},{3,99},{4,28},{5,101},{6,30},{7,103},{8,0},{9... | collective-permute-start | bytes 3145736 | tf_op jit(solution)/shard_map/ppermute | solution.py:543
  95.4 3.2 %back_products.5.after_ref = bf16[32,64,256]{2,1,0:T(8,128)(2,1)S(1)} custom-call(s32[32]{0:T(128)S(1)} %get-tuple-element.94.refs_1_.code_ref, bf16[64,4096]{1,0:T(8,128)(2,1)S(1)} %get-tuple-element.46.scaled_ref, bf16[128,256,256]{2,1,0:T(8,128)(2,1)} %tiles_ref.5, bf16[1,64,512]{2,1,0:T(8,128)(2,1)S(1)} %get-tuple-element.51.after_ref.own_ref), custom_call_target="tpu_custom_call" | custom-call | tf_op jit(solution)/shard_map/back_products/pallas_call | solution.py:419
  98.6 0.9 collective-permute-start.22
  99.5 2.3 %collective-permute-start.24 = (bf16[1,64,512]{2,1,0:T(8,128)(2,1)S(1)}, bf16[1,64,512]{2,1,0:T(8,128)(2,1)S(1)}, u32[]{:S(2)}, u32[]{:S(2)}) collective-permute-start(bf16[1,64,512]{2,1,0:T(8,128)(2,1)S(1)} %get-tuple-element.52), channel_id=1, source_target_pairs={{0,4},{1,5},{2,6},{3,7},{4,0},{5,1},{6,2},{7,3},{8,12},{9,13},{10,... | collective-permute-start | bytes 196616 | tf_op jit(solution)/shard_map/ppermute | solution.py:337
  101.8 3.2 %back_products.7.after_ref.refs_2_.refs_4_ = bf16[32,64,256]{2,1,0:T(8,128)(2,1)S(1)} custom-call(s32[32]{0:T(128)S(1)} %get-tuple-element.93.code_ref.refs_0_, bf16[64,4096]{1,0:T(8,128)(2,1)S(1)} %get-tuple-element.46.scaled_ref, bf16[128,256,256]{2,1,0:T(8,128)(2,1)} %tiles_ref.5, bf16[32,64,256]{2,1,0:T(8,128)(2,1)S(1)} %back_products.5.after_ref), custom_call_target="tpu_custom_call" | custom-call | tf_op jit(solution)/shard_map/back_products/pallas_call | solution.py:419
  105.3 0.8 gw_order.1
  106.0 2.4 %collective-permute-start.26 = (bf16[64,128]{1,0:T(8,128)(2,1)S(1)}, bf16[64,128]{1,0:T(8,128)(2,1)S(1)}, u32[]{:S(2)}, u32[]{:S(2)}) collective-permute-start(bf16[64,128]{1,0:T(8,128)(2,1)S(1)} %get-tuple-element.54), channel_id=1, source_target_pairs={{0,24},{1,97},{2,26},{3,99},{4,28},{5,101},{6,30},{7,103},{8,0},{9... | collective-permute-start | bytes 49160 | tf_op jit(solution)/shard_map/ppermute | solution.py:543
  108.5 1.7 %collective-permute-start.27 = (bf16[64,128]{1,0:T(8,128)(2,1)S(1)}, bf16[64,128]{1,0:T(8,128)(2,1)S(1)}, u32[]{:S(2)}, u32[]{:S(2)}) collective-permute-start(bf16[64,128]{1,0:T(8,128)(2,1)S(1)} %get-tuple-element.55), channel_id=1, source_target_pairs={{0,16},{1,65},{2,18},{3,67},{4,20},{5,69},{6,22},{7,71},{8,24},{9,... | collective-permute-start | bytes 49160 | tf_op jit(solution)/shard_map/ppermute | solution.py:543
  110.2 1.3 collect.2.refs_3_
  111.5 5.4 %collective-permute-done.23.refs_1_ = bf16[32,64,256]{2,1,0:T(8,128)(2,1)S(1)} collective-permute-done((bf16[32,64,256]{2,1,0:T(8,128)(2,1)S(1)}, bf16[32,64,256]{2,1,0:T(8,128)(2,1)S(1)}, u32[]{:S(2)}, u32[]{:S(2)}) %collective-permute-start.23) | collective-permute-done | bytes 1048608 | tf_op jit(solution)/shard_map/ppermute | solution.py:543
  117.0 1.1 collect.3.before_ref
  118.1 1.3 finish_slabs.1
  119.4 0.9 collective-permute-start.30
  120.2 0.7 collective-permute-start.31
  120.9 2.6 %collective-permute-start.29 = (bf16[64,4224]{1,0:T(8,128)(2,1)S(1)}, bf16[64,4224]{1,0:T(8,128)(2,1)S(1)}, u32[]{:S(2)}, u32[]{:S(2)}) collective-permute-start(bf16[64,4224]{1,0:T(8,128)(2,1)S(1)} %get-tuple-element.58.after_ref), channel_id=1, source_target_pairs={{0,96},{1,25},{2,98},{3,27},{4,100},{5,29},{6,102},{7,31},{8,104},... | collective-permute-start | bytes 1622024 | tf_op jit(solution)/shard_map/ppermute | solution.py:543
  123.5 0.7 collective-permute-start.32
  124.2 2.4 %collective-permute-start.33 = (bf16[2,64,512]{2,1,0:T(8,128)(2,1)S(1)}, bf16[2,64,512]{2,1,0:T(8,128)(2,1)S(1)}, u32[]{:S(2)}, u32[]{:S(2)}) collective-permute-start(bf16[2,64,512]{2,1,0:T(8,128)(2,1)S(1)} %get-tuple-element.64), channel_id=1, source_target_pairs={{0,4},{1,5},{2,6},{3,7},{4,0},{5,1},{6,2},{7,3},{8,12},{9,13},{10,... | collective-permute-start | bytes 393224 | tf_op jit(solution)/shard_map/ppermute | solution.py:576
  126.6 4.6 %collective-permute-done.32.refs_5_ = bf16[2,64,512]{2,1,0:T(8,128)(2,1)S(1)} collective-permute-done((bf16[2,64,512]{2,1,0:T(8,128)(2,1)S(1)}, bf16[2,64,512]{2,1,0:T(8,128)(2,1)S(1)}, u32[]{:S(2)}, u32[]{:S(2)}) %collective-permute-start.32) | collective-permute-done | bytes 131104 | tf_op jit(solution)/shard_map/ppermute | solution.py:576
  131.2 5.0 %collective-permute-done.34.refs_7_ = bf16[2,64,512]{2,1,0:T(8,128)(2,1)S(1)} collective-permute-done((bf16[2,64,512]{2,1,0:T(8,128)(2,1)S(1)}, bf16[2,64,512]{2,1,0:T(8,128)(2,1)S(1)}, u32[]{:S(2)}, u32[]{:S(2)}) %collective-permute-start.34) | collective-permute-done | bytes 131104 | tf_op jit(solution)/shard_map/ppermute | solution.py:576
  136.2 2.0 %finish.1 = (bf16[64,4096]{1,0:T(8,128)(2,1)}, f32[32,64]{1,0:T(8,128)}, bf16[64,4096]{1,0:T(8,128)(2,1)}) custom-call(s32[3]{0:T(128)S(1)} %pad_add_fusion.place_ref, bf16[64,4096]{1,0:T(8,128)(2,1)S(1)} %get-tuple-element.45.grad_ref, bf16[64,4224]{1,0:T(8,128)(2,1)S(1)} %get-tuple-element.57.refs_0_, ...), custom_call_target="tpu_custom_call" | custom-call | tf_op jit(solution)/shard_map/finish/pallas_call | solution.py:522
  (66 shorter events, 2.6 us)
Async XLA Ops:
  0.6 15.6 %collective-permute-start.4 = (bf16[64,4096]{1,0:T(8,128)(2,1)}, bf16[64,4096]{1,0:T(8,128)(2,1)S(1)}, u32[]{:S(2)}, u32[]{:S(2)}) collective-permute-start(bf16[64,4096]{1,0:T(8,128)(2,1)} %bitcast.9), channel_id=1, source_target_pairs={{0,96},{1,25},{2,98},{3,27},{4,100},{5,29},{6,102},{7,31},{8,104},... | collective-permute-start | bytes 1572872 | tf_op jit(solution)/shard_map/ppermute | solution.py:543
  3.5 12.6 %collective-permute-start.3 = (bf16[64,4096]{1,0:T(8,128)(2,1)}, bf16[64,4096]{1,0:T(8,128)(2,1)S(1)}, u32[]{:S(2)}, u32[]{:S(2)}) collective-permute-start(bf16[64,4096]{1,0:T(8,128)(2,1)} %bitcast.10), channel_id=1, source_target_pairs={{0,64},{1,17},{2,66},{3,19},{4,68},{5,21},{6,70},{7,23},{8,72},{9,... | collective-permute-start | bytes 1572872 | tf_op jit(solution)/shard_map/ppermute | solution.py:543
  4.3 15.7 %collective-permute-start.2 = (bf16[64,4096]{1,0:T(8,128)(2,1)}, bf16[64,4096]{1,0:T(8,128)(2,1)S(1)}, u32[]{:S(2)}, u32[]{:S(2)}) collective-permute-start(bf16[64,4096]{1,0:T(8,128)(2,1)} %bitcast.11), channel_id=1, source_target_pairs={{0,32},{1,9},{2,34},{3,11},{4,36},{5,13},{6,38},{7,15},{8,40},{9,1... | collective-permute-start | bytes 1572872 | tf_op jit(solution)/shard_map/ppermute | solution.py:543
  6.3 16.1 %collective-permute-start.5 = (s32[32]{0:T(128)S(1)}, s32[32]{0:T(128)S(1)}, u32[]{:S(2)}, u32[]{:S(2)}) collective-permute-start(s32[32]{0:T(128)S(1)} %get-tuple-element.94.refs_1_.code_ref), channel_id=1, source_target_pairs={{0,8},{1,33},{2,10},{3,35},{4,12},{5,37},{6,14},{7,39},{8,16},{9,4... | collective-permute-start | bytes 392 | tf_op jit(solution)/shard_map/ppermute | solution.py:543
  7.9 3.6 %collective-permute-start.1 = (s32[32]{0:T(128)S(1)}, s32[32]{0:T(128)S(1)}, u32[]{:S(2)}, u32[]{:S(2)}) collective-permute-start(s32[32]{0:T(128)S(1)} %get-tuple-element.95.refs_0_.code_ref), channel_id=1, source_target_pairs={{0,24},{1,97},{2,26},{3,99},{4,28},{5,101},{6,30},{7,103},{8,0},{9... | collective-permute-start | bytes 392 | tf_op jit(solution)/shard_map/ppermute | solution.py:543
  11.5 13.3 %collective-permute-start = (s32[32]{0:T(128)S(1)}, s32[32]{0:T(128)S(1)}, u32[]{:S(2)}, u32[]{:S(2)}) collective-permute-start(s32[32]{0:T(128)S(1)} %get-tuple-element.96.refs_6_.code_ref), channel_id=1, source_target_pairs={{0,16},{1,65},{2,18},{3,67},{4,20},{5,69},{6,22},{7,71},{8,24},{9,... | collective-permute-start | bytes 392 | tf_op jit(solution)/shard_map/ppermute | solution.py:543
  14.4 1.0 copy-start.3
  20.8 27.2 %collective-permute-start.7 = (bf16[32,64,256]{2,1,0:T(8,128)(2,1)S(1)}, bf16[32,64,256]{2,1,0:T(8,128)(2,1)S(1)}, u32[]{:S(2)}, u32[]{:S(2)}) collective-permute-start(bf16[32,64,256]{2,1,0:T(8,128)(2,1)S(1)} %gather_blocks.4.refs_4_), channel_id=1, source_target_pairs={{0,8},{1,33},{2,10},{3,35},{4,12},{5,37},{6,14},{7,39},{8,16},{9,4... | collective-permute-start | bytes 3145736 | tf_op jit(solution)/shard_map/ppermute | solution.py:543
  23.1 24.9 %collective-permute-start.8 = (bf16[32,64,256]{2,1,0:T(8,128)(2,1)S(1)}, bf16[32,64,256]{2,1,0:T(8,128)(2,1)S(1)}, u32[]{:S(2)}, u32[]{:S(2)}) collective-permute-start(bf16[32,64,256]{2,1,0:T(8,128)(2,1)S(1)} %gather_blocks.5.refs_4_), channel_id=1, source_target_pairs={{0,24},{1,97},{2,26},{3,99},{4,28},{5,101},{6,30},{7,103},{8,0},{9... | collective-permute-start | bytes 3145736 | tf_op jit(solution)/shard_map/ppermute | solution.py:543
  25.5 28.2 %collective-permute-start.6 = (bf16[32,64,256]{2,1,0:T(8,128)(2,1)S(1)}, bf16[32,64,256]{2,1,0:T(8,128)(2,1)S(1)}, u32[]{:S(2)}, u32[]{:S(2)}) collective-permute-start(bf16[32,64,256]{2,1,0:T(8,128)(2,1)S(1)} %gather_blocks.6.refs_4_), channel_id=1, source_target_pairs={{0,16},{1,65},{2,18},{3,67},{4,20},{5,69},{6,22},{7,71},{8,24},{9,... | collective-permute-start | bytes 3145736 | tf_op jit(solution)/shard_map/ppermute | solution.py:543
  28.3 3.8 %copy-start.5 = (bf16[4096,64]{0,1:T(8,128)(2,1)S(1)}, bf16[4096,64]{0,1:T(8,128)(2,1)}, u32[]{:S(2)}) copy-start(bf16[4096,64]{0,1:T(8,128)(2,1)} %param.13) | copy-start | bytes 1572868
  32.7 1.6 %collective-permute-start.9 = (bf16[4,64,512]{2,1,0:T(8,128)(2,1)S(1)}, bf16[4,64,512]{2,1,0:T(8,128)(2,1)S(1)}, u32[]{:S(2)}, u32[]{:S(2)}) collective-permute-start(bf16[4,64,512]{2,1,0:T(8,128)(2,1)S(1)} %get-tuple-element.37), channel_id=1, source_target_pairs={{0,1},{1,0},{2,3},{3,2},{4,5},{5,4},{6,7},{7,6},{8,9},{9,8},{10,11... | collective-permute-start | bytes 786440 | tf_op jit(solution)/shard_map/ppermute | solution.py:571
  34.4 7.9 %collective-permute-start.10 = (bf16[2,64,512]{2,1,0:T(8,128)(2,1)S(1)}, bf16[2,64,512]{2,1,0:T(8,128)(2,1)S(1)}, u32[]{:S(2)}, u32[]{:S(2)}) collective-permute-start(bf16[2,64,512]{2,1,0:T(8,128)(2,1)S(1)} %pad_maximum_fusion.1), channel_id=1, source_target_pairs={{0,2},{1,3},{2,4},{3,5},{4,6},{5,7},{6,0},{7,1},{8,10},{9,11},{10,... | collective-permute-start | bytes 393224 | tf_op jit(solution)/shard_map/ppermute | solution.py:576
  36.4 9.9 %collective-permute-start.11 = (bf16[2,64,512]{2,1,0:T(8,128)(2,1)S(1)}, bf16[2,64,512]{2,1,0:T(8,128)(2,1)S(1)}, u32[]{:S(2)}, u32[]{:S(2)}) collective-permute-start(bf16[2,64,512]{2,1,0:T(8,128)(2,1)S(1)} %pad_maximum_fusion.2), channel_id=1, source_target_pairs={{0,4},{1,5},{2,6},{3,7},{4,0},{5,1},{6,2},{7,3},{8,12},{9,13},{10,... | collective-permute-start | bytes 393224 | tf_op jit(solution)/shard_map/ppermute | solution.py:576
  42.3 5.1 %collective-permute-start.12 = (bf16[2,64,512]{2,1,0:T(8,128)(2,1)S(1)}, bf16[2,64,512]{2,1,0:T(8,128)(2,1)S(1)}, u32[]{:S(2)}, u32[]{:S(2)}) collective-permute-start(bf16[2,64,512]{2,1,0:T(8,128)(2,1)S(1)} %pad_maximum_fusion.3), channel_id=1, source_target_pairs={{0,6},{1,7},{2,0},{3,1},{4,2},{5,3},{6,4},{7,5},{8,14},{9,15},{10,... | collective-permute-start | bytes 393224 | tf_op jit(solution)/shard_map/ppermute | solution.py:576
  47.9 5.8 %copy-start.4 = (bf16[4096,64]{0,1:T(8,128)(2,1)S(1)}, bf16[4096,64]{0,1:T(8,128)(2,1)}, u32[]{:S(2)}) copy-start(bf16[4096,64]{0,1:T(8,128)(2,1)} %param.7) | copy-start | bytes 1572868
  53.7 4.3 %copy-start = (bf16[4,8,256,256]{3,2,1,0:T(8,128)(2,1)}, bf16[4,8,256,256]{3,2,1,0:T(8,128)(2,1)S(1)}, u32[]{:S(2)}) copy-start(bf16[4,8,256,256]{3,2,1,0:T(8,128)(2,1)S(1)} %get-tuple-element.38.tiles_ref.refs_5_) | copy-start | bytes 12582916
  53.7 9.7 %copy-start.2 = (bf16[512,512]{1,0:T(8,128)(2,1)S(1)}, bf16[512,512]{1,0:T(8,128)(2,1)}, u32[]{:S(2)}) copy-start(bf16[512,512]{1,0:T(8,128)(2,1)} %refs_5_.1) | copy-start | bytes 1572868
  56.4 1.6 %collective-permute-start.13 = (bf16[4,64,512]{2,1,0:T(8,128)(2,1)S(1)}, bf16[4,64,512]{2,1,0:T(8,128)(2,1)S(1)}, u32[]{:S(2)}, u32[]{:S(2)}) collective-permute-start(bf16[4,64,512]{2,1,0:T(8,128)(2,1)S(1)} %get-tuple-element.41), channel_id=1, source_target_pairs={{0,1},{1,0},{2,3},{3,2},{4,5},{5,4},{6,7},{7,6},{8,9},{9,8},{10,11... | collective-permute-start | bytes 786440 | tf_op jit(solution)/shard_map/ppermute | solution.py:571
  58.0 7.5 %collective-permute-start.14 = (bf16[2,64,512]{2,1,0:T(8,128)(2,1)S(1)}, bf16[2,64,512]{2,1,0:T(8,128)(2,1)S(1)}, u32[]{:S(2)}, u32[]{:S(2)}) collective-permute-start(bf16[2,64,512]{2,1,0:T(8,128)(2,1)S(1)} %pad_maximum_fusion.5), channel_id=1, source_target_pairs={{0,2},{1,3},{2,4},{3,5},{4,6},{5,7},{6,0},{7,1},{8,10},{9,11},{10,... | collective-permute-start | bytes 393224 | tf_op jit(solution)/shard_map/ppermute | solution.py:576
  58.7 10.8 %collective-permute-start.15 = (bf16[2,64,512]{2,1,0:T(8,128)(2,1)S(1)}, bf16[2,64,512]{2,1,0:T(8,128)(2,1)S(1)}, u32[]{:S(2)}, u32[]{:S(2)}) collective-permute-start(bf16[2,64,512]{2,1,0:T(8,128)(2,1)S(1)} %pad_maximum_fusion.6), channel_id=1, source_target_pairs={{0,4},{1,5},{2,6},{3,7},{4,0},{5,1},{6,2},{7,3},{8,12},{9,13},{10,... | collective-permute-start | bytes 393224 | tf_op jit(solution)/shard_map/ppermute | solution.py:576
  63.3 6.2 %collective-permute-start.16 = (bf16[2,64,512]{2,1,0:T(8,128)(2,1)S(1)}, bf16[2,64,512]{2,1,0:T(8,128)(2,1)S(1)}, u32[]{:S(2)}, u32[]{:S(2)}) collective-permute-start(bf16[2,64,512]{2,1,0:T(8,128)(2,1)S(1)} %pad_maximum_fusion.7), channel_id=1, source_target_pairs={{0,6},{1,7},{2,0},{3,1},{4,2},{5,3},{6,4},{7,5},{8,14},{9,15},{10,... | collective-permute-start | bytes 393224 | tf_op jit(solution)/shard_map/ppermute | solution.py:576
  63.7 22.0 %copy-start.1 = (bf16[4,8,256,256]{3,2,1,0:T(8,128)(2,1)S(1)}, bf16[4,8,256,256]{3,2,1,0:T(8,128)(2,1)}, u32[]{:S(2)}) copy-start(bf16[4,8,256,256]{3,2,1,0:T(8,128)(2,1)} %copy-done) | copy-start | bytes 12582916
  71.8 2.4 %collective-permute-start.17 = (bf16[4,192,512]{2,1,0:T(8,128)(2,1)S(1)}, bf16[4,192,512]{2,1,0:T(8,128)(2,1)S(1)}, u32[]{:S(2)}, u32[]{:S(2)}) collective-permute-start(bf16[4,192,512]{2,1,0:T(8,128)(2,1)S(1)} %get-tuple-element.43), channel_id=1, source_target_pairs={{0,1},{1,0},{2,3},{3,2},{4,5},{5,4},{6,7},{7,6},{8,9},{9,8},{10,11... | collective-permute-start | bytes 2359304 | tf_op jit(solution)/shard_map/ppermute | solution.py:571
  74.2 7.2 %collective-permute-start.18 = (bf16[2,64,512]{2,1,0:T(8,128)(2,1)S(1)}, bf16[2,64,512]{2,1,0:T(8,128)(2,1)S(1)}, u32[]{:S(2)}, u32[]{:S(2)}) collective-permute-start(bf16[2,64,512]{2,1,0:T(8,128)(2,1)S(1)} %pad_maximum_fusion.9), channel_id=1, source_target_pairs={{0,2},{1,3},{2,4},{3,5},{4,6},{5,7},{6,0},{7,1},{8,10},{9,11},{10,... | collective-permute-start | bytes 393224 | tf_op jit(solution)/shard_map/ppermute | solution.py:576
  74.4 10.6 %collective-permute-start.19 = (bf16[2,64,512]{2,1,0:T(8,128)(2,1)S(1)}, bf16[2,64,512]{2,1,0:T(8,128)(2,1)S(1)}, u32[]{:S(2)}, u32[]{:S(2)}) collective-permute-start(bf16[2,64,512]{2,1,0:T(8,128)(2,1)S(1)} %pad_maximum_fusion.10), channel_id=1, source_target_pairs={{0,4},{1,5},{2,6},{3,7},{4,0},{5,1},{6,2},{7,3},{8,12},{9,13},{10,... | collective-permute-start | bytes 393224 | tf_op jit(solution)/shard_map/ppermute | solution.py:576
  78.0 7.6 %collective-permute-start.20 = (bf16[2,64,512]{2,1,0:T(8,128)(2,1)S(1)}, bf16[2,64,512]{2,1,0:T(8,128)(2,1)S(1)}, u32[]{:S(2)}, u32[]{:S(2)}) collective-permute-start(bf16[2,64,512]{2,1,0:T(8,128)(2,1)S(1)} %pad_maximum_fusion.11), channel_id=1, source_target_pairs={{0,6},{1,7},{2,0},{3,1},{4,2},{5,3},{6,4},{7,5},{8,14},{9,15},{10,... | collective-permute-start | bytes 393224 | tf_op jit(solution)/shard_map/ppermute | solution.py:576
  78.2 17.2 %collective-permute-start.21 = (bf16[2,64,512]{2,1,0:T(8,128)(2,1)S(1)}, bf16[2,64,512]{2,1,0:T(8,128)(2,1)S(1)}, u32[]{:S(2)}, u32[]{:S(2)}) collective-permute-start(bf16[2,64,512]{2,1,0:T(8,128)(2,1)S(1)} %get-tuple-element.49), channel_id=1, source_target_pairs={{0,2},{1,3},{2,0},{3,1},{4,6},{5,7},{6,4},{7,5},{8,10},{9,11},{10,... | collective-permute-start | bytes 393224 | tf_op jit(solution)/shard_map/ppermute | solution.py:337
  87.5 22.7 %collective-permute-start.25 = (bf16[32,64,256]{2,1,0:T(8,128)(2,1)S(1)}, bf16[32,64,256]{2,1,0:T(8,128)(2,1)S(1)}, u32[]{:S(2)}, u32[]{:S(2)}) collective-permute-start(bf16[32,64,256]{2,1,0:T(8,128)(2,1)S(1)} %get-tuple-element.50.after_ref), channel_id=1, source_target_pairs={{0,16},{1,65},{2,18},{3,67},{4,20},{5,69},{6,22},{7,71},{8,24},{9,... | collective-permute-start | bytes 3145736 | tf_op jit(solution)/shard_map/ppermute | solution.py:543
  93.2 23.7 %collective-permute-start.23 = (bf16[32,64,256]{2,1,0:T(8,128)(2,1)S(1)}, bf16[32,64,256]{2,1,0:T(8,128)(2,1)S(1)}, u32[]{:S(2)}, u32[]{:S(2)}) collective-permute-start(bf16[32,64,256]{2,1,0:T(8,128)(2,1)S(1)} %back_products.6), channel_id=1, source_target_pairs={{0,24},{1,97},{2,26},{3,99},{4,28},{5,101},{6,30},{7,103},{8,0},{9... | collective-permute-start | bytes 3145736 | tf_op jit(solution)/shard_map/ppermute | solution.py:543
  98.6 19.5 %collective-permute-start.22 = (bf16[32,64,256]{2,1,0:T(8,128)(2,1)S(1)}, bf16[32,64,256]{2,1,0:T(8,128)(2,1)S(1)}, u32[]{:S(2)}, u32[]{:S(2)}) collective-permute-start(bf16[32,64,256]{2,1,0:T(8,128)(2,1)S(1)} %back_products.5.after_ref), channel_id=1, source_target_pairs={{0,8},{1,33},{2,10},{3,35},{4,12},{5,37},{6,14},{7,39},{8,16},{9,4... | collective-permute-start | bytes 3145736 | tf_op jit(solution)/shard_map/ppermute | solution.py:543
  99.5 5.8 %collective-permute-start.24 = (bf16[1,64,512]{2,1,0:T(8,128)(2,1)S(1)}, bf16[1,64,512]{2,1,0:T(8,128)(2,1)S(1)}, u32[]{:S(2)}, u32[]{:S(2)}) collective-permute-start(bf16[1,64,512]{2,1,0:T(8,128)(2,1)S(1)} %get-tuple-element.52), channel_id=1, source_target_pairs={{0,4},{1,5},{2,6},{3,7},{4,0},{5,1},{6,2},{7,3},{8,12},{9,13},{10,... | collective-permute-start | bytes 196616 | tf_op jit(solution)/shard_map/ppermute | solution.py:337
  106.0 12.0 %collective-permute-start.26 = (bf16[64,128]{1,0:T(8,128)(2,1)S(1)}, bf16[64,128]{1,0:T(8,128)(2,1)S(1)}, u32[]{:S(2)}, u32[]{:S(2)}) collective-permute-start(bf16[64,128]{1,0:T(8,128)(2,1)S(1)} %get-tuple-element.54), channel_id=1, source_target_pairs={{0,24},{1,97},{2,26},{3,99},{4,28},{5,101},{6,30},{7,103},{8,0},{9... | collective-permute-start | bytes 49160 | tf_op jit(solution)/shard_map/ppermute | solution.py:543
  108.5 9.6 %collective-permute-start.27 = (bf16[64,128]{1,0:T(8,128)(2,1)S(1)}, bf16[64,128]{1,0:T(8,128)(2,1)S(1)}, u32[]{:S(2)}, u32[]{:S(2)}) collective-permute-start(bf16[64,128]{1,0:T(8,128)(2,1)S(1)} %get-tuple-element.55), channel_id=1, source_target_pairs={{0,16},{1,65},{2,18},{3,67},{4,20},{5,69},{6,22},{7,71},{8,24},{9,... | collective-permute-start | bytes 49160 | tf_op jit(solution)/shard_map/ppermute | solution.py:543
  110.2 7.9 %collective-permute-start.28 = (bf16[64,128]{1,0:T(8,128)(2,1)S(1)}, bf16[64,128]{1,0:T(8,128)(2,1)S(1)}, u32[]{:S(2)}, u32[]{:S(2)}) collective-permute-start(bf16[64,128]{1,0:T(8,128)(2,1)S(1)} %get-tuple-element.56), channel_id=1, source_target_pairs={{0,8},{1,33},{2,10},{3,35},{4,12},{5,37},{6,14},{7,39},{8,16},{9,4... | collective-permute-start | bytes 49160 | tf_op jit(solution)/shard_map/ppermute | solution.py:543
  119.4 16.8 %collective-permute-start.30 = (bf16[64,4224]{1,0:T(8,128)(2,1)S(1)}, bf16[64,4224]{1,0:T(8,128)(2,1)S(1)}, u32[]{:S(2)}, u32[]{:S(2)}) collective-permute-start(bf16[64,4224]{1,0:T(8,128)(2,1)S(1)} %get-tuple-element.59), channel_id=1, source_target_pairs={{0,64},{1,17},{2,66},{3,19},{4,68},{5,21},{6,70},{7,23},{8,72},{9,... | collective-permute-start | bytes 1622024 | tf_op jit(solution)/shard_map/ppermute | solution.py:543
  120.2 15.9 %collective-permute-start.31 = (bf16[64,4224]{1,0:T(8,128)(2,1)S(1)}, bf16[64,4224]{1,0:T(8,128)(2,1)S(1)}, u32[]{:S(2)}, u32[]{:S(2)}) collective-permute-start(bf16[64,4224]{1,0:T(8,128)(2,1)S(1)} %get-tuple-element.60), channel_id=1, source_target_pairs={{0,32},{1,9},{2,34},{3,11},{4,36},{5,13},{6,38},{7,15},{8,40},{9,1... | collective-permute-start | bytes 1622024 | tf_op jit(solution)/shard_map/ppermute | solution.py:543
  120.9 15.2 %collective-permute-start.29 = (bf16[64,4224]{1,0:T(8,128)(2,1)S(1)}, bf16[64,4224]{1,0:T(8,128)(2,1)S(1)}, u32[]{:S(2)}, u32[]{:S(2)}) collective-permute-start(bf16[64,4224]{1,0:T(8,128)(2,1)S(1)} %get-tuple-element.58.after_ref), channel_id=1, source_target_pairs={{0,96},{1,25},{2,98},{3,27},{4,100},{5,29},{6,102},{7,31},{8,104},... | collective-permute-start | bytes 1622024 | tf_op jit(solution)/shard_map/ppermute | solution.py:543
  123.5 7.7 %collective-permute-start.32 = (bf16[2,64,512]{2,1,0:T(8,128)(2,1)S(1)}, bf16[2,64,512]{2,1,0:T(8,128)(2,1)S(1)}, u32[]{:S(2)}, u32[]{:S(2)}) collective-permute-start(bf16[2,64,512]{2,1,0:T(8,128)(2,1)S(1)} %get-tuple-element.63), channel_id=1, source_target_pairs={{0,2},{1,3},{2,4},{3,5},{4,6},{5,7},{6,0},{7,1},{8,10},{9,11},{10,... | collective-permute-start | bytes 393224 | tf_op jit(solution)/shard_map/ppermute | solution.py:576
  124.2 7.0 %collective-permute-start.33 = (bf16[2,64,512]{2,1,0:T(8,128)(2,1)S(1)}, bf16[2,64,512]{2,1,0:T(8,128)(2,1)S(1)}, u32[]{:S(2)}, u32[]{:S(2)}) collective-permute-start(bf16[2,64,512]{2,1,0:T(8,128)(2,1)S(1)} %get-tuple-element.64), channel_id=1, source_target_pairs={{0,4},{1,5},{2,6},{3,7},{4,0},{5,1},{6,2},{7,3},{8,12},{9,13},{10,... | collective-permute-start | bytes 393224 | tf_op jit(solution)/shard_map/ppermute | solution.py:576
  131.2 5.0 %collective-permute-start.34 = (bf16[2,64,512]{2,1,0:T(8,128)(2,1)S(1)}, bf16[2,64,512]{2,1,0:T(8,128)(2,1)S(1)}, u32[]{:S(2)}, u32[]{:S(2)}) collective-permute-start(bf16[2,64,512]{2,1,0:T(8,128)(2,1)S(1)} %get-tuple-element.65), channel_id=1, source_target_pairs={{0,6},{1,7},{2,0},{3,1},{4,2},{5,3},{6,4},{7,5},{8,14},{9,15},{10,... | collective-permute-start | bytes 393224 | tf_op jit(solution)/shard_map/ppermute | solution.py:576

commit v7 on v6

--- a/solution.py
+++ b/solution.py
@@ -616,7 +616,7 @@
 
     recv = [None] * SIDE
     sent = own
-    for e in (1, 3, 2):
+    for e in (2, 1, 3):
         sent = gather_blocks(asked[e], slabs, [sent])
         recv[e] = shift(sent, False, e)
     recv[0] = gather_blocks(asked[0], slabs, [sent])

time: 138 us -> 138 us (level)
    ppermute x12, starting transfers between devices: 20.5 us -> 23.2 us  [shift_z(): lax.ppermute(value, 'col', [(c, (c + 2 * dz) % chunks) for c in range(chu...]
    ppermute x12, waiting for transfers between devices: 25.3 us -> 23 us  [shift_z(): lax.ppermute(value, 'col', [(c, (c + 2 * dz) % chunks) for c in range(chu...]
    ppermute x18, waiting for transfers between devices: 12 us -> 13.8 us  [shift(): return lax.ppermute(value, ('row', 'col'), pairs)]
    ppermute x18, starting transfers between devices: 30 us -> 28.3 us  [shift(): return lax.ppermute(value, ('row', 'col'), pairs)]
  transfers between devices with their start and end apart: 35 -> 35, of which waited for: 18 -> 21; matrix products, arithmetic and copies ran while one was open for 1% -> 1% of each run, Pallas kernels for 20% -> 20%
where the time goes in v7:
time: 138 us; the launch traced here: 137 us
  starting transfers between devices  55.1 us (40%)
  waiting for transfers between devices  42.3 us (31%)
  Pallas kernels  36.3 us (26%)
  local copies, waits for them, and re-layouts  1.47 us (1%)
    ppermute x18, starting transfers between devices, shift(): return lax.ppermute(value, ('row', 'col'), pairs)  28.3 us
    ppermute x12, starting transfers between devices, shift_z(): lax.ppermute(value, 'col', [(c, (c + 2 * dz) % chunks) for c in range(chu...  23.2 us
    ppermute x12, waiting for transfers between devices, shift_z(): lax.ppermute(value, 'col', [(c, (c + 2 * dz) % chunks) for c in range(chu...  23 us
    ppermute x18, waiting for transfers between devices, shift(): return lax.ppermute(value, ('row', 'col'), pairs)  13.8 us
    pallas_call x3, Pallas kernels, back_products(): pl.pallas_call(back_kernel, out_shape=jax.ShapeDtypeStruct((PART, scaled....  9.56 us
    pallas_call x1, Pallas kernels, spread(): pl.pallas_call(functools.partial(spread_kernel, parts, False), out_shape=...  5.7 us
    ppermute x3, waiting for transfers between devices, swap_core(): return lax.ppermute(value, 'col', [(c, c ^ 1) for c in range(chunks)])  5.23 us
    pallas_call x1, Pallas kernels, first_spread(): pl.pallas_call(functools.partial(spread_kernel, 1, True), out_shape=total...  3.74 us
  transfers between devices with their start and end apart: 35, of which 21 were waited for; matrix products, arithmetic and copies ran while one was open for 1% of the time, Pallas kernels for 20%

profile of v7, /device:TPU:0, one launch (start us, length us, event | category | flops | bytes accessed | tf_op | source)
XLA Modules:
  0.0 137.5 jit_solution(134227403183095265)
XLA Ops:
  0.6 2.9 %collective-permute-start.4 = (bf16[64,4096]{1,0:T(8,128)(2,1)}, bf16[64,4096]{1,0:T(8,128)(2,1)S(1)}, u32[]{:S(2)}, u32[]{:S(2)}) collective-permute-start(bf16[64,4096]{1,0:T(8,128)(2,1)} %bitcast.9), channel_id=1, source_target_pairs={{0,96},{1,25},{2,98},{3,27},{4,100},{5,29},{6,102},{7,31},{8,104},... | collective-permute-start | bytes 1572872 | tf_op jit(solution)/shard_map/ppermute | solution.py:543
  3.5 0.8 collective-permute-start.3
  4.3 0.9 collective-permute-start.2
  5.2 0.7 broadcast_select_fusion
  6.3 3.0 %collective-permute-start.1 = (s32[32]{0:T(128)S(1)}, s32[32]{0:T(128)S(1)}, u32[]{:S(2)}, u32[]{:S(2)}) collective-permute-start(s32[32]{0:T(128)S(1)} %get-tuple-element.95.refs_0_.code_ref), channel_id=1, source_target_pairs={{0,24},{1,97},{2,26},{3,99},{4,28},{5,101},{6,30},{7,103},{8,0},{9... | collective-permute-start | bytes 392 | tf_op jit(solution)/shard_map/ppermute | solution.py:543
  10.0 0.7 collective-permute-done.1.after_ref.code_ref.refs_0_
  10.6 0.8 collective-permute-start.7
  11.5 1.0 copy-done.3
  12.5 1.9 %collective-permute-done.code_ref.refs_1_ = s32[32]{0:T(128)S(1)} collective-permute-done((s32[32]{0:T(128)S(1)}, s32[32]{0:T(128)S(1)}, u32[]{:S(2)}, u32[]{:S(2)}) %collective-permute-start) | collective-permute-done | bytes 160 | tf_op jit(solution)/shard_map/ppermute | solution.py:543
  14.5 1.7 %collective-permute-done.4.refs_3_ = bf16[64,4096]{1,0:T(8,128)(2,1)S(1)} collective-permute-done((bf16[64,4096]{1,0:T(8,128)(2,1)}, bf16[64,4096]{1,0:T(8,128)(2,1)S(1)}, u32[]{:S(2)}, u32[]{:S(2)}) %collective-permute-start.4) | collective-permute-done | bytes 524320 | tf_op jit(solution)/shard_map/ppermute | solution.py:543
  16.2 3.9 %collective-permute-done.2.refs_1_ = bf16[64,4096]{1,0:T(8,128)(2,1)S(1)} collective-permute-done((bf16[64,4096]{1,0:T(8,128)(2,1)}, bf16[64,4096]{1,0:T(8,128)(2,1)S(1)}, u32[]{:S(2)}, u32[]{:S(2)}) %collective-permute-start.2) | collective-permute-done | bytes 524320 | tf_op jit(solution)/shard_map/ppermute | solution.py:543
  20.1 0.7 gather_blocks.4.refs_4_
  20.8 3.3 %collective-permute-start.5 = (bf16[32,64,256]{2,1,0:T(8,128)(2,1)S(1)}, bf16[32,64,256]{2,1,0:T(8,128)(2,1)S(1)}, u32[]{:S(2)}, u32[]{:S(2)}) collective-permute-start(bf16[32,64,256]{2,1,0:T(8,128)(2,1)S(1)} %gather_blocks.4.refs_4_), channel_id=1, source_target_pairs={{0,16},{1,65},{2,18},{3,67},{4,20},{5,69},{6,22},{7,71},{8,24},{9,... | collective-permute-start | bytes 3145736 | tf_op jit(solution)/shard_map/ppermute | solution.py:543
  24.0 0.7 gather_blocks.5.refs_4_
  24.7 0.7 collective-permute-start.6
  25.5 0.7 gather_blocks.6.refs_4_
  26.2 2.6 %collective-permute-start.8 = (bf16[32,64,256]{2,1,0:T(8,128)(2,1)S(1)}, bf16[32,64,256]{2,1,0:T(8,128)(2,1)S(1)}, u32[]{:S(2)}, u32[]{:S(2)}) collective-permute-start(bf16[32,64,256]{2,1,0:T(8,128)(2,1)S(1)} %gather_blocks.6.refs_4_), channel_id=1, source_target_pairs={{0,24},{1,97},{2,26},{3,99},{4,28},{5,101},{6,30},{7,103},{8,0},{9... | collective-permute-start | bytes 3145736 | tf_op jit(solution)/shard_map/ppermute | solution.py:543
  28.9 0.7 gather_blocks.7.refs_1_
  29.6 3.7 %spread.2.after_ref.refs_4_.refs_5_ = f32[80,4096]{1,0:T(8,128)S(1)} custom-call(s32[32]{0:T(128)S(1)} %get-tuple-element.93.code_ref.refs_0_, bf16[32,64,256]{2,1,0:T(8,128)(2,1)S(1)} %gather_blocks.7.refs_1_, bf16[128,256,256]{2,1,0:T(8,128)(2,1)} %tiles_ref.5), custom_call_target="tpu_custom_call" | custom-call | tf_op jit(solution)/shard_map/spread/pallas_call | solution.py:157
  34.0 1.5 %collective-permute-done.9 = bf16[4,64,512]{2,1,0:T(8,128)(2,1)S(1)} collective-permute-done((bf16[4,64,512]{2,1,0:T(8,128)(2,1)S(1)}, bf16[4,64,512]{2,1,0:T(8,128)(2,1)S(1)}, u32[]{:S(2)}, u32[]{:S(2)}) %collective-permute-start.9) | collective-permute-done | bytes 262176 | tf_op jit(solution)/shard_map/ppermute | solution.py:571
  35.6 2.0 %collective-permute-start.10 = (bf16[2,64,512]{2,1,0:T(8,128)(2,1)S(1)}, bf16[2,64,512]{2,1,0:T(8,128)(2,1)S(1)}, u32[]{:S(2)}, u32[]{:S(2)}) collective-permute-start(bf16[2,64,512]{2,1,0:T(8,128)(2,1)S(1)} %pad_maximum_fusion.1), channel_id=1, source_target_pairs={{0,2},{1,3},{2,4},{3,5},{4,6},{5,7},{6,0},{7,1},{8,10},{9,11},{10,... | collective-permute-start | bytes 393224 | tf_op jit(solution)/shard_map/ppermute | solution.py:576
  37.6 3.7 %collective-permute-start.11 = (bf16[2,64,512]{2,1,0:T(8,128)(2,1)S(1)}, bf16[2,64,512]{2,1,0:T(8,128)(2,1)S(1)}, u32[]{:S(2)}, u32[]{:S(2)}) collective-permute-start(bf16[2,64,512]{2,1,0:T(8,128)(2,1)S(1)} %pad_maximum_fusion.2), channel_id=1, source_target_pairs={{0,4},{1,5},{2,6},{3,7},{4,0},{5,1},{6,2},{7,3},{8,12},{9,13},{10,... | collective-permute-start | bytes 393224 | tf_op jit(solution)/shard_map/ppermute | solution.py:576
  41.3 2.2 %collective-permute-done.10.refs_1_ = bf16[2,64,512]{2,1,0:T(8,128)(2,1)S(1)} collective-permute-done((bf16[2,64,512]{2,1,0:T(8,128)(2,1)S(1)}, bf16[2,64,512]{2,1,0:T(8,128)(2,1)S(1)}, u32[]{:S(2)}, u32[]{:S(2)}) %collective-permute-start.10) | collective-permute-done | bytes 131104 | tf_op jit(solution)/shard_map/ppermute | solution.py:576
  43.5 2.5 %collective-permute-start.12 = (bf16[2,64,512]{2,1,0:T(8,128)(2,1)S(1)}, bf16[2,64,512]{2,1,0:T(8,128)(2,1)S(1)}, u32[]{:S(2)}, u32[]{:S(2)}) collective-permute-start(bf16[2,64,512]{2,1,0:T(8,128)(2,1)S(1)} %pad_maximum_fusion.3), channel_id=1, source_target_pairs={{0,6},{1,7},{2,0},{3,1},{4,2},{5,3},{6,4},{7,5},{8,14},{9,15},{10,... | collective-permute-start | bytes 393224 | tf_op jit(solution)/shard_map/ppermute | solution.py:576
  46.0 1.4 %collective-permute-done.11.refs_2_ = bf16[2,64,512]{2,1,0:T(8,128)(2,1)S(1)} collective-permute-done((bf16[2,64,512]{2,1,0:T(8,128)(2,1)S(1)}, bf16[2,64,512]{2,1,0:T(8,128)(2,1)S(1)}, u32[]{:S(2)}, u32[]{:S(2)}) %collective-permute-start.11) | collective-permute-done | bytes 131104 | tf_op jit(solution)/shard_map/ppermute | solution.py:576
  47.5 1.1 collective-permute-done.12.refs_3_
  49.2 5.7 %spread.3 = (f32[80,4096]{1,0:T(8,128)S(1)}, bf16[4,8,256,256]{3,2,1,0:T(8,128)(2,1)S(1)}) custom-call(s32[32]{0:T(128)S(1)} %get-tuple-element.95.refs_0_.code_ref, s32[32]{0:T(128)S(1)} %get-tuple-element.94.refs_1_.code_ref, bf16[32,64,256]{2,1,0:T(8,128)(2,1)S(1)} %collective-permute-done.6.refs_2_, ...), custom_call_target="tpu_custom_call" | custom-call | tf_op jit(solution)/shard_map/spread/pallas_call | solution.py:171
  54.9 2.6 %spread_mixed.1 = (bf16[4,64,512]{2,1,0:T(8,128)(2,1)S(1)}, bf16[4,64,512]{2,1,0:T(8,128)(2,1)S(1)}, f32[1,4096]{1,0:T(1,128)S(1)}) custom-call(s32[3]{0:T(128)S(1)} %pad_add_fusion.place_ref, s32[32]{0:T(128)S(1)} %get-tuple-element.96.refs_6_.code_ref, bf16[32,64,256]{2,1,0:T(8,128)(2,1)S(1)} %collective-permute-done.5.recv_ref, ...), custom_call_target="tpu_custom_call" | custom-call | tf_op jit(solution)/shard_map/spread_mixed/pallas_call | solution.py:199
  57.7 1.5 %collective-permute-done.13 = bf16[4,64,512]{2,1,0:T(8,128)(2,1)S(1)} collective-permute-done((bf16[4,64,512]{2,1,0:T(8,128)(2,1)S(1)}, bf16[4,64,512]{2,1,0:T(8,128)(2,1)S(1)}, u32[]{:S(2)}, u32[]{:S(2)}) %collective-permute-start.13) | collective-permute-done | bytes 262176 | tf_op jit(solution)/shard_map/ppermute | solution.py:571
  59.2 1.6 %collective-permute-start.14 = (bf16[2,64,512]{2,1,0:T(8,128)(2,1)S(1)}, bf16[2,64,512]{2,1,0:T(8,128)(2,1)S(1)}, u32[]{:S(2)}, u32[]{:S(2)}) collective-permute-start(bf16[2,64,512]{2,1,0:T(8,128)(2,1)S(1)} %pad_maximum_fusion.5), channel_id=1, source_target_pairs={{0,2},{1,3},{2,4},{3,5},{4,6},{5,7},{6,0},{7,1},{8,10},{9,11},{10,... | collective-permute-start | bytes 393224 | tf_op jit(solution)/shard_map/ppermute | solution.py:576
  60.8 3.7 %collective-permute-start.15 = (bf16[2,64,512]{2,1,0:T(8,128)(2,1)S(1)}, bf16[2,64,512]{2,1,0:T(8,128)(2,1)S(1)}, u32[]{:S(2)}, u32[]{:S(2)}) collective-permute-start(bf16[2,64,512]{2,1,0:T(8,128)(2,1)S(1)} %pad_maximum_fusion.6), channel_id=1, source_target_pairs={{0,4},{1,5},{2,6},{3,7},{4,0},{5,1},{6,2},{7,3},{8,12},{9,13},{10,... | collective-permute-start | bytes 393224 | tf_op jit(solution)/shard_map/ppermute | solution.py:576
  64.6 1.0 collective-permute-start.16
  65.8 0.9 collective-permute-done.14.refs_1_
  66.8 4.0 %collective-permute-done.15.refs_2_ = bf16[2,64,512]{2,1,0:T(8,128)(2,1)S(1)} collective-permute-done((bf16[2,64,512]{2,1,0:T(8,128)(2,1)S(1)}, bf16[2,64,512]{2,1,0:T(8,128)(2,1)S(1)}, u32[]{:S(2)}, u32[]{:S(2)}) %collective-permute-start.15) | collective-permute-done | bytes 131104 | tf_op jit(solution)/shard_map/ppermute | solution.py:576
  70.8 2.2 %dense.1 = (bf16[4,64,512]{2,1,0:T(8,128)(2,1)S(1)}, bf16[4,64,512]{2,1,0:T(8,128)(2,1)S(1)}, bf16[4,192,512]{2,1,0:T(8,128)(2,1)S(1)}, bf16[4,64,512]{2,1,0:T(8,128)(2,1)S(1)}) custom-call(s32[3]{0:T(128)S(1)} %pad_add_fusion.place_ref, bf16[2,64,512]{2,1,0:T(8,128)(2,1)S(1)} %pad_maximum_fusion.4.refs_0_, ...), custom_call_target="tpu_custom_call" | custom-call | tf_op jit(solution)/shard_map/dense/pallas_call | solution.py:282
  73.1 2.2 %collective-permute-done.17.got_ref.after_ref = bf16[4,192,512]{2,1,0:T(8,128)(2,1)S(1)} collective-permute-done((bf16[4,192,512]{2,1,0:T(8,128)(2,1)S(1)}, bf16[4,192,512]{2,1,0:T(8,128)(2,1)S(1)}, u32[]{:S(2)}, u32[]{:S(2)}) %collective-permute-start.17) | collective-permute-done | bytes 786464 | tf_op jit(solution)/shard_map/ppermute | solution.py:571
  75.4 1.4 %collective-permute-start.18 = (bf16[2,64,512]{2,1,0:T(8,128)(2,1)S(1)}, bf16[2,64,512]{2,1,0:T(8,128)(2,1)S(1)}, u32[]{:S(2)}, u32[]{:S(2)}) collective-permute-start(bf16[2,64,512]{2,1,0:T(8,128)(2,1)S(1)} %pad_maximum_fusion.9), channel_id=1, source_target_pairs={{0,2},{1,3},{2,4},{3,5},{4,6},{5,7},{6,0},{7,1},{8,10},{9,11},{10,... | collective-permute-start | bytes 393224 | tf_op jit(solution)/shard_map/ppermute | solution.py:576
  76.8 2.4 %collective-permute-start.19 = (bf16[2,64,512]{2,1,0:T(8,128)(2,1)S(1)}, bf16[2,64,512]{2,1,0:T(8,128)(2,1)S(1)}, u32[]{:S(2)}, u32[]{:S(2)}) collective-permute-start(bf16[2,64,512]{2,1,0:T(8,128)(2,1)S(1)} %pad_maximum_fusion.10), channel_id=1, source_target_pairs={{0,4},{1,5},{2,6},{3,7},{4,0},{5,1},{6,2},{7,3},{8,12},{9,13},{10,... | collective-permute-start | bytes 393224 | tf_op jit(solution)/shard_map/ppermute | solution.py:576
  79.2 1.3 collective-permute-start.20
  80.6 1.0 collective-permute-start.21
  81.7 1.0 collective-permute-done.18.refs_1_
  82.6 3.6 %collective-permute-done.19.refs_2_ = bf16[2,64,512]{2,1,0:T(8,128)(2,1)S(1)} collective-permute-done((bf16[2,64,512]{2,1,0:T(8,128)(2,1)S(1)}, bf16[2,64,512]{2,1,0:T(8,128)(2,1)S(1)}, u32[]{:S(2)}, u32[]{:S(2)}) %collective-permute-start.19) | collective-permute-done | bytes 131104 | tf_op jit(solution)/shard_map/ppermute | solution.py:576
  86.8 1.9 %back_products.4 = (bf16[32,64,256]{2,1,0:T(8,128)(2,1)S(1)}, bf16[64,4096]{1,0:T(8,128)(2,1)S(1)}, bf16[64,4096]{1,0:T(8,128)(2,1)S(1)}) custom-call(s32[3]{0:T(128)S(1)} %pad_add_fusion.place_ref, s32[32]{0:T(128)S(1)} %get-tuple-element.96.refs_6_.code_ref, bf16[2,64,512]{2,1,0:T(8,128)(2,1)S(1)} %pad_maximum_fusion.8.refs_0_, ...), custom_call_target="tpu_custom_call" | custom-call | tf_op jit(solution)/shard_map/back_products/pallas_call | solution.py:408
  88.7 2.8 %collective-permute-start.25 = (bf16[32,64,256]{2,1,0:T(8,128)(2,1)S(1)}, bf16[32,64,256]{2,1,0:T(8,128)(2,1)S(1)}, u32[]{:S(2)}, u32[]{:S(2)}) collective-permute-start(bf16[32,64,256]{2,1,0:T(8,128)(2,1)S(1)} %get-tuple-element.50.after_ref), channel_id=1, source_target_pairs={{0,16},{1,65},{2,18},{3,67},{4,20},{5,69},{6,22},{7,71},{8,24},{9,... | collective-permute-start | bytes 3145736 | tf_op jit(solution)/shard_map/ppermute | solution.py:543
  91.5 3.2 %back_products.6 = bf16[32,64,256]{2,1,0:T(8,128)(2,1)S(1)} custom-call(s32[32]{0:T(128)S(1)} %get-tuple-element.95.refs_0_.code_ref, bf16[64,4096]{1,0:T(8,128)(2,1)S(1)} %get-tuple-element.46.scaled_ref, bf16[128,256,256]{2,1,0:T(8,128)(2,1)} %tiles_ref.5, f32[1,4096]{1,0:T(1,128)S(1)} %get-tuple-element.44.refs_4_.after_ref), custom_call_target="tpu_custom_call" | custom-call | tf_op jit(solution)/shard_map/back_products/pallas_call | solution.py:419
  94.7 1.3 collective-permute-start.23
  96.1 3.2 %back_products.5.after_ref = bf16[32,64,256]{2,1,0:T(8,128)(2,1)S(1)} custom-call(s32[32]{0:T(128)S(1)} %get-tuple-element.94.refs_1_.code_ref, bf16[64,4096]{1,0:T(8,128)(2,1)S(1)} %get-tuple-element.46.scaled_ref, bf16[128,256,256]{2,1,0:T(8,128)(2,1)} %tiles_ref.5, bf16[1,64,512]{2,1,0:T(8,128)(2,1)S(1)} %get-tuple-element.51.after_ref.own_ref), custom_call_target="tpu_custom_call" | custom-call | tf_op jit(solution)/shard_map/back_products/pallas_call | solution.py:419
  99.3 0.9 collective-permute-start.22
  100.1 2.3 %collective-permute-start.24 = (bf16[1,64,512]{2,1,0:T(8,128)(2,1)S(1)}, bf16[1,64,512]{2,1,0:T(8,128)(2,1)S(1)}, u32[]{:S(2)}, u32[]{:S(2)}) collective-permute-start(bf16[1,64,512]{2,1,0:T(8,128)(2,1)S(1)} %get-tuple-element.52), channel_id=1, source_target_pairs={{0,4},{1,5},{2,6},{3,7},{4,0},{5,1},{6,2},{7,3},{8,12},{9,13},{10,... | collective-permute-start | bytes 196616 | tf_op jit(solution)/shard_map/ppermute | solution.py:337
  102.5 3.2 %back_products.7.after_ref.refs_2_.refs_4_ = bf16[32,64,256]{2,1,0:T(8,128)(2,1)S(1)} custom-call(s32[32]{0:T(128)S(1)} %get-tuple-element.93.code_ref.refs_0_, bf16[64,4096]{1,0:T(8,128)(2,1)S(1)} %get-tuple-element.46.scaled_ref, bf16[128,256,256]{2,1,0:T(8,128)(2,1)} %tiles_ref.5, bf16[32,64,256]{2,1,0:T(8,128)(2,1)S(1)} %back_products.5.after_ref), custom_call_target="tpu_custom_call" | custom-call | tf_op jit(solution)/shard_map/back_products/pallas_call | solution.py:419
  105.9 0.8 gw_order.1
  106.7 2.5 %collective-permute-start.26 = (bf16[64,128]{1,0:T(8,128)(2,1)S(1)}, bf16[64,128]{1,0:T(8,128)(2,1)S(1)}, u32[]{:S(2)}, u32[]{:S(2)}) collective-permute-start(bf16[64,128]{1,0:T(8,128)(2,1)S(1)} %get-tuple-element.54), channel_id=1, source_target_pairs={{0,24},{1,97},{2,26},{3,99},{4,28},{5,101},{6,30},{7,103},{8,0},{9... | collective-permute-start | bytes 49160 | tf_op jit(solution)/shard_map/ppermute | solution.py:543
  110.1 1.3 collect.2.refs_3_
  111.5 4.8 %collective-permute-done.23.refs_1_ = bf16[32,64,256]{2,1,0:T(8,128)(2,1)S(1)} collective-permute-done((bf16[32,64,256]{2,1,0:T(8,128)(2,1)S(1)}, bf16[32,64,256]{2,1,0:T(8,128)(2,1)S(1)}, u32[]{:S(2)}, u32[]{:S(2)}) %collective-permute-start.23) | collective-permute-done | bytes 1048608 | tf_op jit(solution)/shard_map/ppermute | solution.py:543
  116.3 1.1 collect.3.before_ref
  117.4 1.3 finish_slabs.1
  118.7 0.9 collective-permute-start.30
  120.2 2.6 %collective-permute-start.29 = (bf16[64,4224]{1,0:T(8,128)(2,1)S(1)}, bf16[64,4224]{1,0:T(8,128)(2,1)S(1)}, u32[]{:S(2)}, u32[]{:S(2)}) collective-permute-start(bf16[64,4224]{1,0:T(8,128)(2,1)S(1)} %get-tuple-element.58.after_ref), channel_id=1, source_target_pairs={{0,96},{1,25},{2,98},{3,27},{4,100},{5,29},{6,102},{7,31},{8,104},... | collective-permute-start | bytes 1622024 | tf_op jit(solution)/shard_map/ppermute | solution.py:543
  123.5 2.4 %collective-permute-start.33 = (bf16[2,64,512]{2,1,0:T(8,128)(2,1)S(1)}, bf16[2,64,512]{2,1,0:T(8,128)(2,1)S(1)}, u32[]{:S(2)}, u32[]{:S(2)}) collective-permute-start(bf16[2,64,512]{2,1,0:T(8,128)(2,1)S(1)} %get-tuple-element.64), channel_id=1, source_target_pairs={{0,4},{1,5},{2,6},{3,7},{4,0},{5,1},{6,2},{7,3},{8,12},{9,13},{10,... | collective-permute-start | bytes 393224 | tf_op jit(solution)/shard_map/ppermute | solution.py:576
  125.9 3.7 %collective-permute-done.32.refs_5_ = bf16[2,64,512]{2,1,0:T(8,128)(2,1)S(1)} collective-permute-done((bf16[2,64,512]{2,1,0:T(8,128)(2,1)S(1)}, bf16[2,64,512]{2,1,0:T(8,128)(2,1)S(1)}, u32[]{:S(2)}, u32[]{:S(2)}) %collective-permute-start.32) | collective-permute-done | bytes 131104 | tf_op jit(solution)/shard_map/ppermute | solution.py:576
  130.1 0.9 collective-permute-done.33.refs_6_
  131.0 3.6 %collective-permute-done.34.refs_7_ = bf16[2,64,512]{2,1,0:T(8,128)(2,1)S(1)} collective-permute-done((bf16[2,64,512]{2,1,0:T(8,128)(2,1)S(1)}, bf16[2,64,512]{2,1,0:T(8,128)(2,1)S(1)}, u32[]{:S(2)}, u32[]{:S(2)}) %collective-permute-start.34) | collective-permute-done | bytes 131104 | tf_op jit(solution)/shard_map/ppermute | solution.py:576
  134.6 0.8 collective-permute-done.31.refs_3_
  135.4 2.0 %finish.1 = (bf16[64,4096]{1,0:T(8,128)(2,1)}, f32[32,64]{1,0:T(8,128)}, bf16[64,4096]{1,0:T(8,128)(2,1)}) custom-call(s32[3]{0:T(128)S(1)} %pad_add_fusion.place_ref, bf16[64,4096]{1,0:T(8,128)(2,1)S(1)} %get-tuple-element.45.grad_ref, bf16[64,4224]{1,0:T(8,128)(2,1)S(1)} %get-tuple-element.57.refs_0_, ...), custom_call_target="tpu_custom_call" | custom-call | tf_op jit(solution)/shard_map/finish/pallas_call | solution.py:522
  (66 shorter events, 6.8 us)
Async XLA Ops:
  0.6 15.6 %collective-permute-start.4 = (bf16[64,4096]{1,0:T(8,128)(2,1)}, bf16[64,4096]{1,0:T(8,128)(2,1)S(1)}, u32[]{:S(2)}, u32[]{:S(2)}) collective-permute-start(bf16[64,4096]{1,0:T(8,128)(2,1)} %bitcast.9), channel_id=1, source_target_pairs={{0,96},{1,25},{2,98},{3,27},{4,100},{5,29},{6,102},{7,31},{8,104},... | collective-permute-start | bytes 1572872 | tf_op jit(solution)/shard_map/ppermute | solution.py:543
  3.5 12.6 %collective-permute-start.3 = (bf16[64,4096]{1,0:T(8,128)(2,1)}, bf16[64,4096]{1,0:T(8,128)(2,1)S(1)}, u32[]{:S(2)}, u32[]{:S(2)}) collective-permute-start(bf16[64,4096]{1,0:T(8,128)(2,1)} %bitcast.10), channel_id=1, source_target_pairs={{0,64},{1,17},{2,66},{3,19},{4,68},{5,21},{6,70},{7,23},{8,72},{9,... | collective-permute-start | bytes 1572872 | tf_op jit(solution)/shard_map/ppermute | solution.py:543
  4.3 15.7 %collective-permute-start.2 = (bf16[64,4096]{1,0:T(8,128)(2,1)}, bf16[64,4096]{1,0:T(8,128)(2,1)S(1)}, u32[]{:S(2)}, u32[]{:S(2)}) collective-permute-start(bf16[64,4096]{1,0:T(8,128)(2,1)} %bitcast.11), channel_id=1, source_target_pairs={{0,32},{1,9},{2,34},{3,11},{4,36},{5,13},{6,38},{7,15},{8,40},{9,1... | collective-permute-start | bytes 1572872 | tf_op jit(solution)/shard_map/ppermute | solution.py:543
  6.3 4.3 %collective-permute-start.1 = (s32[32]{0:T(128)S(1)}, s32[32]{0:T(128)S(1)}, u32[]{:S(2)}, u32[]{:S(2)}) collective-permute-start(s32[32]{0:T(128)S(1)} %get-tuple-element.95.refs_0_.code_ref), channel_id=1, source_target_pairs={{0,24},{1,97},{2,26},{3,99},{4,28},{5,101},{6,30},{7,103},{8,0},{9... | collective-permute-start | bytes 392 | tf_op jit(solution)/shard_map/ppermute | solution.py:543
  9.3 5.1 %collective-permute-start = (s32[32]{0:T(128)S(1)}, s32[32]{0:T(128)S(1)}, u32[]{:S(2)}, u32[]{:S(2)}) collective-permute-start(s32[32]{0:T(128)S(1)} %get-tuple-element.96.refs_6_.code_ref), channel_id=1, source_target_pairs={{0,16},{1,65},{2,18},{3,67},{4,20},{5,69},{6,22},{7,71},{8,24},{9,... | collective-permute-start | bytes 392 | tf_op jit(solution)/shard_map/ppermute | solution.py:543
  10.6 14.8 %collective-permute-start.7 = (s32[32]{0:T(128)S(1)}, s32[32]{0:T(128)S(1)}, u32[]{:S(2)}, u32[]{:S(2)}) collective-permute-start(s32[32]{0:T(128)S(1)} %get-tuple-element.94.refs_1_.code_ref), channel_id=1, source_target_pairs={{0,8},{1,33},{2,10},{3,35},{4,12},{5,37},{6,14},{7,39},{8,16},{9,4... | collective-permute-start | bytes 392 | tf_op jit(solution)/shard_map/ppermute | solution.py:543
  11.5 1.0 copy-start.3
  20.8 34.1 %collective-permute-start.5 = (bf16[32,64,256]{2,1,0:T(8,128)(2,1)S(1)}, bf16[32,64,256]{2,1,0:T(8,128)(2,1)S(1)}, u32[]{:S(2)}, u32[]{:S(2)}) collective-permute-start(bf16[32,64,256]{2,1,0:T(8,128)(2,1)S(1)} %gather_blocks.4.refs_4_), channel_id=1, source_target_pairs={{0,16},{1,65},{2,18},{3,67},{4,20},{5,69},{6,22},{7,71},{8,24},{9,... | collective-permute-start | bytes 3145736 | tf_op jit(solution)/shard_map/ppermute | solution.py:543
  24.7 24.5 %collective-permute-start.6 = (bf16[32,64,256]{2,1,0:T(8,128)(2,1)S(1)}, bf16[32,64,256]{2,1,0:T(8,128)(2,1)S(1)}, u32[]{:S(2)}, u32[]{:S(2)}) collective-permute-start(bf16[32,64,256]{2,1,0:T(8,128)(2,1)S(1)} %gather_blocks.5.refs_4_), channel_id=1, source_target_pairs={{0,8},{1,33},{2,10},{3,35},{4,12},{5,37},{6,14},{7,39},{8,16},{9,4... | collective-permute-start | bytes 3145736 | tf_op jit(solution)/shard_map/ppermute | solution.py:543
  26.2 23.0 %collective-permute-start.8 = (bf16[32,64,256]{2,1,0:T(8,128)(2,1)S(1)}, bf16[32,64,256]{2,1,0:T(8,128)(2,1)S(1)}, u32[]{:S(2)}, u32[]{:S(2)}) collective-permute-start(bf16[32,64,256]{2,1,0:T(8,128)(2,1)S(1)} %gather_blocks.6.refs_4_), channel_id=1, source_target_pairs={{0,24},{1,97},{2,26},{3,99},{4,28},{5,101},{6,30},{7,103},{8,0},{9... | collective-permute-start | bytes 3145736 | tf_op jit(solution)/shard_map/ppermute | solution.py:543
  29.6 3.8 %copy-start.5 = (bf16[4096,64]{0,1:T(8,128)(2,1)S(1)}, bf16[4096,64]{0,1:T(8,128)(2,1)}, u32[]{:S(2)}) copy-start(bf16[4096,64]{0,1:T(8,128)(2,1)} %param.13) | copy-start | bytes 1572868
  33.9 1.6 %collective-permute-start.9 = (bf16[4,64,512]{2,1,0:T(8,128)(2,1)S(1)}, bf16[4,64,512]{2,1,0:T(8,128)(2,1)S(1)}, u32[]{:S(2)}, u32[]{:S(2)}) collective-permute-start(bf16[4,64,512]{2,1,0:T(8,128)(2,1)S(1)} %get-tuple-element.37), channel_id=1, source_target_pairs={{0,1},{1,0},{2,3},{3,2},{4,5},{5,4},{6,7},{7,6},{8,9},{9,8},{10,11... | collective-permute-start | bytes 786440 | tf_op jit(solution)/shard_map/ppermute | solution.py:571
  35.6 7.9 %collective-permute-start.10 = (bf16[2,64,512]{2,1,0:T(8,128)(2,1)S(1)}, bf16[2,64,512]{2,1,0:T(8,128)(2,1)S(1)}, u32[]{:S(2)}, u32[]{:S(2)}) collective-permute-start(bf16[2,64,512]{2,1,0:T(8,128)(2,1)S(1)} %pad_maximum_fusion.1), channel_id=1, source_target_pairs={{0,2},{1,3},{2,4},{3,5},{4,6},{5,7},{6,0},{7,1},{8,10},{9,11},{10,... | collective-permute-start | bytes 393224 | tf_op jit(solution)/shard_map/ppermute | solution.py:576
  37.6 9.9 %collective-permute-start.11 = (bf16[2,64,512]{2,1,0:T(8,128)(2,1)S(1)}, bf16[2,64,512]{2,1,0:T(8,128)(2,1)S(1)}, u32[]{:S(2)}, u32[]{:S(2)}) collective-permute-start(bf16[2,64,512]{2,1,0:T(8,128)(2,1)S(1)} %pad_maximum_fusion.2), channel_id=1, source_target_pairs={{0,4},{1,5},{2,6},{3,7},{4,0},{5,1},{6,2},{7,3},{8,12},{9,13},{10,... | collective-permute-start | bytes 393224 | tf_op jit(solution)/shard_map/ppermute | solution.py:576
  43.5 5.1 %collective-permute-start.12 = (bf16[2,64,512]{2,1,0:T(8,128)(2,1)S(1)}, bf16[2,64,512]{2,1,0:T(8,128)(2,1)S(1)}, u32[]{:S(2)}, u32[]{:S(2)}) collective-permute-start(bf16[2,64,512]{2,1,0:T(8,128)(2,1)S(1)} %pad_maximum_fusion.3), channel_id=1, source_target_pairs={{0,6},{1,7},{2,0},{3,1},{4,2},{5,3},{6,4},{7,5},{8,14},{9,15},{10,... | collective-permute-start | bytes 393224 | tf_op jit(solution)/shard_map/ppermute | solution.py:576
  49.1 5.8 %copy-start.4 = (bf16[4096,64]{0,1:T(8,128)(2,1)S(1)}, bf16[4096,64]{0,1:T(8,128)(2,1)}, u32[]{:S(2)}) copy-start(bf16[4096,64]{0,1:T(8,128)(2,1)} %param.7) | copy-start | bytes 1572868
  54.9 4.3 %copy-start = (bf16[4,8,256,256]{3,2,1,0:T(8,128)(2,1)}, bf16[4,8,256,256]{3,2,1,0:T(8,128)(2,1)S(1)}, u32[]{:S(2)}) copy-start(bf16[4,8,256,256]{3,2,1,0:T(8,128)(2,1)S(1)} %get-tuple-element.38.tiles_ref.refs_5_) | copy-start | bytes 12582916
  54.9 10.7 %copy-start.2 = (bf16[512,512]{1,0:T(8,128)(2,1)S(1)}, bf16[512,512]{1,0:T(8,128)(2,1)}, u32[]{:S(2)}) copy-start(bf16[512,512]{1,0:T(8,128)(2,1)} %refs_5_.1) | copy-start | bytes 1572868
  57.6 1.6 %collective-permute-start.13 = (bf16[4,64,512]{2,1,0:T(8,128)(2,1)S(1)}, bf16[4,64,512]{2,1,0:T(8,128)(2,1)S(1)}, u32[]{:S(2)}, u32[]{:S(2)}) collective-permute-start(bf16[4,64,512]{2,1,0:T(8,128)(2,1)S(1)} %get-tuple-element.41), channel_id=1, source_target_pairs={{0,1},{1,0},{2,3},{3,2},{4,5},{5,4},{6,7},{7,6},{8,9},{9,8},{10,11... | collective-permute-start | bytes 786440 | tf_op jit(solution)/shard_map/ppermute | solution.py:571
  59.2 7.5 %collective-permute-start.14 = (bf16[2,64,512]{2,1,0:T(8,128)(2,1)S(1)}, bf16[2,64,512]{2,1,0:T(8,128)(2,1)S(1)}, u32[]{:S(2)}, u32[]{:S(2)}) collective-permute-start(bf16[2,64,512]{2,1,0:T(8,128)(2,1)S(1)} %pad_maximum_fusion.5), channel_id=1, source_target_pairs={{0,2},{1,3},{2,4},{3,5},{4,6},{5,7},{6,0},{7,1},{8,10},{9,11},{10,... | collective-permute-start | bytes 393224 | tf_op jit(solution)/shard_map/ppermute | solution.py:576
  60.8 9.9 %collective-permute-start.15 = (bf16[2,64,512]{2,1,0:T(8,128)(2,1)S(1)}, bf16[2,64,512]{2,1,0:T(8,128)(2,1)S(1)}, u32[]{:S(2)}, u32[]{:S(2)}) collective-permute-start(bf16[2,64,512]{2,1,0:T(8,128)(2,1)S(1)} %pad_maximum_fusion.6), channel_id=1, source_target_pairs={{0,4},{1,5},{2,6},{3,7},{4,0},{5,1},{6,2},{7,3},{8,12},{9,13},{10,... | collective-permute-start | bytes 393224 | tf_op jit(solution)/shard_map/ppermute | solution.py:576
  64.6 6.2 %collective-permute-start.16 = (bf16[2,64,512]{2,1,0:T(8,128)(2,1)S(1)}, bf16[2,64,512]{2,1,0:T(8,128)(2,1)S(1)}, u32[]{:S(2)}, u32[]{:S(2)}) collective-permute-start(bf16[2,64,512]{2,1,0:T(8,128)(2,1)S(1)} %pad_maximum_fusion.7), channel_id=1, source_target_pairs={{0,6},{1,7},{2,0},{3,1},{4,2},{5,3},{6,4},{7,5},{8,14},{9,15},{10,... | collective-permute-start | bytes 393224 | tf_op jit(solution)/shard_map/ppermute | solution.py:576
  65.8 21.0 %copy-start.1 = (bf16[4,8,256,256]{3,2,1,0:T(8,128)(2,1)S(1)}, bf16[4,8,256,256]{3,2,1,0:T(8,128)(2,1)}, u32[]{:S(2)}) copy-start(bf16[4,8,256,256]{3,2,1,0:T(8,128)(2,1)} %copy-done) | copy-start | bytes 12582916
  73.0 2.4 %collective-permute-start.17 = (bf16[4,192,512]{2,1,0:T(8,128)(2,1)S(1)}, bf16[4,192,512]{2,1,0:T(8,128)(2,1)S(1)}, u32[]{:S(2)}, u32[]{:S(2)}) collective-permute-start(bf16[4,192,512]{2,1,0:T(8,128)(2,1)S(1)} %get-tuple-element.43), channel_id=1, source_target_pairs={{0,1},{1,0},{2,3},{3,2},{4,5},{5,4},{6,7},{7,6},{8,9},{9,8},{10,11... | collective-permute-start | bytes 2359304 | tf_op jit(solution)/shard_map/ppermute | solution.py:571
  75.4 7.2 %collective-permute-start.18 = (bf16[2,64,512]{2,1,0:T(8,128)(2,1)S(1)}, bf16[2,64,512]{2,1,0:T(8,128)(2,1)S(1)}, u32[]{:S(2)}, u32[]{:S(2)}) collective-permute-start(bf16[2,64,512]{2,1,0:T(8,128)(2,1)S(1)} %pad_maximum_fusion.9), channel_id=1, source_target_pairs={{0,2},{1,3},{2,4},{3,5},{4,6},{5,7},{6,0},{7,1},{8,10},{9,11},{10,... | collective-permute-start | bytes 393224 | tf_op jit(solution)/shard_map/ppermute | solution.py:576
  76.8 9.4 %collective-permute-start.19 = (bf16[2,64,512]{2,1,0:T(8,128)(2,1)S(1)}, bf16[2,64,512]{2,1,0:T(8,128)(2,1)S(1)}, u32[]{:S(2)}, u32[]{:S(2)}) collective-permute-start(bf16[2,64,512]{2,1,0:T(8,128)(2,1)S(1)} %pad_maximum_fusion.10), channel_id=1, source_target_pairs={{0,4},{1,5},{2,6},{3,7},{4,0},{5,1},{6,2},{7,3},{8,12},{9,13},{10,... | collective-permute-start | bytes 393224 | tf_op jit(solution)/shard_map/ppermute | solution.py:576
  79.2 7.6 %collective-permute-start.20 = (bf16[2,64,512]{2,1,0:T(8,128)(2,1)S(1)}, bf16[2,64,512]{2,1,0:T(8,128)(2,1)S(1)}, u32[]{:S(2)}, u32[]{:S(2)}) collective-permute-start(bf16[2,64,512]{2,1,0:T(8,128)(2,1)S(1)} %pad_maximum_fusion.11), channel_id=1, source_target_pairs={{0,6},{1,7},{2,0},{3,1},{4,2},{5,3},{6,4},{7,5},{8,14},{9,15},{10,... | collective-permute-start | bytes 393224 | tf_op jit(solution)/shard_map/ppermute | solution.py:576
  80.6 15.4 %collective-permute-start.21 = (bf16[2,64,512]{2,1,0:T(8,128)(2,1)S(1)}, bf16[2,64,512]{2,1,0:T(8,128)(2,1)S(1)}, u32[]{:S(2)}, u32[]{:S(2)}) collective-permute-start(bf16[2,64,512]{2,1,0:T(8,128)(2,1)S(1)} %get-tuple-element.49), channel_id=1, source_target_pairs={{0,2},{1,3},{2,0},{3,1},{4,6},{5,7},{6,4},{7,5},{8,10},{9,11},{10,... | collective-permute-start | bytes 393224 | tf_op jit(solution)/shard_map/ppermute | solution.py:337
  88.7 20.8 %collective-permute-start.25 = (bf16[32,64,256]{2,1,0:T(8,128)(2,1)S(1)}, bf16[32,64,256]{2,1,0:T(8,128)(2,1)S(1)}, u32[]{:S(2)}, u32[]{:S(2)}) collective-permute-start(bf16[32,64,256]{2,1,0:T(8,128)(2,1)S(1)} %get-tuple-element.50.after_ref), channel_id=1, source_target_pairs={{0,16},{1,65},{2,18},{3,67},{4,20},{5,69},{6,22},{7,71},{8,24},{9,... | collective-permute-start | bytes 3145736 | tf_op jit(solution)/shard_map/ppermute | solution.py:543
  94.7 21.6 %collective-permute-start.23 = (bf16[32,64,256]{2,1,0:T(8,128)(2,1)S(1)}, bf16[32,64,256]{2,1,0:T(8,128)(2,1)S(1)}, u32[]{:S(2)}, u32[]{:S(2)}) collective-permute-start(bf16[32,64,256]{2,1,0:T(8,128)(2,1)S(1)} %back_products.6), channel_id=1, source_target_pairs={{0,24},{1,97},{2,26},{3,99},{4,28},{5,101},{6,30},{7,103},{8,0},{9... | collective-permute-start | bytes 3145736 | tf_op jit(solution)/shard_map/ppermute | solution.py:543
  99.3 18.1 %collective-permute-start.22 = (bf16[32,64,256]{2,1,0:T(8,128)(2,1)S(1)}, bf16[32,64,256]{2,1,0:T(8,128)(2,1)S(1)}, u32[]{:S(2)}, u32[]{:S(2)}) collective-permute-start(bf16[32,64,256]{2,1,0:T(8,128)(2,1)S(1)} %back_products.5.after_ref), channel_id=1, source_target_pairs={{0,8},{1,33},{2,10},{3,35},{4,12},{5,37},{6,14},{7,39},{8,16},{9,4... | collective-permute-start | bytes 3145736 | tf_op jit(solution)/shard_map/ppermute | solution.py:543
  100.1 5.8 %collective-permute-start.24 = (bf16[1,64,512]{2,1,0:T(8,128)(2,1)S(1)}, bf16[1,64,512]{2,1,0:T(8,128)(2,1)S(1)}, u32[]{:S(2)}, u32[]{:S(2)}) collective-permute-start(bf16[1,64,512]{2,1,0:T(8,128)(2,1)S(1)} %get-tuple-element.52), channel_id=1, source_target_pairs={{0,4},{1,5},{2,6},{3,7},{4,0},{5,1},{6,2},{7,3},{8,12},{9,13},{10,... | collective-permute-start | bytes 196616 | tf_op jit(solution)/shard_map/ppermute | solution.py:337
  106.7 10.7 %collective-permute-start.26 = (bf16[64,128]{1,0:T(8,128)(2,1)S(1)}, bf16[64,128]{1,0:T(8,128)(2,1)S(1)}, u32[]{:S(2)}, u32[]{:S(2)}) collective-permute-start(bf16[64,128]{1,0:T(8,128)(2,1)S(1)} %get-tuple-element.54), channel_id=1, source_target_pairs={{0,24},{1,97},{2,26},{3,99},{4,28},{5,101},{6,30},{7,103},{8,0},{9... | collective-permute-start | bytes 49160 | tf_op jit(solution)/shard_map/ppermute | solution.py:543
  109.2 8.2 %collective-permute-start.27 = (bf16[64,128]{1,0:T(8,128)(2,1)S(1)}, bf16[64,128]{1,0:T(8,128)(2,1)S(1)}, u32[]{:S(2)}, u32[]{:S(2)}) collective-permute-start(bf16[64,128]{1,0:T(8,128)(2,1)S(1)} %get-tuple-element.55), channel_id=1, source_target_pairs={{0,16},{1,65},{2,18},{3,67},{4,20},{5,69},{6,22},{7,71},{8,24},{9,... | collective-permute-start | bytes 49160 | tf_op jit(solution)/shard_map/ppermute | solution.py:543
  109.5 7.9 %collective-permute-start.28 = (bf16[64,128]{1,0:T(8,128)(2,1)S(1)}, bf16[64,128]{1,0:T(8,128)(2,1)S(1)}, u32[]{:S(2)}, u32[]{:S(2)}) collective-permute-start(bf16[64,128]{1,0:T(8,128)(2,1)S(1)} %get-tuple-element.56), channel_id=1, source_target_pairs={{0,8},{1,33},{2,10},{3,35},{4,12},{5,37},{6,14},{7,39},{8,16},{9,4... | collective-permute-start | bytes 49160 | tf_op jit(solution)/shard_map/ppermute | solution.py:543
  118.7 15.9 %collective-permute-start.30 = (bf16[64,4224]{1,0:T(8,128)(2,1)S(1)}, bf16[64,4224]{1,0:T(8,128)(2,1)S(1)}, u32[]{:S(2)}, u32[]{:S(2)}) collective-permute-start(bf16[64,4224]{1,0:T(8,128)(2,1)S(1)} %get-tuple-element.59), channel_id=1, source_target_pairs={{0,64},{1,17},{2,66},{3,19},{4,68},{5,21},{6,70},{7,23},{8,72},{9,... | collective-permute-start | bytes 1622024 | tf_op jit(solution)/shard_map/ppermute | solution.py:543
  119.6 15.8 %collective-permute-start.31 = (bf16[64,4224]{1,0:T(8,128)(2,1)S(1)}, bf16[64,4224]{1,0:T(8,128)(2,1)S(1)}, u32[]{:S(2)}, u32[]{:S(2)}) collective-permute-start(bf16[64,4224]{1,0:T(8,128)(2,1)S(1)} %get-tuple-element.60), channel_id=1, source_target_pairs={{0,32},{1,9},{2,34},{3,11},{4,36},{5,13},{6,38},{7,15},{8,40},{9,1... | collective-permute-start | bytes 1622024 | tf_op jit(solution)/shard_map/ppermute | solution.py:543
  120.2 15.2 %collective-permute-start.29 = (bf16[64,4224]{1,0:T(8,128)(2,1)S(1)}, bf16[64,4224]{1,0:T(8,128)(2,1)S(1)}, u32[]{:S(2)}, u32[]{:S(2)}) collective-permute-start(bf16[64,4224]{1,0:T(8,128)(2,1)S(1)} %get-tuple-element.58.after_ref), channel_id=1, source_target_pairs={{0,96},{1,25},{2,98},{3,27},{4,100},{5,29},{6,102},{7,31},{8,104},... | collective-permute-start | bytes 1622024 | tf_op jit(solution)/shard_map/ppermute | solution.py:543
  122.8 6.8 %collective-permute-start.32 = (bf16[2,64,512]{2,1,0:T(8,128)(2,1)S(1)}, bf16[2,64,512]{2,1,0:T(8,128)(2,1)S(1)}, u32[]{:S(2)}, u32[]{:S(2)}) collective-permute-start(bf16[2,64,512]{2,1,0:T(8,128)(2,1)S(1)} %get-tuple-element.63), channel_id=1, source_target_pairs={{0,2},{1,3},{2,4},{3,5},{4,6},{5,7},{6,0},{7,1},{8,10},{9,11},{10,... | collective-permute-start | bytes 393224 | tf_op jit(solution)/shard_map/ppermute | solution.py:576
  123.5 7.5 %collective-permute-start.33 = (bf16[2,64,512]{2,1,0:T(8,128)(2,1)S(1)}, bf16[2,64,512]{2,1,0:T(8,128)(2,1)S(1)}, u32[]{:S(2)}, u32[]{:S(2)}) collective-permute-start(bf16[2,64,512]{2,1,0:T(8,128)(2,1)S(1)} %get-tuple-element.64), channel_id=1, source_target_pairs={{0,4},{1,5},{2,6},{3,7},{4,0},{5,1},{6,2},{7,3},{8,12},{9,13},{10,... | collective-permute-start | bytes 393224 | tf_op jit(solution)/shard_map/ppermute | solution.py:576
  129.6 5.0 %collective-permute-start.34 = (bf16[2,64,512]{2,1,0:T(8,128)(2,1)S(1)}, bf16[2,64,512]{2,1,0:T(8,128)(2,1)S(1)}, u32[]{:S(2)}, u32[]{:S(2)}) collective-permute-start(bf16[2,64,512]{2,1,0:T(8,128)(2,1)S(1)} %get-tuple-element.65), channel_id=1, source_target_pairs={{0,6},{1,7},{2,0},{3,1},{4,2},{5,3},{6,4},{7,5},{8,14},{9,15},{10,... | collective-permute-start | bytes 393224 | tf_op jit(solution)/shard_map/ppermute | solution.py:576

commit v8 on v7

--- a/solution.py
+++ b/solution.py
@@ -11,6 +11,7 @@
 SLOTS = 8
 SIDE = 4
 PART = SIDE * SLOTS
+LANES = 128
 VMEM_LIMIT = 16 * 1024 * 1024
 TILES_VMEM_LIMIT = 38 * 1024 * 1024
 GELU_C = 0.7978845608028654
@@ -106,43 +107,43 @@
     pltpu.make_async_copy(tiles_ref.at[pl.ds(0, SLOTS)], buf_ref.at[group], sems.at[group]).wait()
 
 
-def add_products(codes, recvs, buf_ref, total_ref, wait):
-    ones = jnp.ones((16, BLK), jnp.bfloat16)
-    for part, (code_ref, recv_ref) in enumerate(zip(codes, recvs)):
-
-        def step(d, carry):
-            group = part * SIDE + d
-            wait(group)
-            for s in range(SLOTS):
-                q = d * SLOTS + s
-                code = code_ref[q]
-                flag = (code >> 15).astype(jnp.float32).astype(jnp.bfloat16)
-                left = jnp.concatenate([recv_ref[q], ones], axis=0) * flag
-                start = pl.multiple_of(row_block_of(code) * BLK, BLK)
-                total_ref[:, pl.ds(start, BLK)] += lax.dot_general(
-                    left, buf_ref[group, s], (((1,), (1,)), ((), ())), preferred_element_type=jnp.float32
-                )
-            return carry
-
-        lax.fori_loop(0, SIDE, step, 0)
-
-
-def spread_kernel(parts, first, *refs):
-    codes, recvs, tiles_ref = refs[:parts], refs[parts : 2 * parts], refs[2 * parts]
-    if first:
-        total_ref, buf_ref, sems = refs[2 * parts + 1 :]
-    else:
-        before_ref, next_code_ref, _, total_ref, next_ref, buf_ref, sems, next_sems = refs[2 * parts + 1 :]
-    load_tiles(codes, tiles_ref, buf_ref, sems)
-    if first:
-        total_ref[...] = jnp.zeros_like(total_ref)
-    else:
-        load_tiles([next_code_ref], tiles_ref, next_ref, next_sems)
-        total_ref[...] = before_ref[...]
-    add_products(codes, recvs, buf_ref, total_ref, lambda group: wait_tiles(tiles_ref, buf_ref, sems, group))
-    if not first:
-        for d in range(SIDE):
-            wait_tiles(tiles_ref, next_ref, next_sems, d)
+def add_products(code_ref, recv_ref, tiles_ref, total_ref, wait):
+    ones = jnp.ones((LANES - recv_ref.shape[1], BLK), jnp.bfloat16)
+
+    def step(d, carry):
+        wait(d)
+        for s in range(SLOTS):
+            q = d * SLOTS + s
+            code = code_ref[q]
+            flag = (code >> 15).astype(jnp.float32).astype(jnp.bfloat16)
+            right = jnp.concatenate([recv_ref[q], ones], axis=0) * flag
+            start = pl.multiple_of(row_block_of(code) * BLK, BLK)
+            total_ref[pl.ds(start, BLK), :] += lax.dot_general(
+                tiles_ref[d, s], right, (((1,), (1,)), ((), ())), preferred_element_type=jnp.float32
+            )
+        return carry
+
+    lax.fori_loop(0, SIDE, step, 0)
+
+
+def first_spread_kernel(code_ref, next1_ref, next2_ref, recv_ref, tiles_ref, *refs):
+    total_ref, tiles1_ref, tiles2_ref, buf_ref, sems, sems1, sems2 = refs
+    load_tiles([code_ref], tiles_ref, buf_ref, sems)
+    load_tiles([next1_ref], tiles_ref, tiles1_ref, sems1)
+    load_tiles([next2_ref], tiles_ref, tiles2_ref, sems2)
+    total_ref[...] = jnp.zeros_like(total_ref)
+    add_products(code_ref, recv_ref, buf_ref, total_ref, lambda d: wait_tiles(tiles_ref, buf_ref, sems, d))
+    for d in range(SIDE):
+        wait_tiles(tiles_ref, tiles1_ref, sems1, d)
+        wait_tiles(tiles_ref, tiles2_ref, sems2, d)
+
+
+def spread_kernel(code1_ref, code2_ref, recv1_ref, recv2_ref, tiles1_ref, before_ref, tiles_ref, after_ref, *refs):
+    total_ref, buf_ref, sems = refs
+    load_tiles([code2_ref], tiles_ref, buf_ref, sems)
+    total_ref[...] = before_ref[...]
+    add_products(code1_ref, recv1_ref, tiles1_ref, total_ref, lambda d: None)
+    add_products(code2_ref, recv2_ref, buf_ref, total_ref, lambda d: wait_tiles(tiles_ref, buf_ref, sems, d))
 
 
 def tile_scratch(parts):
@@ -152,44 +153,43 @@
     ]
 
 
-def first_spread(code, recv, tile_vals):
-    total = jax.ShapeDtypeStruct((recv.shape[1] + 16, SIDE * SIDE * BLK), jnp.float32)
-    return pl.pallas_call(
-        functools.partial(spread_kernel, 1, True),
-        out_shape=total,
-        in_specs=scalars(1) + arrays(1) + anywhere(1),
+def first_spread(code, recv, tile_vals, next_codes):
+    tiles = jax.ShapeDtypeStruct((SIDE, SLOTS, BLK, BLK), jnp.bfloat16)
+    return pl.pallas_call(
+        first_spread_kernel,
+        out_shape=(jax.ShapeDtypeStruct((SIDE * SIDE * BLK, LANES), jnp.float32), tiles, tiles),
+        in_specs=scalars(3) + arrays(1) + anywhere(1),
+        out_specs=tuple(arrays(3)),
+        scratch_shapes=tile_scratch(1) + [pltpu.SemaphoreType.DMA((SIDE,))] * 2,
+        compiler_params=params(TILES_VMEM_LIMIT),
+        name="spread",
+    )(code, *next_codes, recv, tile_vals)
+
+
+def spread(codes, recvs, tiles, before, tile_vals, after):
+    return pl.pallas_call(
+        spread_kernel,
+        out_shape=jax.ShapeDtypeStruct(before.shape, before.dtype),
+        in_specs=scalars(2) + arrays(4) + anywhere(2),
         out_specs=arrays(1)[0],
         scratch_shapes=tile_scratch(1),
         compiler_params=params(TILES_VMEM_LIMIT),
         name="spread",
-    )(code, recv, tile_vals)
-
-
-def spread(codes, recvs, tile_vals, before, next_code, after):
-    parts = len(codes)
-    tiles = jax.ShapeDtypeStruct((SIDE, SLOTS, BLK, BLK), jnp.bfloat16)
-    return pl.pallas_call(
-        functools.partial(spread_kernel, parts, False),
-        out_shape=(jax.ShapeDtypeStruct(before.shape, before.dtype), tiles),
-        in_specs=scalars(parts) + arrays(parts) + anywhere(1) + arrays(1) + scalars(1) + anywhere(1),
-        out_specs=tuple(arrays(2)),
-        scratch_shapes=tile_scratch(parts) + [pltpu.SemaphoreType.DMA((SIDE,))],
-        compiler_params=params(TILES_VMEM_LIMIT),
-        name="spread",
-    )(*codes, *recvs, tile_vals, before, next_code, after)
+    )(*codes, *recvs, tiles, before, tile_vals, after)
 
 
 def mixed_kernel(place_ref, code_ref, recv_ref, tiles_ref, before_ref, feats_ref, after_ref, *refs):
     own_ref, other_ref, scale_ref, total_ref = refs
     total_ref[...] = before_ref[...]
-    add_products([code_ref], [recv_ref], tiles_ref, total_ref, lambda group: None)
+    add_products(code_ref, recv_ref, tiles_ref, total_ref, lambda d: None)
     _, width, chunk = own_ref.shape
-    scale_ref[...] = lax.rsqrt(1.0 + total_ref[width : width + 1, :])
     for dz in range(SIDE):
         for other, out_ref in enumerate((own_ref, other_ref)):
-            start = chunk_ahead(place_ref, dz, other) * chunk
-            part = pl.ds(pl.multiple_of(start, chunk), chunk)
-            mixed = feats_ref[:, part].astype(jnp.float32) + scale_ref[:, part] * total_ref[:width, part]
+            part = pl.ds(pl.multiple_of(chunk_ahead(place_ref, dz, other) * chunk, chunk), chunk)
+            total = total_ref[part, :].T
+            scale = lax.rsqrt(1.0 + total[width : width + 1, :])
+            scale_ref[:, part] = scale
+            mixed = feats_ref[:, part].astype(jnp.float32) + scale * total[:width, :]
             out_ref[dz] = mixed.astype(jnp.bfloat16)
 
 
@@ -620,9 +620,9 @@
         sent = gather_blocks(asked[e], slabs, [sent])
         recv[e] = shift(sent, False, e)
     recv[0] = gather_blocks(asked[0], slabs, [sent])
-    total = first_spread(codes[0], recv[0], tile_vals)
+    total, near_tiles, far_tiles = first_spread(codes[0], recv[0], tile_vals, [codes[1], codes[2]])
     cot = join(place, regroup(*split(place, cotangent.T, total)), total)
-    total, far_tiles = spread([codes[1], codes[3]], [recv[1], recv[3]], tile_vals, total, codes[2], cot)
+    total = spread([codes[1], codes[3]], [recv[1], recv[3]], near_tiles, total, tile_vals, cot)
     own, other, scale = spread_mixed(place, codes[2], recv[2], far_tiles, total, feats_t, cot)
     hidden_own, own, other, gw_own = dense(place, regroup(own, other), cot, weight, weight_t)
 

time: 138 us -> 139 us (level)
  Pallas kernels: 36.3 us -> 37.7 us
    ppermute x12, starting transfers between devices: 23.2 us -> 20.7 us  [shift_z(): lax.ppermute(value, 'col', [(c, (c + 2 * dz) % chunks) for c in range(chu...]
    ppermute x12, waiting for transfers between devices: 23 us -> 25.5 us  [shift_z(): lax.ppermute(value, 'col', [(c, (c + 2 * dz) % chunks) for c in range(chu...]
    ppermute x18, waiting for transfers between devices: 13.8 us -> 11.9 us  [shift(): return lax.ppermute(value, ('row', 'col'), pairs)]
  transfers between devices with their start and end apart: 35 -> 35, of which waited for: 21 -> 19; matrix products, arithmetic and copies ran while one was open for 1% -> 1% of each run, Pallas kernels for 20% -> 21%
where the time goes in v8:
time: 139 us
  starting transfers between devices  54.4 us (39%)
  waiting for transfers between devices  42.8 us (31%)
  Pallas kernels  37.7 us (27%)
  local copies, waits for them, and re-layouts  1.47 us (1%)
    ppermute x18, starting transfers between devices, shift(): return lax.ppermute(value, ('row', 'col'), pairs)  29.1 us
    ppermute x12, waiting for transfers between devices, shift_z(): lax.ppermute(value, 'col', [(c, (c + 2 * dz) % chunks) for c in range(chu...  25.5 us
    ppermute x12, starting transfers between devices, shift_z(): lax.ppermute(value, 'col', [(c, (c + 2 * dz) % chunks) for c in range(chu...  20.7 us
    ppermute x18, waiting for transfers between devices, shift(): return lax.ppermute(value, ('row', 'col'), pairs)  11.9 us
    pallas_call x3, Pallas kernels, back_products(): pl.pallas_call(back_kernel, out_shape=jax.ShapeDtypeStruct((PART, scaled....  9.56 us
    pallas_call x1, Pallas kernels, first_spread(): pl.pallas_call(first_spread_kernel, out_shape=(jax.ShapeDtypeStruct((SIDE...  5.46 us
    ppermute x3, waiting for transfers between devices, swap_core(): return lax.ppermute(value, 'col', [(c, c ^ 1) for c in range(chunks)])  5.23 us
    pallas_call x1, Pallas kernels, spread(): pl.pallas_call(spread_kernel, out_shape=jax.ShapeDtypeStruct(before.shape...  4.84 us
  transfers between devices with their start and end apart: 35, of which 19 were waited for; matrix products, arithmetic and copies ran while one was open for 1% of the time, Pallas kernels for 21%

profile of v8, /device:TPU:0, one launch (start us, length us, event | category | flops | bytes accessed | tf_op | source)
XLA Modules:
  0.0 138.7 jit_solution(12188112272268829452)
XLA Ops:
  0.6 1.6 %collective-permute-start.2 = (bf16[64,4096]{1,0:T(8,128)(2,1)}, bf16[64,4096]{1,0:T(8,128)(2,1)S(1)}, u32[]{:S(2)}, u32[]{:S(2)}) collective-permute-start(bf16[64,4096]{1,0:T(8,128)(2,1)} %bitcast.9), channel_id=1, source_target_pairs={{0,32},{1,9},{2,34},{3,11},{4,36},{5,13},{6,38},{7,15},{8,40},{9,1... | collective-permute-start | bytes 1572872 | tf_op jit(solution)/shard_map/ppermute | solution.py:543
  2.3 2.7 %collective-permute-start.3 = (bf16[64,4096]{1,0:T(8,128)(2,1)}, bf16[64,4096]{1,0:T(8,128)(2,1)S(1)}, u32[]{:S(2)}, u32[]{:S(2)}) collective-permute-start(bf16[64,4096]{1,0:T(8,128)(2,1)} %bitcast.10), channel_id=1, source_target_pairs={{0,64},{1,17},{2,66},{3,19},{4,68},{5,21},{6,70},{7,23},{8,72},{9,... | collective-permute-start | bytes 1572872 | tf_op jit(solution)/shard_map/ppermute | solution.py:543
  5.0 1.4 %collective-permute-start.4 = (bf16[64,4096]{1,0:T(8,128)(2,1)}, bf16[64,4096]{1,0:T(8,128)(2,1)S(1)}, u32[]{:S(2)}, u32[]{:S(2)}) collective-permute-start(bf16[64,4096]{1,0:T(8,128)(2,1)} %bitcast.11), channel_id=1, source_target_pairs={{0,96},{1,25},{2,98},{3,27},{4,100},{5,29},{6,102},{7,31},{8,104},... | collective-permute-start | bytes 1572872 | tf_op jit(solution)/shard_map/ppermute | solution.py:543
  6.4 0.7 broadcast_select_fusion
  7.5 3.2 %collective-permute-start = (s32[32]{0:T(128)S(1)}, s32[32]{0:T(128)S(1)}, u32[]{:S(2)}, u32[]{:S(2)}) collective-permute-start(s32[32]{0:T(128)S(1)} %get-tuple-element.98.next2_ref.code_ref), channel_id=1, source_target_pairs={{0,16},{1,65},{2,18},{3,67},{4,20},{5,69},{6,22},{7,71},{8,24},{9,... | collective-permute-start | bytes 392 | tf_op jit(solution)/shard_map/ppermute | solution.py:543
  10.7 1.1 collective-permute-start.1
  11.8 2.6 %collective-permute-done.1.after_ref.code_ref.refs_0_ = s32[32]{0:T(128)S(1)} collective-permute-done((s32[32]{0:T(128)S(1)}, s32[32]{0:T(128)S(1)}, u32[]{:S(2)}, u32[]{:S(2)}) %collective-permute-start.1) | collective-permute-done | bytes 160 | tf_op jit(solution)/shard_map/ppermute | solution.py:543
  14.4 0.7 collective-permute-start.6
  15.0 1.0 copy-done.3
  16.1 1.9 %collective-permute-done.3.refs_2_ = bf16[64,4096]{1,0:T(8,128)(2,1)S(1)} collective-permute-done((bf16[64,4096]{1,0:T(8,128)(2,1)}, bf16[64,4096]{1,0:T(8,128)(2,1)S(1)}, u32[]{:S(2)}, u32[]{:S(2)}) %collective-permute-start.3) | collective-permute-done | bytes 524320 | tf_op jit(solution)/shard_map/ppermute | solution.py:543
  18.0 0.7 gather_blocks.4.refs_4_
  18.7 3.3 %collective-permute-start.5 = (bf16[32,64,256]{2,1,0:T(8,128)(2,1)S(1)}, bf16[32,64,256]{2,1,0:T(8,128)(2,1)S(1)}, u32[]{:S(2)}, u32[]{:S(2)}) collective-permute-start(bf16[32,64,256]{2,1,0:T(8,128)(2,1)S(1)} %gather_blocks.4.refs_4_), channel_id=1, source_target_pairs={{0,16},{1,65},{2,18},{3,67},{4,20},{5,69},{6,22},{7,71},{8,24},{9,... | collective-permute-start | bytes 3145736 | tf_op jit(solution)/shard_map/ppermute | solution.py:543
  22.0 0.7 gather_blocks.5.refs_4_
  22.7 0.7 collective-permute-start.7
  23.4 0.7 gather_blocks.6.refs_4_
  24.1 2.6 %collective-permute-start.8 = (bf16[32,64,256]{2,1,0:T(8,128)(2,1)S(1)}, bf16[32,64,256]{2,1,0:T(8,128)(2,1)S(1)}, u32[]{:S(2)}, u32[]{:S(2)}) collective-permute-start(bf16[32,64,256]{2,1,0:T(8,128)(2,1)S(1)} %gather_blocks.6.refs_4_), channel_id=1, source_target_pairs={{0,24},{1,97},{2,26},{3,99},{4,28},{5,101},{6,30},{7,103},{8,0},{9... | collective-permute-start | bytes 3145736 | tf_op jit(solution)/shard_map/ppermute | solution.py:543
  26.8 0.7 gather_blocks.7.recv_ref
  27.5 5.5 %spread.2 = (f32[4096,128]{1,0:T(8,128)S(1)}, bf16[4,8,256,256]{3,2,1,0:T(8,128)(2,1)S(1)}, bf16[4,8,256,256]{3,2,1,0:T(8,128)(2,1)S(1)}) custom-call(s32[32]{0:T(128)S(1)} %get-tuple-element.96.code_ref.refs_0_, s32[32]{0:T(128)S(1)} %get-tuple-element.97.next1_ref.code1_ref.code_ref, s32[32]{0:T(128)S(1)} %get-tuple-element.98.next2_ref.code_ref, ...), custom_call_target="tpu_custom_call" | custom-call | tf_op jit(solution)/shard_map/spread/pallas_call | solution.py:158
  33.0 0.6 split.1
  33.7 1.5 %collective-permute-done.9 = bf16[4,64,512]{2,1,0:T(8,128)(2,1)S(1)} collective-permute-done((bf16[4,64,512]{2,1,0:T(8,128)(2,1)S(1)}, bf16[4,64,512]{2,1,0:T(8,128)(2,1)S(1)}, u32[]{:S(2)}, u32[]{:S(2)}) %collective-permute-start.9) | collective-permute-done | bytes 262176 | tf_op jit(solution)/shard_map/ppermute | solution.py:571
  35.3 2.0 %collective-permute-start.10 = (bf16[2,64,512]{2,1,0:T(8,128)(2,1)S(1)}, bf16[2,64,512]{2,1,0:T(8,128)(2,1)S(1)}, u32[]{:S(2)}, u32[]{:S(2)}) collective-permute-start(bf16[2,64,512]{2,1,0:T(8,128)(2,1)S(1)} %pad_maximum_fusion.1), channel_id=1, source_target_pairs={{0,2},{1,3},{2,4},{3,5},{4,6},{5,7},{6,0},{7,1},{8,10},{9,11},{10,... | collective-permute-start | bytes 393224 | tf_op jit(solution)/shard_map/ppermute | solution.py:576
  37.3 3.7 %collective-permute-start.11 = (bf16[2,64,512]{2,1,0:T(8,128)(2,1)S(1)}, bf16[2,64,512]{2,1,0:T(8,128)(2,1)S(1)}, u32[]{:S(2)}, u32[]{:S(2)}) collective-permute-start(bf16[2,64,512]{2,1,0:T(8,128)(2,1)S(1)} %pad_maximum_fusion.2), channel_id=1, source_target_pairs={{0,4},{1,5},{2,6},{3,7},{4,0},{5,1},{6,2},{7,3},{8,12},{9,13},{10,... | collective-permute-start | bytes 393224 | tf_op jit(solution)/shard_map/ppermute | solution.py:576
  40.9 2.2 %collective-permute-done.10.refs_1_ = bf16[2,64,512]{2,1,0:T(8,128)(2,1)S(1)} collective-permute-done((bf16[2,64,512]{2,1,0:T(8,128)(2,1)S(1)}, bf16[2,64,512]{2,1,0:T(8,128)(2,1)S(1)}, u32[]{:S(2)}, u32[]{:S(2)}) %collective-permute-start.10) | collective-permute-done | bytes 131104 | tf_op jit(solution)/shard_map/ppermute | solution.py:576
  43.2 2.5 %collective-permute-start.12 = (bf16[2,64,512]{2,1,0:T(8,128)(2,1)S(1)}, bf16[2,64,512]{2,1,0:T(8,128)(2,1)S(1)}, u32[]{:S(2)}, u32[]{:S(2)}) collective-permute-start(bf16[2,64,512]{2,1,0:T(8,128)(2,1)S(1)} %pad_maximum_fusion.3), channel_id=1, source_target_pairs={{0,6},{1,7},{2,0},{3,1},{4,2},{5,3},{6,4},{7,5},{8,14},{9,15},{10,... | collective-permute-start | bytes 393224 | tf_op jit(solution)/shard_map/ppermute | solution.py:576
  45.7 1.4 %collective-permute-done.11.refs_2_ = bf16[2,64,512]{2,1,0:T(8,128)(2,1)S(1)} collective-permute-done((bf16[2,64,512]{2,1,0:T(8,128)(2,1)S(1)}, bf16[2,64,512]{2,1,0:T(8,128)(2,1)S(1)}, u32[]{:S(2)}, u32[]{:S(2)}) %collective-permute-start.11) | collective-permute-done | bytes 131104 | tf_op jit(solution)/shard_map/ppermute | solution.py:576
  47.1 1.1 collective-permute-done.12.refs_3_
  48.2 0.6 join.1.after_ref.refs_4_
  48.8 4.8 %spread.3.before_ref = f32[4096,128]{1,0:T(8,128)S(1)} custom-call(s32[32]{0:T(128)S(1)} %get-tuple-element.97.next1_ref.code1_ref.code_ref, s32[32]{0:T(128)S(1)} %get-tuple-element.95.code2_ref.code_ref, bf16[32,64,256]{2,1,0:T(8,128)(2,1)S(1)} %collective-permute-done.7.recv1_ref, bf16[32,64,256]{2,1,0:T(8,128)(2,1)S(1)} %collective-permute-done.8.recv2_ref, ...), custom_call_target="tpu_custom_call" | custom-call | tf_op jit(solution)/shard_map/spread/pallas_call | solution.py:170
  53.7 3.1 %spread_mixed.1 = (bf16[4,64,512]{2,1,0:T(8,128)(2,1)S(1)}, bf16[4,64,512]{2,1,0:T(8,128)(2,1)S(1)}, f32[1,4096]{1,0:T(1,128)S(1)}) custom-call(s32[3]{0:T(128)S(1)} %pad_add_fusion.place_ref, s32[32]{0:T(128)S(1)} %get-tuple-element.98.next2_ref.code_ref, bf16[32,64,256]{2,1,0:T(8,128)(2,1)S(1)} %collective-permute-done.5.recv_ref, ...), custom_call_target="tpu_custom_call" | custom-call | tf_op jit(solution)/shard_map/spread_mixed/pallas_call | solution.py:199
  57.0 1.5 %collective-permute-done.13 = bf16[4,64,512]{2,1,0:T(8,128)(2,1)S(1)} collective-permute-done((bf16[4,64,512]{2,1,0:T(8,128)(2,1)S(1)}, bf16[4,64,512]{2,1,0:T(8,128)(2,1)S(1)}, u32[]{:S(2)}, u32[]{:S(2)}) %collective-permute-start.13) | collective-permute-done | bytes 262176 | tf_op jit(solution)/shard_map/ppermute | solution.py:571
  58.5 0.7 collective-permute-start.14
  59.2 4.6 %collective-permute-start.15 = (bf16[2,64,512]{2,1,0:T(8,128)(2,1)S(1)}, bf16[2,64,512]{2,1,0:T(8,128)(2,1)S(1)}, u32[]{:S(2)}, u32[]{:S(2)}) collective-permute-start(bf16[2,64,512]{2,1,0:T(8,128)(2,1)S(1)} %pad_maximum_fusion.6), channel_id=1, source_target_pairs={{0,4},{1,5},{2,6},{3,7},{4,0},{5,1},{6,2},{7,3},{8,12},{9,13},{10,... | collective-permute-start | bytes 393224 | tf_op jit(solution)/shard_map/ppermute | solution.py:576
  64.2 1.9 %collective-permute-done.14.refs_1_ = bf16[2,64,512]{2,1,0:T(8,128)(2,1)S(1)} collective-permute-done((bf16[2,64,512]{2,1,0:T(8,128)(2,1)S(1)}, bf16[2,64,512]{2,1,0:T(8,128)(2,1)S(1)}, u32[]{:S(2)}, u32[]{:S(2)}) %collective-permute-start.14) | collective-permute-done | bytes 131104 | tf_op jit(solution)/shard_map/ppermute | solution.py:576
  66.1 4.0 %collective-permute-done.15.refs_2_ = bf16[2,64,512]{2,1,0:T(8,128)(2,1)S(1)} collective-permute-done((bf16[2,64,512]{2,1,0:T(8,128)(2,1)S(1)}, bf16[2,64,512]{2,1,0:T(8,128)(2,1)S(1)}, u32[]{:S(2)}, u32[]{:S(2)}) %collective-permute-start.15) | collective-permute-done | bytes 131104 | tf_op jit(solution)/shard_map/ppermute | solution.py:576
  70.1 2.2 %dense.1 = (bf16[4,64,512]{2,1,0:T(8,128)(2,1)S(1)}, bf16[4,64,512]{2,1,0:T(8,128)(2,1)S(1)}, bf16[4,192,512]{2,1,0:T(8,128)(2,1)S(1)}, bf16[4,64,512]{2,1,0:T(8,128)(2,1)S(1)}) custom-call(s32[3]{0:T(128)S(1)} %pad_add_fusion.place_ref, bf16[2,64,512]{2,1,0:T(8,128)(2,1)S(1)} %pad_maximum_fusion.4.refs_0_, ...), custom_call_target="tpu_custom_call" | custom-call | tf_op jit(solution)/shard_map/dense/pallas_call | solution.py:282
  72.4 2.2 %collective-permute-done.17.got_ref.after_ref = bf16[4,192,512]{2,1,0:T(8,128)(2,1)S(1)} collective-permute-done((bf16[4,192,512]{2,1,0:T(8,128)(2,1)S(1)}, bf16[4,192,512]{2,1,0:T(8,128)(2,1)S(1)}, u32[]{:S(2)}, u32[]{:S(2)}) %collective-permute-start.17) | collective-permute-done | bytes 786464 | tf_op jit(solution)/shard_map/ppermute | solution.py:571
  75.0 3.7 %collective-permute-start.19 = (bf16[2,64,512]{2,1,0:T(8,128)(2,1)S(1)}, bf16[2,64,512]{2,1,0:T(8,128)(2,1)S(1)}, u32[]{:S(2)}, u32[]{:S(2)}) collective-permute-start(bf16[2,64,512]{2,1,0:T(8,128)(2,1)S(1)} %pad_maximum_fusion.10), channel_id=1, source_target_pairs={{0,4},{1,5},{2,6},{3,7},{4,0},{5,1},{6,2},{7,3},{8,12},{9,13},{10,... | collective-permute-start | bytes 393224 | tf_op jit(solution)/shard_map/ppermute | solution.py:576
  78.9 2.1 %collective-permute-start.21 = (bf16[2,64,512]{2,1,0:T(8,128)(2,1)S(1)}, bf16[2,64,512]{2,1,0:T(8,128)(2,1)S(1)}, u32[]{:S(2)}, u32[]{:S(2)}) collective-permute-start(bf16[2,64,512]{2,1,0:T(8,128)(2,1)S(1)} %get-tuple-element.51), channel_id=1, source_target_pairs={{0,2},{1,3},{2,0},{3,1},{4,6},{5,7},{6,4},{7,5},{8,10},{9,11},{10,... | collective-permute-start | bytes 393224 | tf_op jit(solution)/shard_map/ppermute | solution.py:337
  81.0 1.1 collective-permute-done.18.refs_1_
  82.1 3.6 %collective-permute-done.19.refs_2_ = bf16[2,64,512]{2,1,0:T(8,128)(2,1)S(1)} collective-permute-done((bf16[2,64,512]{2,1,0:T(8,128)(2,1)S(1)}, bf16[2,64,512]{2,1,0:T(8,128)(2,1)S(1)}, u32[]{:S(2)}, u32[]{:S(2)}) %collective-permute-start.19) | collective-permute-done | bytes 131104 | tf_op jit(solution)/shard_map/ppermute | solution.py:576
  85.7 0.6 collective-permute-done.20.refs_3_
  86.3 1.9 %back_products.4 = (bf16[32,64,256]{2,1,0:T(8,128)(2,1)S(1)}, bf16[64,4096]{1,0:T(8,128)(2,1)S(1)}, bf16[64,4096]{1,0:T(8,128)(2,1)S(1)}) custom-call(s32[3]{0:T(128)S(1)} %pad_add_fusion.place_ref, s32[32]{0:T(128)S(1)} %get-tuple-element.98.next2_ref.code_ref, bf16[2,64,512]{2,1,0:T(8,128)(2,1)S(1)} %pad_maximum_fusion.8.refs_0_, ...), custom_call_target="tpu_custom_call" | custom-call | tf_op jit(solution)/shard_map/back_products/pallas_call | solution.py:408
  88.2 1.1 collective-permute-start.25
  89.3 3.2 %back_products.6 = bf16[32,64,256]{2,1,0:T(8,128)(2,1)S(1)} custom-call(s32[32]{0:T(128)S(1)} %get-tuple-element.97.next1_ref.code1_ref.code_ref, bf16[64,4096]{1,0:T(8,128)(2,1)S(1)} %get-tuple-element.48.scaled_ref, bf16[128,256,256]{2,1,0:T(8,128)(2,1)} %tiles_ref.9, f32[1,4096]{1,0:T(1,128)S(1)} %get-tuple-element.46.refs_4_.after_ref), custom_call_target="tpu_custom_call" | custom-call | tf_op jit(solution)/shard_map/back_products/pallas_call | solution.py:419
  92.5 1.3 collective-permute-start.23
  93.8 3.2 %back_products.5.after_ref = bf16[32,64,256]{2,1,0:T(8,128)(2,1)S(1)} custom-call(s32[32]{0:T(128)S(1)} %get-tuple-element.95.code2_ref.code_ref, bf16[64,4096]{1,0:T(8,128)(2,1)S(1)} %get-tuple-element.48.scaled_ref, bf16[128,256,256]{2,1,0:T(8,128)(2,1)} %tiles_ref.9, bf16[1,64,512]{2,1,0:T(8,128)(2,1)S(1)} %get-tuple-element.53.after_ref.own_ref), custom_call_target="tpu_custom_call" | custom-call | tf_op jit(solution)/shard_map/back_products/pallas_call | solution.py:419
  97.0 0.9 collective-permute-start.22
  97.9 2.4 %collective-permute-start.24 = (bf16[1,64,512]{2,1,0:T(8,128)(2,1)S(1)}, bf16[1,64,512]{2,1,0:T(8,128)(2,1)S(1)}, u32[]{:S(2)}, u32[]{:S(2)}) collective-permute-start(bf16[1,64,512]{2,1,0:T(8,128)(2,1)S(1)} %get-tuple-element.54), channel_id=1, source_target_pairs={{0,4},{1,5},{2,6},{3,7},{4,0},{5,1},{6,2},{7,3},{8,12},{9,13},{10,... | collective-permute-start | bytes 196616 | tf_op jit(solution)/shard_map/ppermute | solution.py:337
  100.2 3.2 %back_products.7.after_ref.refs_2_.refs_4_ = bf16[32,64,256]{2,1,0:T(8,128)(2,1)S(1)} custom-call(s32[32]{0:T(128)S(1)} %get-tuple-element.96.code_ref.refs_0_, bf16[64,4096]{1,0:T(8,128)(2,1)S(1)} %get-tuple-element.48.scaled_ref, bf16[128,256,256]{2,1,0:T(8,128)(2,1)} %tiles_ref.9, bf16[32,64,256]{2,1,0:T(8,128)(2,1)S(1)} %back_products.5.after_ref), custom_call_target="tpu_custom_call" | custom-call | tf_op jit(solution)/shard_map/back_products/pallas_call | solution.py:419
  103.6 0.8 gw_order.1
  104.4 2.5 %collective-permute-start.26 = (bf16[64,128]{1,0:T(8,128)(2,1)S(1)}, bf16[64,128]{1,0:T(8,128)(2,1)S(1)}, u32[]{:S(2)}, u32[]{:S(2)}) collective-permute-start(bf16[64,128]{1,0:T(8,128)(2,1)S(1)} %get-tuple-element.56), channel_id=1, source_target_pairs={{0,24},{1,97},{2,26},{3,99},{4,28},{5,101},{6,30},{7,103},{8,0},{9... | collective-permute-start | bytes 49160 | tf_op jit(solution)/shard_map/ppermute | solution.py:543
  107.3 1.2 collective-permute-start.28
  108.4 1.3 collect.2.refs_3_
  109.8 4.3 %collective-permute-done.23.refs_1_ = bf16[32,64,256]{2,1,0:T(8,128)(2,1)S(1)} collective-permute-done((bf16[32,64,256]{2,1,0:T(8,128)(2,1)S(1)}, bf16[32,64,256]{2,1,0:T(8,128)(2,1)S(1)}, u32[]{:S(2)}, u32[]{:S(2)}) %collective-permute-start.23) | collective-permute-done | bytes 1048608 | tf_op jit(solution)/shard_map/ppermute | solution.py:543
  114.0 1.1 collect.3.before_ref
  115.1 1.0 collective-permute-done.27.refs_2_
  116.1 1.3 finish_slabs.1
  117.4 2.6 %collective-permute-start.29 = (bf16[64,4224]{1,0:T(8,128)(2,1)S(1)}, bf16[64,4224]{1,0:T(8,128)(2,1)S(1)}, u32[]{:S(2)}, u32[]{:S(2)}) collective-permute-start(bf16[64,4224]{1,0:T(8,128)(2,1)S(1)} %get-tuple-element.60.after_ref), channel_id=1, source_target_pairs={{0,96},{1,25},{2,98},{3,27},{4,100},{5,29},{6,102},{7,31},{8,104},... | collective-permute-start | bytes 1622024 | tf_op jit(solution)/shard_map/ppermute | solution.py:543
  120.0 1.4 %collective-permute-start.30 = (bf16[64,4224]{1,0:T(8,128)(2,1)S(1)}, bf16[64,4224]{1,0:T(8,128)(2,1)S(1)}, u32[]{:S(2)}, u32[]{:S(2)}) collective-permute-start(bf16[64,4224]{1,0:T(8,128)(2,1)S(1)} %get-tuple-element.61), channel_id=1, source_target_pairs={{0,64},{1,17},{2,66},{3,19},{4,68},{5,21},{6,70},{7,23},{8,72},{9,... | collective-permute-start | bytes 1622024 | tf_op jit(solution)/shard_map/ppermute | solution.py:543
  122.0 3.0 %collective-permute-start.33 = (bf16[2,64,512]{2,1,0:T(8,128)(2,1)S(1)}, bf16[2,64,512]{2,1,0:T(8,128)(2,1)S(1)}, u32[]{:S(2)}, u32[]{:S(2)}) collective-permute-start(bf16[2,64,512]{2,1,0:T(8,128)(2,1)S(1)} %get-tuple-element.66), channel_id=1, source_target_pairs={{0,4},{1,5},{2,6},{3,7},{4,0},{5,1},{6,2},{7,3},{8,12},{9,13},{10,... | collective-permute-start | bytes 393224 | tf_op jit(solution)/shard_map/ppermute | solution.py:576
  125.0 4.6 %collective-permute-done.32.refs_5_ = bf16[2,64,512]{2,1,0:T(8,128)(2,1)S(1)} collective-permute-done((bf16[2,64,512]{2,1,0:T(8,128)(2,1)S(1)}, bf16[2,64,512]{2,1,0:T(8,128)(2,1)S(1)}, u32[]{:S(2)}, u32[]{:S(2)}) %collective-permute-start.32) | collective-permute-done | bytes 131104 | tf_op jit(solution)/shard_map/ppermute | solution.py:576
  129.5 5.0 %collective-permute-done.34.refs_7_ = bf16[2,64,512]{2,1,0:T(8,128)(2,1)S(1)} collective-permute-done((bf16[2,64,512]{2,1,0:T(8,128)(2,1)S(1)}, bf16[2,64,512]{2,1,0:T(8,128)(2,1)S(1)}, u32[]{:S(2)}, u32[]{:S(2)}) %collective-permute-start.34) | collective-permute-done | bytes 131104 | tf_op jit(solution)/shard_map/ppermute | solution.py:576
  134.5 2.2 %collective-permute-done.31.refs_3_ = bf16[64,4224]{1,0:T(8,128)(2,1)S(1)} collective-permute-done((bf16[64,4224]{1,0:T(8,128)(2,1)S(1)}, bf16[64,4224]{1,0:T(8,128)(2,1)S(1)}, u32[]{:S(2)}, u32[]{:S(2)}) %collective-permute-start.31) | collective-permute-done | bytes 540704 | tf_op jit(solution)/shard_map/ppermute | solution.py:543
  136.7 2.0 %finish.1 = (bf16[64,4096]{1,0:T(8,128)(2,1)}, f32[32,64]{1,0:T(8,128)}, bf16[64,4096]{1,0:T(8,128)(2,1)}) custom-call(s32[3]{0:T(128)S(1)} %pad_add_fusion.place_ref, bf16[64,4096]{1,0:T(8,128)(2,1)S(1)} %get-tuple-element.47.grad_ref, bf16[64,4224]{1,0:T(8,128)(2,1)S(1)} %get-tuple-element.59.refs_0_, ...), custom_call_target="tpu_custom_call" | custom-call | tf_op jit(solution)/shard_map/finish/pallas_call | solution.py:522
  (66 shorter events, 3.0 us)
Async XLA Ops:
  0.6 15.5 %collective-permute-start.2 = (bf16[64,4096]{1,0:T(8,128)(2,1)}, bf16[64,4096]{1,0:T(8,128)(2,1)S(1)}, u32[]{:S(2)}, u32[]{:S(2)}) collective-permute-start(bf16[64,4096]{1,0:T(8,128)(2,1)} %bitcast.9), channel_id=1, source_target_pairs={{0,32},{1,9},{2,34},{3,11},{4,36},{5,13},{6,38},{7,15},{8,40},{9,1... | collective-permute-start | bytes 1572872 | tf_op jit(solution)/shard_map/ppermute | solution.py:543
  2.3 15.7 %collective-permute-start.3 = (bf16[64,4096]{1,0:T(8,128)(2,1)}, bf16[64,4096]{1,0:T(8,128)(2,1)S(1)}, u32[]{:S(2)}, u32[]{:S(2)}) collective-permute-start(bf16[64,4096]{1,0:T(8,128)(2,1)} %bitcast.10), channel_id=1, source_target_pairs={{0,64},{1,17},{2,66},{3,19},{4,68},{5,21},{6,70},{7,23},{8,72},{9,... | collective-permute-start | bytes 1572872 | tf_op jit(solution)/shard_map/ppermute | solution.py:543
  5.0 13.0 %collective-permute-start.4 = (bf16[64,4096]{1,0:T(8,128)(2,1)}, bf16[64,4096]{1,0:T(8,128)(2,1)S(1)}, u32[]{:S(2)}, u32[]{:S(2)}) collective-permute-start(bf16[64,4096]{1,0:T(8,128)(2,1)} %bitcast.11), channel_id=1, source_target_pairs={{0,96},{1,25},{2,98},{3,27},{4,100},{5,29},{6,102},{7,31},{8,104},... | collective-permute-start | bytes 1572872 | tf_op jit(solution)/shard_map/ppermute | solution.py:543
  7.5 8.6 %collective-permute-start = (s32[32]{0:T(128)S(1)}, s32[32]{0:T(128)S(1)}, u32[]{:S(2)}, u32[]{:S(2)}) collective-permute-start(s32[32]{0:T(128)S(1)} %get-tuple-element.98.next2_ref.code_ref), channel_id=1, source_target_pairs={{0,16},{1,65},{2,18},{3,67},{4,20},{5,69},{6,22},{7,71},{8,24},{9,... | collective-permute-start | bytes 392 | tf_op jit(solution)/shard_map/ppermute | solution.py:543
  10.7 3.6 %collective-permute-start.1 = (s32[32]{0:T(128)S(1)}, s32[32]{0:T(128)S(1)}, u32[]{:S(2)}, u32[]{:S(2)}) collective-permute-start(s32[32]{0:T(128)S(1)} %get-tuple-element.97.next1_ref.code1_ref.code_ref), channel_id=1, source_target_pairs={{0,24},{1,97},{2,26},{3,99},{4,28},{5,101},{6,30},{7,103},{8,0},{9... | collective-permute-start | bytes 392 | tf_op jit(solution)/shard_map/ppermute | solution.py:543
  14.4 9.0 %collective-permute-start.6 = (s32[32]{0:T(128)S(1)}, s32[32]{0:T(128)S(1)}, u32[]{:S(2)}, u32[]{:S(2)}) collective-permute-start(s32[32]{0:T(128)S(1)} %get-tuple-element.95.code2_ref.code_ref), channel_id=1, source_target_pairs={{0,8},{1,33},{2,10},{3,35},{4,12},{5,37},{6,14},{7,39},{8,16},{9,4... | collective-permute-start | bytes 392 | tf_op jit(solution)/shard_map/ppermute | solution.py:543
  15.0 1.0 copy-start.3
  18.7 35.0 %collective-permute-start.5 = (bf16[32,64,256]{2,1,0:T(8,128)(2,1)S(1)}, bf16[32,64,256]{2,1,0:T(8,128)(2,1)S(1)}, u32[]{:S(2)}, u32[]{:S(2)}) collective-permute-start(bf16[32,64,256]{2,1,0:T(8,128)(2,1)S(1)} %gather_blocks.4.refs_4_), channel_id=1, source_target_pairs={{0,16},{1,65},{2,18},{3,67},{4,20},{5,69},{6,22},{7,71},{8,24},{9,... | collective-permute-start | bytes 3145736 | tf_op jit(solution)/shard_map/ppermute | solution.py:543
  22.7 26.2 %collective-permute-start.7 = (bf16[32,64,256]{2,1,0:T(8,128)(2,1)S(1)}, bf16[32,64,256]{2,1,0:T(8,128)(2,1)S(1)}, u32[]{:S(2)}, u32[]{:S(2)}) collective-permute-start(bf16[32,64,256]{2,1,0:T(8,128)(2,1)S(1)} %gather_blocks.5.refs_4_), channel_id=1, source_target_pairs={{0,8},{1,33},{2,10},{3,35},{4,12},{5,37},{6,14},{7,39},{8,16},{9,4... | collective-permute-start | bytes 3145736 | tf_op jit(solution)/shard_map/ppermute | solution.py:543
  24.1 24.7 %collective-permute-start.8 = (bf16[32,64,256]{2,1,0:T(8,128)(2,1)S(1)}, bf16[32,64,256]{2,1,0:T(8,128)(2,1)S(1)}, u32[]{:S(2)}, u32[]{:S(2)}) collective-permute-start(bf16[32,64,256]{2,1,0:T(8,128)(2,1)S(1)} %gather_blocks.6.refs_4_), channel_id=1, source_target_pairs={{0,24},{1,97},{2,26},{3,99},{4,28},{5,101},{6,30},{7,103},{8,0},{9... | collective-permute-start | bytes 3145736 | tf_op jit(solution)/shard_map/ppermute | solution.py:543
  27.5 5.5 %copy-start.5 = (bf16[4096,64]{0,1:T(8,128)(2,1)S(1)}, bf16[4096,64]{0,1:T(8,128)(2,1)}, u32[]{:S(2)}) copy-start(bf16[4096,64]{0,1:T(8,128)(2,1)} %param.13) | copy-start | bytes 1572868
  33.0 20.7 %copy-start = (bf16[4,8,256,256]{3,2,1,0:T(8,128)(2,1)}, bf16[4,8,256,256]{3,2,1,0:T(8,128)(2,1)S(1)}, u32[]{:S(2)}) copy-start(bf16[4,8,256,256]{3,2,1,0:T(8,128)(2,1)S(1)} %get-tuple-element.37.tiles_ref.refs_5_) | copy-start | bytes 12582916
  33.6 1.6 %collective-permute-start.9 = (bf16[4,64,512]{2,1,0:T(8,128)(2,1)S(1)}, bf16[4,64,512]{2,1,0:T(8,128)(2,1)S(1)}, u32[]{:S(2)}, u32[]{:S(2)}) collective-permute-start(bf16[4,64,512]{2,1,0:T(8,128)(2,1)S(1)} %get-tuple-element.41), channel_id=1, source_target_pairs={{0,1},{1,0},{2,3},{3,2},{4,5},{5,4},{6,7},{7,6},{8,9},{9,8},{10,11... | collective-permute-start | bytes 786440 | tf_op jit(solution)/shard_map/ppermute | solution.py:571
  35.3 7.9 %collective-permute-start.10 = (bf16[2,64,512]{2,1,0:T(8,128)(2,1)S(1)}, bf16[2,64,512]{2,1,0:T(8,128)(2,1)S(1)}, u32[]{:S(2)}, u32[]{:S(2)}) collective-permute-start(bf16[2,64,512]{2,1,0:T(8,128)(2,1)S(1)} %pad_maximum_fusion.1), channel_id=1, source_target_pairs={{0,2},{1,3},{2,4},{3,5},{4,6},{5,7},{6,0},{7,1},{8,10},{9,11},{10,... | collective-permute-start | bytes 393224 | tf_op jit(solution)/shard_map/ppermute | solution.py:576
  37.3 9.9 %collective-permute-start.11 = (bf16[2,64,512]{2,1,0:T(8,128)(2,1)S(1)}, bf16[2,64,512]{2,1,0:T(8,128)(2,1)S(1)}, u32[]{:S(2)}, u32[]{:S(2)}) collective-permute-start(bf16[2,64,512]{2,1,0:T(8,128)(2,1)S(1)} %pad_maximum_fusion.2), channel_id=1, source_target_pairs={{0,4},{1,5},{2,6},{3,7},{4,0},{5,1},{6,2},{7,3},{8,12},{9,13},{10,... | collective-permute-start | bytes 393224 | tf_op jit(solution)/shard_map/ppermute | solution.py:576
  43.2 5.1 %collective-permute-start.12 = (bf16[2,64,512]{2,1,0:T(8,128)(2,1)S(1)}, bf16[2,64,512]{2,1,0:T(8,128)(2,1)S(1)}, u32[]{:S(2)}, u32[]{:S(2)}) collective-permute-start(bf16[2,64,512]{2,1,0:T(8,128)(2,1)S(1)} %pad_maximum_fusion.3), channel_id=1, source_target_pairs={{0,6},{1,7},{2,0},{3,1},{4,2},{5,3},{6,4},{7,5},{8,14},{9,15},{10,... | collective-permute-start | bytes 393224 | tf_op jit(solution)/shard_map/ppermute | solution.py:576
  48.8 4.9 %copy-start.4 = (bf16[4096,64]{0,1:T(8,128)(2,1)S(1)}, bf16[4096,64]{0,1:T(8,128)(2,1)}, u32[]{:S(2)}) copy-start(bf16[4096,64]{0,1:T(8,128)(2,1)} %param.7) | copy-start | bytes 1572868
  53.7 10.2 %copy-start.2 = (bf16[512,512]{1,0:T(8,128)(2,1)S(1)}, bf16[512,512]{1,0:T(8,128)(2,1)}, u32[]{:S(2)}) copy-start(bf16[512,512]{1,0:T(8,128)(2,1)} %refs_5_.1) | copy-start | bytes 1572868
  56.9 1.6 %collective-permute-start.13 = (bf16[4,64,512]{2,1,0:T(8,128)(2,1)S(1)}, bf16[4,64,512]{2,1,0:T(8,128)(2,1)S(1)}, u32[]{:S(2)}, u32[]{:S(2)}) collective-permute-start(bf16[4,64,512]{2,1,0:T(8,128)(2,1)S(1)} %get-tuple-element.43), channel_id=1, source_target_pairs={{0,1},{1,0},{2,3},{3,2},{4,5},{5,4},{6,7},{7,6},{8,9},{9,8},{10,11... | collective-permute-start | bytes 786440 | tf_op jit(solution)/shard_map/ppermute | solution.py:571
  58.5 7.5 %collective-permute-start.14 = (bf16[2,64,512]{2,1,0:T(8,128)(2,1)S(1)}, bf16[2,64,512]{2,1,0:T(8,128)(2,1)S(1)}, u32[]{:S(2)}, u32[]{:S(2)}) collective-permute-start(bf16[2,64,512]{2,1,0:T(8,128)(2,1)S(1)} %pad_maximum_fusion.5), channel_id=1, source_target_pairs={{0,2},{1,3},{2,4},{3,5},{4,6},{5,7},{6,0},{7,1},{8,10},{9,11},{10,... | collective-permute-start | bytes 393224 | tf_op jit(solution)/shard_map/ppermute | solution.py:576
  59.2 10.8 %collective-permute-start.15 = (bf16[2,64,512]{2,1,0:T(8,128)(2,1)S(1)}, bf16[2,64,512]{2,1,0:T(8,128)(2,1)S(1)}, u32[]{:S(2)}, u32[]{:S(2)}) collective-permute-start(bf16[2,64,512]{2,1,0:T(8,128)(2,1)S(1)} %pad_maximum_fusion.6), channel_id=1, source_target_pairs={{0,4},{1,5},{2,6},{3,7},{4,0},{5,1},{6,2},{7,3},{8,12},{9,13},{10,... | collective-permute-start | bytes 393224 | tf_op jit(solution)/shard_map/ppermute | solution.py:576
  63.9 6.2 %collective-permute-start.16 = (bf16[2,64,512]{2,1,0:T(8,128)(2,1)S(1)}, bf16[2,64,512]{2,1,0:T(8,128)(2,1)S(1)}, u32[]{:S(2)}, u32[]{:S(2)}) collective-permute-start(bf16[2,64,512]{2,1,0:T(8,128)(2,1)S(1)} %pad_maximum_fusion.7), channel_id=1, source_target_pairs={{0,6},{1,7},{2,0},{3,1},{4,2},{5,3},{6,4},{7,5},{8,14},{9,15},{10,... | collective-permute-start | bytes 393224 | tf_op jit(solution)/shard_map/ppermute | solution.py:576
  64.2 22.1 %copy-start.1 = (bf16[4,8,256,256]{3,2,1,0:T(8,128)(2,1)S(1)}, bf16[4,8,256,256]{3,2,1,0:T(8,128)(2,1)}, u32[]{:S(2)}) copy-start(bf16[4,8,256,256]{3,2,1,0:T(8,128)(2,1)} %copy-done) | copy-start | bytes 12582916
  72.3 2.4 %collective-permute-start.17 = (bf16[4,192,512]{2,1,0:T(8,128)(2,1)S(1)}, bf16[4,192,512]{2,1,0:T(8,128)(2,1)S(1)}, u32[]{:S(2)}, u32[]{:S(2)}) collective-permute-start(bf16[4,192,512]{2,1,0:T(8,128)(2,1)S(1)} %get-tuple-element.45), channel_id=1, source_target_pairs={{0,1},{1,0},{2,3},{3,2},{4,5},{5,4},{6,7},{7,6},{8,9},{9,8},{10,11... | collective-permute-start | bytes 2359304 | tf_op jit(solution)/shard_map/ppermute | solution.py:571
  74.7 7.4 %collective-permute-start.18 = (bf16[2,64,512]{2,1,0:T(8,128)(2,1)S(1)}, bf16[2,64,512]{2,1,0:T(8,128)(2,1)S(1)}, u32[]{:S(2)}, u32[]{:S(2)}) collective-permute-start(bf16[2,64,512]{2,1,0:T(8,128)(2,1)S(1)} %pad_maximum_fusion.9), channel_id=1, source_target_pairs={{0,2},{1,3},{2,4},{3,5},{4,6},{5,7},{6,0},{7,1},{8,10},{9,11},{10,... | collective-permute-start | bytes 393224 | tf_op jit(solution)/shard_map/ppermute | solution.py:576
  75.0 10.7 %collective-permute-start.19 = (bf16[2,64,512]{2,1,0:T(8,128)(2,1)S(1)}, bf16[2,64,512]{2,1,0:T(8,128)(2,1)S(1)}, u32[]{:S(2)}, u32[]{:S(2)}) collective-permute-start(bf16[2,64,512]{2,1,0:T(8,128)(2,1)S(1)} %pad_maximum_fusion.10), channel_id=1, source_target_pairs={{0,4},{1,5},{2,6},{3,7},{4,0},{5,1},{6,2},{7,3},{8,12},{9,13},{10,... | collective-permute-start | bytes 393224 | tf_op jit(solution)/shard_map/ppermute | solution.py:576
  78.7 7.6 %collective-permute-start.20 = (bf16[2,64,512]{2,1,0:T(8,128)(2,1)S(1)}, bf16[2,64,512]{2,1,0:T(8,128)(2,1)S(1)}, u32[]{:S(2)}, u32[]{:S(2)}) collective-permute-start(bf16[2,64,512]{2,1,0:T(8,128)(2,1)S(1)} %pad_maximum_fusion.11), channel_id=1, source_target_pairs={{0,6},{1,7},{2,0},{3,1},{4,2},{5,3},{6,4},{7,5},{8,14},{9,15},{10,... | collective-permute-start | bytes 393224 | tf_op jit(solution)/shard_map/ppermute | solution.py:576
  78.9 14.9 %collective-permute-start.21 = (bf16[2,64,512]{2,1,0:T(8,128)(2,1)S(1)}, bf16[2,64,512]{2,1,0:T(8,128)(2,1)S(1)}, u32[]{:S(2)}, u32[]{:S(2)}) collective-permute-start(bf16[2,64,512]{2,1,0:T(8,128)(2,1)S(1)} %get-tuple-element.51), channel_id=1, source_target_pairs={{0,2},{1,3},{2,0},{3,1},{4,6},{5,7},{6,4},{7,5},{8,10},{9,11},{10,... | collective-permute-start | bytes 393224 | tf_op jit(solution)/shard_map/ppermute | solution.py:337
  88.2 19.1 %collective-permute-start.25 = (bf16[32,64,256]{2,1,0:T(8,128)(2,1)S(1)}, bf16[32,64,256]{2,1,0:T(8,128)(2,1)S(1)}, u32[]{:S(2)}, u32[]{:S(2)}) collective-permute-start(bf16[32,64,256]{2,1,0:T(8,128)(2,1)S(1)} %get-tuple-element.52.after_ref), channel_id=1, source_target_pairs={{0,16},{1,65},{2,18},{3,67},{4,20},{5,69},{6,22},{7,71},{8,24},{9,... | collective-permute-start | bytes 3145736 | tf_op jit(solution)/shard_map/ppermute | solution.py:543
  92.5 21.5 %collective-permute-start.23 = (bf16[32,64,256]{2,1,0:T(8,128)(2,1)S(1)}, bf16[32,64,256]{2,1,0:T(8,128)(2,1)S(1)}, u32[]{:S(2)}, u32[]{:S(2)}) collective-permute-start(bf16[32,64,256]{2,1,0:T(8,128)(2,1)S(1)} %back_products.6), channel_id=1, source_target_pairs={{0,24},{1,97},{2,26},{3,99},{4,28},{5,101},{6,30},{7,103},{8,0},{9... | collective-permute-start | bytes 3145736 | tf_op jit(solution)/shard_map/ppermute | solution.py:543
  97.0 19.1 %collective-permute-start.22 = (bf16[32,64,256]{2,1,0:T(8,128)(2,1)S(1)}, bf16[32,64,256]{2,1,0:T(8,128)(2,1)S(1)}, u32[]{:S(2)}, u32[]{:S(2)}) collective-permute-start(bf16[32,64,256]{2,1,0:T(8,128)(2,1)S(1)} %back_products.5.after_ref), channel_id=1, source_target_pairs={{0,8},{1,33},{2,10},{3,35},{4,12},{5,37},{6,14},{7,39},{8,16},{9,4... | collective-permute-start | bytes 3145736 | tf_op jit(solution)/shard_map/ppermute | solution.py:543
  97.9 5.8 %collective-permute-start.24 = (bf16[1,64,512]{2,1,0:T(8,128)(2,1)S(1)}, bf16[1,64,512]{2,1,0:T(8,128)(2,1)S(1)}, u32[]{:S(2)}, u32[]{:S(2)}) collective-permute-start(bf16[1,64,512]{2,1,0:T(8,128)(2,1)S(1)} %get-tuple-element.54), channel_id=1, source_target_pairs={{0,4},{1,5},{2,6},{3,7},{4,0},{5,1},{6,2},{7,3},{8,12},{9,13},{10,... | collective-permute-start | bytes 196616 | tf_op jit(solution)/shard_map/ppermute | solution.py:337
  104.4 10.7 %collective-permute-start.26 = (bf16[64,128]{1,0:T(8,128)(2,1)S(1)}, bf16[64,128]{1,0:T(8,128)(2,1)S(1)}, u32[]{:S(2)}, u32[]{:S(2)}) collective-permute-start(bf16[64,128]{1,0:T(8,128)(2,1)S(1)} %get-tuple-element.56), channel_id=1, source_target_pairs={{0,24},{1,97},{2,26},{3,99},{4,28},{5,101},{6,30},{7,103},{8,0},{9... | collective-permute-start | bytes 49160 | tf_op jit(solution)/shard_map/ppermute | solution.py:543
  106.9 9.2 %collective-permute-start.27 = (bf16[64,128]{1,0:T(8,128)(2,1)S(1)}, bf16[64,128]{1,0:T(8,128)(2,1)S(1)}, u32[]{:S(2)}, u32[]{:S(2)}) collective-permute-start(bf16[64,128]{1,0:T(8,128)(2,1)S(1)} %get-tuple-element.57), channel_id=1, source_target_pairs={{0,16},{1,65},{2,18},{3,67},{4,20},{5,69},{6,22},{7,71},{8,24},{9,... | collective-permute-start | bytes 49160 | tf_op jit(solution)/shard_map/ppermute | solution.py:543
  107.3 8.9 %collective-permute-start.28 = (bf16[64,128]{1,0:T(8,128)(2,1)S(1)}, bf16[64,128]{1,0:T(8,128)(2,1)S(1)}, u32[]{:S(2)}, u32[]{:S(2)}) collective-permute-start(bf16[64,128]{1,0:T(8,128)(2,1)S(1)} %get-tuple-element.58), channel_id=1, source_target_pairs={{0,8},{1,33},{2,10},{3,35},{4,12},{5,37},{6,14},{7,39},{8,16},{9,4... | collective-permute-start | bytes 49160 | tf_op jit(solution)/shard_map/ppermute | solution.py:543
  117.4 17.1 %collective-permute-start.29 = (bf16[64,4224]{1,0:T(8,128)(2,1)S(1)}, bf16[64,4224]{1,0:T(8,128)(2,1)S(1)}, u32[]{:S(2)}, u32[]{:S(2)}) collective-permute-start(bf16[64,4224]{1,0:T(8,128)(2,1)S(1)} %get-tuple-element.60.after_ref), channel_id=1, source_target_pairs={{0,96},{1,25},{2,98},{3,27},{4,100},{5,29},{6,102},{7,31},{8,104},... | collective-permute-start | bytes 1622024 | tf_op jit(solution)/shard_map/ppermute | solution.py:543
  120.0 14.5 %collective-permute-start.30 = (bf16[64,4224]{1,0:T(8,128)(2,1)S(1)}, bf16[64,4224]{1,0:T(8,128)(2,1)S(1)}, u32[]{:S(2)}, u32[]{:S(2)}) collective-permute-start(bf16[64,4224]{1,0:T(8,128)(2,1)S(1)} %get-tuple-element.61), channel_id=1, source_target_pairs={{0,64},{1,17},{2,66},{3,19},{4,68},{5,21},{6,70},{7,23},{8,72},{9,... | collective-permute-start | bytes 1622024 | tf_op jit(solution)/shard_map/ppermute | solution.py:543
  121.5 15.2 %collective-permute-start.31 = (bf16[64,4224]{1,0:T(8,128)(2,1)S(1)}, bf16[64,4224]{1,0:T(8,128)(2,1)S(1)}, u32[]{:S(2)}, u32[]{:S(2)}) collective-permute-start(bf16[64,4224]{1,0:T(8,128)(2,1)S(1)} %get-tuple-element.62), channel_id=1, source_target_pairs={{0,32},{1,9},{2,34},{3,11},{4,36},{5,13},{6,38},{7,15},{8,40},{9,1... | collective-permute-start | bytes 1622024 | tf_op jit(solution)/shard_map/ppermute | solution.py:543
  121.9 7.7 %collective-permute-start.32 = (bf16[2,64,512]{2,1,0:T(8,128)(2,1)S(1)}, bf16[2,64,512]{2,1,0:T(8,128)(2,1)S(1)}, u32[]{:S(2)}, u32[]{:S(2)}) collective-permute-start(bf16[2,64,512]{2,1,0:T(8,128)(2,1)S(1)} %get-tuple-element.65), channel_id=1, source_target_pairs={{0,2},{1,3},{2,4},{3,5},{4,6},{5,7},{6,0},{7,1},{8,10},{9,11},{10,... | collective-permute-start | bytes 393224 | tf_op jit(solution)/shard_map/ppermute | solution.py:576
  122.0 7.6 %collective-permute-start.33 = (bf16[2,64,512]{2,1,0:T(8,128)(2,1)S(1)}, bf16[2,64,512]{2,1,0:T(8,128)(2,1)S(1)}, u32[]{:S(2)}, u32[]{:S(2)}) collective-permute-start(bf16[2,64,512]{2,1,0:T(8,128)(2,1)S(1)} %get-tuple-element.66), channel_id=1, source_target_pairs={{0,4},{1,5},{2,6},{3,7},{4,0},{5,1},{6,2},{7,3},{8,12},{9,13},{10,... | collective-permute-start | bytes 393224 | tf_op jit(solution)/shard_map/ppermute | solution.py:576
  129.5 5.0 %collective-permute-start.34 = (bf16[2,64,512]{2,1,0:T(8,128)(2,1)S(1)}, bf16[2,64,512]{2,1,0:T(8,128)(2,1)S(1)}, u32[]{:S(2)}, u32[]{:S(2)}) collective-permute-start(bf16[2,64,512]{2,1,0:T(8,128)(2,1)S(1)} %get-tuple-element.67), channel_id=1, source_target_pairs={{0,6},{1,7},{2,0},{3,1},{4,2},{5,3},{6,4},{7,5},{8,14},{9,15},{10,... | collective-permute-start | bytes 393224 | tf_op jit(solution)/shard_map/ppermute | solution.py:576
